TPU v7x, 32 devices: a whole 2x2x4 slice. The times are simulated.
32 devices in a mesh: seq: 2 (over core), head: 4 (over z), dp: 4 (over y, x).
Axes of the slice: x: 2, y: 2, z: 4, core: 2. Of those that a mesh axis runs over, the one named last changes fastest.
Arguments:
- tokens: bfloat16 [4, 256, 4096], P('dp', 'seq', 'head'), may hold values from -6 to 6
- w_qkv: bfloat16 [4096, 3, 512], P(('seq', 'dp'), None, 'head'), may hold values from -0.09375 to 0.09375
- w_lr: bfloat16 [4096, 4], P(None, 'head'), may hold values from -0.1875 to 0.1875
- w_out: bfloat16 [4096, 512], P(('seq', 'dp'), 'head'), may hold values from -0.25 to 0.25
- w1_init: float32 [4, 128, 512], P('head'), may hold values from -0.5 to 0.5
- w2_init: float32 [4, 512, 128], P('head'), may hold values from -0.25 to 0.25
- d_out: bfloat16 [4, 256, 4096], P('dp', 'seq', 'head'), may hold values from -6 to 6
Outputs:
- out: bfloat16 [4, 256, 4096], P('dp', 'seq', 'head')
- d_tokens: bfloat16 [4, 256, 4096], P('dp', 'seq', 'head')
- d_w1_init: float32 [4, 128, 512], P('head', None, ('seq', 'dp'))
- d_w2_init: float32 [4, 512, 128], P('head', ('seq', 'dp'))
All inputs are finite; a program needn't handle non-finite values.
Results may differ from a plain program's by a relative error of at most 0.018.
Values may be sent and summed in bfloat16 or wider, within the bound.
No kernel may reach another device: no remote copies, remote signals or barrier semaphores. Data moves between devices by JAX's collectives and lax.ppermute only.
A program may use at most 64 MiB of HBM per device.

v0:
```python
import functools

import jax
import jax.numpy as jnp
from jax import lax
from jax.experimental import pallas as pl
from jax.experimental.pallas import tpu as pltpu
from jax.sharding import PartitionSpec as P

MB = 64
EPSILON = 1e-06
BASE_RATE = 0.1
GELU_SCALE = 0.7978845608028654
GELU_CUBIC = 0.044715
NN = ((1,), (0,))
NT = ((1,), (1,))
TN = ((0,), (0,))
EXTRA = 16
UNROLL_LIMIT = 8
F32 = jnp.float32
BF16 = jnp.bfloat16


def mm(left, right, dims):
    return lax.dot_general(
        left.astype(BF16), right.astype(BF16), (dims, ((), ())), preferred_element_type=F32
    )


def padded(lines):
    return jnp.concatenate([lines, jnp.zeros_like(lines)], axis=1)


def mean(rows):
    return jnp.mean(rows, axis=-1, keepdims=True)


def gelu_parts(v):
    square = v * v
    bend = jnp.tanh(v * (GELU_SCALE + (GELU_SCALE * GELU_CUBIC) * square))
    half = 0.5 + 0.5 * bend
    slope = GELU_SCALE + (3.0 * GELU_SCALE * GELU_CUBIC) * square
    bell = 0.5 - 0.5 * bend * bend
    lean = bell * slope
    second = 2.0 * lean * (1.0 - v * bend * slope) + (6.0 * GELU_SCALE * GELU_CUBIC) * square * bell
    return v * half, half + v * lean, second


def gelu_two(v):
    square = v * v
    bend = jnp.tanh(v * (GELU_SCALE + (GELU_SCALE * GELU_CUBIC) * square))
    half = 0.5 + 0.5 * bend
    slope = GELU_SCALE + (3.0 * GELU_SCALE * GELU_CUBIC) * square
    return v * half, half + v * ((0.5 - 0.5 * bend * bend) * slope)


def mate(index, step, count):
    if count & (count - 1) == 0:
        return index ^ step
    return (index + step) % count


def hop(array, axis, step):
    count = lax.axis_size(axis)
    return lax.ppermute(array, axis, [(mate(i, step, count), i) for i in range(count)])


def peers_of(array, axis):
    return [array] + [hop(array, axis, j) for j in range(1, lax.axis_size(axis))]


def sent_to(arrays, axis):
    count = lax.axis_size(axis)
    back = [arrays[0]]
    for j in range(1, count):
        back.append(lax.ppermute(arrays[j], axis, [(i, mate(i, j, count)) for i in range(count)]))
    return back


def over_seq(near):
    return sum([list(pieces) for pieces in zip(*[peers_of(piece, "seq") for piece in near])], [])


def owner_of(place_ref, seqs, dps, share, j, d):
    seq, dp = place_ref[0], place_ref[2]
    k = mate(seq, j, seqs) * dps + mate(dp, d, dps)
    return k // share, k % share


def rate_line(block, depth):
    rows = block.astype(F32)
    return jnp.concatenate([rows[i : i + 1, :] for i in range(depth // 128)], axis=1)


def outer_kernel(seqs, heads, dps, share, place_ref, tok_ref, dout_ref, *refs):
    w_refs = refs[: seqs * dps]
    out_refs = refs[seqs * dps : seqs * dps + heads]
    tok_s, dout_s, acc = refs[seqs * dps + heads :]
    rows, features = tok_ref.shape
    depth = features // share
    for r in range(share):
        tok_s[r] = tok_ref[:, r * depth : (r + 1) * depth]
        dout_s[r] = dout_ref[:, r * depth : (r + 1) * depth]
    acc[...] = jnp.zeros_like(acc)
    for j in range(seqs):
        for d in range(dps):
            w = w_refs[j * dps + d]
            h, r = owner_of(place_ref, seqs, dps, share, j, d)
            line = rate_line(w[depth:, :], depth)
            logit = mm(jnp.broadcast_to(line, (EXTRA, depth)), tok_s[r], NT)
            back = mm(dout_s[r], w[0:depth, :], NN)
            acc[h] = acc[h] + jnp.concatenate([back, logit], axis=0)
    first_half = lax.broadcasted_iota(jnp.int32, (EXTRA, rows), 0) < EXTRA // 2
    for j in range(heads):
        total = acc[mate(place_ref[1], j, heads)]
        out_refs[j][0:rows, :] = total[0:rows].astype(BF16)
        logit = total[rows:]
        high = logit.astype(BF16).astype(F32)
        out_refs[j][rows:, :] = jnp.where(first_half, high, logit - high).astype(BF16)


def inner_projection_kernel(seqs, heads, dps, share, place_ref, tok_ref, *refs):
    w_refs = refs[: 2 * seqs * dps]
    out_refs = refs[2 * seqs * dps : 2 * seqs * dps + heads]
    tok_s, acc = refs[2 * seqs * dps + heads :]
    rows, features = tok_ref.shape
    depth = features // share
    half = depth // 2
    for r in range(share):
        tok_s[r] = tok_ref[:, r * depth : (r + 1) * depth]
    acc[...] = jnp.zeros_like(acc)
    for part in range(2):
        for j in range(seqs):
            for d in range(dps):
                w = w_refs[(part * seqs + j) * dps + d]
                h, r = owner_of(place_ref, seqs, dps, share, j, d)
                wide = jnp.concatenate([w[c * half : (c + 1) * half, :] for c in range(3)], axis=1)
                acc[h] = acc[h] + mm(tok_s[r][:, part * half : (part + 1) * half], wide, NN)
    for j in range(heads):
        out_refs[j][...] = acc[mate(place_ref[1], j, heads)].astype(BF16)


def inner_kernel(seqs, dps, place_ref, *refs):
    x_refs, y_refs = refs[:seqs], refs[seqs : 2 * seqs]
    w1_ref, w2_ref, res_ref = refs[2 * seqs : 2 * seqs + 3]
    dw_refs = refs[2 * seqs + 3 : 2 * seqs + 3 + dps]
    (
        qs, ks, vs, ds, es, sg, os, lg,
        w1c, w2c, w1b, w2b,
        x2s, g1s, pgs, gfs, xqs, zqs, dx2s, dg1s,
        dys, ns, rs, ss, cs, g2s, dg2s, dks, des, ws,
    ) = refs[2 * seqs + 3 + dps :]
    rows = x_refs[0].shape[0]
    hd = y_refs[0].shape[1]
    width = 4 * hd
    blocks = seqs * rows // MB
    per = rows // MB
    place = place_ref[0]

    for j in range(seqs):
        owner = mate(place, j, seqs)
        at = pl.ds(pl.multiple_of(owner * rows, rows), rows)
        qs[at, :] = x_refs[j][:, 0:hd]
        ks[at, :] = x_refs[j][:, hd : 2 * hd]
        vs[at, :] = x_refs[j][:, 2 * hd : 3 * hd]
        ds[at, :] = y_refs[j][0:rows, :]
        logit = y_refs[j][rows : rows + 8, :] + y_refs[j][rows + 8 : rows + 16, :]
        gate = jax.nn.sigmoid(logit)
        scaled = (BASE_RATE / hd) * gate
        for b in range(per):
            es[owner * per + b] = padded(scaled[:, b * MB : (b + 1) * MB])
            sg[owner * per + b] = padded((scaled * (1.0 - gate))[:, b * MB : (b + 1) * MB])

    w1c[...] = w1_ref[...]
    start = w2_ref[...]
    w2c[...] = (start - mean(start)).T

    at_row = lax.broadcasted_iota(jnp.int32, (MB, MB), 0)
    at_col = lax.broadcasted_iota(jnp.int32, (MB, MB), 1)
    causal = at_col <= at_row
    diagonal = at_col == at_row

    def to_column(line):
        return jnp.sum(jnp.where(diagonal, line, 0.0), axis=1, keepdims=True)

    def to_line(column):
        return jnp.sum(jnp.where(diagonal, column, 0.0), axis=0, keepdims=True)

    def at_block(i):
        if isinstance(i, int):
            return slice(i * MB, (i + 1) * MB)
        return pl.ds(pl.multiple_of(i * MB, MB), MB)

    def forward(i):
        at = at_block(i)
        q, k, v, d_o = qs[at, :], ks[at, :], vs[at, :], ds[at, :]
        line = es[i][0:1, 0:MB]
        e = to_column(line)
        mask = jnp.where(causal, line, 0.0)
        w1 = w1c[...].astype(BF16)
        w2 = w2c[...].astype(BF16)
        w1b[i] = w1
        w2b[i] = w2
        kb, qb = k.astype(BF16), q.astype(BF16)
        gap = v - k
        gap = gap - mean(gap)
        both = mm(jnp.concatenate([kb, qb], axis=0), w1, NN)
        x2, g1, gg1 = gelu_parts(both[:MB])
        x2b = x2.astype(BF16)
        c = mm(x2b, w2, NT)
        var = mean(c * c)
        cross = mean(gap * c)
        s = lax.rsqrt(var + EPSILON)
        n = c * s
        cc = var * s * s - s * cross
        r = n - gap
        g2 = s * (r - n * cc)
        g2b = g2.astype(BF16)
        p = mm(g2b, w2, NN)
        g1f = p * g1
        w1c[...] = w1c[...] - mm(k, e * g1f, TN)
        w2c[...] = w2c[...] - mm(e * g2, x2b, TN)
        g1b = g1f.astype(BF16)
        b1 = mm(qb, kb, NT)
        a1 = (b1 * mask).astype(BF16)
        zq = both[MB:] - mm(a1, g1b, NN)
        xq, gq = gelu_two(zq)
        xqb = xq.astype(BF16)
        b2 = mm(xqb, x2b, NT)
        a2 = (b2 * mask).astype(BF16)
        y = mm(xqb, w2, NT) - mm(a2, g2b, NN)
        sq = lax.rsqrt(mean(y * y) + EPSILON)
        nq = y * sq
        os[at, 3 * hd : 4 * hd] = (q + nq).astype(BF16)
        dy = sq * (d_o - mean(d_o) - nq * mean(d_o * nq))
        dyb = dy.astype(BF16)
        da2 = -mm(dyb, g2b, NT)
        db2 = (da2 * mask).astype(BF16)
        dg2s[i] = -mm(a2, dyb, TN)
        dxq = mm(dyb, w2, NN) + mm(db2, x2b, NN)
        dx2s[i] = mm(db2, xqb, TN)
        dzq = (dxq * gq).astype(BF16)
        da1 = -mm(dzq, g1b, NT)
        db1 = (da1 * mask).astype(BF16)
        dg1s[i] = -mm(a1, dzq, TN)
        dq = d_o + mm(dzq, w1, NT) + mm(db1, kb, NN)
        os[at, 0:hd] = dq.astype(BF16)
        dks[i] = mm(db1, qb, TN)
        de = jnp.sum(jnp.where(causal, da2 * b2 + da1 * b1, 0.0), axis=0, keepdims=True)
        des[i] = padded(jnp.broadcast_to(de, (8, MB)))
        x2s[i] = x2b
        g1s[i] = g1
        pgs[i] = p * gg1
        gfs[i] = g1f
        xqs[i] = xqb
        zqs[i] = dzq
        dys[i] = dyb
        ns[i] = n
        rs[i] = r
        ss[i] = jnp.broadcast_to(s, (MB, hd))
        cs[i] = jnp.broadcast_to(cc, (MB, hd))
        g2s[i] = g2

    def backward(i):
        at = at_block(i)
        q, k = qs[at, :], ks[at, :]
        e = to_column(es[i][0:1, 0:MB])
        w1, w2 = w1b[i], w2b[i]
        d1, d2 = w1c[...].astype(BF16), w2c[...].astype(BF16)
        x2b, g1, g1f, g2 = x2s[i], g1s[i], gfs[i], g2s[i]
        n, s, cc = ns[i], ss[i], cs[i]
        dh1 = -mm(k, d1, NN)
        dh2 = -mm(x2b, d2, NT)
        dg1 = dg1s[i] + e * dh1
        dp = (dg1 * g1).astype(BF16)
        dg2 = dg2s[i] + e * dh2 + mm(dp, w2, NT)
        dt = s * dg2
        mt = mean(dt * n)
        dr = dt - mean(dt) - n * mt
        dn = dr - cc * dt - rs[i] * mt
        du = s * (dn - mean(dn) - n * (mean(dn * n) + mean(dg2 * g2)))
        dub = du.astype(BF16)
        mixed = jnp.concatenate([(-e * g2).astype(BF16), dub], axis=1)
        dx2 = dx2s[i] + mm(mixed, jnp.concatenate([d2, w2], axis=0), NN)
        dz1 = (dg1 * pgs[i] + dx2 * g1).astype(BF16)
        mixed = jnp.concatenate([(-e * g1f).astype(BF16), dz1], axis=1)
        dk = dks[i] + dr + mm(mixed, jnp.concatenate([d1, w1], axis=1), NT)
        w1c[...] = w1c[...] + mm(
            jnp.concatenate([q, k], axis=0), jnp.concatenate([zqs[i], dz1], axis=0), TN
        )
        w2c[...] = w2c[...] + mm(
            jnp.concatenate([dys[i].astype(F32), du, g2], axis=0),
            jnp.concatenate([xqs[i], x2b, dp], axis=0),
            TN,
        )
        extra = jnp.sum(g1f * dh1, axis=1, keepdims=True) + jnp.sum(
            g2 * dh2, axis=1, keepdims=True
        )
        line = (des[i][0:1, 0:MB] + to_line(extra)) * sg[i][0:1, 0:MB]
        lg[i] = padded(jnp.broadcast_to(line, (8, MB)))
        os[at, hd : 2 * hd] = dk.astype(BF16)
        os[at, 2 * hd : 3 * hd] = (-dr).astype(BF16)

    def loop(step, order):
        if blocks <= UNROLL_LIMIT:
            for i in range(blocks):
                step(order(i))
        else:
            lax.fori_loop(0, blocks, lambda i, unused: (step(order(i)), unused)[1], 0)

    loop(forward, lambda i: i)
    w1c[...] = jnp.zeros_like(w1c)
    w2c[...] = jnp.zeros_like(w2c)
    loop(backward, lambda i: blocks - 1 - i)

    res_ref[0:rows, :] = os[pl.ds(pl.multiple_of(place * rows, rows), rows), :]
    res_ref[rows:, :] = jnp.zeros((EXTRA, width), BF16)
    first_row = lax.broadcasted_iota(jnp.int32, (EXTRA, rows), 0) == 0
    lines = jnp.concatenate([lg[place * per + b][0:1, 0:MB] for b in range(per)], axis=1)
    lines = jnp.where(first_row, jnp.broadcast_to(lines, (EXTRA, rows)), 0.0)
    res_ref[rows:, 0:rows] = lines.astype(BF16)

    part = dw_refs[0].shape[0]
    ws[:, 0:hd] = w1c[...].T
    ws[:, hd : 2 * hd] = w2c[...].T
    for d in range(dps):
        first = (place * dps + mate(place_ref[2], d, dps)) * part
        dw_refs[d][...] = ws[pl.ds(pl.multiple_of(first, part), part), :]


def output_kernel(seqs, heads, dps, share, place_ref, *refs):
    got_refs, refs = refs[:heads], refs[heads:]
    o_refs, w_refs = refs[: seqs * dps], refs[seqs * dps : 3 * seqs * dps]
    out_ref, dtok_ref, got, out_s, grad_s = refs[3 * seqs * dps :]
    hd = o_refs[0].shape[1]
    rows, features = out_ref.shape
    depth = features // share
    half = depth // 2
    for j in range(heads):
        got[mate(place_ref[1], j, heads)] = got_refs[j][...]
    out_s[...] = jnp.zeros_like(out_s)
    grad_s[...] = jnp.zeros_like(grad_s)
    for j in range(seqs):
        for d in range(dps):
            o = o_refs[j * dps + d]
            h, r = owner_of(place_ref, seqs, dps, share, j, d)
            out_s[r] = out_s[r] + mm(got[h, 0:rows, 3 * hd :], o[0:depth, :], NT)
            line = rate_line(o[depth:, :], depth)
            logit = got[h, rows:, 0:rows].astype(F32).T
            grad = [mm(logit, jnp.broadcast_to(line, (EXTRA, depth)), NN)]
            mine = got[h, 0:rows, 0 : 3 * hd]
            halves = []
            for part in range(2):
                w = w_refs[(part * seqs + j) * dps + d]
                wide = jnp.concatenate([w[c * half : (c + 1) * half, :] for c in range(3)], axis=1)
                halves.append(mm(mine, wide, NT))
            grad_s[r] = grad_s[r] + grad[0] + jnp.concatenate(halves, axis=1)
    for r in range(share):
        out_ref[:, r * depth : (r + 1) * depth] = out_s[r].astype(BF16)
        dtok_ref[:, r * depth : (r + 1) * depth] = grad_s[r].astype(BF16)


VMEM = pl.BlockSpec(memory_space=pltpu.VMEM)
SMEM = pl.BlockSpec(memory_space=pltpu.SMEM)
PARAMS = pltpu.CompilerParams(vmem_limit_bytes=48 * 1024 * 1024)


def call(kernel, outs, operands, scratch=()):
    return pl.pallas_call(
        kernel,
        out_shape=outs,
        in_specs=[SMEM] + [VMEM] * (len(operands) - 1),
        out_specs=jax.tree.map(lambda unused: VMEM, outs),
        scratch_shapes=list(scratch),
        compiler_params=PARAMS,
    )(*operands)


def body(tokens, w_qkv, w_lr, w_out, w1_init, w2_init, d_out):
    seqs, heads, dps = (lax.axis_size(a) for a in ("seq", "head", "dp"))
    share = seqs * dps // heads
    rows, features = tokens.shape[1:]
    depth, unused, hd = w_qkv.shape
    inner = w1_init.shape[2]
    blocks = seqs * rows // MB
    place = jnp.stack([lax.axis_index(a).astype(jnp.int32) for a in ("seq", "head", "dp")])
    sizes = (seqs, heads, dps, share)

    pairs = []
    for seq in range(seqs):
        for head in range(heads):
            for dp in range(dps):
                k = seq * dps + dp
                target = head * share + k % share
                to = ((target // dps) * heads + k // share) * dps + target % dps
                pairs.append(((seq * heads + head) * dps + dp, to))

    def swapped(array):
        return lax.ppermute(array, ("seq", "head", "dp"), pairs)

    half = depth // 2
    lines = w_lr[:, 0].reshape(seqs * dps, depth // 128, 128)
    line = lax.dynamic_index_in_dim(
        lines, lax.axis_index("seq") * dps + lax.axis_index("dp"), 0, keepdims=False
    )
    line = jnp.pad(line, ((0, EXTRA - depth // 128), (0, 0)))
    outer_w = swapped(jnp.concatenate([w_out, line], axis=0))
    by_kind = w_qkv.transpose(1, 0, 2)
    first_w = swapped(by_kind[:, :half].reshape(3 * half, hd))
    second = by_kind[:, half:].reshape(3 * half, hd)
    second_w = swapped(second)
    outer_near = peers_of(outer_w, "dp")
    first_near = [first_w, hop(first_w, "dp", 1), hop(first_w, "dp", 2)]
    second_w, *outer_near = lax.optimization_barrier((second_w, *outer_near))
    second_near = [second_w, hop(second_w, "dp", 1), hop(second_w, "dp", 2)]
    outer_ws = over_seq(outer_near)
    if dps == 4:
        first_near[1], second_near[2], unused = lax.optimization_barrier(
            (first_near[1], second_near[2], outer_ws[-1])
        )
        first_near.append(hop(first_near[1], "dp", 2))
        second_near.append(hop(second_near[2], "dp", 1))
    else:
        first_near += [hop(first_w, "dp", j) for j in range(3, dps)]
        second_near += [hop(second_w, "dp", j) for j in range(3, dps)]
    inner_ws = over_seq(first_near) + over_seq(second_near)

    def summed(arrays):
        return functools.reduce(lambda a, b: a + b, [a.astype(F32) for a in arrays])

    outer_part = call(
        functools.partial(outer_kernel, *sizes),
        (jax.ShapeDtypeStruct((rows + EXTRA, hd), BF16),) * heads,
        (place, tokens[0], d_out[0], *outer_ws),
        [pltpu.VMEM((share, rows, features // share), BF16)] * 2
        + [pltpu.VMEM((heads, rows + EXTRA, hd), F32)],
    )
    outer_all = peers_of(summed(sent_to(outer_part, "head")), "seq")
    own_tokens, unused = lax.optimization_barrier((tokens[0], outer_part[0]))
    inner_part = call(
        functools.partial(inner_projection_kernel, *sizes),
        (jax.ShapeDtypeStruct((rows, 3 * hd), BF16),) * heads,
        (place, own_tokens, *inner_ws),
        [
            pltpu.VMEM((share, rows, features // share), BF16),
            pltpu.VMEM((heads, rows, 3 * hd), F32),
        ],
    )
    inner_all = peers_of(summed(sent_to(inner_part, "head")), "seq")

    long = seqs * rows
    scratch = (
        [pltpu.VMEM((long, hd), F32)] * 4
        + [pltpu.VMEM((blocks, 8, 2 * MB), F32)] * 2
        + [pltpu.VMEM((long, 4 * hd), BF16), pltpu.VMEM((blocks, 8, 2 * MB), F32)]
        + [pltpu.VMEM((hd, inner), F32)] * 2
        + [pltpu.VMEM((blocks, hd, inner), BF16)] * 2
        + [pltpu.VMEM((blocks, MB, inner), t) for t in (BF16, F32, F32, F32, BF16, BF16, F32, F32)]
        + [pltpu.VMEM((blocks, MB, hd), t) for t in (BF16, F32, F32, F32, F32, F32, F32, F32)]
        + [pltpu.VMEM((blocks, 8, 2 * MB), F32), pltpu.VMEM((inner, 2 * hd), F32)]
    )
    part = inner // (seqs * dps)
    result, *d_inner = call(
        functools.partial(inner_kernel, seqs, dps),
        (jax.ShapeDtypeStruct((rows + EXTRA, 4 * hd), BF16),)
        + (jax.ShapeDtypeStruct((part, 2 * hd), F32),) * dps,
        (place, *inner_all, *outer_all, w1_init[0], w2_init[0]),
        scratch,
    )
    got = peers_of(result, "head")
    unused, *d_inner = lax.optimization_barrier((got[1], *d_inner))
    shares = summed(sent_to(d_inner, "dp"))
    out, d_tokens = call(
        functools.partial(output_kernel, *sizes),
        (jax.ShapeDtypeStruct((rows, features), BF16),) * 2,
        (place, *got, *outer_ws, *inner_ws),
        [
            pltpu.VMEM((heads, rows + EXTRA, 4 * hd), BF16),
            pltpu.VMEM((share, rows, features // share), F32),
            pltpu.VMEM((share, rows, features // share), F32),
        ],
    )
    return (out[None], d_tokens[None], shares[:, :hd].transpose(1, 0)[None], shares[:, hd:][None])


def solution(mesh):
    placed = (
        P("dp", "seq", "head"),
        P(("seq", "dp"), None, "head"),
        P(None, "head"),
        P(("seq", "dp"), "head"),
        P("head", None, None),
        P("head", None, None),
        P("dp", "seq", "head"),
    )
    return jax.shard_map(
        body,
        mesh=mesh,
        in_specs=placed,
        out_specs=(
            P("dp", "seq", "head"),
            P("dp", "seq", "head"),
            P("head", None, ("seq", "dp")),
            P("head", ("seq", "dp"), None),
        ),
        check_vma=False,
    )
```

profile of v0, /device:TPU:0, one launch (start us, length us, event | category | flops | bytes accessed | tf_op | source)
XLA Modules:
  0.0 112.9 jit_solution(1594365091289788612)
XLA Ops:
  0.7 0.7 copy-done
  1.4 0.9 fusion.1
  2.3 0.7 collective-permute-start.1
  3.0 1.1 fusion.2
  4.1 0.7 collective-permute-start.9
  4.8 0.7 collective-permute-start
  5.5 3.0 %collective-permute-start.2 = (bf16[528,128]{1,0:T(8,128)(2,1)S(1)}, bf16[528,128]{1,0:T(8,128)(2,1)S(1)}, u32[]{:S(2)}, u32[]{:S(2)}) collective-permute-start(bf16[528,128]{1,0:T(8,128)(2,1)S(1)} %collective-permute-done.1.refs_0_.refs_4_), channel_id=1, source_target_pairs={{1,0},{0,1},{3,2},{2,3},{5,4},{4,5},{7,6},{6,7},{9,8},{8,9},{11,10... | collective-permute-start | bytes 405512 | tf_op jit(solution)/shard_map/ppermute | solution.py:65
  8.5 9.7 %collective-permute-start.3 = (bf16[528,128]{1,0:T(8,128)(2,1)S(1)}, bf16[528,128]{1,0:T(8,128)(2,1)S(1)}, u32[]{:S(2)}, u32[]{:S(2)}) collective-permute-start(bf16[528,128]{1,0:T(8,128)(2,1)S(1)} %collective-permute-done.1.refs_0_.refs_4_), channel_id=1, source_target_pairs={{2,0},{3,1},{0,2},{1,3},{6,4},{7,5},{4,6},{5,7},{10,8},{11,9},{8,1... | collective-permute-start | bytes 405512 | tf_op jit(solution)/shard_map/ppermute | solution.py:65
  18.2 1.5 %collective-permute-start.10 = (bf16[768,128]{1,0:T(8,128)(2,1)S(1)}, bf16[768,128]{1,0:T(8,128)(2,1)S(1)}, u32[]{:S(2)}, u32[]{:S(2)}) collective-permute-start(bf16[768,128]{1,0:T(8,128)(2,1)S(1)} %collective-permute-done.9.refs_0_.refs_12_), channel_id=1, source_target_pairs={{1,0},{0,1},{3,2},{2,3},{5,4},{4,5},{7,6},{6,7},{9,8},{8,9},{11,10... | collective-permute-start | bytes 589832 | tf_op jit(solution)/shard_map/ppermute | solution.py:65
  19.7 11.4 %collective-permute-done.3.refs_2_.refs_6_ = bf16[528,128]{1,0:T(8,128)(2,1)S(1)} collective-permute-done((bf16[528,128]{1,0:T(8,128)(2,1)S(1)}, bf16[528,128]{1,0:T(8,128)(2,1)S(1)}, u32[]{:S(2)}, u32[]{:S(2)}) %collective-permute-start.3) | collective-permute-done | bytes 135200 | tf_op jit(solution)/shard_map/ppermute | solution.py:65
  31.0 2.5 %collective-permute-start.11 = (bf16[768,128]{1,0:T(8,128)(2,1)S(1)}, bf16[768,128]{1,0:T(8,128)(2,1)S(1)}, u32[]{:S(2)}, u32[]{:S(2)}) collective-permute-start(bf16[768,128]{1,0:T(8,128)(2,1)S(1)} %collective-permute-done.refs_8_.refs_20_), channel_id=1, source_target_pairs={{2,0},{3,1},{0,2},{1,3},{6,4},{7,5},{4,6},{5,7},{10,8},{11,9},{8,1... | collective-permute-start | bytes 589832 | tf_op jit(solution)/shard_map/ppermute | solution.py:65
  33.5 0.5 collective-permute-start.8
  33.9 0.7 copy-done.11
  34.6 0.3 collective-permute-start.12
  34.9 0.5 collective-permute-start.5
  35.4 0.7 copy-done.2
  36.1 0.6 copy-done.14
  36.7 0.7 copy-done.5
  37.4 1.8 %collective-permute-done.11.refs_10_.refs_22_ = bf16[768,128]{1,0:T(8,128)(2,1)S(1)} collective-permute-done((bf16[768,128]{1,0:T(8,128)(2,1)S(1)}, bf16[768,128]{1,0:T(8,128)(2,1)S(1)}, u32[]{:S(2)}, u32[]{:S(2)}) %collective-permute-start.11) | collective-permute-done | bytes 196640 | tf_op jit(solution)/shard_map/ppermute | solution.py:65
  39.2 0.2 collective-permute-start.7
  39.4 0.6 copy-done.8
  40.1 3.4 %collective-permute-done.12.refs_2_.refs_14_ = bf16[768,128]{1,0:T(8,128)(2,1)S(1)} collective-permute-done((bf16[768,128]{1,0:T(8,128)(2,1)S(1)}, bf16[768,128]{1,0:T(8,128)(2,1)S(1)}, u32[]{:S(2)}, u32[]{:S(2)}) %collective-permute-start.12) | collective-permute-done | bytes 196640 | tf_op jit(solution)/shard_map/ppermute | solution.py:65
  43.4 1.0 collective-permute-start.18
  44.4 0.7 copy-done.17
  45.1 0.5 collective-permute-start.16
  45.6 0.6 copy-done.20
  46.2 1.9 %collective-permute-start.13 = (bf16[768,128]{1,0:T(8,128)(2,1)S(1)}, bf16[768,128]{1,0:T(8,128)(2,1)S(1)}, u32[]{:S(2)}, u32[]{:S(2)}) collective-permute-start(bf16[768,128]{1,0:T(8,128)(2,1)S(1)} %collective-permute-done.10.refs_1_.refs_13_), channel_id=1, source_target_pairs={{2,0},{3,1},{0,2},{1,3},{6,4},{7,5},{4,6},{5,7},{10,8},{11,9},{8,1... | collective-permute-start | bytes 589832 | tf_op jit(solution)/shard_map/ppermute | solution.py:65
  48.1 0.6 copy-done.23
  48.8 1.0 collective-permute-start.19
  49.8 0.6 collective-permute-done.18.refs_9_.refs_21_
  50.3 0.5 collective-permute-start.22
  50.9 2.2 %collective-permute-done.13.refs_3_.refs_15_ = bf16[768,128]{1,0:T(8,128)(2,1)S(1)} collective-permute-done((bf16[768,128]{1,0:T(8,128)(2,1)S(1)}, bf16[768,128]{1,0:T(8,128)(2,1)S(1)}, u32[]{:S(2)}, u32[]{:S(2)}) %collective-permute-start.13) | collective-permute-done | bytes 196640 | tf_op jit(solution)/shard_map/ppermute | solution.py:65
  53.2 2.1 %collective-permute-done.19.refs_11_.refs_23_ = bf16[768,128]{1,0:T(8,128)(2,1)S(1)} collective-permute-done((bf16[768,128]{1,0:T(8,128)(2,1)S(1)}, bf16[768,128]{1,0:T(8,128)(2,1)S(1)}, u32[]{:S(2)}, u32[]{:S(2)}) %collective-permute-start.19) | collective-permute-done | bytes 196640 | tf_op jit(solution)/shard_map/ppermute | solution.py:65
  55.3 0.1 pad_add_fusion.place_ref
  55.4 0.9 copy-done.3
  56.3 0.9 copy-done.6
  57.2 0.9 copy-done.9
  58.1 0.9 copy-done.12
  59.0 0.9 copy-done.15
  59.9 0.9 copy-done.18
  60.8 0.9 copy-done.21
  61.7 0.9 copy-done.24
  62.6 0.9 copy-done.26
  63.6 1.3 %shard_map.102 = (bf16[144,128]{1,0:T(8,128)(2,1)S(1)}, bf16[144,128]{1,0:T(8,128)(2,1)S(1)}, bf16[144,128]{1,0:T(8,128)(2,1)S(1)}, bf16[144,128]{1,0:T(8,128)(2,1)S(1)}) custom-call(s32[3]{0:T(128)S(1)} %pad_add_fusion.place_ref, bf16[128,1024]{1,0:T(8,128)(2,1)S(1)} %bitcast.21, bf16[128,1024]{1,0:T(8,128)(2,1)S(1)} %bitcast.23, ...), custom_call_target="tpu_custom_call" | custom-call | tf_op jit(solution)/shard_map/pallas_call | solution.py:369
  64.9 1.4 %shard_map.103 = (bf16[128,384]{1,0:T(8,128)(2,1)S(1)}, bf16[128,384]{1,0:T(8,128)(2,1)S(1)}, bf16[128,384]{1,0:T(8,128)(2,1)S(1)}, bf16[128,384]{1,0:T(8,128)(2,1)S(1)}) custom-call(s32[3]{0:T(128)S(1)} %pad_add_fusion.place_ref, bf16[128,1024]{1,0:T(8,128)(2,1)S(1)} %bitcast.22, bf16[768,128]{1,0:T(8,128)(2,1)S(1)} %collective-permute-done.9.refs_0_.refs_12_, ...), custom_call_target="tpu_custom_call" | custom-call | tf_op jit(solution)/shard_map/pallas_call | solution.py:369
  66.4 0.4 collective-permute-start.25
  66.8 4.0 %collective-permute-start.26 = (bf16[128,384]{1,0:T(8,128)(2,1)S(1)}, bf16[128,384]{1,0:T(8,128)(2,1)S(1)}, u32[]{:S(2)}, u32[]{:S(2)}) collective-permute-start(bf16[128,384]{1,0:T(8,128)(2,1)S(1)} %get-tuple-element.43), channel_id=1, source_target_pairs={{0,12},{4,8},{8,4},{12,0},{1,13},{5,9},{9,5},{13,1},{2,14},{6,10},... | collective-permute-start | bytes 294920 | tf_op jit(solution)/shard_map/ppermute | solution.py:76
  70.8 0.6 collective-permute-start.29
  71.3 1.4 %collective-permute-done.24 = bf16[128,384]{1,0:T(8,128)(2,1)S(1)} collective-permute-done((bf16[128,384]{1,0:T(8,128)(2,1)S(1)}, bf16[128,384]{1,0:T(8,128)(2,1)S(1)}, u32[]{:S(2)}, u32[]{:S(2)}) %collective-permute-start.24) | collective-permute-done | bytes 98336 | tf_op jit(solution)/shard_map/ppermute | solution.py:76
  72.7 2.4 %collective-permute-start.30 = (bf16[144,128]{1,0:T(8,128)(2,1)S(1)}, bf16[144,128]{1,0:T(8,128)(2,1)S(1)}, u32[]{:S(2)}, u32[]{:S(2)}) collective-permute-start(bf16[144,128]{1,0:T(8,128)(2,1)S(1)} %get-tuple-element.46), channel_id=1, source_target_pairs={{0,12},{4,8},{8,4},{12,0},{1,13},{5,9},{9,5},{13,1},{2,14},{6,10},... | collective-permute-start | bytes 110600 | tf_op jit(solution)/shard_map/ppermute | solution.py:76
  75.1 3.7 %collective-permute-done.25 = bf16[128,384]{1,0:T(8,128)(2,1)S(1)} collective-permute-done((bf16[128,384]{1,0:T(8,128)(2,1)S(1)}, bf16[128,384]{1,0:T(8,128)(2,1)S(1)}, u32[]{:S(2)}, u32[]{:S(2)}) %collective-permute-start.25) | collective-permute-done | bytes 98336 | tf_op jit(solution)/shard_map/ppermute | solution.py:76
  79.0 2.7 %collective-permute-done.29 = bf16[144,128]{1,0:T(8,128)(2,1)S(1)} collective-permute-done((bf16[144,128]{1,0:T(8,128)(2,1)S(1)}, bf16[144,128]{1,0:T(8,128)(2,1)S(1)}, u32[]{:S(2)}, u32[]{:S(2)}) %collective-permute-start.29) | collective-permute-done | bytes 36896 | tf_op jit(solution)/shard_map/ppermute | solution.py:76
  81.8 1.3 %collective-permute-done.31.refs_3_ = f32[144,128]{1,0:T(8,128)S(1)} collective-permute-done((f32[144,128]{1,0:T(8,128)S(1)}, f32[144,128]{1,0:T(8,128)S(1)}, u32[]{:S(2)}, u32[]{:S(2)}) %collective-permute-start.31) | collective-permute-done | bytes 73760 | tf_op jit(solution)/shard_map/ppermute | solution.py:65
  83.2 10.8 %shard_map.104 = (bf16[144,512]{1,0:T(8,128)(2,1)S(1)}, f32[64,256]{1,0:T(8,128)S(1)}, f32[64,256]{1,0:T(8,128)S(1)}, f32[64,256]{1,0:T(8,128)S(1)}, f32[64,256]{1,0:T(8,128)S(1)}) custom-call(s32[3]{0:T(128)S(1)} %pad_add_fusion.place_ref, f32[128,384]{1,0:T(8,128)S(1)} %convert_add_fusion.refs_0_, f32[128,384]{1,0:T(8,128)S(1)} %collective-permute-done.27.refs_1_, ...), custom_call_target="tpu_custom_call" | custom-call | tf_op jit(solution)/shard_map/pallas_call | solution.py:369
  94.0 1.0 collective-permute-start.32
  95.0 0.9 collective-permute-start.33
  95.9 2.5 %collective-permute-start.34 = (bf16[144,512]{1,0:T(8,128)(2,1)S(1)}, bf16[144,512]{1,0:T(8,128)(2,1)S(1)}, u32[]{:S(2)}, u32[]{:S(2)}) collective-permute-start(bf16[144,512]{1,0:T(8,128)(2,1)S(1)} %get-tuple-element.47.refs_0_), channel_id=1, source_target_pairs={{12,0},{8,4},{4,8},{0,12},{13,1},{9,5},{5,9},{1,13},{14,2},{10,6},... | collective-permute-start | bytes 442376 | tf_op jit(solution)/shard_map/ppermute | solution.py:65
  98.5 3.4 %collective-permute-done.32.refs_1_ = bf16[144,512]{1,0:T(8,128)(2,1)S(1)} collective-permute-done((bf16[144,512]{1,0:T(8,128)(2,1)S(1)}, bf16[144,512]{1,0:T(8,128)(2,1)S(1)}, u32[]{:S(2)}, u32[]{:S(2)}) %collective-permute-start.32) | collective-permute-done | bytes 147488 | tf_op jit(solution)/shard_map/ppermute | solution.py:65
  101.8 1.0 collective-permute-start.35
  102.9 0.9 collective-permute-start.36
  103.7 1.6 %collective-permute-start.37 = (f32[64,256]{1,0:T(8,128)S(1)}, f32[64,256]{1,0:T(8,128)S(1)}, u32[]{:S(2)}, u32[]{:S(2)}) collective-permute-start(f32[64,256]{1,0:T(8,128)S(1)} %get-tuple-element.57), channel_id=1, source_target_pairs={{0,3},{1,2},{2,1},{3,0},{4,7},{5,6},{6,5},{7,4},{8,11},{9,10},{10,... | collective-permute-start | bytes 196616 | tf_op jit(solution)/shard_map/ppermute | solution.py:76
  105.3 3.6 %collective-permute-done.33.refs_2_ = bf16[144,512]{1,0:T(8,128)(2,1)S(1)} collective-permute-done((bf16[144,512]{1,0:T(8,128)(2,1)S(1)}, bf16[144,512]{1,0:T(8,128)(2,1)S(1)}, u32[]{:S(2)}, u32[]{:S(2)}) %collective-permute-start.33) | collective-permute-done | bytes 147488 | tf_op jit(solution)/shard_map/ppermute | solution.py:65
  109.0 3.2 %shard_map.105 = (bf16[128,1024]{1,0:T(8,128)(2,1)}, bf16[128,1024]{1,0:T(8,128)(2,1)}) custom-call(s32[3]{0:T(128)S(1)} %pad_add_fusion.place_ref, bf16[144,512]{1,0:T(8,128)(2,1)S(1)} %get-tuple-element.47.refs_0_, bf16[144,512]{1,0:T(8,128)(2,1)S(1)} %collective-permute-done.32.refs_1_, bf16[144,512]{1,0:T(8,128)(2,1)S(1)} %collective-permute-done.33.refs_2_, ...), custom_call_target="tpu_custom_call" | custom-call | tf_op jit(solution)/shard_map/pallas_call | solution.py:369
  112.2 0.6 slice_bitcast_fusion
  (83 shorter events, 0.6 us)
Async XLA Ops:
  0.6 0.7 copy-start
  2.3 3.2 %collective-permute-start.1 = (bf16[528,128]{1,0:T(8,128)(2,1)S(1)}, bf16[528,128]{1,0:T(8,128)(2,1)S(1)}, u32[]{:S(2)}, u32[]{:S(2)}) collective-permute-start(bf16[528,128]{1,0:T(8,128)(2,1)S(1)} %fusion.1), channel_id=1, source_target_pairs={{0,0},{1,1},{2,4},{3,5},{4,2},{5,3},{6,6},{7,7},{8,16},{9,17},{10,... | collective-permute-start | bytes 405512 | tf_op jit(solution)/shard_map/ppermute | solution.py:399
  3.0 52.4 %copy-start.1 = (bf16[1,128,1024]{2,1,0:T(8,128)(2,1)S(1)}, bf16[1,128,1024]{2,1,0:T(8,128)(2,1)}, u32[]{:S(2)}) copy-start(bf16[1,128,1024]{2,1,0:T(8,128)(2,1)} %param.7) | copy-start | bytes 786436
  4.1 14.1 %collective-permute-start.9 = (bf16[768,128]{1,0:T(8,128)(2,1)S(1)}, bf16[768,128]{1,0:T(8,128)(2,1)S(1)}, u32[]{:S(2)}, u32[]{:S(2)}) collective-permute-start(bf16[768,128]{1,0:T(8,128)(2,1)S(1)} %bitcast.28), channel_id=1, source_target_pairs={{0,0},{1,1},{2,4},{3,5},{4,2},{5,3},{6,6},{7,7},{8,16},{9,17},{10,... | collective-permute-start | bytes 589832 | tf_op jit(solution)/shard_map/ppermute | solution.py:399
  4.8 14.8 %collective-permute-start = (bf16[768,128]{1,0:T(8,128)(2,1)S(1)}, bf16[768,128]{1,0:T(8,128)(2,1)S(1)}, u32[]{:S(2)}, u32[]{:S(2)}) collective-permute-start(bf16[768,128]{1,0:T(8,128)(2,1)S(1)} %bitcast.27), channel_id=1, source_target_pairs={{0,0},{1,1},{2,4},{3,5},{4,2},{5,3},{6,6},{7,7},{8,16},{9,17},{10,... | collective-permute-start | bytes 589832 | tf_op jit(solution)/shard_map/ppermute | solution.py:399
  5.5 14.2 %collective-permute-start.2 = (bf16[528,128]{1,0:T(8,128)(2,1)S(1)}, bf16[528,128]{1,0:T(8,128)(2,1)S(1)}, u32[]{:S(2)}, u32[]{:S(2)}) collective-permute-start(bf16[528,128]{1,0:T(8,128)(2,1)S(1)} %collective-permute-done.1.refs_0_.refs_4_), channel_id=1, source_target_pairs={{1,0},{0,1},{3,2},{2,3},{5,4},{4,5},{7,6},{6,7},{9,8},{8,9},{11,10... | collective-permute-start | bytes 405512 | tf_op jit(solution)/shard_map/ppermute | solution.py:65
  8.5 22.5 %collective-permute-start.3 = (bf16[528,128]{1,0:T(8,128)(2,1)S(1)}, bf16[528,128]{1,0:T(8,128)(2,1)S(1)}, u32[]{:S(2)}, u32[]{:S(2)}) collective-permute-start(bf16[528,128]{1,0:T(8,128)(2,1)S(1)} %collective-permute-done.1.refs_0_.refs_4_), channel_id=1, source_target_pairs={{2,0},{3,1},{0,2},{1,3},{6,4},{7,5},{4,6},{5,7},{10,8},{11,9},{8,1... | collective-permute-start | bytes 405512 | tf_op jit(solution)/shard_map/ppermute | solution.py:65
  18.2 12.8 %collective-permute-start.4 = (bf16[528,128]{1,0:T(8,128)(2,1)S(1)}, bf16[528,128]{1,0:T(8,128)(2,1)S(1)}, u32[]{:S(2)}, u32[]{:S(2)}) collective-permute-start(bf16[528,128]{1,0:T(8,128)(2,1)S(1)} %collective-permute-done.1.refs_0_.refs_4_), channel_id=1, source_target_pairs={{3,0},{2,1},{1,2},{0,3},{7,4},{6,5},{5,6},{4,7},{11,8},{10,9},{9,1... | collective-permute-start | bytes 405512 | tf_op jit(solution)/shard_map/ppermute | solution.py:65
  18.2 16.7 %collective-permute-start.10 = (bf16[768,128]{1,0:T(8,128)(2,1)S(1)}, bf16[768,128]{1,0:T(8,128)(2,1)S(1)}, u32[]{:S(2)}, u32[]{:S(2)}) collective-permute-start(bf16[768,128]{1,0:T(8,128)(2,1)S(1)} %collective-permute-done.9.refs_0_.refs_12_), channel_id=1, source_target_pairs={{1,0},{0,1},{3,2},{2,3},{5,4},{4,5},{7,6},{6,7},{9,8},{8,9},{11,10... | collective-permute-start | bytes 589832 | tf_op jit(solution)/shard_map/ppermute | solution.py:65
  31.0 8.2 %collective-permute-start.11 = (bf16[768,128]{1,0:T(8,128)(2,1)S(1)}, bf16[768,128]{1,0:T(8,128)(2,1)S(1)}, u32[]{:S(2)}, u32[]{:S(2)}) collective-permute-start(bf16[768,128]{1,0:T(8,128)(2,1)S(1)} %collective-permute-done.refs_8_.refs_20_), channel_id=1, source_target_pairs={{2,0},{3,1},{0,2},{1,3},{6,4},{7,5},{4,6},{5,7},{10,8},{11,9},{8,1... | collective-permute-start | bytes 589832 | tf_op jit(solution)/shard_map/ppermute | solution.py:65
  33.5 2.6 %collective-permute-start.8 = (bf16[528,128]{1,0:T(8,128)(2,1)S(1)}, bf16[528,128]{1,0:T(8,128)(2,1)S(1)}, u32[]{:S(2)}, u32[]{:S(2)}) collective-permute-start(bf16[528,128]{1,0:T(8,128)(2,1)S(1)} %collective-permute-done.4.refs_3_.refs_7_), channel_id=1, source_target_pairs={{16,0},{0,16},{17,1},{1,17},{18,2},{2,18},{19,3},{3,19},{20,4},{4,... | collective-permute-start | bytes 405512 | tf_op jit(solution)/shard_map/ppermute | solution.py:65
  33.9 0.7 copy-start.11
  34.6 8.8 %collective-permute-start.12 = (bf16[768,128]{1,0:T(8,128)(2,1)S(1)}, bf16[768,128]{1,0:T(8,128)(2,1)S(1)}, u32[]{:S(2)}, u32[]{:S(2)}) collective-permute-start(bf16[768,128]{1,0:T(8,128)(2,1)S(1)} %collective-permute-done.9.refs_0_.refs_12_), channel_id=1, source_target_pairs={{2,0},{3,1},{0,2},{1,3},{6,4},{7,5},{4,6},{5,7},{10,8},{11,9},{8,1... | collective-permute-start | bytes 589832 | tf_op jit(solution)/shard_map/ppermute | solution.py:65
  34.9 9.5 %collective-permute-start.14 = (bf16[768,128]{1,0:T(8,128)(2,1)S(1)}, bf16[768,128]{1,0:T(8,128)(2,1)S(1)}, u32[]{:S(2)}, u32[]{:S(2)}) collective-permute-start(bf16[768,128]{1,0:T(8,128)(2,1)S(1)} %collective-permute-done.9.refs_0_.refs_12_), channel_id=1, source_target_pairs={{16,0},{0,16},{17,1},{1,17},{18,2},{2,18},{19,3},{3,19},{20,4},{4,... | collective-permute-start | bytes 589832 | tf_op jit(solution)/shard_map/ppermute | solution.py:65
  34.9 9.5 %collective-permute-start.5 = (bf16[528,128]{1,0:T(8,128)(2,1)S(1)}, bf16[528,128]{1,0:T(8,128)(2,1)S(1)}, u32[]{:S(2)}, u32[]{:S(2)}) collective-permute-start(bf16[528,128]{1,0:T(8,128)(2,1)S(1)} %collective-permute-done.1.refs_0_.refs_4_), channel_id=1, source_target_pairs={{16,0},{0,16},{17,1},{1,17},{18,2},{2,18},{19,3},{3,19},{20,4},{4,... | collective-permute-start | bytes 405512 | tf_op jit(solution)/shard_map/ppermute | solution.py:65
  35.4 0.7 copy-start.2
  36.7 8.9 %collective-permute-start.6 = (bf16[528,128]{1,0:T(8,128)(2,1)S(1)}, bf16[528,128]{1,0:T(8,128)(2,1)S(1)}, u32[]{:S(2)}, u32[]{:S(2)}) collective-permute-start(bf16[528,128]{1,0:T(8,128)(2,1)S(1)} %collective-permute-done.2.refs_1_.refs_5_), channel_id=1, source_target_pairs={{16,0},{0,16},{17,1},{1,17},{18,2},{2,18},{19,3},{3,19},{20,4},{4,... | collective-permute-start | bytes 405512 | tf_op jit(solution)/shard_map/ppermute | solution.py:65
  36.7 0.7 copy-start.5
  39.2 8.9 %collective-permute-start.7 = (bf16[528,128]{1,0:T(8,128)(2,1)S(1)}, bf16[528,128]{1,0:T(8,128)(2,1)S(1)}, u32[]{:S(2)}, u32[]{:S(2)}) collective-permute-start(bf16[528,128]{1,0:T(8,128)(2,1)S(1)} %collective-permute-done.3.refs_2_.refs_6_), channel_id=1, source_target_pairs={{16,0},{0,16},{17,1},{1,17},{18,2},{2,18},{19,3},{3,19},{20,4},{4,... | collective-permute-start | bytes 405512 | tf_op jit(solution)/shard_map/ppermute | solution.py:65
  39.4 0.7 copy-start.8
  43.4 6.9 %collective-permute-start.18 = (bf16[768,128]{1,0:T(8,128)(2,1)S(1)}, bf16[768,128]{1,0:T(8,128)(2,1)S(1)}, u32[]{:S(2)}, u32[]{:S(2)}) collective-permute-start(bf16[768,128]{1,0:T(8,128)(2,1)S(1)} %collective-permute-done.refs_8_.refs_20_), channel_id=1, source_target_pairs={{1,0},{0,1},{3,2},{2,3},{5,4},{4,5},{7,6},{6,7},{9,8},{8,9},{11,10... | collective-permute-start | bytes 589832 | tf_op jit(solution)/shard_map/ppermute | solution.py:65
  44.4 5.9 %collective-permute-start.20 = (bf16[768,128]{1,0:T(8,128)(2,1)S(1)}, bf16[768,128]{1,0:T(8,128)(2,1)S(1)}, u32[]{:S(2)}, u32[]{:S(2)}) collective-permute-start(bf16[768,128]{1,0:T(8,128)(2,1)S(1)} %collective-permute-done.refs_8_.refs_20_), channel_id=1, source_target_pairs={{16,0},{0,16},{17,1},{1,17},{18,2},{2,18},{19,3},{3,19},{20,4},{4,... | collective-permute-start | bytes 589832 | tf_op jit(solution)/shard_map/ppermute | solution.py:65
  44.4 0.7 copy-start.17
  45.1 5.8 %collective-permute-start.16 = (bf16[768,128]{1,0:T(8,128)(2,1)S(1)}, bf16[768,128]{1,0:T(8,128)(2,1)S(1)}, u32[]{:S(2)}, u32[]{:S(2)}) collective-permute-start(bf16[768,128]{1,0:T(8,128)(2,1)S(1)} %collective-permute-done.12.refs_2_.refs_14_), channel_id=1, source_target_pairs={{16,0},{0,16},{17,1},{1,17},{18,2},{2,18},{19,3},{3,19},{20,4},{4,... | collective-permute-start | bytes 589832 | tf_op jit(solution)/shard_map/ppermute | solution.py:65
  46.2 6.9 %collective-permute-start.13 = (bf16[768,128]{1,0:T(8,128)(2,1)S(1)}, bf16[768,128]{1,0:T(8,128)(2,1)S(1)}, u32[]{:S(2)}, u32[]{:S(2)}) collective-permute-start(bf16[768,128]{1,0:T(8,128)(2,1)S(1)} %collective-permute-done.10.refs_1_.refs_13_), channel_id=1, source_target_pairs={{2,0},{3,1},{0,2},{1,3},{6,4},{7,5},{4,6},{5,7},{10,8},{11,9},{8,1... | collective-permute-start | bytes 589832 | tf_op jit(solution)/shard_map/ppermute | solution.py:65
  48.8 6.5 %collective-permute-start.19 = (bf16[768,128]{1,0:T(8,128)(2,1)S(1)}, bf16[768,128]{1,0:T(8,128)(2,1)S(1)}, u32[]{:S(2)}, u32[]{:S(2)}) collective-permute-start(bf16[768,128]{1,0:T(8,128)(2,1)S(1)} %collective-permute-done.11.refs_10_.refs_22_), channel_id=1, source_target_pairs={{1,0},{0,1},{3,2},{2,3},{5,4},{4,5},{7,6},{6,7},{9,8},{8,9},{11,10... | collective-permute-start | bytes 589832 | tf_op jit(solution)/shard_map/ppermute | solution.py:65
  50.3 14.5 %collective-permute-start.15 = (bf16[768,128]{1,0:T(8,128)(2,1)S(1)}, bf16[768,128]{1,0:T(8,128)(2,1)S(1)}, u32[]{:S(2)}, u32[]{:S(2)}) collective-permute-start(bf16[768,128]{1,0:T(8,128)(2,1)S(1)} %collective-permute-done.10.refs_1_.refs_13_), channel_id=1, source_target_pairs={{16,0},{0,16},{17,1},{1,17},{18,2},{2,18},{19,3},{3,19},{20,4},{4,... | collective-permute-start | bytes 589832 | tf_op jit(solution)/shard_map/ppermute | solution.py:65
  50.3 14.5 %collective-permute-start.22 = (bf16[768,128]{1,0:T(8,128)(2,1)S(1)}, bf16[768,128]{1,0:T(8,128)(2,1)S(1)}, u32[]{:S(2)}, u32[]{:S(2)}) collective-permute-start(bf16[768,128]{1,0:T(8,128)(2,1)S(1)} %collective-permute-done.11.refs_10_.refs_22_), channel_id=1, source_target_pairs={{16,0},{0,16},{17,1},{1,17},{18,2},{2,18},{19,3},{3,19},{20,4},{4,... | collective-permute-start | bytes 589832 | tf_op jit(solution)/shard_map/ppermute | solution.py:65
  50.9 14.0 %collective-permute-start.21 = (bf16[768,128]{1,0:T(8,128)(2,1)S(1)}, bf16[768,128]{1,0:T(8,128)(2,1)S(1)}, u32[]{:S(2)}, u32[]{:S(2)}) collective-permute-start(bf16[768,128]{1,0:T(8,128)(2,1)S(1)} %collective-permute-done.18.refs_9_.refs_21_), channel_id=1, source_target_pairs={{16,0},{0,16},{17,1},{1,17},{18,2},{2,18},{19,3},{3,19},{20,4},{4,... | collective-permute-start | bytes 589832 | tf_op jit(solution)/shard_map/ppermute | solution.py:65
  53.2 11.7 %collective-permute-start.17 = (bf16[768,128]{1,0:T(8,128)(2,1)S(1)}, bf16[768,128]{1,0:T(8,128)(2,1)S(1)}, u32[]{:S(2)}, u32[]{:S(2)}) collective-permute-start(bf16[768,128]{1,0:T(8,128)(2,1)S(1)} %collective-permute-done.13.refs_3_.refs_15_), channel_id=1, source_target_pairs={{16,0},{0,16},{17,1},{1,17},{18,2},{2,18},{19,3},{3,19},{20,4},{4,... | collective-permute-start | bytes 589832 | tf_op jit(solution)/shard_map/ppermute | solution.py:65
  55.3 9.6 %collective-permute-start.23 = (bf16[768,128]{1,0:T(8,128)(2,1)S(1)}, bf16[768,128]{1,0:T(8,128)(2,1)S(1)}, u32[]{:S(2)}, u32[]{:S(2)}) collective-permute-start(bf16[768,128]{1,0:T(8,128)(2,1)S(1)} %collective-permute-done.19.refs_11_.refs_23_), channel_id=1, source_target_pairs={{16,0},{0,16},{17,1},{1,17},{18,2},{2,18},{19,3},{3,19},{20,4},{4,... | collective-permute-start | bytes 589832 | tf_op jit(solution)/shard_map/ppermute | solution.py:65
  55.4 0.9 copy-start.3
  56.3 0.9 copy-start.6
  57.2 0.9 copy-start.9
  58.1 0.9 copy-start.12
  59.0 0.9 copy-start.15
  59.9 0.9 copy-start.18
  60.8 0.9 copy-start.21
  61.7 0.9 copy-start.24
  62.6 0.9 copy-start.26
  66.3 6.4 %collective-permute-start.24 = (bf16[128,384]{1,0:T(8,128)(2,1)S(1)}, bf16[128,384]{1,0:T(8,128)(2,1)S(1)}, u32[]{:S(2)}, u32[]{:S(2)}) collective-permute-start(bf16[128,384]{1,0:T(8,128)(2,1)S(1)} %get-tuple-element.41), channel_id=1, source_target_pairs={{0,4},{4,0},{8,12},{12,8},{1,5},{5,1},{9,13},{13,9},{2,6},{6,2},{1... | collective-permute-start | bytes 294920 | tf_op jit(solution)/shard_map/ppermute | solution.py:76
  66.4 12.4 %collective-permute-start.25 = (bf16[128,384]{1,0:T(8,128)(2,1)S(1)}, bf16[128,384]{1,0:T(8,128)(2,1)S(1)}, u32[]{:S(2)}, u32[]{:S(2)}) collective-permute-start(bf16[128,384]{1,0:T(8,128)(2,1)S(1)} %get-tuple-element.42), channel_id=1, source_target_pairs={{0,8},{4,12},{8,0},{12,4},{1,9},{5,13},{9,1},{13,5},{2,10},{6,14},... | collective-permute-start | bytes 294920 | tf_op jit(solution)/shard_map/ppermute | solution.py:76
  66.8 12.1 %collective-permute-start.26 = (bf16[128,384]{1,0:T(8,128)(2,1)S(1)}, bf16[128,384]{1,0:T(8,128)(2,1)S(1)}, u32[]{:S(2)}, u32[]{:S(2)}) collective-permute-start(bf16[128,384]{1,0:T(8,128)(2,1)S(1)} %get-tuple-element.43), channel_id=1, source_target_pairs={{0,12},{4,8},{8,4},{12,0},{1,13},{5,9},{9,5},{13,1},{2,14},{6,10},... | collective-permute-start | bytes 294920 | tf_op jit(solution)/shard_map/ppermute | solution.py:76
  70.7 8.2 %collective-permute-start.28 = (bf16[144,128]{1,0:T(8,128)(2,1)S(1)}, bf16[144,128]{1,0:T(8,128)(2,1)S(1)}, u32[]{:S(2)}, u32[]{:S(2)}) collective-permute-start(bf16[144,128]{1,0:T(8,128)(2,1)S(1)} %get-tuple-element.44), channel_id=1, source_target_pairs={{0,4},{4,0},{8,12},{12,8},{1,5},{5,1},{9,13},{13,9},{2,6},{6,2},{1... | collective-permute-start | bytes 110600 | tf_op jit(solution)/shard_map/ppermute | solution.py:76
  70.8 11.0 %collective-permute-start.29 = (bf16[144,128]{1,0:T(8,128)(2,1)S(1)}, bf16[144,128]{1,0:T(8,128)(2,1)S(1)}, u32[]{:S(2)}, u32[]{:S(2)}) collective-permute-start(bf16[144,128]{1,0:T(8,128)(2,1)S(1)} %get-tuple-element.45), channel_id=1, source_target_pairs={{0,8},{4,12},{8,0},{12,4},{1,9},{5,13},{9,1},{13,5},{2,10},{6,14},... | collective-permute-start | bytes 110600 | tf_op jit(solution)/shard_map/ppermute | solution.py:76
  72.7 9.0 %collective-permute-start.30 = (bf16[144,128]{1,0:T(8,128)(2,1)S(1)}, bf16[144,128]{1,0:T(8,128)(2,1)S(1)}, u32[]{:S(2)}, u32[]{:S(2)}) collective-permute-start(bf16[144,128]{1,0:T(8,128)(2,1)S(1)} %get-tuple-element.46), channel_id=1, source_target_pairs={{0,12},{4,8},{8,4},{12,0},{1,13},{5,9},{9,5},{13,1},{2,14},{6,10},... | collective-permute-start | bytes 110600 | tf_op jit(solution)/shard_map/ppermute | solution.py:76
  78.8 4.3 %copy-start.27 = (f32[1,128,512]{2,1,0:T(8,128)S(1)}, f32[1,128,512]{2,1,0:T(8,128)}, u32[]{:S(2)}) copy-start(f32[1,128,512]{2,1,0:T(8,128)} %param.11) | copy-start | bytes 786436
  78.8 4.3 %copy-start.28 = (f32[1,512,128]{2,1,0:T(8,128)S(1)}, f32[1,512,128]{2,1,0:T(8,128)}, u32[]{:S(2)}) copy-start(f32[1,512,128]{2,1,0:T(8,128)} %param.12) | copy-start | bytes 786436
  78.9 4.2 %collective-permute-start.27 = (f32[128,384]{1,0:T(8,128)S(1)}, f32[128,384]{1,0:T(8,128)S(1)}, u32[]{:S(2)}, u32[]{:S(2)}) collective-permute-start(f32[128,384]{1,0:T(8,128)S(1)} %convert_add_fusion.refs_0_), channel_id=1, source_target_pairs={{16,0},{0,16},{17,1},{1,17},{18,2},{2,18},{19,3},{3,19},{20,4},{4,... | collective-permute-start | bytes 589832 | tf_op jit(solution)/shard_map/ppermute | solution.py:65
  81.7 27.3 %copy-start.25 = (bf16[528,128]{1,0:T(8,128)(2,1)S(1)}, bf16[528,128]{1,0:T(8,128)(2,1)}, u32[]{:S(2)}) copy-start(bf16[528,128]{1,0:T(8,128)(2,1)} %copy-done.23) | copy-start | bytes 405508
  81.7 1.3 %collective-permute-start.31 = (f32[144,128]{1,0:T(8,128)S(1)}, f32[144,128]{1,0:T(8,128)S(1)}, u32[]{:S(2)}, u32[]{:S(2)}) collective-permute-start(f32[144,128]{1,0:T(8,128)S(1)} %convert_add_fusion.1.refs_2_), channel_id=1, source_target_pairs={{16,0},{0,16},{17,1},{1,17},{18,2},{2,18},{19,3},{3,19},{20,4},{4,... | collective-permute-start | bytes 221192 | tf_op jit(solution)/shard_map/ppermute | solution.py:65
  83.1 25.9 %copy-start.4 = (bf16[528,128]{1,0:T(8,128)(2,1)S(1)}, bf16[528,128]{1,0:T(8,128)(2,1)}, u32[]{:S(2)}) copy-start(bf16[528,128]{1,0:T(8,128)(2,1)} %copy-done.2) | copy-start | bytes 405508
  83.1 25.9 %copy-start.7 = (bf16[528,128]{1,0:T(8,128)(2,1)S(1)}, bf16[528,128]{1,0:T(8,128)(2,1)}, u32[]{:S(2)}) copy-start(bf16[528,128]{1,0:T(8,128)(2,1)} %copy-done.5) | copy-start | bytes 405508
  83.1 25.9 %copy-start.10 = (bf16[528,128]{1,0:T(8,128)(2,1)S(1)}, bf16[528,128]{1,0:T(8,128)(2,1)}, u32[]{:S(2)}) copy-start(bf16[528,128]{1,0:T(8,128)(2,1)} %copy-done.8) | copy-start | bytes 405508
  83.1 25.9 %copy-start.13 = (bf16[528,128]{1,0:T(8,128)(2,1)S(1)}, bf16[528,128]{1,0:T(8,128)(2,1)}, u32[]{:S(2)}) copy-start(bf16[528,128]{1,0:T(8,128)(2,1)} %copy-done.11) | copy-start | bytes 405508
  83.1 25.9 %copy-start.16 = (bf16[528,128]{1,0:T(8,128)(2,1)S(1)}, bf16[528,128]{1,0:T(8,128)(2,1)}, u32[]{:S(2)}) copy-start(bf16[528,128]{1,0:T(8,128)(2,1)} %copy-done.14) | copy-start | bytes 405508
  83.1 25.9 %copy-start.19 = (bf16[528,128]{1,0:T(8,128)(2,1)S(1)}, bf16[528,128]{1,0:T(8,128)(2,1)}, u32[]{:S(2)}) copy-start(bf16[528,128]{1,0:T(8,128)(2,1)} %copy-done.17) | copy-start | bytes 405508
  83.1 25.9 %copy-start.22 = (bf16[528,128]{1,0:T(8,128)(2,1)S(1)}, bf16[528,128]{1,0:T(8,128)(2,1)}, u32[]{:S(2)}) copy-start(bf16[528,128]{1,0:T(8,128)(2,1)} %copy-done.20) | copy-start | bytes 405508
  94.0 7.8 %collective-permute-start.32 = (bf16[144,512]{1,0:T(8,128)(2,1)S(1)}, bf16[144,512]{1,0:T(8,128)(2,1)S(1)}, u32[]{:S(2)}, u32[]{:S(2)}) collective-permute-start(bf16[144,512]{1,0:T(8,128)(2,1)S(1)} %get-tuple-element.47.refs_0_), channel_id=1, source_target_pairs={{4,0},{0,4},{12,8},{8,12},{5,1},{1,5},{13,9},{9,13},{6,2},{2,6},{1... | collective-permute-start | bytes 442376 | tf_op jit(solution)/shard_map/ppermute | solution.py:65
  95.0 13.9 %collective-permute-start.33 = (bf16[144,512]{1,0:T(8,128)(2,1)S(1)}, bf16[144,512]{1,0:T(8,128)(2,1)S(1)}, u32[]{:S(2)}, u32[]{:S(2)}) collective-permute-start(bf16[144,512]{1,0:T(8,128)(2,1)S(1)} %get-tuple-element.47.refs_0_), channel_id=1, source_target_pairs={{8,0},{12,4},{0,8},{4,12},{9,1},{13,5},{1,9},{5,13},{10,2},{14,6},... | collective-permute-start | bytes 442376 | tf_op jit(solution)/shard_map/ppermute | solution.py:65
  95.9 13.0 %collective-permute-start.34 = (bf16[144,512]{1,0:T(8,128)(2,1)S(1)}, bf16[144,512]{1,0:T(8,128)(2,1)S(1)}, u32[]{:S(2)}, u32[]{:S(2)}) collective-permute-start(bf16[144,512]{1,0:T(8,128)(2,1)S(1)} %get-tuple-element.47.refs_0_), channel_id=1, source_target_pairs={{12,0},{8,4},{4,8},{0,12},{13,1},{9,5},{5,9},{1,13},{14,2},{10,6},... | collective-permute-start | bytes 442376 | tf_op jit(solution)/shard_map/ppermute | solution.py:65
  101.8 10.4 %collective-permute-start.35 = (f32[64,256]{1,0:T(8,128)S(1)}, f32[64,256]{1,0:T(8,128)S(1)}, u32[]{:S(2)}, u32[]{:S(2)}) collective-permute-start(f32[64,256]{1,0:T(8,128)S(1)} %get-tuple-element.55), channel_id=1, source_target_pairs={{0,1},{1,0},{2,3},{3,2},{4,5},{5,4},{6,7},{7,6},{8,9},{9,8},{10,11... | collective-permute-start | bytes 196616 | tf_op jit(solution)/shard_map/ppermute | solution.py:76
  102.9 9.3 %collective-permute-start.36 = (f32[64,256]{1,0:T(8,128)S(1)}, f32[64,256]{1,0:T(8,128)S(1)}, u32[]{:S(2)}, u32[]{:S(2)}) collective-permute-start(f32[64,256]{1,0:T(8,128)S(1)} %get-tuple-element.56), channel_id=1, source_target_pairs={{0,2},{1,3},{2,0},{3,1},{4,6},{5,7},{6,4},{7,5},{8,10},{9,11},{10,... | collective-permute-start | bytes 196616 | tf_op jit(solution)/shard_map/ppermute | solution.py:76
  103.7 8.5 %collective-permute-start.37 = (f32[64,256]{1,0:T(8,128)S(1)}, f32[64,256]{1,0:T(8,128)S(1)}, u32[]{:S(2)}, u32[]{:S(2)}) collective-permute-start(f32[64,256]{1,0:T(8,128)S(1)} %get-tuple-element.57), channel_id=1, source_target_pairs={{0,3},{1,2},{2,1},{3,0},{4,7},{5,6},{6,5},{7,4},{8,11},{9,10},{10,... | collective-permute-start | bytes 196616 | tf_op jit(solution)/shard_map/ppermute | solution.py:76
  (3 other events, 1.9 us)
where the time goes:
time: 113 us
  starting transfers between devices  40.6 us (36%)
  waiting for transfers between devices  37.6 us (33%)
  Pallas kernels  16.7 us (15%)
  local copies, waits for them, and re-layouts  15.9 us (14%)
  other arithmetic  1.14 us (1%)
    ppermute x26, waiting for transfers between devices, hop(): lax.ppermute(array, axis, [(mate(i, step, count), i) for i in range(count)])  29.8 us
    ppermute x26, starting transfers between devices, hop(): lax.ppermute(array, axis, [(mate(i, step, count), i) for i in range(count)])  27.6 us
    pallas_call x4, Pallas kernels, call(): pl.pallas_call(kernel, out_shape=outs, in_specs=[SMEM] + [VMEM] * (len(op...  16.7 us
    unnamed x58, local copies, waits for them, and re-layouts  14.2 us
    ppermute x9, starting transfers between devices, sent_to(): lax.ppermute(arrays[j], axis, [(i, mate(i, j, count)) for i in range(coun...  10.9 us
    ppermute x9, waiting for transfers between devices, sent_to(): lax.ppermute(arrays[j], axis, [(i, mate(i, j, count)) for i in range(coun...  7.84 us
  transfers between devices with their start and end apart: 38, of which 12 were waited for; matrix products, arithmetic and copies ran while one was open for 1% of the time, Pallas kernels for 4%

commit v1 on v0

--- a/solution.py
+++ b/solution.py
@@ -362,17 +362,17 @@
 
 VMEM = pl.BlockSpec(memory_space=pltpu.VMEM)
 SMEM = pl.BlockSpec(memory_space=pltpu.SMEM)
-PARAMS = pltpu.CompilerParams(vmem_limit_bytes=48 * 1024 * 1024)
-
-
-def call(kernel, outs, operands, scratch=()):
+MIB = 1024 * 1024
+
+
+def call(kernel, outs, operands, scratch=(), mib=16):
     return pl.pallas_call(
         kernel,
         out_shape=outs,
         in_specs=[SMEM] + [VMEM] * (len(operands) - 1),
         out_specs=jax.tree.map(lambda unused: VMEM, outs),
         scratch_shapes=list(scratch),
-        compiler_params=PARAMS,
+        compiler_params=pltpu.CompilerParams(vmem_limit_bytes=mib * MIB),
     )(*operands)
 
 
@@ -385,6 +385,7 @@
     blocks = seqs * rows // MB
     place = jnp.stack([lax.axis_index(a).astype(jnp.int32) for a in ("seq", "head", "dp")])
     sizes = (seqs, heads, dps, share)
+    place, w_out, w_qkv = lax.optimization_barrier((place, w_out, w_qkv))
 
     pairs = []
     for seq in range(seqs):
@@ -414,9 +415,20 @@
     second_w, *outer_near = lax.optimization_barrier((second_w, *outer_near))
     second_near = [second_w, hop(second_w, "dp", 1), hop(second_w, "dp", 2)]
     outer_ws = over_seq(outer_near)
+    def summed(arrays):
+        return functools.reduce(lambda a, b: a + b, [a.astype(F32) for a in arrays])
+
+    outer_part = call(
+        functools.partial(outer_kernel, *sizes),
+        (jax.ShapeDtypeStruct((rows + EXTRA, hd), BF16),) * heads,
+        (place, tokens[0], d_out[0], *outer_ws),
+        [pltpu.VMEM((share, rows, features // share), BF16)] * 2
+        + [pltpu.VMEM((heads, rows + EXTRA, hd), F32)],
+    )
+    outer_all = peers_of(summed(sent_to(outer_part, "head")), "seq")
     if dps == 4:
         first_near[1], second_near[2], unused = lax.optimization_barrier(
-            (first_near[1], second_near[2], outer_ws[-1])
+            (first_near[1], second_near[2], outer_part[0])
         )
         first_near.append(hop(first_near[1], "dp", 2))
         second_near.append(hop(second_near[2], "dp", 1))
@@ -424,23 +436,10 @@
         first_near += [hop(first_w, "dp", j) for j in range(3, dps)]
         second_near += [hop(second_w, "dp", j) for j in range(3, dps)]
     inner_ws = over_seq(first_near) + over_seq(second_near)
-
-    def summed(arrays):
-        return functools.reduce(lambda a, b: a + b, [a.astype(F32) for a in arrays])
-
-    outer_part = call(
-        functools.partial(outer_kernel, *sizes),
-        (jax.ShapeDtypeStruct((rows + EXTRA, hd), BF16),) * heads,
-        (place, tokens[0], d_out[0], *outer_ws),
-        [pltpu.VMEM((share, rows, features // share), BF16)] * 2
-        + [pltpu.VMEM((heads, rows + EXTRA, hd), F32)],
-    )
-    outer_all = peers_of(summed(sent_to(outer_part, "head")), "seq")
-    own_tokens, unused = lax.optimization_barrier((tokens[0], outer_part[0]))
     inner_part = call(
         functools.partial(inner_projection_kernel, *sizes),
         (jax.ShapeDtypeStruct((rows, 3 * hd), BF16),) * heads,
-        (place, own_tokens, *inner_ws),
+        (place, tokens[0], *inner_ws),
         [
             pltpu.VMEM((share, rows, features // share), BF16),
             pltpu.VMEM((heads, rows, 3 * hd), F32),
@@ -466,6 +465,7 @@
         + (jax.ShapeDtypeStruct((part, 2 * hd), F32),) * dps,
         (place, *inner_all, *outer_all, w1_init[0], w2_init[0]),
         scratch,
+        14 + 2 * blocks,
     )
     got = peers_of(result, "head")
     unused, *d_inner = lax.optimization_barrier((got[1], *d_inner))

time: 113 us -> 99.9 us (0.88)
  local copies, waits for them, and re-layouts: 15.9 us -> 2.4 us
    unnamed x58 -> x10, local copies, waits for them, and re-layouts: 14.2 us -> 0.65 us
    ppermute x26, waiting for transfers between devices: 29.8 us -> 31.8 us  [hop(): lax.ppermute(array, axis, [(mate(i, step, count), i) for i in range(count)])]
    ppermute x9, waiting for transfers between devices: 7.84 us -> 6.51 us  [sent_to(): lax.ppermute(arrays[j], axis, [(i, mate(i, j, count)) for i in range(coun...]
    ppermute x26, starting transfers between devices: 27.6 us -> 26.4 us  [hop(): lax.ppermute(array, axis, [(mate(i, step, count), i) for i in range(count)])]
  transfers between devices with their start and end apart: 38 -> 38, of which waited for: 12 -> 14; matrix products, arithmetic and copies ran while one was open for 1% -> 1% of each run, Pallas kernels for 4% -> 4%
where the time goes in v1:
time: 99.9 us; the launch traced here: 99.6 us
  starting transfers between devices  40.2 us (40%)
  waiting for transfers between devices  38.3 us (38%)
  Pallas kernels  16.7 us (17%)
  local copies, waits for them, and re-layouts  2.4 us (2%)
  other arithmetic  1.14 us (1%)
    ppermute x26, waiting for transfers between devices, hop(): lax.ppermute(array, axis, [(mate(i, step, count), i) for i in range(count)])  31.8 us
    ppermute x26, starting transfers between devices, hop(): lax.ppermute(array, axis, [(mate(i, step, count), i) for i in range(count)])  26.4 us
    pallas_call x4, Pallas kernels, call(): pl.pallas_call(kernel, out_shape=outs, in_specs=[SMEM] + [VMEM] * (len(op...  16.7 us
    ppermute x9, starting transfers between devices, sent_to(): lax.ppermute(arrays[j], axis, [(i, mate(i, j, count)) for i in range(coun...  11.8 us
    ppermute x9, waiting for transfers between devices, sent_to(): lax.ppermute(arrays[j], axis, [(i, mate(i, j, count)) for i in range(coun...  6.51 us
    ppermute x3, starting transfers between devices, swapped(): return lax.ppermute(array, ('seq', 'head', 'dp'), pairs)  2 us
  transfers between devices with their start and end apart: 38, of which 14 were waited for; matrix products, arithmetic and copies ran while one was open for 1% of the time, Pallas kernels for 4%

profile of v1, /device:TPU:0, one launch (start us, length us, event | category | flops | bytes accessed | tf_op | source)
XLA Modules:
  0.0 99.6 jit_solution(11137177240764361521)
XLA Ops:
  0.6 0.0 copy-start
  0.7 0.1 pad_add_fusion.place_ref
  0.7 0.6 copy-done
  1.4 0.1 reduce
  1.4 0.9 fusion.1
  2.3 0.7 collective-permute-start.3
  3.0 0.0 copy-start.1
  3.0 0.0 copy-start.2
  3.0 1.1 %fusion.2 = (bf16[3,256,128]{2,1,0:T(8,128)(2,1)S(1)}, bf16[3,256,128]{2,1,0:T(8,128)(2,1)S(1)}) fusion(bf16[3,512,128]{2,1,0:T(8,128)(2,1)} %bitcast.26), kind=kLoop, calls=%fused_computation.10 | loop fusion | bytes 786432 | tf_op jit(solution)/shard_map/slice | solution.py:411
  4.2 0.7 collective-permute-start.2
  4.8 0.0 collective-permute-done.3.refs_0_.refs_4_
  4.8 3.0 %collective-permute-start.4 = (bf16[528,128]{1,0:T(8,128)(2,1)S(1)}, bf16[528,128]{1,0:T(8,128)(2,1)S(1)}, u32[]{:S(2)}, u32[]{:S(2)}) collective-permute-start(bf16[528,128]{1,0:T(8,128)(2,1)S(1)} %collective-permute-done.3.refs_0_.refs_4_), channel_id=1, source_target_pairs={{1,0},{0,1},{3,2},{2,3},{5,4},{4,5},{7,6},{6,7},{9,8},{8,9},{11,10... | collective-permute-start | bytes 405512 | tf_op jit(solution)/shard_map/ppermute | solution.py:65
  7.9 9.3 %collective-permute-start.5 = (bf16[528,128]{1,0:T(8,128)(2,1)S(1)}, bf16[528,128]{1,0:T(8,128)(2,1)S(1)}, u32[]{:S(2)}, u32[]{:S(2)}) collective-permute-start(bf16[528,128]{1,0:T(8,128)(2,1)S(1)} %collective-permute-done.3.refs_0_.refs_4_), channel_id=1, source_target_pairs={{2,0},{3,1},{0,2},{1,3},{6,4},{7,5},{4,6},{5,7},{10,8},{11,9},{8,1... | collective-permute-start | bytes 405512 | tf_op jit(solution)/shard_map/ppermute | solution.py:65
  17.1 0.0 collective-permute-start.6
  17.1 0.7 collective-permute-start
  17.8 0.0 collective-permute-done.4.refs_1_.refs_5_
  17.8 12.2 %collective-permute-done.5.refs_2_.refs_6_ = bf16[528,128]{1,0:T(8,128)(2,1)S(1)} collective-permute-done((bf16[528,128]{1,0:T(8,128)(2,1)S(1)}, bf16[528,128]{1,0:T(8,128)(2,1)S(1)}, u32[]{:S(2)}, u32[]{:S(2)}) %collective-permute-start.5) | collective-permute-done | bytes 135200 | tf_op jit(solution)/shard_map/ppermute | solution.py:65
  30.0 0.0 collective-permute-done.6.refs_3_.refs_7_
  30.0 0.5 collective-permute-start.11
  30.5 0.0 collective-permute-start.8
  30.5 0.0 collective-permute-done.refs_0_.refs_12_
  30.5 0.5 collective-permute-start.1
  31.0 2.5 %collective-permute-start.12 = (bf16[768,128]{1,0:T(8,128)(2,1)S(1)}, bf16[768,128]{1,0:T(8,128)(2,1)S(1)}, u32[]{:S(2)}, u32[]{:S(2)}) collective-permute-start(bf16[768,128]{1,0:T(8,128)(2,1)S(1)} %collective-permute-done.refs_0_.refs_12_), channel_id=1, source_target_pairs={{2,0},{3,1},{0,2},{1,3},{6,4},{7,5},{4,6},{5,7},{10,8},{11,9},{8,1... | collective-permute-start | bytes 589832 | tf_op jit(solution)/shard_map/ppermute | solution.py:65
  33.5 0.3 collective-permute-start.7
  33.8 0.0 collective-permute-done.11.refs_7_.refs_11_
  33.8 0.5 collective-permute-start.9
  34.3 1.1 %collective-permute-done.9.refs_5_.refs_9_ = bf16[528,128]{1,0:T(8,128)(2,1)S(1)} collective-permute-done((bf16[528,128]{1,0:T(8,128)(2,1)S(1)}, bf16[528,128]{1,0:T(8,128)(2,1)S(1)}, u32[]{:S(2)}, u32[]{:S(2)}) %collective-permute-start.9) | collective-permute-done | bytes 135200 | tf_op jit(solution)/shard_map/ppermute | solution.py:65
  35.5 1.3 %collective-permute-start.18 = (bf16[768,128]{1,0:T(8,128)(2,1)S(1)}, bf16[768,128]{1,0:T(8,128)(2,1)S(1)}, u32[]{:S(2)}, u32[]{:S(2)}) collective-permute-start(bf16[768,128]{1,0:T(8,128)(2,1)S(1)} %collective-permute-done.2.refs_8_.refs_20_), channel_id=1, source_target_pairs={{1,0},{0,1},{3,2},{2,3},{5,4},{4,5},{7,6},{6,7},{9,8},{8,9},{11,10... | collective-permute-start | bytes 589832 | tf_op jit(solution)/shard_map/ppermute | solution.py:65
  36.7 1.3 %shard_map.102 = (bf16[144,128]{1,0:T(8,128)(2,1)S(1)}, bf16[144,128]{1,0:T(8,128)(2,1)S(1)}, bf16[144,128]{1,0:T(8,128)(2,1)S(1)}, bf16[144,128]{1,0:T(8,128)(2,1)S(1)}) custom-call(s32[3]{0:T(128)S(1)} %pad_add_fusion.place_ref, bf16[128,1024]{1,0:T(8,128)(2,1)S(1)} %bitcast.21, bf16[128,1024]{1,0:T(8,128)(2,1)S(1)} %bitcast.23, ...), custom_call_target="tpu_custom_call" | custom-call | tf_op jit(solution)/shard_map/pallas_call | solution.py:369
  38.1 0.1 collective-permute-start.20
  38.1 1.1 %collective-permute-done.12.refs_2_.refs_14_ = bf16[768,128]{1,0:T(8,128)(2,1)S(1)} collective-permute-done((bf16[768,128]{1,0:T(8,128)(2,1)S(1)}, bf16[768,128]{1,0:T(8,128)(2,1)S(1)}, u32[]{:S(2)}, u32[]{:S(2)}) %collective-permute-start.12) | collective-permute-done | bytes 196640 | tf_op jit(solution)/shard_map/ppermute | solution.py:65
  39.2 3.8 %collective-permute-done.7.refs_10_.refs_22_ = bf16[768,128]{1,0:T(8,128)(2,1)S(1)} collective-permute-done((bf16[768,128]{1,0:T(8,128)(2,1)S(1)}, bf16[768,128]{1,0:T(8,128)(2,1)S(1)}, u32[]{:S(2)}, u32[]{:S(2)}) %collective-permute-start.7) | collective-permute-done | bytes 196640 | tf_op jit(solution)/shard_map/ppermute | solution.py:65
  43.0 1.7 %collective-permute-start.13 = (bf16[768,128]{1,0:T(8,128)(2,1)S(1)}, bf16[768,128]{1,0:T(8,128)(2,1)S(1)}, u32[]{:S(2)}, u32[]{:S(2)}) collective-permute-start(bf16[768,128]{1,0:T(8,128)(2,1)S(1)} %collective-permute-done.1.refs_1_.refs_13_), channel_id=1, source_target_pairs={{2,0},{3,1},{0,2},{1,3},{6,4},{7,5},{4,6},{5,7},{10,8},{11,9},{8,1... | collective-permute-start | bytes 589832 | tf_op jit(solution)/shard_map/ppermute | solution.py:65
  44.8 1.5 %collective-permute-start.19 = (bf16[768,128]{1,0:T(8,128)(2,1)S(1)}, bf16[768,128]{1,0:T(8,128)(2,1)S(1)}, u32[]{:S(2)}, u32[]{:S(2)}) collective-permute-start(bf16[768,128]{1,0:T(8,128)(2,1)S(1)} %collective-permute-done.7.refs_10_.refs_22_), channel_id=1, source_target_pairs={{1,0},{0,1},{3,2},{2,3},{5,4},{4,5},{7,6},{6,7},{9,8},{8,9},{11,10... | collective-permute-start | bytes 589832 | tf_op jit(solution)/shard_map/ppermute | solution.py:65
  46.3 0.5 collective-permute-start.22
  46.8 0.1 collective-permute-start.21
  46.9 2.7 %collective-permute-done.13.refs_3_.refs_15_ = bf16[768,128]{1,0:T(8,128)(2,1)S(1)} collective-permute-done((bf16[768,128]{1,0:T(8,128)(2,1)S(1)}, bf16[768,128]{1,0:T(8,128)(2,1)S(1)}, u32[]{:S(2)}, u32[]{:S(2)}) %collective-permute-start.13) | collective-permute-done | bytes 196640 | tf_op jit(solution)/shard_map/ppermute | solution.py:65
  49.6 1.1 %collective-permute-done.19.refs_11_.refs_23_ = bf16[768,128]{1,0:T(8,128)(2,1)S(1)} collective-permute-done((bf16[768,128]{1,0:T(8,128)(2,1)S(1)}, bf16[768,128]{1,0:T(8,128)(2,1)S(1)}, u32[]{:S(2)}, u32[]{:S(2)}) %collective-permute-start.19) | collective-permute-done | bytes 196640 | tf_op jit(solution)/shard_map/ppermute | solution.py:65
  50.7 0.3 collective-permute-done.17.refs_7_.refs_19_
  51.0 1.1 %collective-permute-done.23.refs_15_.refs_27_ = bf16[768,128]{1,0:T(8,128)(2,1)S(1)} collective-permute-done((bf16[768,128]{1,0:T(8,128)(2,1)S(1)}, bf16[768,128]{1,0:T(8,128)(2,1)S(1)}, u32[]{:S(2)}, u32[]{:S(2)}) %collective-permute-start.23) | collective-permute-done | bytes 196640 | tf_op jit(solution)/shard_map/ppermute | solution.py:65
  52.2 1.4 %shard_map.103 = (bf16[128,384]{1,0:T(8,128)(2,1)S(1)}, bf16[128,384]{1,0:T(8,128)(2,1)S(1)}, bf16[128,384]{1,0:T(8,128)(2,1)S(1)}, bf16[128,384]{1,0:T(8,128)(2,1)S(1)}) custom-call(s32[3]{0:T(128)S(1)} %pad_add_fusion.place_ref, bf16[128,1024]{1,0:T(8,128)(2,1)S(1)} %bitcast.22, bf16[768,128]{1,0:T(8,128)(2,1)S(1)} %collective-permute-done.refs_0_.refs_12_, ...), custom_call_target="tpu_custom_call" | custom-call | tf_op jit(solution)/shard_map/pallas_call | solution.py:369
  53.6 0.1 collective-permute-start.24
  53.7 1.1 %collective-permute-start.25 = (bf16[128,384]{1,0:T(8,128)(2,1)S(1)}, bf16[128,384]{1,0:T(8,128)(2,1)S(1)}, u32[]{:S(2)}, u32[]{:S(2)}) collective-permute-start(bf16[128,384]{1,0:T(8,128)(2,1)S(1)} %get-tuple-element.46), channel_id=1, source_target_pairs={{0,8},{4,12},{8,0},{12,4},{1,9},{5,13},{9,1},{13,5},{2,10},{6,14},... | collective-permute-start | bytes 294920 | tf_op jit(solution)/shard_map/ppermute | solution.py:76
  54.8 3.3 %collective-permute-start.26 = (bf16[128,384]{1,0:T(8,128)(2,1)S(1)}, bf16[128,384]{1,0:T(8,128)(2,1)S(1)}, u32[]{:S(2)}, u32[]{:S(2)}) collective-permute-start(bf16[128,384]{1,0:T(8,128)(2,1)S(1)} %get-tuple-element.47), channel_id=1, source_target_pairs={{0,12},{4,8},{8,4},{12,0},{1,13},{5,9},{9,5},{13,1},{2,14},{6,10},... | collective-permute-start | bytes 294920 | tf_op jit(solution)/shard_map/ppermute | solution.py:76
  58.0 1.1 %collective-permute-start.29 = (bf16[144,128]{1,0:T(8,128)(2,1)S(1)}, bf16[144,128]{1,0:T(8,128)(2,1)S(1)}, u32[]{:S(2)}, u32[]{:S(2)}) collective-permute-start(bf16[144,128]{1,0:T(8,128)(2,1)S(1)} %get-tuple-element.49), channel_id=1, source_target_pairs={{0,8},{4,12},{8,0},{12,4},{1,9},{5,13},{9,1},{13,5},{2,10},{6,14},... | collective-permute-start | bytes 110600 | tf_op jit(solution)/shard_map/ppermute | solution.py:76
  59.2 0.5 collective-permute-done.24
  59.7 2.8 %collective-permute-start.30 = (bf16[144,128]{1,0:T(8,128)(2,1)S(1)}, bf16[144,128]{1,0:T(8,128)(2,1)S(1)}, u32[]{:S(2)}, u32[]{:S(2)}) collective-permute-start(bf16[144,128]{1,0:T(8,128)(2,1)S(1)} %get-tuple-element.50), channel_id=1, source_target_pairs={{0,12},{4,8},{8,4},{12,0},{1,13},{5,9},{9,5},{13,1},{2,14},{6,10},... | collective-permute-start | bytes 110600 | tf_op jit(solution)/shard_map/ppermute | solution.py:76
  62.4 3.7 %collective-permute-done.25 = bf16[128,384]{1,0:T(8,128)(2,1)S(1)} collective-permute-done((bf16[128,384]{1,0:T(8,128)(2,1)S(1)}, bf16[128,384]{1,0:T(8,128)(2,1)S(1)}, u32[]{:S(2)}, u32[]{:S(2)}) %collective-permute-start.25) | collective-permute-done | bytes 98336 | tf_op jit(solution)/shard_map/ppermute | solution.py:76
  66.1 0.1 convert_add_fusion.refs_0_
  66.2 0.1 collective-permute-start.27
  66.3 2.3 %collective-permute-done.29 = bf16[144,128]{1,0:T(8,128)(2,1)S(1)} collective-permute-done((bf16[144,128]{1,0:T(8,128)(2,1)S(1)}, bf16[144,128]{1,0:T(8,128)(2,1)S(1)}, u32[]{:S(2)}, u32[]{:S(2)}) %collective-permute-start.29) | collective-permute-done | bytes 36896 | tf_op jit(solution)/shard_map/ppermute | solution.py:76
  68.6 0.1 collective-permute-start.31
  68.7 1.3 %collective-permute-done.31.refs_3_ = f32[144,128]{1,0:T(8,128)S(1)} collective-permute-done((f32[144,128]{1,0:T(8,128)S(1)}, f32[144,128]{1,0:T(8,128)S(1)}, u32[]{:S(2)}, u32[]{:S(2)}) %collective-permute-start.31) | collective-permute-done | bytes 73760 | tf_op jit(solution)/shard_map/ppermute | solution.py:65
  70.0 10.8 %shard_map.104 = (bf16[144,512]{1,0:T(8,128)(2,1)S(1)}, f32[64,256]{1,0:T(8,128)S(1)}, f32[64,256]{1,0:T(8,128)S(1)}, f32[64,256]{1,0:T(8,128)S(1)}, f32[64,256]{1,0:T(8,128)S(1)}) custom-call(s32[3]{0:T(128)S(1)} %pad_add_fusion.place_ref, f32[128,384]{1,0:T(8,128)S(1)} %convert_add_fusion.refs_0_, f32[128,384]{1,0:T(8,128)S(1)} %collective-permute-done.27.refs_1_, ...), custom_call_target="tpu_custom_call" | custom-call | tf_op jit(solution)/shard_map/pallas_call | solution.py:369
  80.8 1.0 %collective-permute-start.32 = (bf16[144,512]{1,0:T(8,128)(2,1)S(1)}, bf16[144,512]{1,0:T(8,128)(2,1)S(1)}, u32[]{:S(2)}, u32[]{:S(2)}) collective-permute-start(bf16[144,512]{1,0:T(8,128)(2,1)S(1)} %get-tuple-element.51.refs_0_), channel_id=1, source_target_pairs={{4,0},{0,4},{12,8},{8,12},{5,1},{1,5},{13,9},{9,13},{6,2},{2,6},{1... | collective-permute-start | bytes 442376 | tf_op jit(solution)/shard_map/ppermute | solution.py:65
  81.8 1.0 %collective-permute-start.33 = (bf16[144,512]{1,0:T(8,128)(2,1)S(1)}, bf16[144,512]{1,0:T(8,128)(2,1)S(1)}, u32[]{:S(2)}, u32[]{:S(2)}) collective-permute-start(bf16[144,512]{1,0:T(8,128)(2,1)S(1)} %get-tuple-element.51.refs_0_), channel_id=1, source_target_pairs={{8,0},{12,4},{0,8},{4,12},{9,1},{13,5},{1,9},{5,13},{10,2},{14,6},... | collective-permute-start | bytes 442376 | tf_op jit(solution)/shard_map/ppermute | solution.py:65
  82.8 2.4 %collective-permute-start.34 = (bf16[144,512]{1,0:T(8,128)(2,1)S(1)}, bf16[144,512]{1,0:T(8,128)(2,1)S(1)}, u32[]{:S(2)}, u32[]{:S(2)}) collective-permute-start(bf16[144,512]{1,0:T(8,128)(2,1)S(1)} %get-tuple-element.51.refs_0_), channel_id=1, source_target_pairs={{12,0},{8,4},{4,8},{0,12},{13,1},{9,5},{5,9},{1,13},{14,2},{10,6},... | collective-permute-start | bytes 442376 | tf_op jit(solution)/shard_map/ppermute | solution.py:65
  85.3 3.5 %collective-permute-done.32.refs_1_ = bf16[144,512]{1,0:T(8,128)(2,1)S(1)} collective-permute-done((bf16[144,512]{1,0:T(8,128)(2,1)S(1)}, bf16[144,512]{1,0:T(8,128)(2,1)S(1)}, u32[]{:S(2)}, u32[]{:S(2)}) %collective-permute-start.32) | collective-permute-done | bytes 147488 | tf_op jit(solution)/shard_map/ppermute | solution.py:65
  88.7 1.5 %collective-permute-start.35 = (f32[64,256]{1,0:T(8,128)S(1)}, f32[64,256]{1,0:T(8,128)S(1)}, u32[]{:S(2)}, u32[]{:S(2)}) collective-permute-start(f32[64,256]{1,0:T(8,128)S(1)} %get-tuple-element.59), channel_id=1, source_target_pairs={{0,1},{1,0},{2,3},{3,2},{4,5},{5,4},{6,7},{7,6},{8,9},{9,8},{10,11... | collective-permute-start | bytes 196616 | tf_op jit(solution)/shard_map/ppermute | solution.py:76
  90.3 0.7 collective-permute-start.36
  91.0 1.3 %collective-permute-start.37 = (f32[64,256]{1,0:T(8,128)S(1)}, f32[64,256]{1,0:T(8,128)S(1)}, u32[]{:S(2)}, u32[]{:S(2)}) collective-permute-start(f32[64,256]{1,0:T(8,128)S(1)} %get-tuple-element.61), channel_id=1, source_target_pairs={{0,3},{1,2},{2,1},{3,0},{4,7},{5,6},{6,5},{7,4},{8,11},{9,10},{10,... | collective-permute-start | bytes 196616 | tf_op jit(solution)/shard_map/ppermute | solution.py:76
  92.2 3.6 %collective-permute-done.33.refs_2_ = bf16[144,512]{1,0:T(8,128)(2,1)S(1)} collective-permute-done((bf16[144,512]{1,0:T(8,128)(2,1)S(1)}, bf16[144,512]{1,0:T(8,128)(2,1)S(1)}, u32[]{:S(2)}, u32[]{:S(2)}) %collective-permute-start.33) | collective-permute-done | bytes 147488 | tf_op jit(solution)/shard_map/ppermute | solution.py:65
  95.8 3.1 %shard_map.105 = (bf16[128,1024]{1,0:T(8,128)(2,1)}, bf16[128,1024]{1,0:T(8,128)(2,1)}) custom-call(s32[3]{0:T(128)S(1)} %pad_add_fusion.place_ref, bf16[144,512]{1,0:T(8,128)(2,1)S(1)} %get-tuple-element.51.refs_0_, bf16[144,512]{1,0:T(8,128)(2,1)S(1)} %collective-permute-done.32.refs_1_, bf16[144,512]{1,0:T(8,128)(2,1)S(1)} %collective-permute-done.33.refs_2_, ...), custom_call_target="tpu_custom_call" | custom-call | tf_op jit(solution)/shard_map/pallas_call | solution.py:369
  99.0 0.6 slice_bitcast_fusion
  (35 shorter events, 0.1 us)
Async XLA Ops:
  0.6 0.7 copy-start
  2.3 2.5 %collective-permute-start.3 = (bf16[528,128]{1,0:T(8,128)(2,1)S(1)}, bf16[528,128]{1,0:T(8,128)(2,1)S(1)}, u32[]{:S(2)}, u32[]{:S(2)}) collective-permute-start(bf16[528,128]{1,0:T(8,128)(2,1)S(1)} %fusion.1), channel_id=1, source_target_pairs={{0,0},{1,1},{2,4},{3,5},{4,2},{5,3},{6,6},{7,7},{8,16},{9,17},{10,... | collective-permute-start | bytes 405512 | tf_op jit(solution)/shard_map/ppermute | solution.py:400
  3.0 33.7 %copy-start.1 = (bf16[1,128,1024]{2,1,0:T(8,128)(2,1)S(1)}, bf16[1,128,1024]{2,1,0:T(8,128)(2,1)}, u32[]{:S(2)}) copy-start(bf16[1,128,1024]{2,1,0:T(8,128)(2,1)} %param.7) | copy-start | bytes 786436
  3.0 33.7 %copy-start.2 = (bf16[1,128,1024]{2,1,0:T(8,128)(2,1)S(1)}, bf16[1,128,1024]{2,1,0:T(8,128)(2,1)}, u32[]{:S(2)}) copy-start(bf16[1,128,1024]{2,1,0:T(8,128)(2,1)} %param.13) | copy-start | bytes 786436
  4.2 13.6 %collective-permute-start.2 = (bf16[768,128]{1,0:T(8,128)(2,1)S(1)}, bf16[768,128]{1,0:T(8,128)(2,1)S(1)}, u32[]{:S(2)}, u32[]{:S(2)}) collective-permute-start(bf16[768,128]{1,0:T(8,128)(2,1)S(1)} %bitcast.28), channel_id=1, source_target_pairs={{0,0},{1,1},{2,4},{3,5},{4,2},{5,3},{6,6},{7,7},{8,16},{9,17},{10,... | collective-permute-start | bytes 589832 | tf_op jit(solution)/shard_map/ppermute | solution.py:400
  4.8 13.0 %collective-permute-start.4 = (bf16[528,128]{1,0:T(8,128)(2,1)S(1)}, bf16[528,128]{1,0:T(8,128)(2,1)S(1)}, u32[]{:S(2)}, u32[]{:S(2)}) collective-permute-start(bf16[528,128]{1,0:T(8,128)(2,1)S(1)} %collective-permute-done.3.refs_0_.refs_4_), channel_id=1, source_target_pairs={{1,0},{0,1},{3,2},{2,3},{5,4},{4,5},{7,6},{6,7},{9,8},{8,9},{11,10... | collective-permute-start | bytes 405512 | tf_op jit(solution)/shard_map/ppermute | solution.py:65
  7.9 22.1 %collective-permute-start.5 = (bf16[528,128]{1,0:T(8,128)(2,1)S(1)}, bf16[528,128]{1,0:T(8,128)(2,1)S(1)}, u32[]{:S(2)}, u32[]{:S(2)}) collective-permute-start(bf16[528,128]{1,0:T(8,128)(2,1)S(1)} %collective-permute-done.3.refs_0_.refs_4_), channel_id=1, source_target_pairs={{2,0},{3,1},{0,2},{1,3},{6,4},{7,5},{4,6},{5,7},{10,8},{11,9},{8,1... | collective-permute-start | bytes 405512 | tf_op jit(solution)/shard_map/ppermute | solution.py:65
  17.1 12.9 %collective-permute-start.6 = (bf16[528,128]{1,0:T(8,128)(2,1)S(1)}, bf16[528,128]{1,0:T(8,128)(2,1)S(1)}, u32[]{:S(2)}, u32[]{:S(2)}) collective-permute-start(bf16[528,128]{1,0:T(8,128)(2,1)S(1)} %collective-permute-done.3.refs_0_.refs_4_), channel_id=1, source_target_pairs={{3,0},{2,1},{1,2},{0,3},{7,4},{6,5},{5,6},{4,7},{11,8},{10,9},{9,1... | collective-permute-start | bytes 405512 | tf_op jit(solution)/shard_map/ppermute | solution.py:65
  17.1 13.4 %collective-permute-start = (bf16[768,128]{1,0:T(8,128)(2,1)S(1)}, bf16[768,128]{1,0:T(8,128)(2,1)S(1)}, u32[]{:S(2)}, u32[]{:S(2)}) collective-permute-start(bf16[768,128]{1,0:T(8,128)(2,1)S(1)} %bitcast.27), channel_id=1, source_target_pairs={{0,0},{1,1},{2,4},{3,5},{4,2},{5,3},{6,6},{7,7},{8,16},{9,17},{10,... | collective-permute-start | bytes 589832 | tf_op jit(solution)/shard_map/ppermute | solution.py:400
  30.0 3.5 %collective-permute-start.10 = (bf16[528,128]{1,0:T(8,128)(2,1)S(1)}, bf16[528,128]{1,0:T(8,128)(2,1)S(1)}, u32[]{:S(2)}, u32[]{:S(2)}) collective-permute-start(bf16[528,128]{1,0:T(8,128)(2,1)S(1)} %collective-permute-done.5.refs_2_.refs_6_), channel_id=1, source_target_pairs={{16,0},{0,16},{17,1},{1,17},{18,2},{2,18},{19,3},{3,19},{20,4},{4,... | collective-permute-start | bytes 405512 | tf_op jit(solution)/shard_map/ppermute | solution.py:65
  30.0 3.8 %collective-permute-start.11 = (bf16[528,128]{1,0:T(8,128)(2,1)S(1)}, bf16[528,128]{1,0:T(8,128)(2,1)S(1)}, u32[]{:S(2)}, u32[]{:S(2)}) collective-permute-start(bf16[528,128]{1,0:T(8,128)(2,1)S(1)} %collective-permute-done.6.refs_3_.refs_7_), channel_id=1, source_target_pairs={{16,0},{0,16},{17,1},{1,17},{18,2},{2,18},{19,3},{3,19},{20,4},{4,... | collective-permute-start | bytes 405512 | tf_op jit(solution)/shard_map/ppermute | solution.py:65
  30.5 3.3 %collective-permute-start.8 = (bf16[528,128]{1,0:T(8,128)(2,1)S(1)}, bf16[528,128]{1,0:T(8,128)(2,1)S(1)}, u32[]{:S(2)}, u32[]{:S(2)}) collective-permute-start(bf16[528,128]{1,0:T(8,128)(2,1)S(1)} %collective-permute-done.3.refs_0_.refs_4_), channel_id=1, source_target_pairs={{16,0},{0,16},{17,1},{1,17},{18,2},{2,18},{19,3},{3,19},{20,4},{4,... | collective-permute-start | bytes 405512 | tf_op jit(solution)/shard_map/ppermute | solution.py:65
  30.5 7.5 %collective-permute-start.1 = (bf16[768,128]{1,0:T(8,128)(2,1)S(1)}, bf16[768,128]{1,0:T(8,128)(2,1)S(1)}, u32[]{:S(2)}, u32[]{:S(2)}) collective-permute-start(bf16[768,128]{1,0:T(8,128)(2,1)S(1)} %collective-permute-done.refs_0_.refs_12_), channel_id=1, source_target_pairs={{1,0},{0,1},{3,2},{2,3},{5,4},{4,5},{7,6},{6,7},{9,8},{8,9},{11,10... | collective-permute-start | bytes 589832 | tf_op jit(solution)/shard_map/ppermute | solution.py:65
  31.0 8.2 %collective-permute-start.12 = (bf16[768,128]{1,0:T(8,128)(2,1)S(1)}, bf16[768,128]{1,0:T(8,128)(2,1)S(1)}, u32[]{:S(2)}, u32[]{:S(2)}) collective-permute-start(bf16[768,128]{1,0:T(8,128)(2,1)S(1)} %collective-permute-done.refs_0_.refs_12_), channel_id=1, source_target_pairs={{2,0},{3,1},{0,2},{1,3},{6,4},{7,5},{4,6},{5,7},{10,8},{11,9},{8,1... | collective-permute-start | bytes 589832 | tf_op jit(solution)/shard_map/ppermute | solution.py:65
  33.5 9.5 %collective-permute-start.7 = (bf16[768,128]{1,0:T(8,128)(2,1)S(1)}, bf16[768,128]{1,0:T(8,128)(2,1)S(1)}, u32[]{:S(2)}, u32[]{:S(2)}) collective-permute-start(bf16[768,128]{1,0:T(8,128)(2,1)S(1)} %collective-permute-done.2.refs_8_.refs_20_), channel_id=1, source_target_pairs={{2,0},{3,1},{0,2},{1,3},{6,4},{7,5},{4,6},{5,7},{10,8},{11,9},{8,1... | collective-permute-start | bytes 589832 | tf_op jit(solution)/shard_map/ppermute | solution.py:65
  33.8 10.9 %collective-permute-start.14 = (bf16[768,128]{1,0:T(8,128)(2,1)S(1)}, bf16[768,128]{1,0:T(8,128)(2,1)S(1)}, u32[]{:S(2)}, u32[]{:S(2)}) collective-permute-start(bf16[768,128]{1,0:T(8,128)(2,1)S(1)} %collective-permute-done.refs_0_.refs_12_), channel_id=1, source_target_pairs={{16,0},{0,16},{17,1},{1,17},{18,2},{2,18},{19,3},{3,19},{20,4},{4,... | collective-permute-start | bytes 589832 | tf_op jit(solution)/shard_map/ppermute | solution.py:65
  33.8 1.6 %collective-permute-start.9 = (bf16[528,128]{1,0:T(8,128)(2,1)S(1)}, bf16[528,128]{1,0:T(8,128)(2,1)S(1)}, u32[]{:S(2)}, u32[]{:S(2)}) collective-permute-start(bf16[528,128]{1,0:T(8,128)(2,1)S(1)} %collective-permute-done.4.refs_1_.refs_5_), channel_id=1, source_target_pairs={{16,0},{0,16},{17,1},{1,17},{18,2},{2,18},{19,3},{3,19},{20,4},{4,... | collective-permute-start | bytes 405512 | tf_op jit(solution)/shard_map/ppermute | solution.py:65
  35.5 10.8 %collective-permute-start.18 = (bf16[768,128]{1,0:T(8,128)(2,1)S(1)}, bf16[768,128]{1,0:T(8,128)(2,1)S(1)}, u32[]{:S(2)}, u32[]{:S(2)}) collective-permute-start(bf16[768,128]{1,0:T(8,128)(2,1)S(1)} %collective-permute-done.2.refs_8_.refs_20_), channel_id=1, source_target_pairs={{1,0},{0,1},{3,2},{2,3},{5,4},{4,5},{7,6},{6,7},{9,8},{8,9},{11,10... | collective-permute-start | bytes 589832 | tf_op jit(solution)/shard_map/ppermute | solution.py:65
  38.1 8.2 %collective-permute-start.20 = (bf16[768,128]{1,0:T(8,128)(2,1)S(1)}, bf16[768,128]{1,0:T(8,128)(2,1)S(1)}, u32[]{:S(2)}, u32[]{:S(2)}) collective-permute-start(bf16[768,128]{1,0:T(8,128)(2,1)S(1)} %collective-permute-done.2.refs_8_.refs_20_), channel_id=1, source_target_pairs={{16,0},{0,16},{17,1},{1,17},{18,2},{2,18},{19,3},{3,19},{20,4},{4,... | collective-permute-start | bytes 589832 | tf_op jit(solution)/shard_map/ppermute | solution.py:65
  39.2 7.6 %collective-permute-start.16 = (bf16[768,128]{1,0:T(8,128)(2,1)S(1)}, bf16[768,128]{1,0:T(8,128)(2,1)S(1)}, u32[]{:S(2)}, u32[]{:S(2)}) collective-permute-start(bf16[768,128]{1,0:T(8,128)(2,1)S(1)} %collective-permute-done.12.refs_2_.refs_14_), channel_id=1, source_target_pairs={{16,0},{0,16},{17,1},{1,17},{18,2},{2,18},{19,3},{3,19},{20,4},{4,... | collective-permute-start | bytes 589832 | tf_op jit(solution)/shard_map/ppermute | solution.py:65
  43.0 6.5 %collective-permute-start.13 = (bf16[768,128]{1,0:T(8,128)(2,1)S(1)}, bf16[768,128]{1,0:T(8,128)(2,1)S(1)}, u32[]{:S(2)}, u32[]{:S(2)}) collective-permute-start(bf16[768,128]{1,0:T(8,128)(2,1)S(1)} %collective-permute-done.1.refs_1_.refs_13_), channel_id=1, source_target_pairs={{2,0},{3,1},{0,2},{1,3},{6,4},{7,5},{4,6},{5,7},{10,8},{11,9},{8,1... | collective-permute-start | bytes 589832 | tf_op jit(solution)/shard_map/ppermute | solution.py:65
  44.8 5.9 %collective-permute-start.19 = (bf16[768,128]{1,0:T(8,128)(2,1)S(1)}, bf16[768,128]{1,0:T(8,128)(2,1)S(1)}, u32[]{:S(2)}, u32[]{:S(2)}) collective-permute-start(bf16[768,128]{1,0:T(8,128)(2,1)S(1)} %collective-permute-done.7.refs_10_.refs_22_), channel_id=1, source_target_pairs={{1,0},{0,1},{3,2},{2,3},{5,4},{4,5},{7,6},{6,7},{9,8},{8,9},{11,10... | collective-permute-start | bytes 589832 | tf_op jit(solution)/shard_map/ppermute | solution.py:65
  46.3 4.4 %collective-permute-start.15 = (bf16[768,128]{1,0:T(8,128)(2,1)S(1)}, bf16[768,128]{1,0:T(8,128)(2,1)S(1)}, u32[]{:S(2)}, u32[]{:S(2)}) collective-permute-start(bf16[768,128]{1,0:T(8,128)(2,1)S(1)} %collective-permute-done.1.refs_1_.refs_13_), channel_id=1, source_target_pairs={{16,0},{0,16},{17,1},{1,17},{18,2},{2,18},{19,3},{3,19},{20,4},{4,... | collective-permute-start | bytes 589832 | tf_op jit(solution)/shard_map/ppermute | solution.py:65
  46.3 4.4 %collective-permute-start.22 = (bf16[768,128]{1,0:T(8,128)(2,1)S(1)}, bf16[768,128]{1,0:T(8,128)(2,1)S(1)}, u32[]{:S(2)}, u32[]{:S(2)}) collective-permute-start(bf16[768,128]{1,0:T(8,128)(2,1)S(1)} %collective-permute-done.7.refs_10_.refs_22_), channel_id=1, source_target_pairs={{16,0},{0,16},{17,1},{1,17},{18,2},{2,18},{19,3},{3,19},{20,4},{4,... | collective-permute-start | bytes 589832 | tf_op jit(solution)/shard_map/ppermute | solution.py:65
  46.8 3.9 %collective-permute-start.21 = (bf16[768,128]{1,0:T(8,128)(2,1)S(1)}, bf16[768,128]{1,0:T(8,128)(2,1)S(1)}, u32[]{:S(2)}, u32[]{:S(2)}) collective-permute-start(bf16[768,128]{1,0:T(8,128)(2,1)S(1)} %collective-permute-done.18.refs_9_.refs_21_), channel_id=1, source_target_pairs={{16,0},{0,16},{17,1},{1,17},{18,2},{2,18},{19,3},{3,19},{20,4},{4,... | collective-permute-start | bytes 589832 | tf_op jit(solution)/shard_map/ppermute | solution.py:65
  49.6 1.4 %collective-permute-start.17 = (bf16[768,128]{1,0:T(8,128)(2,1)S(1)}, bf16[768,128]{1,0:T(8,128)(2,1)S(1)}, u32[]{:S(2)}, u32[]{:S(2)}) collective-permute-start(bf16[768,128]{1,0:T(8,128)(2,1)S(1)} %collective-permute-done.13.refs_3_.refs_15_), channel_id=1, source_target_pairs={{16,0},{0,16},{17,1},{1,17},{18,2},{2,18},{19,3},{3,19},{20,4},{4,... | collective-permute-start | bytes 589832 | tf_op jit(solution)/shard_map/ppermute | solution.py:65
  50.7 1.4 %collective-permute-start.23 = (bf16[768,128]{1,0:T(8,128)(2,1)S(1)}, bf16[768,128]{1,0:T(8,128)(2,1)S(1)}, u32[]{:S(2)}, u32[]{:S(2)}) collective-permute-start(bf16[768,128]{1,0:T(8,128)(2,1)S(1)} %collective-permute-done.19.refs_11_.refs_23_), channel_id=1, source_target_pairs={{16,0},{0,16},{17,1},{1,17},{18,2},{2,18},{19,3},{3,19},{20,4},{4,... | collective-permute-start | bytes 589832 | tf_op jit(solution)/shard_map/ppermute | solution.py:65
  53.6 6.1 %collective-permute-start.24 = (bf16[128,384]{1,0:T(8,128)(2,1)S(1)}, bf16[128,384]{1,0:T(8,128)(2,1)S(1)}, u32[]{:S(2)}, u32[]{:S(2)}) collective-permute-start(bf16[128,384]{1,0:T(8,128)(2,1)S(1)} %get-tuple-element.45), channel_id=1, source_target_pairs={{0,4},{4,0},{8,12},{12,8},{1,5},{5,1},{9,13},{13,9},{2,6},{6,2},{1... | collective-permute-start | bytes 294920 | tf_op jit(solution)/shard_map/ppermute | solution.py:76
  53.7 12.4 %collective-permute-start.25 = (bf16[128,384]{1,0:T(8,128)(2,1)S(1)}, bf16[128,384]{1,0:T(8,128)(2,1)S(1)}, u32[]{:S(2)}, u32[]{:S(2)}) collective-permute-start(bf16[128,384]{1,0:T(8,128)(2,1)S(1)} %get-tuple-element.46), channel_id=1, source_target_pairs={{0,8},{4,12},{8,0},{12,4},{1,9},{5,13},{9,1},{13,5},{2,10},{6,14},... | collective-permute-start | bytes 294920 | tf_op jit(solution)/shard_map/ppermute | solution.py:76
  54.8 11.3 %collective-permute-start.26 = (bf16[128,384]{1,0:T(8,128)(2,1)S(1)}, bf16[128,384]{1,0:T(8,128)(2,1)S(1)}, u32[]{:S(2)}, u32[]{:S(2)}) collective-permute-start(bf16[128,384]{1,0:T(8,128)(2,1)S(1)} %get-tuple-element.47), channel_id=1, source_target_pairs={{0,12},{4,8},{8,4},{12,0},{1,13},{5,9},{9,5},{13,1},{2,14},{6,10},... | collective-permute-start | bytes 294920 | tf_op jit(solution)/shard_map/ppermute | solution.py:76
  58.0 8.2 %collective-permute-start.28 = (bf16[144,128]{1,0:T(8,128)(2,1)S(1)}, bf16[144,128]{1,0:T(8,128)(2,1)S(1)}, u32[]{:S(2)}, u32[]{:S(2)}) collective-permute-start(bf16[144,128]{1,0:T(8,128)(2,1)S(1)} %get-tuple-element.48), channel_id=1, source_target_pairs={{0,4},{4,0},{8,12},{12,8},{1,5},{5,1},{9,13},{13,9},{2,6},{6,2},{1... | collective-permute-start | bytes 110600 | tf_op jit(solution)/shard_map/ppermute | solution.py:76
  58.0 10.6 %collective-permute-start.29 = (bf16[144,128]{1,0:T(8,128)(2,1)S(1)}, bf16[144,128]{1,0:T(8,128)(2,1)S(1)}, u32[]{:S(2)}, u32[]{:S(2)}) collective-permute-start(bf16[144,128]{1,0:T(8,128)(2,1)S(1)} %get-tuple-element.49), channel_id=1, source_target_pairs={{0,8},{4,12},{8,0},{12,4},{1,9},{5,13},{9,1},{13,5},{2,10},{6,14},... | collective-permute-start | bytes 110600 | tf_op jit(solution)/shard_map/ppermute | solution.py:76
  59.7 8.9 %collective-permute-start.30 = (bf16[144,128]{1,0:T(8,128)(2,1)S(1)}, bf16[144,128]{1,0:T(8,128)(2,1)S(1)}, u32[]{:S(2)}, u32[]{:S(2)}) collective-permute-start(bf16[144,128]{1,0:T(8,128)(2,1)S(1)} %get-tuple-element.50), channel_id=1, source_target_pairs={{0,12},{4,8},{8,4},{12,0},{1,13},{5,9},{9,5},{13,1},{2,14},{6,10},... | collective-permute-start | bytes 110600 | tf_op jit(solution)/shard_map/ppermute | solution.py:76
  66.1 3.8 %copy-start.3 = (f32[1,128,512]{2,1,0:T(8,128)S(1)}, f32[1,128,512]{2,1,0:T(8,128)}, u32[]{:S(2)}) copy-start(f32[1,128,512]{2,1,0:T(8,128)} %param.11) | copy-start | bytes 786436
  66.1 3.8 %copy-start.4 = (f32[1,512,128]{2,1,0:T(8,128)S(1)}, f32[1,512,128]{2,1,0:T(8,128)}, u32[]{:S(2)}) copy-start(f32[1,512,128]{2,1,0:T(8,128)} %param.12) | copy-start | bytes 786436
  66.2 3.8 %collective-permute-start.27 = (f32[128,384]{1,0:T(8,128)S(1)}, f32[128,384]{1,0:T(8,128)S(1)}, u32[]{:S(2)}, u32[]{:S(2)}) collective-permute-start(f32[128,384]{1,0:T(8,128)S(1)} %convert_add_fusion.refs_0_), channel_id=1, source_target_pairs={{16,0},{0,16},{17,1},{1,17},{18,2},{2,18},{19,3},{3,19},{20,4},{4,... | collective-permute-start | bytes 589832 | tf_op jit(solution)/shard_map/ppermute | solution.py:65
  68.6 1.3 %collective-permute-start.31 = (f32[144,128]{1,0:T(8,128)S(1)}, f32[144,128]{1,0:T(8,128)S(1)}, u32[]{:S(2)}, u32[]{:S(2)}) collective-permute-start(f32[144,128]{1,0:T(8,128)S(1)} %convert_add_fusion.1.refs_2_), channel_id=1, source_target_pairs={{16,0},{0,16},{17,1},{1,17},{18,2},{2,18},{19,3},{3,19},{20,4},{4,... | collective-permute-start | bytes 221192 | tf_op jit(solution)/shard_map/ppermute | solution.py:65
  80.8 7.9 %collective-permute-start.32 = (bf16[144,512]{1,0:T(8,128)(2,1)S(1)}, bf16[144,512]{1,0:T(8,128)(2,1)S(1)}, u32[]{:S(2)}, u32[]{:S(2)}) collective-permute-start(bf16[144,512]{1,0:T(8,128)(2,1)S(1)} %get-tuple-element.51.refs_0_), channel_id=1, source_target_pairs={{4,0},{0,4},{12,8},{8,12},{5,1},{1,5},{13,9},{9,13},{6,2},{2,6},{1... | collective-permute-start | bytes 442376 | tf_op jit(solution)/shard_map/ppermute | solution.py:65
  81.8 14.0 %collective-permute-start.33 = (bf16[144,512]{1,0:T(8,128)(2,1)S(1)}, bf16[144,512]{1,0:T(8,128)(2,1)S(1)}, u32[]{:S(2)}, u32[]{:S(2)}) collective-permute-start(bf16[144,512]{1,0:T(8,128)(2,1)S(1)} %get-tuple-element.51.refs_0_), channel_id=1, source_target_pairs={{8,0},{12,4},{0,8},{4,12},{9,1},{13,5},{1,9},{5,13},{10,2},{14,6},... | collective-permute-start | bytes 442376 | tf_op jit(solution)/shard_map/ppermute | solution.py:65
  82.8 13.0 %collective-permute-start.34 = (bf16[144,512]{1,0:T(8,128)(2,1)S(1)}, bf16[144,512]{1,0:T(8,128)(2,1)S(1)}, u32[]{:S(2)}, u32[]{:S(2)}) collective-permute-start(bf16[144,512]{1,0:T(8,128)(2,1)S(1)} %get-tuple-element.51.refs_0_), channel_id=1, source_target_pairs={{12,0},{8,4},{4,8},{0,12},{13,1},{9,5},{5,9},{1,13},{14,2},{10,6},... | collective-permute-start | bytes 442376 | tf_op jit(solution)/shard_map/ppermute | solution.py:65
  88.7 10.2 %collective-permute-start.35 = (f32[64,256]{1,0:T(8,128)S(1)}, f32[64,256]{1,0:T(8,128)S(1)}, u32[]{:S(2)}, u32[]{:S(2)}) collective-permute-start(f32[64,256]{1,0:T(8,128)S(1)} %get-tuple-element.59), channel_id=1, source_target_pairs={{0,1},{1,0},{2,3},{3,2},{4,5},{5,4},{6,7},{7,6},{8,9},{9,8},{10,11... | collective-permute-start | bytes 196616 | tf_op jit(solution)/shard_map/ppermute | solution.py:76
  90.3 8.7 %collective-permute-start.36 = (f32[64,256]{1,0:T(8,128)S(1)}, f32[64,256]{1,0:T(8,128)S(1)}, u32[]{:S(2)}, u32[]{:S(2)}) collective-permute-start(f32[64,256]{1,0:T(8,128)S(1)} %get-tuple-element.60), channel_id=1, source_target_pairs={{0,2},{1,3},{2,0},{3,1},{4,6},{5,7},{6,4},{7,5},{8,10},{9,11},{10,... | collective-permute-start | bytes 196616 | tf_op jit(solution)/shard_map/ppermute | solution.py:76
  91.0 8.0 %collective-permute-start.37 = (f32[64,256]{1,0:T(8,128)S(1)}, f32[64,256]{1,0:T(8,128)S(1)}, u32[]{:S(2)}, u32[]{:S(2)}) collective-permute-start(f32[64,256]{1,0:T(8,128)S(1)} %get-tuple-element.61), channel_id=1, source_target_pairs={{0,3},{1,2},{2,1},{3,0},{4,7},{5,6},{6,5},{7,4},{8,11},{9,10},{10,... | collective-permute-start | bytes 196616 | tf_op jit(solution)/shard_map/ppermute | solution.py:76

commit v2 on v1

--- a/solution.py
+++ b/solution.py
@@ -412,7 +412,6 @@
     second_w = swapped(second)
     outer_near = peers_of(outer_w, "dp")
     first_near = [first_w, hop(first_w, "dp", 1), hop(first_w, "dp", 2)]
-    second_w, *outer_near = lax.optimization_barrier((second_w, *outer_near))
     second_near = [second_w, hop(second_w, "dp", 1), hop(second_w, "dp", 2)]
     outer_ws = over_seq(outer_near)
     def summed(arrays):
@@ -436,10 +435,11 @@
         first_near += [hop(first_w, "dp", j) for j in range(3, dps)]
         second_near += [hop(second_w, "dp", j) for j in range(3, dps)]
     inner_ws = over_seq(first_near) + over_seq(second_near)
+    later_place, unused = lax.optimization_barrier((place, outer_all[-1]))
     inner_part = call(
         functools.partial(inner_projection_kernel, *sizes),
         (jax.ShapeDtypeStruct((rows, 3 * hd), BF16),) * heads,
-        (place, tokens[0], *inner_ws),
+        (later_place, tokens[0], *inner_ws),
         [
             pltpu.VMEM((share, rows, features // share), BF16),
             pltpu.VMEM((heads, rows, 3 * hd), F32),

time: 99.9 us -> 98.6 us (0.987)
  waiting for transfers between devices: 38.3 us -> 32.9 us
  starting transfers between devices: 40.2 us -> 44.3 us
    ppermute x26, waiting for transfers between devices: 31.8 us -> 25.5 us  [hop(): lax.ppermute(array, axis, [(mate(i, step, count), i) for i in range(count)])]
    ppermute x26, starting transfers between devices: 26.4 us -> 30 us  [hop(): lax.ppermute(array, axis, [(mate(i, step, count), i) for i in range(count)])]
  transfers between devices with their start and end apart: 38 -> 38, of which waited for: 14 -> 14; matrix products, arithmetic and copies ran while one was open for 1% -> 1% of each run, Pallas kernels for 4% -> 5%
where the time goes in v2:
time: 98.6 us; the launch traced here: 98.4 us
  starting transfers between devices  44.3 us (45%)
  waiting for transfers between devices  32.9 us (33%)
  Pallas kernels  16.7 us (17%)
  local copies, waits for them, and re-layouts  2.4 us (2%)
  other arithmetic  1.14 us (1%)
    ppermute x26, starting transfers between devices, hop(): lax.ppermute(array, axis, [(mate(i, step, count), i) for i in range(count)])  30 us
    ppermute x26, waiting for transfers between devices, hop(): lax.ppermute(array, axis, [(mate(i, step, count), i) for i in range(count)])  25.5 us
    pallas_call x4, Pallas kernels, call(): pl.pallas_call(kernel, out_shape=outs, in_specs=[SMEM] + [VMEM] * (len(op...  16.7 us
    ppermute x9, starting transfers between devices, sent_to(): lax.ppermute(arrays[j], axis, [(i, mate(i, j, count)) for i in range(coun...  12.4 us
    ppermute x9, waiting for transfers between devices, sent_to(): lax.ppermute(arrays[j], axis, [(i, mate(i, j, count)) for i in range(coun...  7.44 us
    ppermute x3, starting transfers between devices, swapped(): return lax.ppermute(array, ('seq', 'head', 'dp'), pairs)  2 us
  transfers between devices with their start and end apart: 38, of which 14 were waited for; matrix products, arithmetic and copies ran while one was open for 1% of the time, Pallas kernels for 5%

profile of v2, /device:TPU:0, one launch (start us, length us, event | category | flops | bytes accessed | tf_op | source)
XLA Modules:
  0.0 98.4 jit_solution(13412929061000051144)
XLA Ops:
  0.6 0.0 copy-start
  0.7 0.1 pad_add_fusion.place_ref
  0.7 0.6 copy-done
  1.4 0.1 reduce
  1.4 0.9 fusion.1
  2.3 0.7 collective-permute-start
  3.0 0.0 copy-start.1
  3.0 0.0 copy-start.2
  3.0 1.1 %fusion.2 = (bf16[3,256,128]{2,1,0:T(8,128)(2,1)S(1)}, bf16[3,256,128]{2,1,0:T(8,128)(2,1)S(1)}) fusion(bf16[3,512,128]{2,1,0:T(8,128)(2,1)} %bitcast.26), kind=kLoop, calls=%fused_computation.10 | loop fusion | bytes 786432 | tf_op jit(solution)/shard_map/slice | solution.py:411
  4.2 0.7 collective-permute-start.12
  4.8 0.0 collective-permute-done.refs_0_.refs_4_
  4.8 3.0 %collective-permute-start.1 = (bf16[528,128]{1,0:T(8,128)(2,1)S(1)}, bf16[528,128]{1,0:T(8,128)(2,1)S(1)}, u32[]{:S(2)}, u32[]{:S(2)}) collective-permute-start(bf16[528,128]{1,0:T(8,128)(2,1)S(1)} %collective-permute-done.refs_0_.refs_4_), channel_id=1, source_target_pairs={{1,0},{0,1},{3,2},{2,3},{5,4},{4,5},{7,6},{6,7},{9,8},{8,9},{11,10... | collective-permute-start | bytes 405512 | tf_op jit(solution)/shard_map/ppermute | solution.py:65
  7.9 9.3 %collective-permute-start.2 = (bf16[528,128]{1,0:T(8,128)(2,1)S(1)}, bf16[528,128]{1,0:T(8,128)(2,1)S(1)}, u32[]{:S(2)}, u32[]{:S(2)}) collective-permute-start(bf16[528,128]{1,0:T(8,128)(2,1)S(1)} %collective-permute-done.refs_0_.refs_4_), channel_id=1, source_target_pairs={{2,0},{3,1},{0,2},{1,3},{6,4},{7,5},{4,6},{5,7},{10,8},{11,9},{8,1... | collective-permute-start | bytes 405512 | tf_op jit(solution)/shard_map/ppermute | solution.py:65
  17.1 0.7 collective-permute-start.14
  17.8 1.3 %collective-permute-start.3 = (bf16[528,128]{1,0:T(8,128)(2,1)S(1)}, bf16[528,128]{1,0:T(8,128)(2,1)S(1)}, u32[]{:S(2)}, u32[]{:S(2)}) collective-permute-start(bf16[528,128]{1,0:T(8,128)(2,1)S(1)} %collective-permute-done.refs_0_.refs_4_), channel_id=1, source_target_pairs={{3,0},{2,1},{1,2},{0,3},{7,4},{6,5},{5,6},{4,7},{11,8},{10,9},{9,1... | collective-permute-start | bytes 405512 | tf_op jit(solution)/shard_map/ppermute | solution.py:65
  19.1 3.3 %collective-permute-start.4 = (bf16[528,128]{1,0:T(8,128)(2,1)S(1)}, bf16[528,128]{1,0:T(8,128)(2,1)S(1)}, u32[]{:S(2)}, u32[]{:S(2)}) collective-permute-start(bf16[528,128]{1,0:T(8,128)(2,1)S(1)} %collective-permute-done.refs_0_.refs_4_), channel_id=1, source_target_pairs={{16,0},{0,16},{17,1},{1,17},{18,2},{2,18},{19,3},{3,19},{20,4},{4,... | collective-permute-start | bytes 405512 | tf_op jit(solution)/shard_map/ppermute | solution.py:65
  22.3 0.0 collective-permute-done.1.refs_1_.refs_5_
  22.3 0.1 collective-permute-start.5
  22.4 7.6 %collective-permute-done.2.refs_2_.refs_6_ = bf16[528,128]{1,0:T(8,128)(2,1)S(1)} collective-permute-done((bf16[528,128]{1,0:T(8,128)(2,1)S(1)}, bf16[528,128]{1,0:T(8,128)(2,1)S(1)}, u32[]{:S(2)}, u32[]{:S(2)}) %collective-permute-start.2) | collective-permute-done | bytes 135200 | tf_op jit(solution)/shard_map/ppermute | solution.py:65
  30.0 0.5 collective-permute-start.13
  30.5 0.0 collective-permute-done.3.refs_3_.refs_7_
  30.5 2.5 %collective-permute-start.15 = (bf16[768,128]{1,0:T(8,128)(2,1)S(1)}, bf16[768,128]{1,0:T(8,128)(2,1)S(1)}, u32[]{:S(2)}, u32[]{:S(2)}) collective-permute-start(bf16[768,128]{1,0:T(8,128)(2,1)S(1)} %collective-permute-done.14.refs_8_.refs_20_), channel_id=1, source_target_pairs={{2,0},{3,1},{0,2},{1,3},{6,4},{7,5},{4,6},{5,7},{10,8},{11,9},{8,1... | collective-permute-start | bytes 589832 | tf_op jit(solution)/shard_map/ppermute | solution.py:65
  33.0 0.1 collective-permute-start.16
  33.1 0.0 collective-permute-done.5.refs_5_.refs_9_
  33.1 1.5 %collective-permute-start.22 = (bf16[768,128]{1,0:T(8,128)(2,1)S(1)}, bf16[768,128]{1,0:T(8,128)(2,1)S(1)}, u32[]{:S(2)}, u32[]{:S(2)}) collective-permute-start(bf16[768,128]{1,0:T(8,128)(2,1)S(1)} %collective-permute-done.14.refs_8_.refs_20_), channel_id=1, source_target_pairs={{1,0},{0,1},{3,2},{2,3},{5,4},{4,5},{7,6},{6,7},{9,8},{8,9},{11,10... | collective-permute-start | bytes 589832 | tf_op jit(solution)/shard_map/ppermute | solution.py:65
  34.6 0.0 collective-permute-done.6.refs_6_.refs_10_
  34.6 1.4 %collective-permute-done.7.refs_7_.refs_11_ = bf16[528,128]{1,0:T(8,128)(2,1)S(1)} collective-permute-done((bf16[528,128]{1,0:T(8,128)(2,1)S(1)}, bf16[528,128]{1,0:T(8,128)(2,1)S(1)}, u32[]{:S(2)}, u32[]{:S(2)}) %collective-permute-start.7) | collective-permute-done | bytes 135200 | tf_op jit(solution)/shard_map/ppermute | solution.py:65
  35.9 1.3 %shard_map.102 = (bf16[144,128]{1,0:T(8,128)(2,1)S(1)}, bf16[144,128]{1,0:T(8,128)(2,1)S(1)}, bf16[144,128]{1,0:T(8,128)(2,1)S(1)}, bf16[144,128]{1,0:T(8,128)(2,1)S(1)}) custom-call(s32[3]{0:T(128)S(1)} %pad_add_fusion.place_ref, bf16[128,1024]{1,0:T(8,128)(2,1)S(1)} %bitcast.21, bf16[128,1024]{1,0:T(8,128)(2,1)S(1)} %bitcast.23, ...), custom_call_target="tpu_custom_call" | custom-call | tf_op jit(solution)/shard_map/pallas_call | solution.py:369
  37.3 2.0 %collective-permute-start.10 = (bf16[144,128]{1,0:T(8,128)(2,1)S(1)}, bf16[144,128]{1,0:T(8,128)(2,1)S(1)}, u32[]{:S(2)}, u32[]{:S(2)}) collective-permute-start(bf16[144,128]{1,0:T(8,128)(2,1)S(1)} %get-tuple-element.34), channel_id=1, source_target_pairs={{0,12},{4,8},{8,4},{12,0},{1,13},{5,9},{9,5},{13,1},{2,14},{6,10},... | collective-permute-start | bytes 110600 | tf_op jit(solution)/shard_map/ppermute | solution.py:76
  39.3 2.4 %collective-permute-start.9 = (bf16[144,128]{1,0:T(8,128)(2,1)S(1)}, bf16[144,128]{1,0:T(8,128)(2,1)S(1)}, u32[]{:S(2)}, u32[]{:S(2)}) collective-permute-start(bf16[144,128]{1,0:T(8,128)(2,1)S(1)} %get-tuple-element.33), channel_id=1, source_target_pairs={{0,8},{4,12},{8,0},{12,4},{1,9},{5,13},{9,1},{13,5},{2,10},{6,14},... | collective-permute-start | bytes 110600 | tf_op jit(solution)/shard_map/ppermute | solution.py:76
  41.7 0.8 collective-permute-done.16.refs_2_.refs_14_
  42.5 0.5 collective-permute-start.24
  43.0 0.1 collective-permute-done.10
  43.1 0.8 collective-permute-done.8
  44.0 1.4 %collective-permute-start.17 = (bf16[768,128]{1,0:T(8,128)(2,1)S(1)}, bf16[768,128]{1,0:T(8,128)(2,1)S(1)}, u32[]{:S(2)}, u32[]{:S(2)}) collective-permute-start(bf16[768,128]{1,0:T(8,128)(2,1)S(1)} %collective-permute-done.13.refs_1_.refs_13_), channel_id=1, source_target_pairs={{2,0},{3,1},{0,2},{1,3},{6,4},{7,5},{4,6},{5,7},{10,8},{11,9},{8,1... | collective-permute-start | bytes 589832 | tf_op jit(solution)/shard_map/ppermute | solution.py:65
  45.4 0.9 collective-permute-start.23
  46.4 0.1 collective-permute-start.11
  46.5 0.5 collective-permute-start.25
  47.0 0.8 collective-permute-done.11.refs_3_
  47.7 0.2 collective-permute-start.19
  47.9 0.4 collective-permute-start.26
  48.2 2.7 %collective-permute-done.17.refs_3_.refs_15_ = bf16[768,128]{1,0:T(8,128)(2,1)S(1)} collective-permute-done((bf16[768,128]{1,0:T(8,128)(2,1)S(1)}, bf16[768,128]{1,0:T(8,128)(2,1)S(1)}, u32[]{:S(2)}, u32[]{:S(2)}) %collective-permute-start.17) | collective-permute-done | bytes 196640 | tf_op jit(solution)/shard_map/ppermute | solution.py:65
  51.0 1.5 %collective-permute-done.23.refs_11_.refs_23_ = bf16[768,128]{1,0:T(8,128)(2,1)S(1)} collective-permute-done((bf16[768,128]{1,0:T(8,128)(2,1)S(1)}, bf16[768,128]{1,0:T(8,128)(2,1)S(1)}, u32[]{:S(2)}, u32[]{:S(2)}) %collective-permute-start.23) | collective-permute-done | bytes 196640 | tf_op jit(solution)/shard_map/ppermute | solution.py:65
  52.5 1.4 %collective-permute-done.27.refs_15_.refs_27_ = bf16[768,128]{1,0:T(8,128)(2,1)S(1)} collective-permute-done((bf16[768,128]{1,0:T(8,128)(2,1)S(1)}, bf16[768,128]{1,0:T(8,128)(2,1)S(1)}, u32[]{:S(2)}, u32[]{:S(2)}) %collective-permute-start.27) | collective-permute-done | bytes 196640 | tf_op jit(solution)/shard_map/ppermute | solution.py:65
  53.9 1.4 %shard_map.103 = (bf16[128,384]{1,0:T(8,128)(2,1)S(1)}, bf16[128,384]{1,0:T(8,128)(2,1)S(1)}, bf16[128,384]{1,0:T(8,128)(2,1)S(1)}, bf16[128,384]{1,0:T(8,128)(2,1)S(1)}) custom-call(s32[3]{0:T(128)S(1)} %pad_add_fusion.place_ref, bf16[128,1024]{1,0:T(8,128)(2,1)S(1)} %bitcast.22, bf16[768,128]{1,0:T(8,128)(2,1)S(1)} %collective-permute-done.12.refs_0_.refs_12_, ...), custom_call_target="tpu_custom_call" | custom-call | tf_op jit(solution)/shard_map/pallas_call | solution.py:369
  55.3 0.1 collective-permute-start.28
  55.4 1.1 %collective-permute-start.29 = (bf16[128,384]{1,0:T(8,128)(2,1)S(1)}, bf16[128,384]{1,0:T(8,128)(2,1)S(1)}, u32[]{:S(2)}, u32[]{:S(2)}) collective-permute-start(bf16[128,384]{1,0:T(8,128)(2,1)S(1)} %get-tuple-element.41), channel_id=1, source_target_pairs={{0,8},{4,12},{8,0},{12,4},{1,9},{5,13},{9,1},{13,5},{2,10},{6,14},... | collective-permute-start | bytes 294920 | tf_op jit(solution)/shard_map/ppermute | solution.py:76
  56.5 3.3 %collective-permute-start.30 = (bf16[128,384]{1,0:T(8,128)(2,1)S(1)}, bf16[128,384]{1,0:T(8,128)(2,1)S(1)}, u32[]{:S(2)}, u32[]{:S(2)}) collective-permute-start(bf16[128,384]{1,0:T(8,128)(2,1)S(1)} %get-tuple-element.42), channel_id=1, source_target_pairs={{0,12},{4,8},{8,4},{12,0},{1,13},{5,9},{9,5},{13,1},{2,14},{6,10},... | collective-permute-start | bytes 294920 | tf_op jit(solution)/shard_map/ppermute | solution.py:76
  59.8 1.6 %collective-permute-done.28 = bf16[128,384]{1,0:T(8,128)(2,1)S(1)} collective-permute-done((bf16[128,384]{1,0:T(8,128)(2,1)S(1)}, bf16[128,384]{1,0:T(8,128)(2,1)S(1)}, u32[]{:S(2)}, u32[]{:S(2)}) %collective-permute-start.28) | collective-permute-done | bytes 98336 | tf_op jit(solution)/shard_map/ppermute | solution.py:76
  61.4 4.9 %collective-permute-done.29 = bf16[128,384]{1,0:T(8,128)(2,1)S(1)} collective-permute-done((bf16[128,384]{1,0:T(8,128)(2,1)S(1)}, bf16[128,384]{1,0:T(8,128)(2,1)S(1)}, u32[]{:S(2)}, u32[]{:S(2)}) %collective-permute-start.29) | collective-permute-done | bytes 98336 | tf_op jit(solution)/shard_map/ppermute | solution.py:76
  66.3 0.1 convert_add_fusion.refs_0_
  66.3 0.1 collective-permute-start.31
  66.4 1.4 %collective-permute-done.31.refs_1_ = f32[128,384]{1,0:T(8,128)S(1)} collective-permute-done((f32[128,384]{1,0:T(8,128)S(1)}, f32[128,384]{1,0:T(8,128)S(1)}, u32[]{:S(2)}, u32[]{:S(2)}) %collective-permute-start.31) | collective-permute-done | bytes 196640 | tf_op jit(solution)/shard_map/ppermute | solution.py:65
  67.8 10.8 %shard_map.104 = (bf16[144,512]{1,0:T(8,128)(2,1)S(1)}, f32[64,256]{1,0:T(8,128)S(1)}, f32[64,256]{1,0:T(8,128)S(1)}, f32[64,256]{1,0:T(8,128)S(1)}, f32[64,256]{1,0:T(8,128)S(1)}) custom-call(s32[3]{0:T(128)S(1)} %pad_add_fusion.place_ref, f32[128,384]{1,0:T(8,128)S(1)} %convert_add_fusion.refs_0_, f32[128,384]{1,0:T(8,128)S(1)} %collective-permute-done.31.refs_1_, ...), custom_call_target="tpu_custom_call" | custom-call | tf_op jit(solution)/shard_map/pallas_call | solution.py:369
  78.7 1.9 %collective-permute-start.32 = (bf16[144,512]{1,0:T(8,128)(2,1)S(1)}, bf16[144,512]{1,0:T(8,128)(2,1)S(1)}, u32[]{:S(2)}, u32[]{:S(2)}) collective-permute-start(bf16[144,512]{1,0:T(8,128)(2,1)S(1)} %get-tuple-element.43.refs_0_), channel_id=1, source_target_pairs={{4,0},{0,4},{12,8},{8,12},{5,1},{1,5},{13,9},{9,13},{6,2},{2,6},{1... | collective-permute-start | bytes 442376 | tf_op jit(solution)/shard_map/ppermute | solution.py:65
  80.6 0.1 collective-permute-start.33
  80.7 2.4 %collective-permute-start.34 = (bf16[144,512]{1,0:T(8,128)(2,1)S(1)}, bf16[144,512]{1,0:T(8,128)(2,1)S(1)}, u32[]{:S(2)}, u32[]{:S(2)}) collective-permute-start(bf16[144,512]{1,0:T(8,128)(2,1)S(1)} %get-tuple-element.43.refs_0_), channel_id=1, source_target_pairs={{12,0},{8,4},{4,8},{0,12},{13,1},{9,5},{5,9},{1,13},{14,2},{10,6},... | collective-permute-start | bytes 442376 | tf_op jit(solution)/shard_map/ppermute | solution.py:65
  83.1 3.4 %collective-permute-done.32.refs_1_ = bf16[144,512]{1,0:T(8,128)(2,1)S(1)} collective-permute-done((bf16[144,512]{1,0:T(8,128)(2,1)S(1)}, bf16[144,512]{1,0:T(8,128)(2,1)S(1)}, u32[]{:S(2)}, u32[]{:S(2)}) %collective-permute-start.32) | collective-permute-done | bytes 147488 | tf_op jit(solution)/shard_map/ppermute | solution.py:65
  86.6 0.9 collective-permute-start.35
  87.5 1.0 %collective-permute-start.36 = (f32[64,256]{1,0:T(8,128)S(1)}, f32[64,256]{1,0:T(8,128)S(1)}, u32[]{:S(2)}, u32[]{:S(2)}) collective-permute-start(f32[64,256]{1,0:T(8,128)S(1)} %get-tuple-element.52), channel_id=1, source_target_pairs={{0,2},{1,3},{2,0},{3,1},{4,6},{5,7},{6,4},{7,5},{8,10},{9,11},{10,... | collective-permute-start | bytes 196616 | tf_op jit(solution)/shard_map/ppermute | solution.py:76
  88.4 1.6 %collective-permute-start.37 = (f32[64,256]{1,0:T(8,128)S(1)}, f32[64,256]{1,0:T(8,128)S(1)}, u32[]{:S(2)}, u32[]{:S(2)}) collective-permute-start(f32[64,256]{1,0:T(8,128)S(1)} %get-tuple-element.53), channel_id=1, source_target_pairs={{0,3},{1,2},{2,1},{3,0},{4,7},{5,6},{6,5},{7,4},{8,11},{9,10},{10,... | collective-permute-start | bytes 196616 | tf_op jit(solution)/shard_map/ppermute | solution.py:76
  90.1 4.5 %collective-permute-done.33.refs_2_ = bf16[144,512]{1,0:T(8,128)(2,1)S(1)} collective-permute-done((bf16[144,512]{1,0:T(8,128)(2,1)S(1)}, bf16[144,512]{1,0:T(8,128)(2,1)S(1)}, u32[]{:S(2)}, u32[]{:S(2)}) %collective-permute-start.33) | collective-permute-done | bytes 147488 | tf_op jit(solution)/shard_map/ppermute | solution.py:65
  94.6 3.1 %shard_map.105 = (bf16[128,1024]{1,0:T(8,128)(2,1)}, bf16[128,1024]{1,0:T(8,128)(2,1)}) custom-call(s32[3]{0:T(128)S(1)} %pad_add_fusion.place_ref, bf16[144,512]{1,0:T(8,128)(2,1)S(1)} %get-tuple-element.43.refs_0_, bf16[144,512]{1,0:T(8,128)(2,1)S(1)} %collective-permute-done.32.refs_1_, bf16[144,512]{1,0:T(8,128)(2,1)S(1)} %collective-permute-done.33.refs_2_, ...), custom_call_target="tpu_custom_call" | custom-call | tf_op jit(solution)/shard_map/pallas_call | solution.py:369
  97.7 0.6 slice_bitcast_fusion
  (35 shorter events, 0.1 us)
Async XLA Ops:
  0.6 0.7 copy-start
  2.3 2.5 %collective-permute-start = (bf16[528,128]{1,0:T(8,128)(2,1)S(1)}, bf16[528,128]{1,0:T(8,128)(2,1)S(1)}, u32[]{:S(2)}, u32[]{:S(2)}) collective-permute-start(bf16[528,128]{1,0:T(8,128)(2,1)S(1)} %fusion.1), channel_id=1, source_target_pairs={{0,0},{1,1},{2,4},{3,5},{4,2},{5,3},{6,6},{7,7},{8,16},{9,17},{10,... | collective-permute-start | bytes 405512 | tf_op jit(solution)/shard_map/ppermute | solution.py:400
  3.0 32.9 %copy-start.1 = (bf16[1,128,1024]{2,1,0:T(8,128)(2,1)S(1)}, bf16[1,128,1024]{2,1,0:T(8,128)(2,1)}, u32[]{:S(2)}) copy-start(bf16[1,128,1024]{2,1,0:T(8,128)(2,1)} %param.7) | copy-start | bytes 786436
  3.0 32.9 %copy-start.2 = (bf16[1,128,1024]{2,1,0:T(8,128)(2,1)S(1)}, bf16[1,128,1024]{2,1,0:T(8,128)(2,1)}, u32[]{:S(2)}) copy-start(bf16[1,128,1024]{2,1,0:T(8,128)(2,1)} %param.13) | copy-start | bytes 786436
  4.2 14.9 %collective-permute-start.12 = (bf16[768,128]{1,0:T(8,128)(2,1)S(1)}, bf16[768,128]{1,0:T(8,128)(2,1)S(1)}, u32[]{:S(2)}, u32[]{:S(2)}) collective-permute-start(bf16[768,128]{1,0:T(8,128)(2,1)S(1)} %bitcast.28), channel_id=1, source_target_pairs={{0,0},{1,1},{2,4},{3,5},{4,2},{5,3},{6,6},{7,7},{8,16},{9,17},{10,... | collective-permute-start | bytes 589832 | tf_op jit(solution)/shard_map/ppermute | solution.py:400
  4.8 17.5 %collective-permute-start.1 = (bf16[528,128]{1,0:T(8,128)(2,1)S(1)}, bf16[528,128]{1,0:T(8,128)(2,1)S(1)}, u32[]{:S(2)}, u32[]{:S(2)}) collective-permute-start(bf16[528,128]{1,0:T(8,128)(2,1)S(1)} %collective-permute-done.refs_0_.refs_4_), channel_id=1, source_target_pairs={{1,0},{0,1},{3,2},{2,3},{5,4},{4,5},{7,6},{6,7},{9,8},{8,9},{11,10... | collective-permute-start | bytes 405512 | tf_op jit(solution)/shard_map/ppermute | solution.py:65
  7.9 22.1 %collective-permute-start.2 = (bf16[528,128]{1,0:T(8,128)(2,1)S(1)}, bf16[528,128]{1,0:T(8,128)(2,1)S(1)}, u32[]{:S(2)}, u32[]{:S(2)}) collective-permute-start(bf16[528,128]{1,0:T(8,128)(2,1)S(1)} %collective-permute-done.refs_0_.refs_4_), channel_id=1, source_target_pairs={{2,0},{3,1},{0,2},{1,3},{6,4},{7,5},{4,6},{5,7},{10,8},{11,9},{8,1... | collective-permute-start | bytes 405512 | tf_op jit(solution)/shard_map/ppermute | solution.py:65
  17.1 12.9 %collective-permute-start.14 = (bf16[768,128]{1,0:T(8,128)(2,1)S(1)}, bf16[768,128]{1,0:T(8,128)(2,1)S(1)}, u32[]{:S(2)}, u32[]{:S(2)}) collective-permute-start(bf16[768,128]{1,0:T(8,128)(2,1)S(1)} %bitcast.27), channel_id=1, source_target_pairs={{0,0},{1,1},{2,4},{3,5},{4,2},{5,3},{6,6},{7,7},{8,16},{9,17},{10,... | collective-permute-start | bytes 589832 | tf_op jit(solution)/shard_map/ppermute | solution.py:400
  17.8 12.7 %collective-permute-start.3 = (bf16[528,128]{1,0:T(8,128)(2,1)S(1)}, bf16[528,128]{1,0:T(8,128)(2,1)S(1)}, u32[]{:S(2)}, u32[]{:S(2)}) collective-permute-start(bf16[528,128]{1,0:T(8,128)(2,1)S(1)} %collective-permute-done.refs_0_.refs_4_), channel_id=1, source_target_pairs={{3,0},{2,1},{1,2},{0,3},{7,4},{6,5},{5,6},{4,7},{11,8},{10,9},{9,1... | collective-permute-start | bytes 405512 | tf_op jit(solution)/shard_map/ppermute | solution.py:65
  19.1 13.9 %collective-permute-start.4 = (bf16[528,128]{1,0:T(8,128)(2,1)S(1)}, bf16[528,128]{1,0:T(8,128)(2,1)S(1)}, u32[]{:S(2)}, u32[]{:S(2)}) collective-permute-start(bf16[528,128]{1,0:T(8,128)(2,1)S(1)} %collective-permute-done.refs_0_.refs_4_), channel_id=1, source_target_pairs={{16,0},{0,16},{17,1},{1,17},{18,2},{2,18},{19,3},{3,19},{20,4},{4,... | collective-permute-start | bytes 405512 | tf_op jit(solution)/shard_map/ppermute | solution.py:65
  22.3 10.7 %collective-permute-start.5 = (bf16[528,128]{1,0:T(8,128)(2,1)S(1)}, bf16[528,128]{1,0:T(8,128)(2,1)S(1)}, u32[]{:S(2)}, u32[]{:S(2)}) collective-permute-start(bf16[528,128]{1,0:T(8,128)(2,1)S(1)} %collective-permute-done.1.refs_1_.refs_5_), channel_id=1, source_target_pairs={{16,0},{0,16},{17,1},{1,17},{18,2},{2,18},{19,3},{3,19},{20,4},{4,... | collective-permute-start | bytes 405512 | tf_op jit(solution)/shard_map/ppermute | solution.py:65
  30.0 4.6 %collective-permute-start.6 = (bf16[528,128]{1,0:T(8,128)(2,1)S(1)}, bf16[528,128]{1,0:T(8,128)(2,1)S(1)}, u32[]{:S(2)}, u32[]{:S(2)}) collective-permute-start(bf16[528,128]{1,0:T(8,128)(2,1)S(1)} %collective-permute-done.2.refs_2_.refs_6_), channel_id=1, source_target_pairs={{16,0},{0,16},{17,1},{1,17},{18,2},{2,18},{19,3},{3,19},{20,4},{4,... | collective-permute-start | bytes 405512 | tf_op jit(solution)/shard_map/ppermute | solution.py:65
  30.0 9.3 %collective-permute-start.13 = (bf16[768,128]{1,0:T(8,128)(2,1)S(1)}, bf16[768,128]{1,0:T(8,128)(2,1)S(1)}, u32[]{:S(2)}, u32[]{:S(2)}) collective-permute-start(bf16[768,128]{1,0:T(8,128)(2,1)S(1)} %collective-permute-done.12.refs_0_.refs_12_), channel_id=1, source_target_pairs={{1,0},{0,1},{3,2},{2,3},{5,4},{4,5},{7,6},{6,7},{9,8},{8,9},{11,10... | collective-permute-start | bytes 589832 | tf_op jit(solution)/shard_map/ppermute | solution.py:65
  30.5 8.8 %collective-permute-start.15 = (bf16[768,128]{1,0:T(8,128)(2,1)S(1)}, bf16[768,128]{1,0:T(8,128)(2,1)S(1)}, u32[]{:S(2)}, u32[]{:S(2)}) collective-permute-start(bf16[768,128]{1,0:T(8,128)(2,1)S(1)} %collective-permute-done.14.refs_8_.refs_20_), channel_id=1, source_target_pairs={{2,0},{3,1},{0,2},{1,3},{6,4},{7,5},{4,6},{5,7},{10,8},{11,9},{8,1... | collective-permute-start | bytes 589832 | tf_op jit(solution)/shard_map/ppermute | solution.py:65
  33.0 9.5 %collective-permute-start.16 = (bf16[768,128]{1,0:T(8,128)(2,1)S(1)}, bf16[768,128]{1,0:T(8,128)(2,1)S(1)}, u32[]{:S(2)}, u32[]{:S(2)}) collective-permute-start(bf16[768,128]{1,0:T(8,128)(2,1)S(1)} %collective-permute-done.12.refs_0_.refs_12_), channel_id=1, source_target_pairs={{2,0},{3,1},{0,2},{1,3},{6,4},{7,5},{4,6},{5,7},{10,8},{11,9},{8,1... | collective-permute-start | bytes 589832 | tf_op jit(solution)/shard_map/ppermute | solution.py:65
  33.1 9.4 %collective-permute-start.22 = (bf16[768,128]{1,0:T(8,128)(2,1)S(1)}, bf16[768,128]{1,0:T(8,128)(2,1)S(1)}, u32[]{:S(2)}, u32[]{:S(2)}) collective-permute-start(bf16[768,128]{1,0:T(8,128)(2,1)S(1)} %collective-permute-done.14.refs_8_.refs_20_), channel_id=1, source_target_pairs={{1,0},{0,1},{3,2},{2,3},{5,4},{4,5},{7,6},{6,7},{9,8},{8,9},{11,10... | collective-permute-start | bytes 589832 | tf_op jit(solution)/shard_map/ppermute | solution.py:65
  34.6 1.4 %collective-permute-start.7 = (bf16[528,128]{1,0:T(8,128)(2,1)S(1)}, bf16[528,128]{1,0:T(8,128)(2,1)S(1)}, u32[]{:S(2)}, u32[]{:S(2)}) collective-permute-start(bf16[528,128]{1,0:T(8,128)(2,1)S(1)} %collective-permute-done.3.refs_3_.refs_7_), channel_id=1, source_target_pairs={{16,0},{0,16},{17,1},{1,17},{18,2},{2,18},{19,3},{3,19},{20,4},{4,... | collective-permute-start | bytes 405512 | tf_op jit(solution)/shard_map/ppermute | solution.py:65
  37.3 5.9 %collective-permute-start.10 = (bf16[144,128]{1,0:T(8,128)(2,1)S(1)}, bf16[144,128]{1,0:T(8,128)(2,1)S(1)}, u32[]{:S(2)}, u32[]{:S(2)}) collective-permute-start(bf16[144,128]{1,0:T(8,128)(2,1)S(1)} %get-tuple-element.34), channel_id=1, source_target_pairs={{0,12},{4,8},{8,4},{12,0},{1,13},{5,9},{9,5},{13,1},{2,14},{6,10},... | collective-permute-start | bytes 110600 | tf_op jit(solution)/shard_map/ppermute | solution.py:76
  39.3 4.7 %collective-permute-start.8 = (bf16[144,128]{1,0:T(8,128)(2,1)S(1)}, bf16[144,128]{1,0:T(8,128)(2,1)S(1)}, u32[]{:S(2)}, u32[]{:S(2)}) collective-permute-start(bf16[144,128]{1,0:T(8,128)(2,1)S(1)} %get-tuple-element.32), channel_id=1, source_target_pairs={{0,4},{4,0},{8,12},{12,8},{1,5},{5,1},{9,13},{13,9},{2,6},{6,2},{1... | collective-permute-start | bytes 110600 | tf_op jit(solution)/shard_map/ppermute | solution.py:76
  39.3 6.1 %collective-permute-start.9 = (bf16[144,128]{1,0:T(8,128)(2,1)S(1)}, bf16[144,128]{1,0:T(8,128)(2,1)S(1)}, u32[]{:S(2)}, u32[]{:S(2)}) collective-permute-start(bf16[144,128]{1,0:T(8,128)(2,1)S(1)} %get-tuple-element.33), channel_id=1, source_target_pairs={{0,8},{4,12},{8,0},{12,4},{1,9},{5,13},{9,1},{13,5},{2,10},{6,14},... | collective-permute-start | bytes 110600 | tf_op jit(solution)/shard_map/ppermute | solution.py:76
  42.5 3.9 %collective-permute-start.18 = (bf16[768,128]{1,0:T(8,128)(2,1)S(1)}, bf16[768,128]{1,0:T(8,128)(2,1)S(1)}, u32[]{:S(2)}, u32[]{:S(2)}) collective-permute-start(bf16[768,128]{1,0:T(8,128)(2,1)S(1)} %collective-permute-done.12.refs_0_.refs_12_), channel_id=1, source_target_pairs={{16,0},{0,16},{17,1},{1,17},{18,2},{2,18},{19,3},{3,19},{20,4},{4,... | collective-permute-start | bytes 589832 | tf_op jit(solution)/shard_map/ppermute | solution.py:65
  42.5 3.9 %collective-permute-start.24 = (bf16[768,128]{1,0:T(8,128)(2,1)S(1)}, bf16[768,128]{1,0:T(8,128)(2,1)S(1)}, u32[]{:S(2)}, u32[]{:S(2)}) collective-permute-start(bf16[768,128]{1,0:T(8,128)(2,1)S(1)} %collective-permute-done.14.refs_8_.refs_20_), channel_id=1, source_target_pairs={{16,0},{0,16},{17,1},{1,17},{18,2},{2,18},{19,3},{3,19},{20,4},{4,... | collective-permute-start | bytes 589832 | tf_op jit(solution)/shard_map/ppermute | solution.py:65
  43.1 4.7 %collective-permute-start.20 = (bf16[768,128]{1,0:T(8,128)(2,1)S(1)}, bf16[768,128]{1,0:T(8,128)(2,1)S(1)}, u32[]{:S(2)}, u32[]{:S(2)}) collective-permute-start(bf16[768,128]{1,0:T(8,128)(2,1)S(1)} %collective-permute-done.16.refs_2_.refs_14_), channel_id=1, source_target_pairs={{16,0},{0,16},{17,1},{1,17},{18,2},{2,18},{19,3},{3,19},{20,4},{4,... | collective-permute-start | bytes 589832 | tf_op jit(solution)/shard_map/ppermute | solution.py:65
  44.0 7.0 %collective-permute-start.17 = (bf16[768,128]{1,0:T(8,128)(2,1)S(1)}, bf16[768,128]{1,0:T(8,128)(2,1)S(1)}, u32[]{:S(2)}, u32[]{:S(2)}) collective-permute-start(bf16[768,128]{1,0:T(8,128)(2,1)S(1)} %collective-permute-done.13.refs_1_.refs_13_), channel_id=1, source_target_pairs={{2,0},{3,1},{0,2},{1,3},{6,4},{7,5},{4,6},{5,7},{10,8},{11,9},{8,1... | collective-permute-start | bytes 589832 | tf_op jit(solution)/shard_map/ppermute | solution.py:65
  45.4 7.0 %collective-permute-start.23 = (bf16[768,128]{1,0:T(8,128)(2,1)S(1)}, bf16[768,128]{1,0:T(8,128)(2,1)S(1)}, u32[]{:S(2)}, u32[]{:S(2)}) collective-permute-start(bf16[768,128]{1,0:T(8,128)(2,1)S(1)} %collective-permute-done.15.refs_10_.refs_22_), channel_id=1, source_target_pairs={{1,0},{0,1},{3,2},{2,3},{5,4},{4,5},{7,6},{6,7},{9,8},{8,9},{11,10... | collective-permute-start | bytes 589832 | tf_op jit(solution)/shard_map/ppermute | solution.py:65
  46.4 1.3 %collective-permute-start.11 = (f32[144,128]{1,0:T(8,128)S(1)}, f32[144,128]{1,0:T(8,128)S(1)}, u32[]{:S(2)}, u32[]{:S(2)}) collective-permute-start(f32[144,128]{1,0:T(8,128)S(1)} %convert_add_fusion.1.refs_2_), channel_id=1, source_target_pairs={{16,0},{0,16},{17,1},{1,17},{18,2},{2,18},{19,3},{3,19},{20,4},{4,... | collective-permute-start | bytes 221192 | tf_op jit(solution)/shard_map/ppermute | solution.py:65
  46.5 6.0 %collective-permute-start.25 = (bf16[768,128]{1,0:T(8,128)(2,1)S(1)}, bf16[768,128]{1,0:T(8,128)(2,1)S(1)}, u32[]{:S(2)}, u32[]{:S(2)}) collective-permute-start(bf16[768,128]{1,0:T(8,128)(2,1)S(1)} %collective-permute-done.22.refs_9_.refs_21_), channel_id=1, source_target_pairs={{16,0},{0,16},{17,1},{1,17},{18,2},{2,18},{19,3},{3,19},{20,4},{4,... | collective-permute-start | bytes 589832 | tf_op jit(solution)/shard_map/ppermute | solution.py:65
  47.7 4.7 %collective-permute-start.19 = (bf16[768,128]{1,0:T(8,128)(2,1)S(1)}, bf16[768,128]{1,0:T(8,128)(2,1)S(1)}, u32[]{:S(2)}, u32[]{:S(2)}) collective-permute-start(bf16[768,128]{1,0:T(8,128)(2,1)S(1)} %collective-permute-done.13.refs_1_.refs_13_), channel_id=1, source_target_pairs={{16,0},{0,16},{17,1},{1,17},{18,2},{2,18},{19,3},{3,19},{20,4},{4,... | collective-permute-start | bytes 589832 | tf_op jit(solution)/shard_map/ppermute | solution.py:65
  47.9 4.6 %collective-permute-start.26 = (bf16[768,128]{1,0:T(8,128)(2,1)S(1)}, bf16[768,128]{1,0:T(8,128)(2,1)S(1)}, u32[]{:S(2)}, u32[]{:S(2)}) collective-permute-start(bf16[768,128]{1,0:T(8,128)(2,1)S(1)} %collective-permute-done.15.refs_10_.refs_22_), channel_id=1, source_target_pairs={{16,0},{0,16},{17,1},{1,17},{18,2},{2,18},{19,3},{3,19},{20,4},{4,... | collective-permute-start | bytes 589832 | tf_op jit(solution)/shard_map/ppermute | solution.py:65
  51.0 1.5 %collective-permute-start.21 = (bf16[768,128]{1,0:T(8,128)(2,1)S(1)}, bf16[768,128]{1,0:T(8,128)(2,1)S(1)}, u32[]{:S(2)}, u32[]{:S(2)}) collective-permute-start(bf16[768,128]{1,0:T(8,128)(2,1)S(1)} %collective-permute-done.17.refs_3_.refs_15_), channel_id=1, source_target_pairs={{16,0},{0,16},{17,1},{1,17},{18,2},{2,18},{19,3},{3,19},{20,4},{4,... | collective-permute-start | bytes 589832 | tf_op jit(solution)/shard_map/ppermute | solution.py:65
  52.4 1.4 %collective-permute-start.27 = (bf16[768,128]{1,0:T(8,128)(2,1)S(1)}, bf16[768,128]{1,0:T(8,128)(2,1)S(1)}, u32[]{:S(2)}, u32[]{:S(2)}) collective-permute-start(bf16[768,128]{1,0:T(8,128)(2,1)S(1)} %collective-permute-done.23.refs_11_.refs_23_), channel_id=1, source_target_pairs={{16,0},{0,16},{17,1},{1,17},{18,2},{2,18},{19,3},{3,19},{20,4},{4,... | collective-permute-start | bytes 589832 | tf_op jit(solution)/shard_map/ppermute | solution.py:65
  55.3 6.1 %collective-permute-start.28 = (bf16[128,384]{1,0:T(8,128)(2,1)S(1)}, bf16[128,384]{1,0:T(8,128)(2,1)S(1)}, u32[]{:S(2)}, u32[]{:S(2)}) collective-permute-start(bf16[128,384]{1,0:T(8,128)(2,1)S(1)} %get-tuple-element.40), channel_id=1, source_target_pairs={{0,4},{4,0},{8,12},{12,8},{1,5},{5,1},{9,13},{13,9},{2,6},{6,2},{1... | collective-permute-start | bytes 294920 | tf_op jit(solution)/shard_map/ppermute | solution.py:76
  55.4 10.9 %collective-permute-start.29 = (bf16[128,384]{1,0:T(8,128)(2,1)S(1)}, bf16[128,384]{1,0:T(8,128)(2,1)S(1)}, u32[]{:S(2)}, u32[]{:S(2)}) collective-permute-start(bf16[128,384]{1,0:T(8,128)(2,1)S(1)} %get-tuple-element.41), channel_id=1, source_target_pairs={{0,8},{4,12},{8,0},{12,4},{1,9},{5,13},{9,1},{13,5},{2,10},{6,14},... | collective-permute-start | bytes 294920 | tf_op jit(solution)/shard_map/ppermute | solution.py:76
  56.5 9.8 %collective-permute-start.30 = (bf16[128,384]{1,0:T(8,128)(2,1)S(1)}, bf16[128,384]{1,0:T(8,128)(2,1)S(1)}, u32[]{:S(2)}, u32[]{:S(2)}) collective-permute-start(bf16[128,384]{1,0:T(8,128)(2,1)S(1)} %get-tuple-element.42), channel_id=1, source_target_pairs={{0,12},{4,8},{8,4},{12,0},{1,13},{5,9},{9,5},{13,1},{2,14},{6,10},... | collective-permute-start | bytes 294920 | tf_op jit(solution)/shard_map/ppermute | solution.py:76
  66.3 1.6 %copy-start.3 = (f32[1,128,512]{2,1,0:T(8,128)S(1)}, f32[1,128,512]{2,1,0:T(8,128)}, u32[]{:S(2)}) copy-start(f32[1,128,512]{2,1,0:T(8,128)} %param.11) | copy-start | bytes 786436
  66.3 1.6 %copy-start.4 = (f32[1,512,128]{2,1,0:T(8,128)S(1)}, f32[1,512,128]{2,1,0:T(8,128)}, u32[]{:S(2)}) copy-start(f32[1,512,128]{2,1,0:T(8,128)} %param.12) | copy-start | bytes 786436
  66.3 1.5 %collective-permute-start.31 = (f32[128,384]{1,0:T(8,128)S(1)}, f32[128,384]{1,0:T(8,128)S(1)}, u32[]{:S(2)}, u32[]{:S(2)}) collective-permute-start(f32[128,384]{1,0:T(8,128)S(1)} %convert_add_fusion.refs_0_), channel_id=1, source_target_pairs={{16,0},{0,16},{17,1},{1,17},{18,2},{2,18},{19,3},{3,19},{20,4},{4,... | collective-permute-start | bytes 589832 | tf_op jit(solution)/shard_map/ppermute | solution.py:65
  78.7 7.9 %collective-permute-start.32 = (bf16[144,512]{1,0:T(8,128)(2,1)S(1)}, bf16[144,512]{1,0:T(8,128)(2,1)S(1)}, u32[]{:S(2)}, u32[]{:S(2)}) collective-permute-start(bf16[144,512]{1,0:T(8,128)(2,1)S(1)} %get-tuple-element.43.refs_0_), channel_id=1, source_target_pairs={{4,0},{0,4},{12,8},{8,12},{5,1},{1,5},{13,9},{9,13},{6,2},{2,6},{1... | collective-permute-start | bytes 442376 | tf_op jit(solution)/shard_map/ppermute | solution.py:65
  80.6 13.9 %collective-permute-start.33 = (bf16[144,512]{1,0:T(8,128)(2,1)S(1)}, bf16[144,512]{1,0:T(8,128)(2,1)S(1)}, u32[]{:S(2)}, u32[]{:S(2)}) collective-permute-start(bf16[144,512]{1,0:T(8,128)(2,1)S(1)} %get-tuple-element.43.refs_0_), channel_id=1, source_target_pairs={{8,0},{12,4},{0,8},{4,12},{9,1},{13,5},{1,9},{5,13},{10,2},{14,6},... | collective-permute-start | bytes 442376 | tf_op jit(solution)/shard_map/ppermute | solution.py:65
  80.7 13.9 %collective-permute-start.34 = (bf16[144,512]{1,0:T(8,128)(2,1)S(1)}, bf16[144,512]{1,0:T(8,128)(2,1)S(1)}, u32[]{:S(2)}, u32[]{:S(2)}) collective-permute-start(bf16[144,512]{1,0:T(8,128)(2,1)S(1)} %get-tuple-element.43.refs_0_), channel_id=1, source_target_pairs={{12,0},{8,4},{4,8},{0,12},{13,1},{9,5},{5,9},{1,13},{14,2},{10,6},... | collective-permute-start | bytes 442376 | tf_op jit(solution)/shard_map/ppermute | solution.py:65
  86.6 11.1 %collective-permute-start.35 = (f32[64,256]{1,0:T(8,128)S(1)}, f32[64,256]{1,0:T(8,128)S(1)}, u32[]{:S(2)}, u32[]{:S(2)}) collective-permute-start(f32[64,256]{1,0:T(8,128)S(1)} %get-tuple-element.51), channel_id=1, source_target_pairs={{0,1},{1,0},{2,3},{3,2},{4,5},{5,4},{6,7},{7,6},{8,9},{9,8},{10,11... | collective-permute-start | bytes 196616 | tf_op jit(solution)/shard_map/ppermute | solution.py:76
  87.5 10.3 %collective-permute-start.36 = (f32[64,256]{1,0:T(8,128)S(1)}, f32[64,256]{1,0:T(8,128)S(1)}, u32[]{:S(2)}, u32[]{:S(2)}) collective-permute-start(f32[64,256]{1,0:T(8,128)S(1)} %get-tuple-element.52), channel_id=1, source_target_pairs={{0,2},{1,3},{2,0},{3,1},{4,6},{5,7},{6,4},{7,5},{8,10},{9,11},{10,... | collective-permute-start | bytes 196616 | tf_op jit(solution)/shard_map/ppermute | solution.py:76
  88.4 9.3 %collective-permute-start.37 = (f32[64,256]{1,0:T(8,128)S(1)}, f32[64,256]{1,0:T(8,128)S(1)}, u32[]{:S(2)}, u32[]{:S(2)}) collective-permute-start(f32[64,256]{1,0:T(8,128)S(1)} %get-tuple-element.53), channel_id=1, source_target_pairs={{0,3},{1,2},{2,1},{3,0},{4,7},{5,6},{6,5},{7,4},{8,11},{9,10},{10,... | collective-permute-start | bytes 196616 | tf_op jit(solution)/shard_map/ppermute | solution.py:76

commit v3 on v2

--- a/solution.py
+++ b/solution.py
@@ -405,13 +405,18 @@
         lines, lax.axis_index("seq") * dps + lax.axis_index("dp"), 0, keepdims=False
     )
     line = jnp.pad(line, ((0, EXTRA - depth // 128), (0, 0)))
-    outer_w = swapped(jnp.concatenate([w_out, line], axis=0))
     by_kind = w_qkv.transpose(1, 0, 2)
-    first_w = swapped(by_kind[:, :half].reshape(3 * half, hd))
-    second = by_kind[:, half:].reshape(3 * half, hd)
-    second_w = swapped(second)
+    first, second, outer = lax.optimization_barrier(
+        (
+            by_kind[:, :half].reshape(3 * half, hd),
+            by_kind[:, half:].reshape(3 * half, hd),
+            jnp.concatenate([w_out, line], axis=0),
+        )
+    )
+    first_w, second_w, outer_w = swapped(first), swapped(second), swapped(outer)
+    first_near = [first_w, hop(first_w, "dp", 1), hop(first_w, "dp", 2)]
+    outer_w, unused = lax.optimization_barrier((outer_w, second_w))
     outer_near = peers_of(outer_w, "dp")
-    first_near = [first_w, hop(first_w, "dp", 1), hop(first_w, "dp", 2)]
     second_near = [second_w, hop(second_w, "dp", 1), hop(second_w, "dp", 2)]
     outer_ws = over_seq(outer_near)
     def summed(arrays):

time: 98.6 us -> 101 us (1.024)
  starting transfers between devices: 44.3 us -> 55.1 us
  waiting for transfers between devices: 32.9 us -> 26.5 us
    ppermute x26, starting transfers between devices: 30 us -> 42.3 us  [hop(): lax.ppermute(array, axis, [(mate(i, step, count), i) for i in range(count)])]
    ppermute x26, waiting for transfers between devices: 25.5 us -> 17.9 us  [hop(): lax.ppermute(array, axis, [(mate(i, step, count), i) for i in range(count)])]
    ppermute x9, starting transfers between devices: 12.4 us -> 10.9 us  [sent_to(): lax.ppermute(arrays[j], axis, [(i, mate(i, j, count)) for i in range(coun...]
    ppermute x9, waiting for transfers between devices: 7.44 us -> 8.5 us  [sent_to(): lax.ppermute(arrays[j], axis, [(i, mate(i, j, count)) for i in range(coun...]
  transfers between devices with their start and end apart: 38 -> 38, of which waited for: 14 -> 15; matrix products, arithmetic and copies ran while one was open for 1% -> 0% of each run, Pallas kernels for 5% -> 4%
where the time goes in v3:
time: 101 us
  starting transfers between devices  55.1 us (55%)
  waiting for transfers between devices  26.5 us (26%)
  Pallas kernels  16.7 us (17%)
  local copies, waits for them, and re-layouts  1.77 us (2%)
    ppermute x26, starting transfers between devices, hop(): lax.ppermute(array, axis, [(mate(i, step, count), i) for i in range(count)])  42.3 us
    ppermute x26, waiting for transfers between devices, hop(): lax.ppermute(array, axis, [(mate(i, step, count), i) for i in range(count)])  17.9 us
    pallas_call x4, Pallas kernels, call(): pl.pallas_call(kernel, out_shape=outs, in_specs=[SMEM] + [VMEM] * (len(op...  16.7 us
    ppermute x9, starting transfers between devices, sent_to(): lax.ppermute(arrays[j], axis, [(i, mate(i, j, count)) for i in range(coun...  10.9 us
    ppermute x9, waiting for transfers between devices, sent_to(): lax.ppermute(arrays[j], axis, [(i, mate(i, j, count)) for i in range(coun...  8.5 us
  transfers between devices with their start and end apart: 38, of which 15 were waited for; matrix products, arithmetic and copies ran while one was open for 0% of the time, Pallas kernels for 4%

profile of v3, /device:TPU:0, one launch (start us, length us, event | category | flops | bytes accessed | tf_op | source)
XLA Modules:
  0.0 101.2 jit_solution(9606834717672811138)
XLA Ops:
  0.6 0.0 copy-start
  0.7 0.1 pad_add_fusion.place_ref
  0.7 1.1 %fusion.2 = (bf16[3,256,128]{2,1,0:T(8,128)(2,1)S(1)}, bf16[3,256,128]{2,1,0:T(8,128)(2,1)S(1)}) fusion(bf16[3,512,128]{2,1,0:T(8,128)(2,1)} %bitcast.26), kind=kLoop, calls=%fused_computation.10 | loop fusion | bytes 786432 | tf_op jit(solution)/shard_map/slice | solution.py:412
  1.8 0.0 copy-start.1
  1.9 0.1 reduce
  2.0 0.7 collective-permute-start.1
  2.6 0.7 collective-permute-start
  3.3 3.0 %collective-permute-start.2 = (bf16[528,128]{1,0:T(8,128)(2,1)S(1)}, bf16[528,128]{1,0:T(8,128)(2,1)S(1)}, u32[]{:S(2)}, u32[]{:S(2)}) collective-permute-start(bf16[528,128]{1,0:T(8,128)(2,1)S(1)} %collective-permute-done.refs_0_.refs_4_), channel_id=1, source_target_pairs={{1,0},{0,1},{3,2},{2,3},{5,4},{4,5},{7,6},{6,7},{9,8},{8,9},{11,10... | collective-permute-start | bytes 405512 | tf_op jit(solution)/shard_map/ppermute | solution.py:65
  6.3 16.7 %collective-permute-start.3 = (bf16[528,128]{1,0:T(8,128)(2,1)S(1)}, bf16[528,128]{1,0:T(8,128)(2,1)S(1)}, u32[]{:S(2)}, u32[]{:S(2)}) collective-permute-start(bf16[528,128]{1,0:T(8,128)(2,1)S(1)} %collective-permute-done.refs_0_.refs_4_), channel_id=1, source_target_pairs={{2,0},{3,1},{0,2},{1,3},{6,4},{7,5},{4,6},{5,7},{10,8},{11,9},{8,1... | collective-permute-start | bytes 405512 | tf_op jit(solution)/shard_map/ppermute | solution.py:65
  23.1 0.7 collective-permute-start.13
  23.7 1.3 %collective-permute-start.4 = (bf16[528,128]{1,0:T(8,128)(2,1)S(1)}, bf16[528,128]{1,0:T(8,128)(2,1)S(1)}, u32[]{:S(2)}, u32[]{:S(2)}) collective-permute-start(bf16[528,128]{1,0:T(8,128)(2,1)S(1)} %collective-permute-done.refs_0_.refs_4_), channel_id=1, source_target_pairs={{3,0},{2,1},{1,2},{0,3},{7,4},{6,5},{5,6},{4,7},{11,8},{10,9},{9,1... | collective-permute-start | bytes 405512 | tf_op jit(solution)/shard_map/ppermute | solution.py:65
  25.0 1.2 %collective-permute-start.5 = (bf16[528,128]{1,0:T(8,128)(2,1)S(1)}, bf16[528,128]{1,0:T(8,128)(2,1)S(1)}, u32[]{:S(2)}, u32[]{:S(2)}) collective-permute-start(bf16[528,128]{1,0:T(8,128)(2,1)S(1)} %collective-permute-done.refs_0_.refs_4_), channel_id=1, source_target_pairs={{16,0},{0,16},{17,1},{1,17},{18,2},{2,18},{19,3},{3,19},{20,4},{4,... | collective-permute-start | bytes 405512 | tf_op jit(solution)/shard_map/ppermute | solution.py:65
  26.3 0.0 collective-permute-done.2.refs_1_.refs_5_
  26.3 0.0 collective-permute-start.6
  26.3 0.5 collective-permute-start.7
  26.8 0.0 collective-permute-done.13.refs_0_.refs_12_
  26.8 9.3 %collective-permute-start.15 = (bf16[768,128]{1,0:T(8,128)(2,1)S(1)}, bf16[768,128]{1,0:T(8,128)(2,1)S(1)}, u32[]{:S(2)}, u32[]{:S(2)}) collective-permute-start(bf16[768,128]{1,0:T(8,128)(2,1)S(1)} %collective-permute-done.1.refs_8_.refs_20_), channel_id=1, source_target_pairs={{2,0},{3,1},{0,2},{1,3},{6,4},{7,5},{4,6},{5,7},{10,8},{11,9},{8,1... | collective-permute-start | bytes 589832 | tf_op jit(solution)/shard_map/ppermute | solution.py:65
  36.1 0.5 collective-permute-start.14
  36.7 0.0 collective-permute-done.5.refs_4_.refs_8_
  36.7 1.5 %collective-permute-start.22 = (bf16[768,128]{1,0:T(8,128)(2,1)S(1)}, bf16[768,128]{1,0:T(8,128)(2,1)S(1)}, u32[]{:S(2)}, u32[]{:S(2)}) collective-permute-start(bf16[768,128]{1,0:T(8,128)(2,1)S(1)} %collective-permute-done.1.refs_8_.refs_20_), channel_id=1, source_target_pairs={{1,0},{0,1},{3,2},{2,3},{5,4},{4,5},{7,6},{6,7},{9,8},{8,9},{11,10... | collective-permute-start | bytes 589832 | tf_op jit(solution)/shard_map/ppermute | solution.py:65
  38.2 0.0 collective-permute-done.6.refs_5_.refs_9_
  38.2 0.0 collective-permute-start.16
  38.2 0.1 collective-permute-start.8
  38.3 1.3 %collective-permute-done.8.refs_7_.refs_11_ = bf16[528,128]{1,0:T(8,128)(2,1)S(1)} collective-permute-done((bf16[528,128]{1,0:T(8,128)(2,1)S(1)}, bf16[528,128]{1,0:T(8,128)(2,1)S(1)}, u32[]{:S(2)}, u32[]{:S(2)}) %collective-permute-start.8) | collective-permute-done | bytes 135200 | tf_op jit(solution)/shard_map/ppermute | solution.py:65
  39.6 1.3 %shard_map.102 = (bf16[144,128]{1,0:T(8,128)(2,1)S(1)}, bf16[144,128]{1,0:T(8,128)(2,1)S(1)}, bf16[144,128]{1,0:T(8,128)(2,1)S(1)}, bf16[144,128]{1,0:T(8,128)(2,1)S(1)}) custom-call(s32[3]{0:T(128)S(1)} %pad_add_fusion.place_ref, bf16[128,1024]{1,0:T(8,128)(2,1)S(1)} %bitcast.21, bf16[128,1024]{1,0:T(8,128)(2,1)S(1)} %bitcast.23, ...), custom_call_target="tpu_custom_call" | custom-call | tf_op jit(solution)/shard_map/pallas_call | solution.py:369
  40.9 0.1 collective-permute-start.10
  41.0 0.6 collective-permute-done.15.refs_10_.refs_22_
  41.6 1.7 %collective-permute-start.11 = (bf16[144,128]{1,0:T(8,128)(2,1)S(1)}, bf16[144,128]{1,0:T(8,128)(2,1)S(1)}, u32[]{:S(2)}, u32[]{:S(2)}) collective-permute-start(bf16[144,128]{1,0:T(8,128)(2,1)S(1)} %get-tuple-element.42), channel_id=1, source_target_pairs={{0,12},{4,8},{8,4},{12,0},{1,13},{5,9},{9,5},{13,1},{2,14},{6,10},... | collective-permute-start | bytes 110600 | tf_op jit(solution)/shard_map/ppermute | solution.py:76
  43.3 1.1 %collective-permute-start.9 = (bf16[144,128]{1,0:T(8,128)(2,1)S(1)}, bf16[144,128]{1,0:T(8,128)(2,1)S(1)}, u32[]{:S(2)}, u32[]{:S(2)}) collective-permute-start(bf16[144,128]{1,0:T(8,128)(2,1)S(1)} %get-tuple-element.40), channel_id=1, source_target_pairs={{0,4},{4,0},{8,12},{12,8},{1,5},{5,1},{9,13},{13,9},{2,6},{6,2},{1... | collective-permute-start | bytes 110600 | tf_op jit(solution)/shard_map/ppermute | solution.py:76
  44.5 0.4 collective-permute-done.22.refs_9_.refs_21_
  44.9 0.5 collective-permute-start.18
  45.4 1.2 %collective-permute-done.10 = bf16[144,128]{1,0:T(8,128)(2,1)S(1)} collective-permute-done((bf16[144,128]{1,0:T(8,128)(2,1)S(1)}, bf16[144,128]{1,0:T(8,128)(2,1)S(1)}, u32[]{:S(2)}, u32[]{:S(2)}) %collective-permute-start.10) | collective-permute-done | bytes 36896 | tf_op jit(solution)/shard_map/ppermute | solution.py:76
  46.6 0.8 collective-permute-done.11
  47.4 1.4 %collective-permute-start.17 = (bf16[768,128]{1,0:T(8,128)(2,1)S(1)}, bf16[768,128]{1,0:T(8,128)(2,1)S(1)}, u32[]{:S(2)}, u32[]{:S(2)}) collective-permute-start(bf16[768,128]{1,0:T(8,128)(2,1)S(1)} %collective-permute-done.14.refs_1_.refs_13_), channel_id=1, source_target_pairs={{2,0},{3,1},{0,2},{1,3},{6,4},{7,5},{4,6},{5,7},{10,8},{11,9},{8,1... | collective-permute-start | bytes 589832 | tf_op jit(solution)/shard_map/ppermute | solution.py:65
  48.9 0.5 collective-permute-start.23
  49.4 0.1 collective-permute-start.12
  49.5 0.5 collective-permute-start.20
  50.0 0.8 collective-permute-done.12.refs_3_
  50.7 0.2 collective-permute-start.19
  50.9 0.4 collective-permute-start.26
  51.3 2.6 %collective-permute-done.17.refs_3_.refs_15_ = bf16[768,128]{1,0:T(8,128)(2,1)S(1)} collective-permute-done((bf16[768,128]{1,0:T(8,128)(2,1)S(1)}, bf16[768,128]{1,0:T(8,128)(2,1)S(1)}, u32[]{:S(2)}, u32[]{:S(2)}) %collective-permute-start.17) | collective-permute-done | bytes 196640 | tf_op jit(solution)/shard_map/ppermute | solution.py:65
  53.9 1.3 %collective-permute-done.23.refs_11_.refs_23_ = bf16[768,128]{1,0:T(8,128)(2,1)S(1)} collective-permute-done((bf16[768,128]{1,0:T(8,128)(2,1)S(1)}, bf16[768,128]{1,0:T(8,128)(2,1)S(1)}, u32[]{:S(2)}, u32[]{:S(2)}) %collective-permute-start.23) | collective-permute-done | bytes 196640 | tf_op jit(solution)/shard_map/ppermute | solution.py:65
  55.3 0.1 collective-permute-done.21.refs_7_.refs_19_
  55.3 1.3 %collective-permute-done.27.refs_15_.refs_27_ = bf16[768,128]{1,0:T(8,128)(2,1)S(1)} collective-permute-done((bf16[768,128]{1,0:T(8,128)(2,1)S(1)}, bf16[768,128]{1,0:T(8,128)(2,1)S(1)}, u32[]{:S(2)}, u32[]{:S(2)}) %collective-permute-start.27) | collective-permute-done | bytes 196640 | tf_op jit(solution)/shard_map/ppermute | solution.py:65
  56.7 1.4 %shard_map.103 = (bf16[128,384]{1,0:T(8,128)(2,1)S(1)}, bf16[128,384]{1,0:T(8,128)(2,1)S(1)}, bf16[128,384]{1,0:T(8,128)(2,1)S(1)}, bf16[128,384]{1,0:T(8,128)(2,1)S(1)}) custom-call(s32[3]{0:T(128)S(1)} %pad_add_fusion.place_ref, bf16[128,1024]{1,0:T(8,128)(2,1)S(1)} %bitcast.22, bf16[768,128]{1,0:T(8,128)(2,1)S(1)} %collective-permute-done.13.refs_0_.refs_12_, ...), custom_call_target="tpu_custom_call" | custom-call | tf_op jit(solution)/shard_map/pallas_call | solution.py:369
  58.1 0.1 collective-permute-start.28
  58.2 1.2 %collective-permute-start.29 = (bf16[128,384]{1,0:T(8,128)(2,1)S(1)}, bf16[128,384]{1,0:T(8,128)(2,1)S(1)}, u32[]{:S(2)}, u32[]{:S(2)}) collective-permute-start(bf16[128,384]{1,0:T(8,128)(2,1)S(1)} %get-tuple-element.49), channel_id=1, source_target_pairs={{0,8},{4,12},{8,0},{12,4},{1,9},{5,13},{9,1},{13,5},{2,10},{6,14},... | collective-permute-start | bytes 294920 | tf_op jit(solution)/shard_map/ppermute | solution.py:76
  59.4 3.1 %collective-permute-start.30 = (bf16[128,384]{1,0:T(8,128)(2,1)S(1)}, bf16[128,384]{1,0:T(8,128)(2,1)S(1)}, u32[]{:S(2)}, u32[]{:S(2)}) collective-permute-start(bf16[128,384]{1,0:T(8,128)(2,1)S(1)} %get-tuple-element.50), channel_id=1, source_target_pairs={{0,12},{4,8},{8,4},{12,0},{1,13},{5,9},{9,5},{13,1},{2,14},{6,10},... | collective-permute-start | bytes 294920 | tf_op jit(solution)/shard_map/ppermute | solution.py:76
  62.6 1.6 %collective-permute-done.28 = bf16[128,384]{1,0:T(8,128)(2,1)S(1)} collective-permute-done((bf16[128,384]{1,0:T(8,128)(2,1)S(1)}, bf16[128,384]{1,0:T(8,128)(2,1)S(1)}, u32[]{:S(2)}, u32[]{:S(2)}) %collective-permute-start.28) | collective-permute-done | bytes 98336 | tf_op jit(solution)/shard_map/ppermute | solution.py:76
  64.2 4.9 %collective-permute-done.29 = bf16[128,384]{1,0:T(8,128)(2,1)S(1)} collective-permute-done((bf16[128,384]{1,0:T(8,128)(2,1)S(1)}, bf16[128,384]{1,0:T(8,128)(2,1)S(1)}, u32[]{:S(2)}, u32[]{:S(2)}) %collective-permute-start.29) | collective-permute-done | bytes 98336 | tf_op jit(solution)/shard_map/ppermute | solution.py:76
  69.1 0.1 convert_add_fusion.refs_0_
  69.1 0.1 collective-permute-start.31
  69.2 1.4 %collective-permute-done.31.refs_1_ = f32[128,384]{1,0:T(8,128)S(1)} collective-permute-done((f32[128,384]{1,0:T(8,128)S(1)}, f32[128,384]{1,0:T(8,128)S(1)}, u32[]{:S(2)}, u32[]{:S(2)}) %collective-permute-start.31) | collective-permute-done | bytes 196640 | tf_op jit(solution)/shard_map/ppermute | solution.py:65
  70.6 10.8 %shard_map.104 = (bf16[144,512]{1,0:T(8,128)(2,1)S(1)}, f32[64,256]{1,0:T(8,128)S(1)}, f32[64,256]{1,0:T(8,128)S(1)}, f32[64,256]{1,0:T(8,128)S(1)}, f32[64,256]{1,0:T(8,128)S(1)}) custom-call(s32[3]{0:T(128)S(1)} %pad_add_fusion.place_ref, f32[128,384]{1,0:T(8,128)S(1)} %convert_add_fusion.refs_0_, f32[128,384]{1,0:T(8,128)S(1)} %collective-permute-done.31.refs_1_, ...), custom_call_target="tpu_custom_call" | custom-call | tf_op jit(solution)/shard_map/pallas_call | solution.py:369
  81.5 1.9 %collective-permute-start.32 = (bf16[144,512]{1,0:T(8,128)(2,1)S(1)}, bf16[144,512]{1,0:T(8,128)(2,1)S(1)}, u32[]{:S(2)}, u32[]{:S(2)}) collective-permute-start(bf16[144,512]{1,0:T(8,128)(2,1)S(1)} %get-tuple-element.51.refs_0_), channel_id=1, source_target_pairs={{4,0},{0,4},{12,8},{8,12},{5,1},{1,5},{13,9},{9,13},{6,2},{2,6},{1... | collective-permute-start | bytes 442376 | tf_op jit(solution)/shard_map/ppermute | solution.py:65
  83.4 0.2 collective-permute-start.33
  83.6 2.4 %collective-permute-start.34 = (bf16[144,512]{1,0:T(8,128)(2,1)S(1)}, bf16[144,512]{1,0:T(8,128)(2,1)S(1)}, u32[]{:S(2)}, u32[]{:S(2)}) collective-permute-start(bf16[144,512]{1,0:T(8,128)(2,1)S(1)} %get-tuple-element.51.refs_0_), channel_id=1, source_target_pairs={{12,0},{8,4},{4,8},{0,12},{13,1},{9,5},{5,9},{1,13},{14,2},{10,6},... | collective-permute-start | bytes 442376 | tf_op jit(solution)/shard_map/ppermute | solution.py:65
  85.9 3.4 %collective-permute-done.32.refs_1_ = bf16[144,512]{1,0:T(8,128)(2,1)S(1)} collective-permute-done((bf16[144,512]{1,0:T(8,128)(2,1)S(1)}, bf16[144,512]{1,0:T(8,128)(2,1)S(1)}, u32[]{:S(2)}, u32[]{:S(2)}) %collective-permute-start.32) | collective-permute-done | bytes 147488 | tf_op jit(solution)/shard_map/ppermute | solution.py:65
  89.4 0.5 collective-permute-start.35
  89.9 0.7 collective-permute-start.36
  90.6 2.3 %collective-permute-start.37 = (f32[64,256]{1,0:T(8,128)S(1)}, f32[64,256]{1,0:T(8,128)S(1)}, u32[]{:S(2)}, u32[]{:S(2)}) collective-permute-start(f32[64,256]{1,0:T(8,128)S(1)} %get-tuple-element.61), channel_id=1, source_target_pairs={{0,3},{1,2},{2,1},{3,0},{4,7},{5,6},{6,5},{7,4},{8,11},{9,10},{10,... | collective-permute-start | bytes 196616 | tf_op jit(solution)/shard_map/ppermute | solution.py:76
  92.9 4.5 %collective-permute-done.33.refs_2_ = bf16[144,512]{1,0:T(8,128)(2,1)S(1)} collective-permute-done((bf16[144,512]{1,0:T(8,128)(2,1)S(1)}, bf16[144,512]{1,0:T(8,128)(2,1)S(1)}, u32[]{:S(2)}, u32[]{:S(2)}) %collective-permute-start.33) | collective-permute-done | bytes 147488 | tf_op jit(solution)/shard_map/ppermute | solution.py:65
  97.4 3.1 %shard_map.105 = (bf16[128,1024]{1,0:T(8,128)(2,1)}, bf16[128,1024]{1,0:T(8,128)(2,1)}) custom-call(s32[3]{0:T(128)S(1)} %pad_add_fusion.place_ref, bf16[144,512]{1,0:T(8,128)(2,1)S(1)} %get-tuple-element.51.refs_0_, bf16[144,512]{1,0:T(8,128)(2,1)S(1)} %collective-permute-done.32.refs_1_, bf16[144,512]{1,0:T(8,128)(2,1)S(1)} %collective-permute-done.33.refs_2_, ...), custom_call_target="tpu_custom_call" | custom-call | tf_op jit(solution)/shard_map/pallas_call | solution.py:369
  100.5 0.6 slice_bitcast_fusion
  (37 shorter events, 0.1 us)
Async XLA Ops:
  0.6 1.2 %copy-start = (bf16[4096,1]{0,1:T(2,128)(2,1)S(1)}, bf16[4096,1]{0,1:T(2,128)(2,1)}, u32[]{:S(2)}) copy-start(bf16[4096,1]{0,1:T(2,128)(2,1)} %param.9) | copy-start | bytes 24580
  0.7 1.2 %copy-start.5 = (bf16[512,128]{1,0:T(8,128)(2,1)S(1)}, bf16[512,128]{1,0:T(8,128)(2,1)}, u32[]{:S(2)}) copy-start(bf16[512,128]{1,0:T(8,128)(2,1)} %param.10) | copy-start | bytes 393220
  0.7 38.9 %copy-start.2 = (bf16[1,128,1024]{2,1,0:T(8,128)(2,1)S(1)}, bf16[1,128,1024]{2,1,0:T(8,128)(2,1)}, u32[]{:S(2)}) copy-start(bf16[1,128,1024]{2,1,0:T(8,128)(2,1)} %param.13) | copy-start | bytes 786436
  1.8 37.8 %copy-start.1 = (bf16[1,128,1024]{2,1,0:T(8,128)(2,1)S(1)}, bf16[1,128,1024]{2,1,0:T(8,128)(2,1)}, u32[]{:S(2)}) copy-start(bf16[1,128,1024]{2,1,0:T(8,128)(2,1)} %param.7) | copy-start | bytes 786436
  2.0 1.4 %collective-permute-start.1 = (bf16[768,128]{1,0:T(8,128)(2,1)S(1)}, bf16[768,128]{1,0:T(8,128)(2,1)S(1)}, u32[]{:S(2)}, u32[]{:S(2)}) collective-permute-start(bf16[768,128]{1,0:T(8,128)(2,1)S(1)} %bitcast.28), channel_id=1, source_target_pairs={{0,0},{1,1},{2,4},{3,5},{4,2},{5,3},{6,6},{7,7},{8,16},{9,17},{10,... | collective-permute-start | bytes 589832 | tf_op jit(solution)/shard_map/ppermute | solution.py:400
  2.6 0.7 collective-permute-start
  3.3 22.9 %collective-permute-start.2 = (bf16[528,128]{1,0:T(8,128)(2,1)S(1)}, bf16[528,128]{1,0:T(8,128)(2,1)S(1)}, u32[]{:S(2)}, u32[]{:S(2)}) collective-permute-start(bf16[528,128]{1,0:T(8,128)(2,1)S(1)} %collective-permute-done.refs_0_.refs_4_), channel_id=1, source_target_pairs={{1,0},{0,1},{3,2},{2,3},{5,4},{4,5},{7,6},{6,7},{9,8},{8,9},{11,10... | collective-permute-start | bytes 405512 | tf_op jit(solution)/shard_map/ppermute | solution.py:65
  6.3 19.9 %collective-permute-start.3 = (bf16[528,128]{1,0:T(8,128)(2,1)S(1)}, bf16[528,128]{1,0:T(8,128)(2,1)S(1)}, u32[]{:S(2)}, u32[]{:S(2)}) collective-permute-start(bf16[528,128]{1,0:T(8,128)(2,1)S(1)} %collective-permute-done.refs_0_.refs_4_), channel_id=1, source_target_pairs={{2,0},{3,1},{0,2},{1,3},{6,4},{7,5},{4,6},{5,7},{10,8},{11,9},{8,1... | collective-permute-start | bytes 405512 | tf_op jit(solution)/shard_map/ppermute | solution.py:65
  23.1 3.7 %collective-permute-start.13 = (bf16[768,128]{1,0:T(8,128)(2,1)S(1)}, bf16[768,128]{1,0:T(8,128)(2,1)S(1)}, u32[]{:S(2)}, u32[]{:S(2)}) collective-permute-start(bf16[768,128]{1,0:T(8,128)(2,1)S(1)} %bitcast.27), channel_id=1, source_target_pairs={{0,0},{1,1},{2,4},{3,5},{4,2},{5,3},{6,6},{7,7},{8,16},{9,17},{10,... | collective-permute-start | bytes 589832 | tf_op jit(solution)/shard_map/ppermute | solution.py:400
  23.7 12.4 %collective-permute-start.4 = (bf16[528,128]{1,0:T(8,128)(2,1)S(1)}, bf16[528,128]{1,0:T(8,128)(2,1)S(1)}, u32[]{:S(2)}, u32[]{:S(2)}) collective-permute-start(bf16[528,128]{1,0:T(8,128)(2,1)S(1)} %collective-permute-done.refs_0_.refs_4_), channel_id=1, source_target_pairs={{3,0},{2,1},{1,2},{0,3},{7,4},{6,5},{5,6},{4,7},{11,8},{10,9},{9,1... | collective-permute-start | bytes 405512 | tf_op jit(solution)/shard_map/ppermute | solution.py:65
  25.0 11.6 %collective-permute-start.5 = (bf16[528,128]{1,0:T(8,128)(2,1)S(1)}, bf16[528,128]{1,0:T(8,128)(2,1)S(1)}, u32[]{:S(2)}, u32[]{:S(2)}) collective-permute-start(bf16[528,128]{1,0:T(8,128)(2,1)S(1)} %collective-permute-done.refs_0_.refs_4_), channel_id=1, source_target_pairs={{16,0},{0,16},{17,1},{1,17},{18,2},{2,18},{19,3},{3,19},{20,4},{4,... | collective-permute-start | bytes 405512 | tf_op jit(solution)/shard_map/ppermute | solution.py:65
  26.3 11.9 %collective-permute-start.6 = (bf16[528,128]{1,0:T(8,128)(2,1)S(1)}, bf16[528,128]{1,0:T(8,128)(2,1)S(1)}, u32[]{:S(2)}, u32[]{:S(2)}) collective-permute-start(bf16[528,128]{1,0:T(8,128)(2,1)S(1)} %collective-permute-done.2.refs_1_.refs_5_), channel_id=1, source_target_pairs={{16,0},{0,16},{17,1},{1,17},{18,2},{2,18},{19,3},{3,19},{20,4},{4,... | collective-permute-start | bytes 405512 | tf_op jit(solution)/shard_map/ppermute | solution.py:65
  26.3 11.9 %collective-permute-start.7 = (bf16[528,128]{1,0:T(8,128)(2,1)S(1)}, bf16[528,128]{1,0:T(8,128)(2,1)S(1)}, u32[]{:S(2)}, u32[]{:S(2)}) collective-permute-start(bf16[528,128]{1,0:T(8,128)(2,1)S(1)} %collective-permute-done.3.refs_2_.refs_6_), channel_id=1, source_target_pairs={{16,0},{0,16},{17,1},{1,17},{18,2},{2,18},{19,3},{3,19},{20,4},{4,... | collective-permute-start | bytes 405512 | tf_op jit(solution)/shard_map/ppermute | solution.py:65
  26.8 14.8 %collective-permute-start.15 = (bf16[768,128]{1,0:T(8,128)(2,1)S(1)}, bf16[768,128]{1,0:T(8,128)(2,1)S(1)}, u32[]{:S(2)}, u32[]{:S(2)}) collective-permute-start(bf16[768,128]{1,0:T(8,128)(2,1)S(1)} %collective-permute-done.1.refs_8_.refs_20_), channel_id=1, source_target_pairs={{2,0},{3,1},{0,2},{1,3},{6,4},{7,5},{4,6},{5,7},{10,8},{11,9},{8,1... | collective-permute-start | bytes 589832 | tf_op jit(solution)/shard_map/ppermute | solution.py:65
  36.1 7.2 %collective-permute-start.14 = (bf16[768,128]{1,0:T(8,128)(2,1)S(1)}, bf16[768,128]{1,0:T(8,128)(2,1)S(1)}, u32[]{:S(2)}, u32[]{:S(2)}) collective-permute-start(bf16[768,128]{1,0:T(8,128)(2,1)S(1)} %collective-permute-done.13.refs_0_.refs_12_), channel_id=1, source_target_pairs={{1,0},{0,1},{3,2},{2,3},{5,4},{4,5},{7,6},{6,7},{9,8},{8,9},{11,10... | collective-permute-start | bytes 589832 | tf_op jit(solution)/shard_map/ppermute | solution.py:65
  36.7 8.2 %collective-permute-start.22 = (bf16[768,128]{1,0:T(8,128)(2,1)S(1)}, bf16[768,128]{1,0:T(8,128)(2,1)S(1)}, u32[]{:S(2)}, u32[]{:S(2)}) collective-permute-start(bf16[768,128]{1,0:T(8,128)(2,1)S(1)} %collective-permute-done.1.refs_8_.refs_20_), channel_id=1, source_target_pairs={{1,0},{0,1},{3,2},{2,3},{5,4},{4,5},{7,6},{6,7},{9,8},{8,9},{11,10... | collective-permute-start | bytes 589832 | tf_op jit(solution)/shard_map/ppermute | solution.py:65
  38.2 6.7 %collective-permute-start.16 = (bf16[768,128]{1,0:T(8,128)(2,1)S(1)}, bf16[768,128]{1,0:T(8,128)(2,1)S(1)}, u32[]{:S(2)}, u32[]{:S(2)}) collective-permute-start(bf16[768,128]{1,0:T(8,128)(2,1)S(1)} %collective-permute-done.13.refs_0_.refs_12_), channel_id=1, source_target_pairs={{2,0},{3,1},{0,2},{1,3},{6,4},{7,5},{4,6},{5,7},{10,8},{11,9},{8,1... | collective-permute-start | bytes 589832 | tf_op jit(solution)/shard_map/ppermute | solution.py:65
  38.2 1.4 %collective-permute-start.8 = (bf16[528,128]{1,0:T(8,128)(2,1)S(1)}, bf16[528,128]{1,0:T(8,128)(2,1)S(1)}, u32[]{:S(2)}, u32[]{:S(2)}) collective-permute-start(bf16[528,128]{1,0:T(8,128)(2,1)S(1)} %collective-permute-done.4.refs_3_.refs_7_), channel_id=1, source_target_pairs={{16,0},{0,16},{17,1},{1,17},{18,2},{2,18},{19,3},{3,19},{20,4},{4,... | collective-permute-start | bytes 405512 | tf_op jit(solution)/shard_map/ppermute | solution.py:65
  40.9 5.7 %collective-permute-start.10 = (bf16[144,128]{1,0:T(8,128)(2,1)S(1)}, bf16[144,128]{1,0:T(8,128)(2,1)S(1)}, u32[]{:S(2)}, u32[]{:S(2)}) collective-permute-start(bf16[144,128]{1,0:T(8,128)(2,1)S(1)} %get-tuple-element.41), channel_id=1, source_target_pairs={{0,8},{4,12},{8,0},{12,4},{1,9},{5,13},{9,1},{13,5},{2,10},{6,14},... | collective-permute-start | bytes 110600 | tf_op jit(solution)/shard_map/ppermute | solution.py:76
  41.6 5.8 %collective-permute-start.11 = (bf16[144,128]{1,0:T(8,128)(2,1)S(1)}, bf16[144,128]{1,0:T(8,128)(2,1)S(1)}, u32[]{:S(2)}, u32[]{:S(2)}) collective-permute-start(bf16[144,128]{1,0:T(8,128)(2,1)S(1)} %get-tuple-element.42), channel_id=1, source_target_pairs={{0,12},{4,8},{8,4},{12,0},{1,13},{5,9},{9,5},{13,1},{2,14},{6,10},... | collective-permute-start | bytes 110600 | tf_op jit(solution)/shard_map/ppermute | solution.py:76
  43.3 5.5 %collective-permute-start.9 = (bf16[144,128]{1,0:T(8,128)(2,1)S(1)}, bf16[144,128]{1,0:T(8,128)(2,1)S(1)}, u32[]{:S(2)}, u32[]{:S(2)}) collective-permute-start(bf16[144,128]{1,0:T(8,128)(2,1)S(1)} %get-tuple-element.40), channel_id=1, source_target_pairs={{0,4},{4,0},{8,12},{12,8},{1,5},{5,1},{9,13},{13,9},{2,6},{6,2},{1... | collective-permute-start | bytes 110600 | tf_op jit(solution)/shard_map/ppermute | solution.py:76
  44.9 4.5 %collective-permute-start.24 = (bf16[768,128]{1,0:T(8,128)(2,1)S(1)}, bf16[768,128]{1,0:T(8,128)(2,1)S(1)}, u32[]{:S(2)}, u32[]{:S(2)}) collective-permute-start(bf16[768,128]{1,0:T(8,128)(2,1)S(1)} %collective-permute-done.1.refs_8_.refs_20_), channel_id=1, source_target_pairs={{16,0},{0,16},{17,1},{1,17},{18,2},{2,18},{19,3},{3,19},{20,4},{4,... | collective-permute-start | bytes 589832 | tf_op jit(solution)/shard_map/ppermute | solution.py:65
  44.9 4.6 %collective-permute-start.18 = (bf16[768,128]{1,0:T(8,128)(2,1)S(1)}, bf16[768,128]{1,0:T(8,128)(2,1)S(1)}, u32[]{:S(2)}, u32[]{:S(2)}) collective-permute-start(bf16[768,128]{1,0:T(8,128)(2,1)S(1)} %collective-permute-done.13.refs_0_.refs_12_), channel_id=1, source_target_pairs={{16,0},{0,16},{17,1},{1,17},{18,2},{2,18},{19,3},{3,19},{20,4},{4,... | collective-permute-start | bytes 589832 | tf_op jit(solution)/shard_map/ppermute | solution.py:65
  46.6 4.3 %collective-permute-start.25 = (bf16[768,128]{1,0:T(8,128)(2,1)S(1)}, bf16[768,128]{1,0:T(8,128)(2,1)S(1)}, u32[]{:S(2)}, u32[]{:S(2)}) collective-permute-start(bf16[768,128]{1,0:T(8,128)(2,1)S(1)} %collective-permute-done.22.refs_9_.refs_21_), channel_id=1, source_target_pairs={{16,0},{0,16},{17,1},{1,17},{18,2},{2,18},{19,3},{3,19},{20,4},{4,... | collective-permute-start | bytes 589832 | tf_op jit(solution)/shard_map/ppermute | solution.py:65
  47.4 6.5 %collective-permute-start.17 = (bf16[768,128]{1,0:T(8,128)(2,1)S(1)}, bf16[768,128]{1,0:T(8,128)(2,1)S(1)}, u32[]{:S(2)}, u32[]{:S(2)}) collective-permute-start(bf16[768,128]{1,0:T(8,128)(2,1)S(1)} %collective-permute-done.14.refs_1_.refs_13_), channel_id=1, source_target_pairs={{2,0},{3,1},{0,2},{1,3},{6,4},{7,5},{4,6},{5,7},{10,8},{11,9},{8,1... | collective-permute-start | bytes 589832 | tf_op jit(solution)/shard_map/ppermute | solution.py:65
  48.9 6.4 %collective-permute-start.23 = (bf16[768,128]{1,0:T(8,128)(2,1)S(1)}, bf16[768,128]{1,0:T(8,128)(2,1)S(1)}, u32[]{:S(2)}, u32[]{:S(2)}) collective-permute-start(bf16[768,128]{1,0:T(8,128)(2,1)S(1)} %collective-permute-done.15.refs_10_.refs_22_), channel_id=1, source_target_pairs={{1,0},{0,1},{3,2},{2,3},{5,4},{4,5},{7,6},{6,7},{9,8},{8,9},{11,10... | collective-permute-start | bytes 589832 | tf_op jit(solution)/shard_map/ppermute | solution.py:65
  49.4 1.3 %collective-permute-start.12 = (f32[144,128]{1,0:T(8,128)S(1)}, f32[144,128]{1,0:T(8,128)S(1)}, u32[]{:S(2)}, u32[]{:S(2)}) collective-permute-start(f32[144,128]{1,0:T(8,128)S(1)} %convert_add_fusion.1.refs_2_), channel_id=1, source_target_pairs={{16,0},{0,16},{17,1},{1,17},{18,2},{2,18},{19,3},{3,19},{20,4},{4,... | collective-permute-start | bytes 221192 | tf_op jit(solution)/shard_map/ppermute | solution.py:65
  49.5 5.8 %collective-permute-start.20 = (bf16[768,128]{1,0:T(8,128)(2,1)S(1)}, bf16[768,128]{1,0:T(8,128)(2,1)S(1)}, u32[]{:S(2)}, u32[]{:S(2)}) collective-permute-start(bf16[768,128]{1,0:T(8,128)(2,1)S(1)} %collective-permute-done.16.refs_2_.refs_14_), channel_id=1, source_target_pairs={{16,0},{0,16},{17,1},{1,17},{18,2},{2,18},{19,3},{3,19},{20,4},{4,... | collective-permute-start | bytes 589832 | tf_op jit(solution)/shard_map/ppermute | solution.py:65
  50.7 4.5 %collective-permute-start.19 = (bf16[768,128]{1,0:T(8,128)(2,1)S(1)}, bf16[768,128]{1,0:T(8,128)(2,1)S(1)}, u32[]{:S(2)}, u32[]{:S(2)}) collective-permute-start(bf16[768,128]{1,0:T(8,128)(2,1)S(1)} %collective-permute-done.14.refs_1_.refs_13_), channel_id=1, source_target_pairs={{16,0},{0,16},{17,1},{1,17},{18,2},{2,18},{19,3},{3,19},{20,4},{4,... | collective-permute-start | bytes 589832 | tf_op jit(solution)/shard_map/ppermute | solution.py:65
  50.9 4.4 %collective-permute-start.26 = (bf16[768,128]{1,0:T(8,128)(2,1)S(1)}, bf16[768,128]{1,0:T(8,128)(2,1)S(1)}, u32[]{:S(2)}, u32[]{:S(2)}) collective-permute-start(bf16[768,128]{1,0:T(8,128)(2,1)S(1)} %collective-permute-done.15.refs_10_.refs_22_), channel_id=1, source_target_pairs={{16,0},{0,16},{17,1},{1,17},{18,2},{2,18},{19,3},{3,19},{20,4},{4,... | collective-permute-start | bytes 589832 | tf_op jit(solution)/shard_map/ppermute | solution.py:65
  53.9 1.4 %collective-permute-start.21 = (bf16[768,128]{1,0:T(8,128)(2,1)S(1)}, bf16[768,128]{1,0:T(8,128)(2,1)S(1)}, u32[]{:S(2)}, u32[]{:S(2)}) collective-permute-start(bf16[768,128]{1,0:T(8,128)(2,1)S(1)} %collective-permute-done.17.refs_3_.refs_15_), channel_id=1, source_target_pairs={{16,0},{0,16},{17,1},{1,17},{18,2},{2,18},{19,3},{3,19},{20,4},{4,... | collective-permute-start | bytes 589832 | tf_op jit(solution)/shard_map/ppermute | solution.py:65
  55.2 1.4 %collective-permute-start.27 = (bf16[768,128]{1,0:T(8,128)(2,1)S(1)}, bf16[768,128]{1,0:T(8,128)(2,1)S(1)}, u32[]{:S(2)}, u32[]{:S(2)}) collective-permute-start(bf16[768,128]{1,0:T(8,128)(2,1)S(1)} %collective-permute-done.23.refs_11_.refs_23_), channel_id=1, source_target_pairs={{16,0},{0,16},{17,1},{1,17},{18,2},{2,18},{19,3},{3,19},{20,4},{4,... | collective-permute-start | bytes 589832 | tf_op jit(solution)/shard_map/ppermute | solution.py:65
  58.1 6.1 %collective-permute-start.28 = (bf16[128,384]{1,0:T(8,128)(2,1)S(1)}, bf16[128,384]{1,0:T(8,128)(2,1)S(1)}, u32[]{:S(2)}, u32[]{:S(2)}) collective-permute-start(bf16[128,384]{1,0:T(8,128)(2,1)S(1)} %get-tuple-element.48), channel_id=1, source_target_pairs={{0,4},{4,0},{8,12},{12,8},{1,5},{5,1},{9,13},{13,9},{2,6},{6,2},{1... | collective-permute-start | bytes 294920 | tf_op jit(solution)/shard_map/ppermute | solution.py:76
  58.2 10.9 %collective-permute-start.29 = (bf16[128,384]{1,0:T(8,128)(2,1)S(1)}, bf16[128,384]{1,0:T(8,128)(2,1)S(1)}, u32[]{:S(2)}, u32[]{:S(2)}) collective-permute-start(bf16[128,384]{1,0:T(8,128)(2,1)S(1)} %get-tuple-element.49), channel_id=1, source_target_pairs={{0,8},{4,12},{8,0},{12,4},{1,9},{5,13},{9,1},{13,5},{2,10},{6,14},... | collective-permute-start | bytes 294920 | tf_op jit(solution)/shard_map/ppermute | solution.py:76
  59.4 9.6 %collective-permute-start.30 = (bf16[128,384]{1,0:T(8,128)(2,1)S(1)}, bf16[128,384]{1,0:T(8,128)(2,1)S(1)}, u32[]{:S(2)}, u32[]{:S(2)}) collective-permute-start(bf16[128,384]{1,0:T(8,128)(2,1)S(1)} %get-tuple-element.50), channel_id=1, source_target_pairs={{0,12},{4,8},{8,4},{12,0},{1,13},{5,9},{9,5},{13,1},{2,14},{6,10},... | collective-permute-start | bytes 294920 | tf_op jit(solution)/shard_map/ppermute | solution.py:76
  69.1 1.6 %copy-start.3 = (f32[1,128,512]{2,1,0:T(8,128)S(1)}, f32[1,128,512]{2,1,0:T(8,128)}, u32[]{:S(2)}) copy-start(f32[1,128,512]{2,1,0:T(8,128)} %param.11) | copy-start | bytes 786436
  69.1 1.6 %copy-start.4 = (f32[1,512,128]{2,1,0:T(8,128)S(1)}, f32[1,512,128]{2,1,0:T(8,128)}, u32[]{:S(2)}) copy-start(f32[1,512,128]{2,1,0:T(8,128)} %param.12) | copy-start | bytes 786436
  69.1 1.5 %collective-permute-start.31 = (f32[128,384]{1,0:T(8,128)S(1)}, f32[128,384]{1,0:T(8,128)S(1)}, u32[]{:S(2)}, u32[]{:S(2)}) collective-permute-start(f32[128,384]{1,0:T(8,128)S(1)} %convert_add_fusion.refs_0_), channel_id=1, source_target_pairs={{16,0},{0,16},{17,1},{1,17},{18,2},{2,18},{19,3},{3,19},{20,4},{4,... | collective-permute-start | bytes 589832 | tf_op jit(solution)/shard_map/ppermute | solution.py:65
  81.5 7.9 %collective-permute-start.32 = (bf16[144,512]{1,0:T(8,128)(2,1)S(1)}, bf16[144,512]{1,0:T(8,128)(2,1)S(1)}, u32[]{:S(2)}, u32[]{:S(2)}) collective-permute-start(bf16[144,512]{1,0:T(8,128)(2,1)S(1)} %get-tuple-element.51.refs_0_), channel_id=1, source_target_pairs={{4,0},{0,4},{12,8},{8,12},{5,1},{1,5},{13,9},{9,13},{6,2},{2,6},{1... | collective-permute-start | bytes 442376 | tf_op jit(solution)/shard_map/ppermute | solution.py:65
  83.4 13.9 %collective-permute-start.33 = (bf16[144,512]{1,0:T(8,128)(2,1)S(1)}, bf16[144,512]{1,0:T(8,128)(2,1)S(1)}, u32[]{:S(2)}, u32[]{:S(2)}) collective-permute-start(bf16[144,512]{1,0:T(8,128)(2,1)S(1)} %get-tuple-element.51.refs_0_), channel_id=1, source_target_pairs={{8,0},{12,4},{0,8},{4,12},{9,1},{13,5},{1,9},{5,13},{10,2},{14,6},... | collective-permute-start | bytes 442376 | tf_op jit(solution)/shard_map/ppermute | solution.py:65
  83.6 13.8 %collective-permute-start.34 = (bf16[144,512]{1,0:T(8,128)(2,1)S(1)}, bf16[144,512]{1,0:T(8,128)(2,1)S(1)}, u32[]{:S(2)}, u32[]{:S(2)}) collective-permute-start(bf16[144,512]{1,0:T(8,128)(2,1)S(1)} %get-tuple-element.51.refs_0_), channel_id=1, source_target_pairs={{12,0},{8,4},{4,8},{0,12},{13,1},{9,5},{5,9},{1,13},{14,2},{10,6},... | collective-permute-start | bytes 442376 | tf_op jit(solution)/shard_map/ppermute | solution.py:65
  89.4 11.1 %collective-permute-start.35 = (f32[64,256]{1,0:T(8,128)S(1)}, f32[64,256]{1,0:T(8,128)S(1)}, u32[]{:S(2)}, u32[]{:S(2)}) collective-permute-start(f32[64,256]{1,0:T(8,128)S(1)} %get-tuple-element.59), channel_id=1, source_target_pairs={{0,1},{1,0},{2,3},{3,2},{4,5},{5,4},{6,7},{7,6},{8,9},{9,8},{10,11... | collective-permute-start | bytes 196616 | tf_op jit(solution)/shard_map/ppermute | solution.py:76
  89.9 10.6 %collective-permute-start.36 = (f32[64,256]{1,0:T(8,128)S(1)}, f32[64,256]{1,0:T(8,128)S(1)}, u32[]{:S(2)}, u32[]{:S(2)}) collective-permute-start(f32[64,256]{1,0:T(8,128)S(1)} %get-tuple-element.60), channel_id=1, source_target_pairs={{0,2},{1,3},{2,0},{3,1},{4,6},{5,7},{6,4},{7,5},{8,10},{9,11},{10,... | collective-permute-start | bytes 196616 | tf_op jit(solution)/shard_map/ppermute | solution.py:76
  90.6 9.9 %collective-permute-start.37 = (f32[64,256]{1,0:T(8,128)S(1)}, f32[64,256]{1,0:T(8,128)S(1)}, u32[]{:S(2)}, u32[]{:S(2)}) collective-permute-start(f32[64,256]{1,0:T(8,128)S(1)} %get-tuple-element.61), channel_id=1, source_target_pairs={{0,3},{1,2},{2,1},{3,0},{4,7},{5,6},{6,5},{7,4},{8,11},{9,10},{10,... | collective-permute-start | bytes 196616 | tf_op jit(solution)/shard_map/ppermute | solution.py:76

commit v4 on v3

--- a/solution.py
+++ b/solution.py
@@ -414,8 +414,8 @@
         )
     )
     first_w, second_w, outer_w = swapped(first), swapped(second), swapped(outer)
+    outer_w, first_w, second_w = lax.optimization_barrier((outer_w, first_w, second_w))
     first_near = [first_w, hop(first_w, "dp", 1), hop(first_w, "dp", 2)]
-    outer_w, unused = lax.optimization_barrier((outer_w, second_w))
     outer_near = peers_of(outer_w, "dp")
     second_near = [second_w, hop(second_w, "dp", 1), hop(second_w, "dp", 2)]
     outer_ws = over_seq(outer_near)

time: 101 us -> 102 us (level)
  waiting for transfers between devices: 26.5 us -> 29.8 us
  starting transfers between devices: 55.1 us -> 52.2 us
    ppermute x26, waiting for transfers between devices: 17.9 us -> 23 us  [hop(): lax.ppermute(array, axis, [(mate(i, step, count), i) for i in range(count)])]
    ppermute x26, starting transfers between devices: 42.3 us -> 38.8 us  [hop(): lax.ppermute(array, axis, [(mate(i, step, count), i) for i in range(count)])]
    ppermute x9, waiting for transfers between devices: 8.5 us -> 6.75 us  [sent_to(): lax.ppermute(arrays[j], axis, [(i, mate(i, j, count)) for i in range(coun...]
  transfers between devices with their start and end apart: 38 -> 38, of which waited for: 15 -> 16; matrix products, arithmetic and copies ran while one was open for 0% -> 0% of each run, Pallas kernels for 4% -> 4%
where the time goes in v4:
time: 102 us
  starting transfers between devices  52.2 us (51%)
  waiting for transfers between devices  29.8 us (29%)
  Pallas kernels  16.7 us (16%)
  local copies, waits for them, and re-layouts  1.77 us (2%)
    ppermute x26, starting transfers between devices, hop(): lax.ppermute(array, axis, [(mate(i, step, count), i) for i in range(count)])  38.8 us
    ppermute x26, waiting for transfers between devices, hop(): lax.ppermute(array, axis, [(mate(i, step, count), i) for i in range(count)])  23 us
    pallas_call x4, Pallas kernels, call(): pl.pallas_call(kernel, out_shape=outs, in_specs=[SMEM] + [VMEM] * (len(op...  16.7 us
    ppermute x9, starting transfers between devices, sent_to(): lax.ppermute(arrays[j], axis, [(i, mate(i, j, count)) for i in range(coun...  11.4 us
    ppermute x9, waiting for transfers between devices, sent_to(): lax.ppermute(arrays[j], axis, [(i, mate(i, j, count)) for i in range(coun...  6.75 us
  transfers between devices with their start and end apart: 38, of which 16 were waited for; matrix products, arithmetic and copies ran while one was open for 0% of the time, Pallas kernels for 4%

profile of v4, /device:TPU:0, one launch (start us, length us, event | category | flops | bytes accessed | tf_op | source)
XLA Modules:
  0.0 101.6 jit_solution(1704076544360485241)
XLA Ops:
  0.6 0.0 copy-start
  0.7 0.1 pad_add_fusion.place_ref
  0.7 1.1 %fusion.2 = (bf16[3,256,128]{2,1,0:T(8,128)(2,1)S(1)}, bf16[3,256,128]{2,1,0:T(8,128)(2,1)S(1)}) fusion(bf16[3,512,128]{2,1,0:T(8,128)(2,1)} %bitcast.26), kind=kLoop, calls=%fused_computation.10 | loop fusion | bytes 786432 | tf_op jit(solution)/shard_map/slice | solution.py:412
  1.8 0.0 copy-start.1
  1.9 0.1 reduce
  2.0 0.7 collective-permute-start.1
  2.6 0.7 collective-permute-start.2
  3.3 0.7 collective-permute-start
  4.0 0.0 collective-permute-done.refs_0_.refs_4_
  4.0 0.0 collective-permute-done.2.refs_8_.refs_20_
  4.0 3.0 %collective-permute-start.3 = (bf16[528,128]{1,0:T(8,128)(2,1)S(1)}, bf16[528,128]{1,0:T(8,128)(2,1)S(1)}, u32[]{:S(2)}, u32[]{:S(2)}) collective-permute-start(bf16[528,128]{1,0:T(8,128)(2,1)S(1)} %collective-permute-done.refs_0_.refs_4_), channel_id=1, source_target_pairs={{1,0},{0,1},{3,2},{2,3},{5,4},{4,5},{7,6},{6,7},{9,8},{8,9},{11,10... | collective-permute-start | bytes 405512 | tf_op jit(solution)/shard_map/ppermute | solution.py:65
  7.0 23.0 %collective-permute-start.4 = (bf16[528,128]{1,0:T(8,128)(2,1)S(1)}, bf16[528,128]{1,0:T(8,128)(2,1)S(1)}, u32[]{:S(2)}, u32[]{:S(2)}) collective-permute-start(bf16[528,128]{1,0:T(8,128)(2,1)S(1)} %collective-permute-done.refs_0_.refs_4_), channel_id=1, source_target_pairs={{2,0},{3,1},{0,2},{1,3},{6,4},{7,5},{4,6},{5,7},{10,8},{11,9},{8,1... | collective-permute-start | bytes 405512 | tf_op jit(solution)/shard_map/ppermute | solution.py:65
  30.1 0.5 collective-permute-start.7
  30.6 3.5 %collective-permute-done.4.refs_2_.refs_6_ = bf16[528,128]{1,0:T(8,128)(2,1)S(1)} collective-permute-done((bf16[528,128]{1,0:T(8,128)(2,1)S(1)}, bf16[528,128]{1,0:T(8,128)(2,1)S(1)}, u32[]{:S(2)}, u32[]{:S(2)}) %collective-permute-start.4) | collective-permute-done | bytes 135200 | tf_op jit(solution)/shard_map/ppermute | solution.py:65
  34.1 0.0 collective-permute-start.8
  34.1 0.0 collective-permute-start.14
  34.1 1.9 %collective-permute-done.5.refs_3_.refs_7_ = bf16[528,128]{1,0:T(8,128)(2,1)S(1)} collective-permute-done((bf16[528,128]{1,0:T(8,128)(2,1)S(1)}, bf16[528,128]{1,0:T(8,128)(2,1)S(1)}, u32[]{:S(2)}, u32[]{:S(2)}) %collective-permute-start.5) | collective-permute-done | bytes 135200 | tf_op jit(solution)/shard_map/ppermute | solution.py:65
  36.0 0.6 collective-permute-start.15
  36.6 1.4 %collective-permute-start.16 = (bf16[768,128]{1,0:T(8,128)(2,1)S(1)}, bf16[768,128]{1,0:T(8,128)(2,1)S(1)}, u32[]{:S(2)}, u32[]{:S(2)}) collective-permute-start(bf16[768,128]{1,0:T(8,128)(2,1)S(1)} %collective-permute-done.1.refs_0_.refs_12_), channel_id=1, source_target_pairs={{2,0},{3,1},{0,2},{1,3},{6,4},{7,5},{4,6},{5,7},{10,8},{11,9},{8,1... | collective-permute-start | bytes 589832 | tf_op jit(solution)/shard_map/ppermute | solution.py:65
  38.0 0.6 collective-permute-start.22
  38.6 0.0 collective-permute-done.8.refs_6_.refs_10_
  38.6 0.0 collective-permute-start.9
  38.6 1.4 %collective-permute-done.9.refs_7_.refs_11_ = bf16[528,128]{1,0:T(8,128)(2,1)S(1)} collective-permute-done((bf16[528,128]{1,0:T(8,128)(2,1)S(1)}, bf16[528,128]{1,0:T(8,128)(2,1)S(1)}, u32[]{:S(2)}, u32[]{:S(2)}) %collective-permute-start.9) | collective-permute-done | bytes 135200 | tf_op jit(solution)/shard_map/ppermute | solution.py:65
  40.0 1.3 %shard_map.102 = (bf16[144,128]{1,0:T(8,128)(2,1)S(1)}, bf16[144,128]{1,0:T(8,128)(2,1)S(1)}, bf16[144,128]{1,0:T(8,128)(2,1)S(1)}, bf16[144,128]{1,0:T(8,128)(2,1)S(1)}) custom-call(s32[3]{0:T(128)S(1)} %pad_add_fusion.place_ref, bf16[128,1024]{1,0:T(8,128)(2,1)S(1)} %bitcast.21, bf16[128,1024]{1,0:T(8,128)(2,1)S(1)} %bitcast.23, ...), custom_call_target="tpu_custom_call" | custom-call | tf_op jit(solution)/shard_map/pallas_call | solution.py:369
  41.3 0.1 collective-permute-start.10
  41.4 0.4 collective-permute-done.14.refs_1_.refs_13_
  41.8 1.4 %collective-permute-start.11 = (bf16[144,128]{1,0:T(8,128)(2,1)S(1)}, bf16[144,128]{1,0:T(8,128)(2,1)S(1)}, u32[]{:S(2)}, u32[]{:S(2)}) collective-permute-start(bf16[144,128]{1,0:T(8,128)(2,1)S(1)} %get-tuple-element.44), channel_id=1, source_target_pairs={{0,8},{4,12},{8,0},{12,4},{1,9},{5,13},{9,1},{13,5},{2,10},{6,14},... | collective-permute-start | bytes 110600 | tf_op jit(solution)/shard_map/ppermute | solution.py:76
  43.2 0.6 collective-permute-done.15.refs_10_.refs_22_
  43.8 2.0 %collective-permute-start.12 = (bf16[144,128]{1,0:T(8,128)(2,1)S(1)}, bf16[144,128]{1,0:T(8,128)(2,1)S(1)}, u32[]{:S(2)}, u32[]{:S(2)}) collective-permute-start(bf16[144,128]{1,0:T(8,128)(2,1)S(1)} %get-tuple-element.45), channel_id=1, source_target_pairs={{0,12},{4,8},{8,4},{12,0},{1,13},{5,9},{9,5},{13,1},{2,14},{6,10},... | collective-permute-start | bytes 110600 | tf_op jit(solution)/shard_map/ppermute | solution.py:76
  45.8 0.6 collective-permute-done.16.refs_2_.refs_14_
  46.3 0.0 collective-permute-start.18
  46.3 0.5 collective-permute-start.24
  46.8 0.1 collective-permute-start.20
  46.9 0.1 collective-permute-done.11
  47.0 2.8 %collective-permute-start.17 = (bf16[768,128]{1,0:T(8,128)(2,1)S(1)}, bf16[768,128]{1,0:T(8,128)(2,1)S(1)}, u32[]{:S(2)}, u32[]{:S(2)}) collective-permute-start(bf16[768,128]{1,0:T(8,128)(2,1)S(1)} %collective-permute-done.14.refs_1_.refs_13_), channel_id=1, source_target_pairs={{2,0},{3,1},{0,2},{1,3},{6,4},{7,5},{4,6},{5,7},{10,8},{11,9},{8,1... | collective-permute-start | bytes 589832 | tf_op jit(solution)/shard_map/ppermute | solution.py:65
  49.7 0.7 collective-permute-start.23
  50.4 0.1 collective-permute-start.13
  50.5 0.5 collective-permute-start.25
  51.0 0.8 collective-permute-done.13.refs_3_
  51.8 0.2 collective-permute-start.19
  51.9 0.4 collective-permute-start.26
  52.3 1.9 %collective-permute-done.17.refs_3_.refs_15_ = bf16[768,128]{1,0:T(8,128)(2,1)S(1)} collective-permute-done((bf16[768,128]{1,0:T(8,128)(2,1)S(1)}, bf16[768,128]{1,0:T(8,128)(2,1)S(1)}, u32[]{:S(2)}, u32[]{:S(2)}) %collective-permute-start.17) | collective-permute-done | bytes 196640 | tf_op jit(solution)/shard_map/ppermute | solution.py:65
  54.2 1.5 %collective-permute-done.23.refs_11_.refs_23_ = bf16[768,128]{1,0:T(8,128)(2,1)S(1)} collective-permute-done((bf16[768,128]{1,0:T(8,128)(2,1)S(1)}, bf16[768,128]{1,0:T(8,128)(2,1)S(1)}, u32[]{:S(2)}, u32[]{:S(2)}) %collective-permute-start.23) | collective-permute-done | bytes 196640 | tf_op jit(solution)/shard_map/ppermute | solution.py:65
  55.7 1.4 %collective-permute-done.27.refs_15_.refs_27_ = bf16[768,128]{1,0:T(8,128)(2,1)S(1)} collective-permute-done((bf16[768,128]{1,0:T(8,128)(2,1)S(1)}, bf16[768,128]{1,0:T(8,128)(2,1)S(1)}, u32[]{:S(2)}, u32[]{:S(2)}) %collective-permute-start.27) | collective-permute-done | bytes 196640 | tf_op jit(solution)/shard_map/ppermute | solution.py:65
  57.1 1.4 %shard_map.103 = (bf16[128,384]{1,0:T(8,128)(2,1)S(1)}, bf16[128,384]{1,0:T(8,128)(2,1)S(1)}, bf16[128,384]{1,0:T(8,128)(2,1)S(1)}, bf16[128,384]{1,0:T(8,128)(2,1)S(1)}) custom-call(s32[3]{0:T(128)S(1)} %pad_add_fusion.place_ref, bf16[128,1024]{1,0:T(8,128)(2,1)S(1)} %bitcast.22, bf16[768,128]{1,0:T(8,128)(2,1)S(1)} %collective-permute-done.1.refs_0_.refs_12_, ...), custom_call_target="tpu_custom_call" | custom-call | tf_op jit(solution)/shard_map/pallas_call | solution.py:369
  58.5 0.3 collective-permute-start.28
  58.8 1.9 %collective-permute-start.29 = (bf16[128,384]{1,0:T(8,128)(2,1)S(1)}, bf16[128,384]{1,0:T(8,128)(2,1)S(1)}, u32[]{:S(2)}, u32[]{:S(2)}) collective-permute-start(bf16[128,384]{1,0:T(8,128)(2,1)S(1)} %get-tuple-element.53), channel_id=1, source_target_pairs={{0,8},{4,12},{8,0},{12,4},{1,9},{5,13},{9,1},{13,5},{2,10},{6,14},... | collective-permute-start | bytes 294920 | tf_op jit(solution)/shard_map/ppermute | solution.py:76
  60.7 2.3 %collective-permute-start.30 = (bf16[128,384]{1,0:T(8,128)(2,1)S(1)}, bf16[128,384]{1,0:T(8,128)(2,1)S(1)}, u32[]{:S(2)}, u32[]{:S(2)}) collective-permute-start(bf16[128,384]{1,0:T(8,128)(2,1)S(1)} %get-tuple-element.54), channel_id=1, source_target_pairs={{0,12},{4,8},{8,4},{12,0},{1,13},{5,9},{9,5},{13,1},{2,14},{6,10},... | collective-permute-start | bytes 294920 | tf_op jit(solution)/shard_map/ppermute | solution.py:76
  63.0 1.6 %collective-permute-done.28 = bf16[128,384]{1,0:T(8,128)(2,1)S(1)} collective-permute-done((bf16[128,384]{1,0:T(8,128)(2,1)S(1)}, bf16[128,384]{1,0:T(8,128)(2,1)S(1)}, u32[]{:S(2)}, u32[]{:S(2)}) %collective-permute-start.28) | collective-permute-done | bytes 98336 | tf_op jit(solution)/shard_map/ppermute | solution.py:76
  64.6 5.1 %collective-permute-done.29 = bf16[128,384]{1,0:T(8,128)(2,1)S(1)} collective-permute-done((bf16[128,384]{1,0:T(8,128)(2,1)S(1)}, bf16[128,384]{1,0:T(8,128)(2,1)S(1)}, u32[]{:S(2)}, u32[]{:S(2)}) %collective-permute-start.29) | collective-permute-done | bytes 98336 | tf_op jit(solution)/shard_map/ppermute | solution.py:76
  69.6 0.1 convert_add_fusion.refs_0_
  69.7 0.1 collective-permute-start.31
  69.8 1.4 %collective-permute-done.31.refs_1_ = f32[128,384]{1,0:T(8,128)S(1)} collective-permute-done((f32[128,384]{1,0:T(8,128)S(1)}, f32[128,384]{1,0:T(8,128)S(1)}, u32[]{:S(2)}, u32[]{:S(2)}) %collective-permute-start.31) | collective-permute-done | bytes 196640 | tf_op jit(solution)/shard_map/ppermute | solution.py:65
  71.2 10.8 %shard_map.104 = (bf16[144,512]{1,0:T(8,128)(2,1)S(1)}, f32[64,256]{1,0:T(8,128)S(1)}, f32[64,256]{1,0:T(8,128)S(1)}, f32[64,256]{1,0:T(8,128)S(1)}, f32[64,256]{1,0:T(8,128)S(1)}) custom-call(s32[3]{0:T(128)S(1)} %pad_add_fusion.place_ref, f32[128,384]{1,0:T(8,128)S(1)} %convert_add_fusion.refs_0_, f32[128,384]{1,0:T(8,128)S(1)} %collective-permute-done.31.refs_1_, ...), custom_call_target="tpu_custom_call" | custom-call | tf_op jit(solution)/shard_map/pallas_call | solution.py:369
  82.1 1.8 %collective-permute-start.32 = (bf16[144,512]{1,0:T(8,128)(2,1)S(1)}, bf16[144,512]{1,0:T(8,128)(2,1)S(1)}, u32[]{:S(2)}, u32[]{:S(2)}) collective-permute-start(bf16[144,512]{1,0:T(8,128)(2,1)S(1)} %get-tuple-element.55.refs_0_), channel_id=1, source_target_pairs={{4,0},{0,4},{12,8},{8,12},{5,1},{1,5},{13,9},{9,13},{6,2},{2,6},{1... | collective-permute-start | bytes 442376 | tf_op jit(solution)/shard_map/ppermute | solution.py:65
  83.8 0.3 collective-permute-start.33
  84.1 2.4 %collective-permute-start.34 = (bf16[144,512]{1,0:T(8,128)(2,1)S(1)}, bf16[144,512]{1,0:T(8,128)(2,1)S(1)}, u32[]{:S(2)}, u32[]{:S(2)}) collective-permute-start(bf16[144,512]{1,0:T(8,128)(2,1)S(1)} %get-tuple-element.55.refs_0_), channel_id=1, source_target_pairs={{12,0},{8,4},{4,8},{0,12},{13,1},{9,5},{5,9},{1,13},{14,2},{10,6},... | collective-permute-start | bytes 442376 | tf_op jit(solution)/shard_map/ppermute | solution.py:65
  86.5 3.5 %collective-permute-done.32.refs_1_ = bf16[144,512]{1,0:T(8,128)(2,1)S(1)} collective-permute-done((bf16[144,512]{1,0:T(8,128)(2,1)S(1)}, bf16[144,512]{1,0:T(8,128)(2,1)S(1)}, u32[]{:S(2)}, u32[]{:S(2)}) %collective-permute-start.32) | collective-permute-done | bytes 147488 | tf_op jit(solution)/shard_map/ppermute | solution.py:65
  90.0 1.5 %collective-permute-start.35 = (f32[64,256]{1,0:T(8,128)S(1)}, f32[64,256]{1,0:T(8,128)S(1)}, u32[]{:S(2)}, u32[]{:S(2)}) collective-permute-start(f32[64,256]{1,0:T(8,128)S(1)} %get-tuple-element.63), channel_id=1, source_target_pairs={{0,1},{1,0},{2,3},{3,2},{4,5},{5,4},{6,7},{7,6},{8,9},{9,8},{10,11... | collective-permute-start | bytes 196616 | tf_op jit(solution)/shard_map/ppermute | solution.py:76
  91.5 0.7 collective-permute-start.36
  92.2 1.4 %collective-permute-start.37 = (f32[64,256]{1,0:T(8,128)S(1)}, f32[64,256]{1,0:T(8,128)S(1)}, u32[]{:S(2)}, u32[]{:S(2)}) collective-permute-start(f32[64,256]{1,0:T(8,128)S(1)} %get-tuple-element.65), channel_id=1, source_target_pairs={{0,3},{1,2},{2,1},{3,0},{4,7},{5,6},{6,5},{7,4},{8,11},{9,10},{10,... | collective-permute-start | bytes 196616 | tf_op jit(solution)/shard_map/ppermute | solution.py:76
  93.5 4.2 %collective-permute-done.33.refs_2_ = bf16[144,512]{1,0:T(8,128)(2,1)S(1)} collective-permute-done((bf16[144,512]{1,0:T(8,128)(2,1)S(1)}, bf16[144,512]{1,0:T(8,128)(2,1)S(1)}, u32[]{:S(2)}, u32[]{:S(2)}) %collective-permute-start.33) | collective-permute-done | bytes 147488 | tf_op jit(solution)/shard_map/ppermute | solution.py:65
  97.8 3.1 %shard_map.105 = (bf16[128,1024]{1,0:T(8,128)(2,1)}, bf16[128,1024]{1,0:T(8,128)(2,1)}) custom-call(s32[3]{0:T(128)S(1)} %pad_add_fusion.place_ref, bf16[144,512]{1,0:T(8,128)(2,1)S(1)} %get-tuple-element.55.refs_0_, bf16[144,512]{1,0:T(8,128)(2,1)S(1)} %collective-permute-done.32.refs_1_, bf16[144,512]{1,0:T(8,128)(2,1)S(1)} %collective-permute-done.33.refs_2_, ...), custom_call_target="tpu_custom_call" | custom-call | tf_op jit(solution)/shard_map/pallas_call | solution.py:369
  100.9 0.6 slice_bitcast_fusion
  (37 shorter events, 0.1 us)
Async XLA Ops:
  0.6 1.2 %copy-start = (bf16[4096,1]{0,1:T(2,128)(2,1)S(1)}, bf16[4096,1]{0,1:T(2,128)(2,1)}, u32[]{:S(2)}) copy-start(bf16[4096,1]{0,1:T(2,128)(2,1)} %param.9) | copy-start | bytes 24580
  0.7 1.2 %copy-start.5 = (bf16[512,128]{1,0:T(8,128)(2,1)S(1)}, bf16[512,128]{1,0:T(8,128)(2,1)}, u32[]{:S(2)}) copy-start(bf16[512,128]{1,0:T(8,128)(2,1)} %param.10) | copy-start | bytes 393220
  0.7 39.3 %copy-start.2 = (bf16[1,128,1024]{2,1,0:T(8,128)(2,1)S(1)}, bf16[1,128,1024]{2,1,0:T(8,128)(2,1)}, u32[]{:S(2)}) copy-start(bf16[1,128,1024]{2,1,0:T(8,128)(2,1)} %param.13) | copy-start | bytes 786436
  1.8 38.2 %copy-start.1 = (bf16[1,128,1024]{2,1,0:T(8,128)(2,1)S(1)}, bf16[1,128,1024]{2,1,0:T(8,128)(2,1)}, u32[]{:S(2)}) copy-start(bf16[1,128,1024]{2,1,0:T(8,128)(2,1)} %param.7) | copy-start | bytes 786436
  2.0 2.1 %collective-permute-start.1 = (bf16[768,128]{1,0:T(8,128)(2,1)S(1)}, bf16[768,128]{1,0:T(8,128)(2,1)S(1)}, u32[]{:S(2)}, u32[]{:S(2)}) collective-permute-start(bf16[768,128]{1,0:T(8,128)(2,1)S(1)} %bitcast.28), channel_id=1, source_target_pairs={{0,0},{1,1},{2,4},{3,5},{4,2},{5,3},{6,6},{7,7},{8,16},{9,17},{10,... | collective-permute-start | bytes 589832 | tf_op jit(solution)/shard_map/ppermute | solution.py:400
  2.6 1.4 %collective-permute-start.2 = (bf16[768,128]{1,0:T(8,128)(2,1)S(1)}, bf16[768,128]{1,0:T(8,128)(2,1)S(1)}, u32[]{:S(2)}, u32[]{:S(2)}) collective-permute-start(bf16[768,128]{1,0:T(8,128)(2,1)S(1)} %bitcast.27), channel_id=1, source_target_pairs={{0,0},{1,1},{2,4},{3,5},{4,2},{5,3},{6,6},{7,7},{8,16},{9,17},{10,... | collective-permute-start | bytes 589832 | tf_op jit(solution)/shard_map/ppermute | solution.py:400
  3.3 0.7 collective-permute-start
  4.0 26.0 %collective-permute-start.3 = (bf16[528,128]{1,0:T(8,128)(2,1)S(1)}, bf16[528,128]{1,0:T(8,128)(2,1)S(1)}, u32[]{:S(2)}, u32[]{:S(2)}) collective-permute-start(bf16[528,128]{1,0:T(8,128)(2,1)S(1)} %collective-permute-done.refs_0_.refs_4_), channel_id=1, source_target_pairs={{1,0},{0,1},{3,2},{2,3},{5,4},{4,5},{7,6},{6,7},{9,8},{8,9},{11,10... | collective-permute-start | bytes 405512 | tf_op jit(solution)/shard_map/ppermute | solution.py:65
  7.0 27.0 %collective-permute-start.4 = (bf16[528,128]{1,0:T(8,128)(2,1)S(1)}, bf16[528,128]{1,0:T(8,128)(2,1)S(1)}, u32[]{:S(2)}, u32[]{:S(2)}) collective-permute-start(bf16[528,128]{1,0:T(8,128)(2,1)S(1)} %collective-permute-done.refs_0_.refs_4_), channel_id=1, source_target_pairs={{2,0},{3,1},{0,2},{1,3},{6,4},{7,5},{4,6},{5,7},{10,8},{11,9},{8,1... | collective-permute-start | bytes 405512 | tf_op jit(solution)/shard_map/ppermute | solution.py:65
  30.1 5.9 %collective-permute-start.5 = (bf16[528,128]{1,0:T(8,128)(2,1)S(1)}, bf16[528,128]{1,0:T(8,128)(2,1)S(1)}, u32[]{:S(2)}, u32[]{:S(2)}) collective-permute-start(bf16[528,128]{1,0:T(8,128)(2,1)S(1)} %collective-permute-done.refs_0_.refs_4_), channel_id=1, source_target_pairs={{3,0},{2,1},{1,2},{0,3},{7,4},{6,5},{5,6},{4,7},{11,8},{10,9},{9,1... | collective-permute-start | bytes 405512 | tf_op jit(solution)/shard_map/ppermute | solution.py:65
  30.1 6.5 %collective-permute-start.6 = (bf16[528,128]{1,0:T(8,128)(2,1)S(1)}, bf16[528,128]{1,0:T(8,128)(2,1)S(1)}, u32[]{:S(2)}, u32[]{:S(2)}) collective-permute-start(bf16[528,128]{1,0:T(8,128)(2,1)S(1)} %collective-permute-done.refs_0_.refs_4_), channel_id=1, source_target_pairs={{16,0},{0,16},{17,1},{1,17},{18,2},{2,18},{19,3},{3,19},{20,4},{4,... | collective-permute-start | bytes 405512 | tf_op jit(solution)/shard_map/ppermute | solution.py:65
  30.1 7.9 %collective-permute-start.7 = (bf16[528,128]{1,0:T(8,128)(2,1)S(1)}, bf16[528,128]{1,0:T(8,128)(2,1)S(1)}, u32[]{:S(2)}, u32[]{:S(2)}) collective-permute-start(bf16[528,128]{1,0:T(8,128)(2,1)S(1)} %collective-permute-done.3.refs_1_.refs_5_), channel_id=1, source_target_pairs={{16,0},{0,16},{17,1},{1,17},{18,2},{2,18},{19,3},{3,19},{20,4},{4,... | collective-permute-start | bytes 405512 | tf_op jit(solution)/shard_map/ppermute | solution.py:65
  34.1 4.6 %collective-permute-start.8 = (bf16[528,128]{1,0:T(8,128)(2,1)S(1)}, bf16[528,128]{1,0:T(8,128)(2,1)S(1)}, u32[]{:S(2)}, u32[]{:S(2)}) collective-permute-start(bf16[528,128]{1,0:T(8,128)(2,1)S(1)} %collective-permute-done.4.refs_2_.refs_6_), channel_id=1, source_target_pairs={{16,0},{0,16},{17,1},{1,17},{18,2},{2,18},{19,3},{3,19},{20,4},{4,... | collective-permute-start | bytes 405512 | tf_op jit(solution)/shard_map/ppermute | solution.py:65
  34.1 7.7 %collective-permute-start.14 = (bf16[768,128]{1,0:T(8,128)(2,1)S(1)}, bf16[768,128]{1,0:T(8,128)(2,1)S(1)}, u32[]{:S(2)}, u32[]{:S(2)}) collective-permute-start(bf16[768,128]{1,0:T(8,128)(2,1)S(1)} %collective-permute-done.1.refs_0_.refs_12_), channel_id=1, source_target_pairs={{1,0},{0,1},{3,2},{2,3},{5,4},{4,5},{7,6},{6,7},{9,8},{8,9},{11,10... | collective-permute-start | bytes 589832 | tf_op jit(solution)/shard_map/ppermute | solution.py:65
  36.0 7.8 %collective-permute-start.15 = (bf16[768,128]{1,0:T(8,128)(2,1)S(1)}, bf16[768,128]{1,0:T(8,128)(2,1)S(1)}, u32[]{:S(2)}, u32[]{:S(2)}) collective-permute-start(bf16[768,128]{1,0:T(8,128)(2,1)S(1)} %collective-permute-done.2.refs_8_.refs_20_), channel_id=1, source_target_pairs={{2,0},{3,1},{0,2},{1,3},{6,4},{7,5},{4,6},{5,7},{10,8},{11,9},{8,1... | collective-permute-start | bytes 589832 | tf_op jit(solution)/shard_map/ppermute | solution.py:65
  36.6 9.7 %collective-permute-start.16 = (bf16[768,128]{1,0:T(8,128)(2,1)S(1)}, bf16[768,128]{1,0:T(8,128)(2,1)S(1)}, u32[]{:S(2)}, u32[]{:S(2)}) collective-permute-start(bf16[768,128]{1,0:T(8,128)(2,1)S(1)} %collective-permute-done.1.refs_0_.refs_12_), channel_id=1, source_target_pairs={{2,0},{3,1},{0,2},{1,3},{6,4},{7,5},{4,6},{5,7},{10,8},{11,9},{8,1... | collective-permute-start | bytes 589832 | tf_op jit(solution)/shard_map/ppermute | solution.py:65
  38.0 8.3 %collective-permute-start.22 = (bf16[768,128]{1,0:T(8,128)(2,1)S(1)}, bf16[768,128]{1,0:T(8,128)(2,1)S(1)}, u32[]{:S(2)}, u32[]{:S(2)}) collective-permute-start(bf16[768,128]{1,0:T(8,128)(2,1)S(1)} %collective-permute-done.2.refs_8_.refs_20_), channel_id=1, source_target_pairs={{1,0},{0,1},{3,2},{2,3},{5,4},{4,5},{7,6},{6,7},{9,8},{8,9},{11,10... | collective-permute-start | bytes 589832 | tf_op jit(solution)/shard_map/ppermute | solution.py:65
  38.6 1.4 %collective-permute-start.9 = (bf16[528,128]{1,0:T(8,128)(2,1)S(1)}, bf16[528,128]{1,0:T(8,128)(2,1)S(1)}, u32[]{:S(2)}, u32[]{:S(2)}) collective-permute-start(bf16[528,128]{1,0:T(8,128)(2,1)S(1)} %collective-permute-done.5.refs_3_.refs_7_), channel_id=1, source_target_pairs={{16,0},{0,16},{17,1},{1,17},{18,2},{2,18},{19,3},{3,19},{20,4},{4,... | collective-permute-start | bytes 405512 | tf_op jit(solution)/shard_map/ppermute | solution.py:65
  41.3 5.5 %collective-permute-start.10 = (bf16[144,128]{1,0:T(8,128)(2,1)S(1)}, bf16[144,128]{1,0:T(8,128)(2,1)S(1)}, u32[]{:S(2)}, u32[]{:S(2)}) collective-permute-start(bf16[144,128]{1,0:T(8,128)(2,1)S(1)} %get-tuple-element.43), channel_id=1, source_target_pairs={{0,4},{4,0},{8,12},{12,8},{1,5},{5,1},{9,13},{13,9},{2,6},{6,2},{1... | collective-permute-start | bytes 110600 | tf_op jit(solution)/shard_map/ppermute | solution.py:76
  41.8 5.2 %collective-permute-start.11 = (bf16[144,128]{1,0:T(8,128)(2,1)S(1)}, bf16[144,128]{1,0:T(8,128)(2,1)S(1)}, u32[]{:S(2)}, u32[]{:S(2)}) collective-permute-start(bf16[144,128]{1,0:T(8,128)(2,1)S(1)} %get-tuple-element.44), channel_id=1, source_target_pairs={{0,8},{4,12},{8,0},{12,4},{1,9},{5,13},{9,1},{13,5},{2,10},{6,14},... | collective-permute-start | bytes 110600 | tf_op jit(solution)/shard_map/ppermute | solution.py:76
  43.8 5.9 %collective-permute-start.12 = (bf16[144,128]{1,0:T(8,128)(2,1)S(1)}, bf16[144,128]{1,0:T(8,128)(2,1)S(1)}, u32[]{:S(2)}, u32[]{:S(2)}) collective-permute-start(bf16[144,128]{1,0:T(8,128)(2,1)S(1)} %get-tuple-element.45), channel_id=1, source_target_pairs={{0,12},{4,8},{8,4},{12,0},{1,13},{5,9},{9,5},{13,1},{2,14},{6,10},... | collective-permute-start | bytes 110600 | tf_op jit(solution)/shard_map/ppermute | solution.py:76
  46.3 4.1 %collective-permute-start.18 = (bf16[768,128]{1,0:T(8,128)(2,1)S(1)}, bf16[768,128]{1,0:T(8,128)(2,1)S(1)}, u32[]{:S(2)}, u32[]{:S(2)}) collective-permute-start(bf16[768,128]{1,0:T(8,128)(2,1)S(1)} %collective-permute-done.1.refs_0_.refs_12_), channel_id=1, source_target_pairs={{16,0},{0,16},{17,1},{1,17},{18,2},{2,18},{19,3},{3,19},{20,4},{4,... | collective-permute-start | bytes 589832 | tf_op jit(solution)/shard_map/ppermute | solution.py:65
  46.3 4.2 %collective-permute-start.24 = (bf16[768,128]{1,0:T(8,128)(2,1)S(1)}, bf16[768,128]{1,0:T(8,128)(2,1)S(1)}, u32[]{:S(2)}, u32[]{:S(2)}) collective-permute-start(bf16[768,128]{1,0:T(8,128)(2,1)S(1)} %collective-permute-done.2.refs_8_.refs_20_), channel_id=1, source_target_pairs={{16,0},{0,16},{17,1},{1,17},{18,2},{2,18},{19,3},{3,19},{20,4},{4,... | collective-permute-start | bytes 589832 | tf_op jit(solution)/shard_map/ppermute | solution.py:65
  46.8 5.1 %collective-permute-start.20 = (bf16[768,128]{1,0:T(8,128)(2,1)S(1)}, bf16[768,128]{1,0:T(8,128)(2,1)S(1)}, u32[]{:S(2)}, u32[]{:S(2)}) collective-permute-start(bf16[768,128]{1,0:T(8,128)(2,1)S(1)} %collective-permute-done.16.refs_2_.refs_14_), channel_id=1, source_target_pairs={{16,0},{0,16},{17,1},{1,17},{18,2},{2,18},{19,3},{3,19},{20,4},{4,... | collective-permute-start | bytes 589832 | tf_op jit(solution)/shard_map/ppermute | solution.py:65
  47.0 7.2 %collective-permute-start.17 = (bf16[768,128]{1,0:T(8,128)(2,1)S(1)}, bf16[768,128]{1,0:T(8,128)(2,1)S(1)}, u32[]{:S(2)}, u32[]{:S(2)}) collective-permute-start(bf16[768,128]{1,0:T(8,128)(2,1)S(1)} %collective-permute-done.14.refs_1_.refs_13_), channel_id=1, source_target_pairs={{2,0},{3,1},{0,2},{1,3},{6,4},{7,5},{4,6},{5,7},{10,8},{11,9},{8,1... | collective-permute-start | bytes 589832 | tf_op jit(solution)/shard_map/ppermute | solution.py:65
  49.7 5.9 %collective-permute-start.23 = (bf16[768,128]{1,0:T(8,128)(2,1)S(1)}, bf16[768,128]{1,0:T(8,128)(2,1)S(1)}, u32[]{:S(2)}, u32[]{:S(2)}) collective-permute-start(bf16[768,128]{1,0:T(8,128)(2,1)S(1)} %collective-permute-done.15.refs_10_.refs_22_), channel_id=1, source_target_pairs={{1,0},{0,1},{3,2},{2,3},{5,4},{4,5},{7,6},{6,7},{9,8},{8,9},{11,10... | collective-permute-start | bytes 589832 | tf_op jit(solution)/shard_map/ppermute | solution.py:65
  50.4 1.3 %collective-permute-start.13 = (f32[144,128]{1,0:T(8,128)S(1)}, f32[144,128]{1,0:T(8,128)S(1)}, u32[]{:S(2)}, u32[]{:S(2)}) collective-permute-start(f32[144,128]{1,0:T(8,128)S(1)} %convert_add_fusion.1.refs_2_), channel_id=1, source_target_pairs={{16,0},{0,16},{17,1},{1,17},{18,2},{2,18},{19,3},{3,19},{20,4},{4,... | collective-permute-start | bytes 221192 | tf_op jit(solution)/shard_map/ppermute | solution.py:65
  50.5 5.1 %collective-permute-start.25 = (bf16[768,128]{1,0:T(8,128)(2,1)S(1)}, bf16[768,128]{1,0:T(8,128)(2,1)S(1)}, u32[]{:S(2)}, u32[]{:S(2)}) collective-permute-start(bf16[768,128]{1,0:T(8,128)(2,1)S(1)} %collective-permute-done.22.refs_9_.refs_21_), channel_id=1, source_target_pairs={{16,0},{0,16},{17,1},{1,17},{18,2},{2,18},{19,3},{3,19},{20,4},{4,... | collective-permute-start | bytes 589832 | tf_op jit(solution)/shard_map/ppermute | solution.py:65
  51.8 3.9 %collective-permute-start.19 = (bf16[768,128]{1,0:T(8,128)(2,1)S(1)}, bf16[768,128]{1,0:T(8,128)(2,1)S(1)}, u32[]{:S(2)}, u32[]{:S(2)}) collective-permute-start(bf16[768,128]{1,0:T(8,128)(2,1)S(1)} %collective-permute-done.14.refs_1_.refs_13_), channel_id=1, source_target_pairs={{16,0},{0,16},{17,1},{1,17},{18,2},{2,18},{19,3},{3,19},{20,4},{4,... | collective-permute-start | bytes 589832 | tf_op jit(solution)/shard_map/ppermute | solution.py:65
  51.9 3.7 %collective-permute-start.26 = (bf16[768,128]{1,0:T(8,128)(2,1)S(1)}, bf16[768,128]{1,0:T(8,128)(2,1)S(1)}, u32[]{:S(2)}, u32[]{:S(2)}) collective-permute-start(bf16[768,128]{1,0:T(8,128)(2,1)S(1)} %collective-permute-done.15.refs_10_.refs_22_), channel_id=1, source_target_pairs={{16,0},{0,16},{17,1},{1,17},{18,2},{2,18},{19,3},{3,19},{20,4},{4,... | collective-permute-start | bytes 589832 | tf_op jit(solution)/shard_map/ppermute | solution.py:65
  54.2 1.5 %collective-permute-start.21 = (bf16[768,128]{1,0:T(8,128)(2,1)S(1)}, bf16[768,128]{1,0:T(8,128)(2,1)S(1)}, u32[]{:S(2)}, u32[]{:S(2)}) collective-permute-start(bf16[768,128]{1,0:T(8,128)(2,1)S(1)} %collective-permute-done.17.refs_3_.refs_15_), channel_id=1, source_target_pairs={{16,0},{0,16},{17,1},{1,17},{18,2},{2,18},{19,3},{3,19},{20,4},{4,... | collective-permute-start | bytes 589832 | tf_op jit(solution)/shard_map/ppermute | solution.py:65
  55.6 1.4 %collective-permute-start.27 = (bf16[768,128]{1,0:T(8,128)(2,1)S(1)}, bf16[768,128]{1,0:T(8,128)(2,1)S(1)}, u32[]{:S(2)}, u32[]{:S(2)}) collective-permute-start(bf16[768,128]{1,0:T(8,128)(2,1)S(1)} %collective-permute-done.23.refs_11_.refs_23_), channel_id=1, source_target_pairs={{16,0},{0,16},{17,1},{1,17},{18,2},{2,18},{19,3},{3,19},{20,4},{4,... | collective-permute-start | bytes 589832 | tf_op jit(solution)/shard_map/ppermute | solution.py:65
  58.5 6.0 %collective-permute-start.28 = (bf16[128,384]{1,0:T(8,128)(2,1)S(1)}, bf16[128,384]{1,0:T(8,128)(2,1)S(1)}, u32[]{:S(2)}, u32[]{:S(2)}) collective-permute-start(bf16[128,384]{1,0:T(8,128)(2,1)S(1)} %get-tuple-element.52), channel_id=1, source_target_pairs={{0,4},{4,0},{8,12},{12,8},{1,5},{5,1},{9,13},{13,9},{2,6},{6,2},{1... | collective-permute-start | bytes 294920 | tf_op jit(solution)/shard_map/ppermute | solution.py:76
  58.8 10.8 %collective-permute-start.29 = (bf16[128,384]{1,0:T(8,128)(2,1)S(1)}, bf16[128,384]{1,0:T(8,128)(2,1)S(1)}, u32[]{:S(2)}, u32[]{:S(2)}) collective-permute-start(bf16[128,384]{1,0:T(8,128)(2,1)S(1)} %get-tuple-element.53), channel_id=1, source_target_pairs={{0,8},{4,12},{8,0},{12,4},{1,9},{5,13},{9,1},{13,5},{2,10},{6,14},... | collective-permute-start | bytes 294920 | tf_op jit(solution)/shard_map/ppermute | solution.py:76
  60.7 8.9 %collective-permute-start.30 = (bf16[128,384]{1,0:T(8,128)(2,1)S(1)}, bf16[128,384]{1,0:T(8,128)(2,1)S(1)}, u32[]{:S(2)}, u32[]{:S(2)}) collective-permute-start(bf16[128,384]{1,0:T(8,128)(2,1)S(1)} %get-tuple-element.54), channel_id=1, source_target_pairs={{0,12},{4,8},{8,4},{12,0},{1,13},{5,9},{9,5},{13,1},{2,14},{6,10},... | collective-permute-start | bytes 294920 | tf_op jit(solution)/shard_map/ppermute | solution.py:76
  69.6 1.6 %copy-start.3 = (f32[1,128,512]{2,1,0:T(8,128)S(1)}, f32[1,128,512]{2,1,0:T(8,128)}, u32[]{:S(2)}) copy-start(f32[1,128,512]{2,1,0:T(8,128)} %param.11) | copy-start | bytes 786436
  69.6 1.6 %copy-start.4 = (f32[1,512,128]{2,1,0:T(8,128)S(1)}, f32[1,512,128]{2,1,0:T(8,128)}, u32[]{:S(2)}) copy-start(f32[1,512,128]{2,1,0:T(8,128)} %param.12) | copy-start | bytes 786436
  69.7 1.5 %collective-permute-start.31 = (f32[128,384]{1,0:T(8,128)S(1)}, f32[128,384]{1,0:T(8,128)S(1)}, u32[]{:S(2)}, u32[]{:S(2)}) collective-permute-start(f32[128,384]{1,0:T(8,128)S(1)} %convert_add_fusion.refs_0_), channel_id=1, source_target_pairs={{16,0},{0,16},{17,1},{1,17},{18,2},{2,18},{19,3},{3,19},{20,4},{4,... | collective-permute-start | bytes 589832 | tf_op jit(solution)/shard_map/ppermute | solution.py:65
  82.1 8.0 %collective-permute-start.32 = (bf16[144,512]{1,0:T(8,128)(2,1)S(1)}, bf16[144,512]{1,0:T(8,128)(2,1)S(1)}, u32[]{:S(2)}, u32[]{:S(2)}) collective-permute-start(bf16[144,512]{1,0:T(8,128)(2,1)S(1)} %get-tuple-element.55.refs_0_), channel_id=1, source_target_pairs={{4,0},{0,4},{12,8},{8,12},{5,1},{1,5},{13,9},{9,13},{6,2},{2,6},{1... | collective-permute-start | bytes 442376 | tf_op jit(solution)/shard_map/ppermute | solution.py:65
  83.8 13.9 %collective-permute-start.33 = (bf16[144,512]{1,0:T(8,128)(2,1)S(1)}, bf16[144,512]{1,0:T(8,128)(2,1)S(1)}, u32[]{:S(2)}, u32[]{:S(2)}) collective-permute-start(bf16[144,512]{1,0:T(8,128)(2,1)S(1)} %get-tuple-element.55.refs_0_), channel_id=1, source_target_pairs={{8,0},{12,4},{0,8},{4,12},{9,1},{13,5},{1,9},{5,13},{10,2},{14,6},... | collective-permute-start | bytes 442376 | tf_op jit(solution)/shard_map/ppermute | solution.py:65
  84.1 13.7 %collective-permute-start.34 = (bf16[144,512]{1,0:T(8,128)(2,1)S(1)}, bf16[144,512]{1,0:T(8,128)(2,1)S(1)}, u32[]{:S(2)}, u32[]{:S(2)}) collective-permute-start(bf16[144,512]{1,0:T(8,128)(2,1)S(1)} %get-tuple-element.55.refs_0_), channel_id=1, source_target_pairs={{12,0},{8,4},{4,8},{0,12},{13,1},{9,5},{5,9},{1,13},{14,2},{10,6},... | collective-permute-start | bytes 442376 | tf_op jit(solution)/shard_map/ppermute | solution.py:65
  90.0 10.9 %collective-permute-start.35 = (f32[64,256]{1,0:T(8,128)S(1)}, f32[64,256]{1,0:T(8,128)S(1)}, u32[]{:S(2)}, u32[]{:S(2)}) collective-permute-start(f32[64,256]{1,0:T(8,128)S(1)} %get-tuple-element.63), channel_id=1, source_target_pairs={{0,1},{1,0},{2,3},{3,2},{4,5},{5,4},{6,7},{7,6},{8,9},{9,8},{10,11... | collective-permute-start | bytes 196616 | tf_op jit(solution)/shard_map/ppermute | solution.py:76
  91.5 9.4 %collective-permute-start.36 = (f32[64,256]{1,0:T(8,128)S(1)}, f32[64,256]{1,0:T(8,128)S(1)}, u32[]{:S(2)}, u32[]{:S(2)}) collective-permute-start(f32[64,256]{1,0:T(8,128)S(1)} %get-tuple-element.64), channel_id=1, source_target_pairs={{0,2},{1,3},{2,0},{3,1},{4,6},{5,7},{6,4},{7,5},{8,10},{9,11},{10,... | collective-permute-start | bytes 196616 | tf_op jit(solution)/shard_map/ppermute | solution.py:76
  92.2 8.7 %collective-permute-start.37 = (f32[64,256]{1,0:T(8,128)S(1)}, f32[64,256]{1,0:T(8,128)S(1)}, u32[]{:S(2)}, u32[]{:S(2)}) collective-permute-start(f32[64,256]{1,0:T(8,128)S(1)} %get-tuple-element.65), channel_id=1, source_target_pairs={{0,3},{1,2},{2,1},{3,0},{4,7},{5,6},{6,5},{7,4},{8,11},{9,10},{10,... | collective-permute-start | bytes 196616 | tf_op jit(solution)/shard_map/ppermute | solution.py:76

commit v5 on v4

--- a/solution.py
+++ b/solution.py
@@ -416,8 +416,11 @@
     first_w, second_w, outer_w = swapped(first), swapped(second), swapped(outer)
     outer_w, first_w, second_w = lax.optimization_barrier((outer_w, first_w, second_w))
     first_near = [first_w, hop(first_w, "dp", 1), hop(first_w, "dp", 2)]
+    second_near = [second_w, hop(second_w, "dp", 1), hop(second_w, "dp", 2)]
+    outer_w, first_near[1], second_near[2] = lax.optimization_barrier(
+        (outer_w, first_near[1], second_near[2])
+    )
     outer_near = peers_of(outer_w, "dp")
-    second_near = [second_w, hop(second_w, "dp", 1), hop(second_w, "dp", 2)]
     outer_ws = over_seq(outer_near)
     def summed(arrays):
         return functools.reduce(lambda a, b: a + b, [a.astype(F32) for a in arrays])
@@ -431,16 +434,13 @@
     )
     outer_all = peers_of(summed(sent_to(outer_part, "head")), "seq")
     if dps == 4:
-        first_near[1], second_near[2], unused = lax.optimization_barrier(
-            (first_near[1], second_near[2], outer_part[0])
-        )
         first_near.append(hop(first_near[1], "dp", 2))
         second_near.append(hop(second_near[2], "dp", 1))
     else:
         first_near += [hop(first_w, "dp", j) for j in range(3, dps)]
         second_near += [hop(second_w, "dp", j) for j in range(3, dps)]
     inner_ws = over_seq(first_near) + over_seq(second_near)
-    later_place, unused = lax.optimization_barrier((place, outer_all[-1]))
+    later_place, unused = lax.optimization_barrier((place, outer_part[0]))
     inner_part = call(
         functools.partial(inner_projection_kernel, *sizes),
         (jax.ShapeDtypeStruct((rows, 3 * hd), BF16),) * heads,

time: 102 us -> 100 us (0.980)
  waiting for transfers between devices: 29.8 us -> 24.4 us
  starting transfers between devices: 52.2 us -> 55.8 us
    ppermute x26, waiting for transfers between devices: 23 us -> 17.4 us  [hop(): lax.ppermute(array, axis, [(mate(i, step, count), i) for i in range(count)])]
    ppermute x9, starting transfers between devices: 11.4 us -> 13.2 us  [sent_to(): lax.ppermute(arrays[j], axis, [(i, mate(i, j, count)) for i in range(coun...]
    ppermute x26, starting transfers between devices: 38.8 us -> 40.5 us  [hop(): lax.ppermute(array, axis, [(mate(i, step, count), i) for i in range(count)])]
  transfers between devices with their start and end apart: 38 -> 38, of which waited for: 16 -> 11; matrix products, arithmetic and copies ran while one was open for 0% -> 0% of each run, Pallas kernels for 4% -> 4%
where the time goes in v5:
time: 100 us; the launch traced here: 99.7 us
  starting transfers between devices  55.8 us (56%)
  waiting for transfers between devices  24.4 us (24%)
  Pallas kernels  16.7 us (17%)
  local copies, waits for them, and re-layouts  1.77 us (2%)
    ppermute x26, starting transfers between devices, hop(): lax.ppermute(array, axis, [(mate(i, step, count), i) for i in range(count)])  40.5 us
    ppermute x26, waiting for transfers between devices, hop(): lax.ppermute(array, axis, [(mate(i, step, count), i) for i in range(count)])  17.4 us
    pallas_call x4, Pallas kernels, call(): pl.pallas_call(kernel, out_shape=outs, in_specs=[SMEM] + [VMEM] * (len(op...  16.7 us
    ppermute x9, starting transfers between devices, sent_to(): lax.ppermute(arrays[j], axis, [(i, mate(i, j, count)) for i in range(coun...  13.2 us
    ppermute x9, waiting for transfers between devices, sent_to(): lax.ppermute(arrays[j], axis, [(i, mate(i, j, count)) for i in range(coun...  6.94 us
    ppermute x3, starting transfers between devices, swapped(): return lax.ppermute(array, ('seq', 'head', 'dp'), pairs)  2.02 us
  transfers between devices with their start and end apart: 38, of which 11 were waited for; matrix products, arithmetic and copies ran while one was open for 0% of the time, Pallas kernels for 4%

profile of v5, /device:TPU:0, one launch (start us, length us, event | category | flops | bytes accessed | tf_op | source)
XLA Modules:
  0.0 99.7 jit_solution(14621154179010493456)
XLA Ops:
  0.6 0.0 copy-start
  0.7 0.1 pad_add_fusion.place_ref
  0.7 1.1 %fusion.2 = (bf16[3,256,128]{2,1,0:T(8,128)(2,1)S(1)}, bf16[3,256,128]{2,1,0:T(8,128)(2,1)S(1)}) fusion(bf16[3,512,128]{2,1,0:T(8,128)(2,1)} %bitcast.26), kind=kLoop, calls=%fused_computation.10 | loop fusion | bytes 786432 | tf_op jit(solution)/shard_map/slice | solution.py:412
  1.8 0.0 copy-start.1
  1.9 0.1 reduce
  2.0 0.7 collective-permute-start.1
  2.6 0.7 collective-permute-start.2
  3.3 0.7 collective-permute-start
  4.0 0.0 collective-permute-done.1.refs_0_.refs_12_
  4.0 0.0 collective-permute-done.2.refs_8_.refs_20_
  4.0 3.0 %collective-permute-start.3 = (bf16[768,128]{1,0:T(8,128)(2,1)S(1)}, bf16[768,128]{1,0:T(8,128)(2,1)S(1)}, u32[]{:S(2)}, u32[]{:S(2)}) collective-permute-start(bf16[768,128]{1,0:T(8,128)(2,1)S(1)} %collective-permute-done.1.refs_0_.refs_12_), channel_id=1, source_target_pairs={{1,0},{0,1},{3,2},{2,3},{5,4},{4,5},{7,6},{6,7},{9,8},{8,9},{11,10... | collective-permute-start | bytes 589832 | tf_op jit(solution)/shard_map/ppermute | solution.py:65
  7.0 22.5 %collective-permute-start.4 = (bf16[768,128]{1,0:T(8,128)(2,1)S(1)}, bf16[768,128]{1,0:T(8,128)(2,1)S(1)}, u32[]{:S(2)}, u32[]{:S(2)}) collective-permute-start(bf16[768,128]{1,0:T(8,128)(2,1)S(1)} %collective-permute-done.2.refs_8_.refs_20_), channel_id=1, source_target_pairs={{2,0},{3,1},{0,2},{1,3},{6,4},{7,5},{4,6},{5,7},{10,8},{11,9},{8,1... | collective-permute-start | bytes 589832 | tf_op jit(solution)/shard_map/ppermute | solution.py:65
  29.5 0.0 collective-permute-start.12
  29.5 0.5 collective-permute-start.18
  30.0 0.0 collective-permute-done.3.refs_1_.refs_13_
  30.0 0.5 collective-permute-start.20
  30.5 2.6 %collective-permute-done.4.refs_10_.refs_22_ = bf16[768,128]{1,0:T(8,128)(2,1)S(1)} collective-permute-done((bf16[768,128]{1,0:T(8,128)(2,1)S(1)}, bf16[768,128]{1,0:T(8,128)(2,1)S(1)}, u32[]{:S(2)}, u32[]{:S(2)}) %collective-permute-start.4) | collective-permute-done | bytes 196640 | tf_op jit(solution)/shard_map/ppermute | solution.py:65
  33.1 2.0 %collective-permute-start.6 = (bf16[528,128]{1,0:T(8,128)(2,1)S(1)}, bf16[528,128]{1,0:T(8,128)(2,1)S(1)}, u32[]{:S(2)}, u32[]{:S(2)}) collective-permute-start(bf16[528,128]{1,0:T(8,128)(2,1)S(1)} %collective-permute-done.refs_0_.refs_4_), channel_id=1, source_target_pairs={{2,0},{3,1},{0,2},{1,3},{6,4},{7,5},{4,6},{5,7},{10,8},{11,9},{8,1... | collective-permute-start | bytes 405512 | tf_op jit(solution)/shard_map/ppermute | solution.py:65
  35.2 0.3 collective-permute-done.12.refs_2_.refs_14_
  35.4 1.8 %collective-permute-start.7 = (bf16[528,128]{1,0:T(8,128)(2,1)S(1)}, bf16[528,128]{1,0:T(8,128)(2,1)S(1)}, u32[]{:S(2)}, u32[]{:S(2)}) collective-permute-start(bf16[528,128]{1,0:T(8,128)(2,1)S(1)} %collective-permute-done.refs_0_.refs_4_), channel_id=1, source_target_pairs={{3,0},{2,1},{1,2},{0,3},{7,4},{6,5},{5,6},{4,7},{11,8},{10,9},{9,1... | collective-permute-start | bytes 405512 | tf_op jit(solution)/shard_map/ppermute | solution.py:65
  37.2 0.0 collective-permute-done.18.refs_9_.refs_21_
  37.2 0.5 collective-permute-start.13
  37.8 0.0 collective-permute-done.14.refs_4_.refs_16_
  37.8 1.5 %collective-permute-start.5 = (bf16[528,128]{1,0:T(8,128)(2,1)S(1)}, bf16[528,128]{1,0:T(8,128)(2,1)S(1)}, u32[]{:S(2)}, u32[]{:S(2)}) collective-permute-start(bf16[528,128]{1,0:T(8,128)(2,1)S(1)} %collective-permute-done.refs_0_.refs_4_), channel_id=1, source_target_pairs={{1,0},{0,1},{3,2},{2,3},{5,4},{4,5},{7,6},{6,7},{9,8},{8,9},{11,10... | collective-permute-start | bytes 405512 | tf_op jit(solution)/shard_map/ppermute | solution.py:65
  39.3 1.4 %collective-permute-done.6.refs_2_.refs_6_ = bf16[528,128]{1,0:T(8,128)(2,1)S(1)} collective-permute-done((bf16[528,128]{1,0:T(8,128)(2,1)S(1)}, bf16[528,128]{1,0:T(8,128)(2,1)S(1)}, u32[]{:S(2)}, u32[]{:S(2)}) %collective-permute-start.6) | collective-permute-done | bytes 135200 | tf_op jit(solution)/shard_map/ppermute | solution.py:65
  40.7 1.9 %collective-permute-start.19 = (bf16[768,128]{1,0:T(8,128)(2,1)S(1)}, bf16[768,128]{1,0:T(8,128)(2,1)S(1)}, u32[]{:S(2)}, u32[]{:S(2)}) collective-permute-start(bf16[768,128]{1,0:T(8,128)(2,1)S(1)} %collective-permute-done.4.refs_10_.refs_22_), channel_id=1, source_target_pairs={{1,0},{0,1},{3,2},{2,3},{5,4},{4,5},{7,6},{6,7},{9,8},{8,9},{11,10... | collective-permute-start | bytes 589832 | tf_op jit(solution)/shard_map/ppermute | solution.py:65
  42.6 2.4 %collective-permute-done.5.refs_1_.refs_5_ = bf16[528,128]{1,0:T(8,128)(2,1)S(1)} collective-permute-done((bf16[528,128]{1,0:T(8,128)(2,1)S(1)}, bf16[528,128]{1,0:T(8,128)(2,1)S(1)}, u32[]{:S(2)}, u32[]{:S(2)}) %collective-permute-start.5) | collective-permute-done | bytes 135200 | tf_op jit(solution)/shard_map/ppermute | solution.py:65
  44.9 0.0 collective-permute-start.10
  44.9 0.5 collective-permute-start.11
  45.4 0.1 collective-permute-start.9
  45.5 2.4 %collective-permute-done.19.refs_11_.refs_23_ = bf16[768,128]{1,0:T(8,128)(2,1)S(1)} collective-permute-done((bf16[768,128]{1,0:T(8,128)(2,1)S(1)}, bf16[768,128]{1,0:T(8,128)(2,1)S(1)}, u32[]{:S(2)}, u32[]{:S(2)}) %collective-permute-start.19) | collective-permute-done | bytes 196640 | tf_op jit(solution)/shard_map/ppermute | solution.py:65
  47.9 0.0 collective-permute-start.22
  47.9 0.5 collective-permute-start.16
  48.4 0.1 collective-permute-start.21
  48.5 0.0 collective-permute-done.11.refs_7_.refs_11_
  48.5 0.4 collective-permute-start.17
  48.9 0.1 collective-permute-start.23
  49.0 1.3 %shard_map.102 = (bf16[144,128]{1,0:T(8,128)(2,1)S(1)}, bf16[144,128]{1,0:T(8,128)(2,1)S(1)}, bf16[144,128]{1,0:T(8,128)(2,1)S(1)}, bf16[144,128]{1,0:T(8,128)(2,1)S(1)}) custom-call(s32[3]{0:T(128)S(1)} %pad_add_fusion.place_ref, bf16[128,1024]{1,0:T(8,128)(2,1)S(1)} %bitcast.21, bf16[128,1024]{1,0:T(8,128)(2,1)S(1)} %bitcast.23, ...), custom_call_target="tpu_custom_call" | custom-call | tf_op jit(solution)/shard_map/pallas_call | solution.py:369
  50.3 0.0 collective-permute-done.22.refs_14_.refs_26_
  50.4 0.1 collective-permute-done.23.refs_15_.refs_27_
  50.5 1.4 %shard_map.103 = (bf16[128,384]{1,0:T(8,128)(2,1)S(1)}, bf16[128,384]{1,0:T(8,128)(2,1)S(1)}, bf16[128,384]{1,0:T(8,128)(2,1)S(1)}, bf16[128,384]{1,0:T(8,128)(2,1)S(1)}) custom-call(s32[3]{0:T(128)S(1)} %pad_add_fusion.place_ref, bf16[128,1024]{1,0:T(8,128)(2,1)S(1)} %bitcast.22, bf16[768,128]{1,0:T(8,128)(2,1)S(1)} %collective-permute-done.1.refs_0_.refs_12_, ...), custom_call_target="tpu_custom_call" | custom-call | tf_op jit(solution)/shard_map/pallas_call | solution.py:369
  51.9 0.7 collective-permute-start.24
  52.6 3.3 %collective-permute-start.25 = (bf16[128,384]{1,0:T(8,128)(2,1)S(1)}, bf16[128,384]{1,0:T(8,128)(2,1)S(1)}, u32[]{:S(2)}, u32[]{:S(2)}) collective-permute-start(bf16[128,384]{1,0:T(8,128)(2,1)S(1)} %get-tuple-element.52), channel_id=1, source_target_pairs={{0,8},{4,12},{8,0},{12,4},{1,9},{5,13},{9,1},{13,5},{2,10},{6,14},... | collective-permute-start | bytes 294920 | tf_op jit(solution)/shard_map/ppermute | solution.py:76
  55.9 1.4 %collective-permute-start.26 = (bf16[128,384]{1,0:T(8,128)(2,1)S(1)}, bf16[128,384]{1,0:T(8,128)(2,1)S(1)}, u32[]{:S(2)}, u32[]{:S(2)}) collective-permute-start(bf16[128,384]{1,0:T(8,128)(2,1)S(1)} %get-tuple-element.53), channel_id=1, source_target_pairs={{0,12},{4,8},{8,4},{12,0},{1,13},{5,9},{9,5},{13,1},{2,14},{6,10},... | collective-permute-start | bytes 294920 | tf_op jit(solution)/shard_map/ppermute | solution.py:76
  57.3 0.6 collective-permute-start.28
  57.8 2.4 %collective-permute-start.29 = (bf16[144,128]{1,0:T(8,128)(2,1)S(1)}, bf16[144,128]{1,0:T(8,128)(2,1)S(1)}, u32[]{:S(2)}, u32[]{:S(2)}) collective-permute-start(bf16[144,128]{1,0:T(8,128)(2,1)S(1)} %get-tuple-element.55), channel_id=1, source_target_pairs={{0,8},{4,12},{8,0},{12,4},{1,9},{5,13},{9,1},{13,5},{2,10},{6,14},... | collective-permute-start | bytes 110600 | tf_op jit(solution)/shard_map/ppermute | solution.py:76
  60.3 1.4 %collective-permute-start.30 = (bf16[144,128]{1,0:T(8,128)(2,1)S(1)}, bf16[144,128]{1,0:T(8,128)(2,1)S(1)}, u32[]{:S(2)}, u32[]{:S(2)}) collective-permute-start(bf16[144,128]{1,0:T(8,128)(2,1)S(1)} %get-tuple-element.56), channel_id=1, source_target_pairs={{0,12},{4,8},{8,4},{12,0},{1,13},{5,9},{9,5},{13,1},{2,14},{6,10},... | collective-permute-start | bytes 110600 | tf_op jit(solution)/shard_map/ppermute | solution.py:76
  61.7 3.5 %collective-permute-done.26 = bf16[128,384]{1,0:T(8,128)(2,1)S(1)} collective-permute-done((bf16[128,384]{1,0:T(8,128)(2,1)S(1)}, bf16[128,384]{1,0:T(8,128)(2,1)S(1)}, u32[]{:S(2)}, u32[]{:S(2)}) %collective-permute-start.26) | collective-permute-done | bytes 98336 | tf_op jit(solution)/shard_map/ppermute | solution.py:76
  65.1 0.1 convert_add_fusion.refs_0_
  65.2 0.1 collective-permute-start.27
  65.3 3.4 %collective-permute-done.29 = bf16[144,128]{1,0:T(8,128)(2,1)S(1)} collective-permute-done((bf16[144,128]{1,0:T(8,128)(2,1)S(1)}, bf16[144,128]{1,0:T(8,128)(2,1)S(1)}, u32[]{:S(2)}, u32[]{:S(2)}) %collective-permute-start.29) | collective-permute-done | bytes 36896 | tf_op jit(solution)/shard_map/ppermute | solution.py:76
  68.8 0.1 collective-permute-start.31
  68.8 1.3 %collective-permute-done.31.refs_3_ = f32[144,128]{1,0:T(8,128)S(1)} collective-permute-done((f32[144,128]{1,0:T(8,128)S(1)}, f32[144,128]{1,0:T(8,128)S(1)}, u32[]{:S(2)}, u32[]{:S(2)}) %collective-permute-start.31) | collective-permute-done | bytes 73760 | tf_op jit(solution)/shard_map/ppermute | solution.py:65
  70.1 10.8 %shard_map.104 = (bf16[144,512]{1,0:T(8,128)(2,1)S(1)}, f32[64,256]{1,0:T(8,128)S(1)}, f32[64,256]{1,0:T(8,128)S(1)}, f32[64,256]{1,0:T(8,128)S(1)}, f32[64,256]{1,0:T(8,128)S(1)}) custom-call(s32[3]{0:T(128)S(1)} %pad_add_fusion.place_ref, f32[128,384]{1,0:T(8,128)S(1)} %convert_add_fusion.refs_0_, f32[128,384]{1,0:T(8,128)S(1)} %collective-permute-done.27.refs_1_, ...), custom_call_target="tpu_custom_call" | custom-call | tf_op jit(solution)/shard_map/pallas_call | solution.py:369
  81.0 1.0 %collective-permute-start.32 = (bf16[144,512]{1,0:T(8,128)(2,1)S(1)}, bf16[144,512]{1,0:T(8,128)(2,1)S(1)}, u32[]{:S(2)}, u32[]{:S(2)}) collective-permute-start(bf16[144,512]{1,0:T(8,128)(2,1)S(1)} %get-tuple-element.57.refs_0_), channel_id=1, source_target_pairs={{4,0},{0,4},{12,8},{8,12},{5,1},{1,5},{13,9},{9,13},{6,2},{2,6},{1... | collective-permute-start | bytes 442376 | tf_op jit(solution)/shard_map/ppermute | solution.py:65
  82.0 2.4 %collective-permute-start.33 = (bf16[144,512]{1,0:T(8,128)(2,1)S(1)}, bf16[144,512]{1,0:T(8,128)(2,1)S(1)}, u32[]{:S(2)}, u32[]{:S(2)}) collective-permute-start(bf16[144,512]{1,0:T(8,128)(2,1)S(1)} %get-tuple-element.57.refs_0_), channel_id=1, source_target_pairs={{8,0},{12,4},{0,8},{4,12},{9,1},{13,5},{1,9},{5,13},{10,2},{14,6},... | collective-permute-start | bytes 442376 | tf_op jit(solution)/shard_map/ppermute | solution.py:65
  84.4 1.0 %collective-permute-start.34 = (bf16[144,512]{1,0:T(8,128)(2,1)S(1)}, bf16[144,512]{1,0:T(8,128)(2,1)S(1)}, u32[]{:S(2)}, u32[]{:S(2)}) collective-permute-start(bf16[144,512]{1,0:T(8,128)(2,1)S(1)} %get-tuple-element.57.refs_0_), channel_id=1, source_target_pairs={{12,0},{8,4},{4,8},{0,12},{13,1},{9,5},{5,9},{1,13},{14,2},{10,6},... | collective-permute-start | bytes 442376 | tf_op jit(solution)/shard_map/ppermute | solution.py:65
  85.4 4.4 %collective-permute-done.32.refs_1_ = bf16[144,512]{1,0:T(8,128)(2,1)S(1)} collective-permute-done((bf16[144,512]{1,0:T(8,128)(2,1)S(1)}, bf16[144,512]{1,0:T(8,128)(2,1)S(1)}, u32[]{:S(2)}, u32[]{:S(2)}) %collective-permute-start.32) | collective-permute-done | bytes 147488 | tf_op jit(solution)/shard_map/ppermute | solution.py:65
  89.8 0.7 collective-permute-start.35
  90.4 0.6 collective-permute-start.36
  91.0 2.2 %collective-permute-start.37 = (f32[64,256]{1,0:T(8,128)S(1)}, f32[64,256]{1,0:T(8,128)S(1)}, u32[]{:S(2)}, u32[]{:S(2)}) collective-permute-start(f32[64,256]{1,0:T(8,128)S(1)} %get-tuple-element.67), channel_id=1, source_target_pairs={{0,3},{1,2},{2,1},{3,0},{4,7},{5,6},{6,5},{7,4},{8,11},{9,10},{10,... | collective-permute-start | bytes 196616 | tf_op jit(solution)/shard_map/ppermute | solution.py:76
  93.3 2.7 %collective-permute-done.33.refs_2_ = bf16[144,512]{1,0:T(8,128)(2,1)S(1)} collective-permute-done((bf16[144,512]{1,0:T(8,128)(2,1)S(1)}, bf16[144,512]{1,0:T(8,128)(2,1)S(1)}, u32[]{:S(2)}, u32[]{:S(2)}) %collective-permute-start.33) | collective-permute-done | bytes 147488 | tf_op jit(solution)/shard_map/ppermute | solution.py:65
  95.9 3.1 %shard_map.105 = (bf16[128,1024]{1,0:T(8,128)(2,1)}, bf16[128,1024]{1,0:T(8,128)(2,1)}) custom-call(s32[3]{0:T(128)S(1)} %pad_add_fusion.place_ref, bf16[144,512]{1,0:T(8,128)(2,1)S(1)} %get-tuple-element.57.refs_0_, bf16[144,512]{1,0:T(8,128)(2,1)S(1)} %collective-permute-done.32.refs_1_, bf16[144,512]{1,0:T(8,128)(2,1)S(1)} %collective-permute-done.33.refs_2_, ...), custom_call_target="tpu_custom_call" | custom-call | tf_op jit(solution)/shard_map/pallas_call | solution.py:369
  99.1 0.6 slice_bitcast_fusion
  (37 shorter events, 0.1 us)
Async XLA Ops:
  0.6 1.2 %copy-start = (bf16[4096,1]{0,1:T(2,128)(2,1)S(1)}, bf16[4096,1]{0,1:T(2,128)(2,1)}, u32[]{:S(2)}) copy-start(bf16[4096,1]{0,1:T(2,128)(2,1)} %param.9) | copy-start | bytes 24580
  0.7 1.2 %copy-start.5 = (bf16[512,128]{1,0:T(8,128)(2,1)S(1)}, bf16[512,128]{1,0:T(8,128)(2,1)}, u32[]{:S(2)}) copy-start(bf16[512,128]{1,0:T(8,128)(2,1)} %param.10) | copy-start | bytes 393220
  0.7 48.3 %copy-start.2 = (bf16[1,128,1024]{2,1,0:T(8,128)(2,1)S(1)}, bf16[1,128,1024]{2,1,0:T(8,128)(2,1)}, u32[]{:S(2)}) copy-start(bf16[1,128,1024]{2,1,0:T(8,128)(2,1)} %param.13) | copy-start | bytes 786436
  1.8 47.2 %copy-start.1 = (bf16[1,128,1024]{2,1,0:T(8,128)(2,1)S(1)}, bf16[1,128,1024]{2,1,0:T(8,128)(2,1)}, u32[]{:S(2)}) copy-start(bf16[1,128,1024]{2,1,0:T(8,128)(2,1)} %param.7) | copy-start | bytes 786436
  2.0 2.1 %collective-permute-start.1 = (bf16[768,128]{1,0:T(8,128)(2,1)S(1)}, bf16[768,128]{1,0:T(8,128)(2,1)S(1)}, u32[]{:S(2)}, u32[]{:S(2)}) collective-permute-start(bf16[768,128]{1,0:T(8,128)(2,1)S(1)} %bitcast.28), channel_id=1, source_target_pairs={{0,0},{1,1},{2,4},{3,5},{4,2},{5,3},{6,6},{7,7},{8,16},{9,17},{10,... | collective-permute-start | bytes 589832 | tf_op jit(solution)/shard_map/ppermute | solution.py:400
  2.6 1.4 %collective-permute-start.2 = (bf16[768,128]{1,0:T(8,128)(2,1)S(1)}, bf16[768,128]{1,0:T(8,128)(2,1)S(1)}, u32[]{:S(2)}, u32[]{:S(2)}) collective-permute-start(bf16[768,128]{1,0:T(8,128)(2,1)S(1)} %bitcast.27), channel_id=1, source_target_pairs={{0,0},{1,1},{2,4},{3,5},{4,2},{5,3},{6,6},{7,7},{8,16},{9,17},{10,... | collective-permute-start | bytes 589832 | tf_op jit(solution)/shard_map/ppermute | solution.py:400
  3.3 0.7 collective-permute-start
  4.0 26.0 %collective-permute-start.3 = (bf16[768,128]{1,0:T(8,128)(2,1)S(1)}, bf16[768,128]{1,0:T(8,128)(2,1)S(1)}, u32[]{:S(2)}, u32[]{:S(2)}) collective-permute-start(bf16[768,128]{1,0:T(8,128)(2,1)S(1)} %collective-permute-done.1.refs_0_.refs_12_), channel_id=1, source_target_pairs={{1,0},{0,1},{3,2},{2,3},{5,4},{4,5},{7,6},{6,7},{9,8},{8,9},{11,10... | collective-permute-start | bytes 589832 | tf_op jit(solution)/shard_map/ppermute | solution.py:65
  7.0 26.1 %collective-permute-start.4 = (bf16[768,128]{1,0:T(8,128)(2,1)S(1)}, bf16[768,128]{1,0:T(8,128)(2,1)S(1)}, u32[]{:S(2)}, u32[]{:S(2)}) collective-permute-start(bf16[768,128]{1,0:T(8,128)(2,1)S(1)} %collective-permute-done.2.refs_8_.refs_20_), channel_id=1, source_target_pairs={{2,0},{3,1},{0,2},{1,3},{6,4},{7,5},{4,6},{5,7},{10,8},{11,9},{8,1... | collective-permute-start | bytes 589832 | tf_op jit(solution)/shard_map/ppermute | solution.py:65
  29.5 5.9 %collective-permute-start.12 = (bf16[768,128]{1,0:T(8,128)(2,1)S(1)}, bf16[768,128]{1,0:T(8,128)(2,1)S(1)}, u32[]{:S(2)}, u32[]{:S(2)}) collective-permute-start(bf16[768,128]{1,0:T(8,128)(2,1)S(1)} %collective-permute-done.1.refs_0_.refs_12_), channel_id=1, source_target_pairs={{2,0},{3,1},{0,2},{1,3},{6,4},{7,5},{4,6},{5,7},{10,8},{11,9},{8,1... | collective-permute-start | bytes 589832 | tf_op jit(solution)/shard_map/ppermute | solution.py:65
  29.5 7.7 %collective-permute-start.18 = (bf16[768,128]{1,0:T(8,128)(2,1)S(1)}, bf16[768,128]{1,0:T(8,128)(2,1)S(1)}, u32[]{:S(2)}, u32[]{:S(2)}) collective-permute-start(bf16[768,128]{1,0:T(8,128)(2,1)S(1)} %collective-permute-done.2.refs_8_.refs_20_), channel_id=1, source_target_pairs={{1,0},{0,1},{3,2},{2,3},{5,4},{4,5},{7,6},{6,7},{9,8},{8,9},{11,10... | collective-permute-start | bytes 589832 | tf_op jit(solution)/shard_map/ppermute | solution.py:65
  30.0 7.7 %collective-permute-start.14 = (bf16[768,128]{1,0:T(8,128)(2,1)S(1)}, bf16[768,128]{1,0:T(8,128)(2,1)S(1)}, u32[]{:S(2)}, u32[]{:S(2)}) collective-permute-start(bf16[768,128]{1,0:T(8,128)(2,1)S(1)} %collective-permute-done.1.refs_0_.refs_12_), channel_id=1, source_target_pairs={{16,0},{0,16},{17,1},{1,17},{18,2},{2,18},{19,3},{3,19},{20,4},{4,... | collective-permute-start | bytes 589832 | tf_op jit(solution)/shard_map/ppermute | solution.py:65
  30.0 9.3 %collective-permute-start.20 = (bf16[768,128]{1,0:T(8,128)(2,1)S(1)}, bf16[768,128]{1,0:T(8,128)(2,1)S(1)}, u32[]{:S(2)}, u32[]{:S(2)}) collective-permute-start(bf16[768,128]{1,0:T(8,128)(2,1)S(1)} %collective-permute-done.2.refs_8_.refs_20_), channel_id=1, source_target_pairs={{16,0},{0,16},{17,1},{1,17},{18,2},{2,18},{19,3},{3,19},{20,4},{4,... | collective-permute-start | bytes 589832 | tf_op jit(solution)/shard_map/ppermute | solution.py:65
  33.1 7.5 %collective-permute-start.6 = (bf16[528,128]{1,0:T(8,128)(2,1)S(1)}, bf16[528,128]{1,0:T(8,128)(2,1)S(1)}, u32[]{:S(2)}, u32[]{:S(2)}) collective-permute-start(bf16[528,128]{1,0:T(8,128)(2,1)S(1)} %collective-permute-done.refs_0_.refs_4_), channel_id=1, source_target_pairs={{2,0},{3,1},{0,2},{1,3},{6,4},{7,5},{4,6},{5,7},{10,8},{11,9},{8,1... | collective-permute-start | bytes 405512 | tf_op jit(solution)/shard_map/ppermute | solution.py:65
  35.4 7.1 %collective-permute-start.7 = (bf16[528,128]{1,0:T(8,128)(2,1)S(1)}, bf16[528,128]{1,0:T(8,128)(2,1)S(1)}, u32[]{:S(2)}, u32[]{:S(2)}) collective-permute-start(bf16[528,128]{1,0:T(8,128)(2,1)S(1)} %collective-permute-done.refs_0_.refs_4_), channel_id=1, source_target_pairs={{3,0},{2,1},{1,2},{0,3},{7,4},{6,5},{5,6},{4,7},{11,8},{10,9},{9,1... | collective-permute-start | bytes 405512 | tf_op jit(solution)/shard_map/ppermute | solution.py:65
  37.2 8.2 %collective-permute-start.13 = (bf16[768,128]{1,0:T(8,128)(2,1)S(1)}, bf16[768,128]{1,0:T(8,128)(2,1)S(1)}, u32[]{:S(2)}, u32[]{:S(2)}) collective-permute-start(bf16[768,128]{1,0:T(8,128)(2,1)S(1)} %collective-permute-done.3.refs_1_.refs_13_), channel_id=1, source_target_pairs={{2,0},{3,1},{0,2},{1,3},{6,4},{7,5},{4,6},{5,7},{10,8},{11,9},{8,1... | collective-permute-start | bytes 589832 | tf_op jit(solution)/shard_map/ppermute | solution.py:65
  37.8 7.2 %collective-permute-start.5 = (bf16[528,128]{1,0:T(8,128)(2,1)S(1)}, bf16[528,128]{1,0:T(8,128)(2,1)S(1)}, u32[]{:S(2)}, u32[]{:S(2)}) collective-permute-start(bf16[528,128]{1,0:T(8,128)(2,1)S(1)} %collective-permute-done.refs_0_.refs_4_), channel_id=1, source_target_pairs={{1,0},{0,1},{3,2},{2,3},{5,4},{4,5},{7,6},{6,7},{9,8},{8,9},{11,10... | collective-permute-start | bytes 405512 | tf_op jit(solution)/shard_map/ppermute | solution.py:65
  39.3 5.6 %collective-permute-start.8 = (bf16[528,128]{1,0:T(8,128)(2,1)S(1)}, bf16[528,128]{1,0:T(8,128)(2,1)S(1)}, u32[]{:S(2)}, u32[]{:S(2)}) collective-permute-start(bf16[528,128]{1,0:T(8,128)(2,1)S(1)} %collective-permute-done.refs_0_.refs_4_), channel_id=1, source_target_pairs={{16,0},{0,16},{17,1},{1,17},{18,2},{2,18},{19,3},{3,19},{20,4},{4,... | collective-permute-start | bytes 405512 | tf_op jit(solution)/shard_map/ppermute | solution.py:65
  40.7 7.2 %collective-permute-start.19 = (bf16[768,128]{1,0:T(8,128)(2,1)S(1)}, bf16[768,128]{1,0:T(8,128)(2,1)S(1)}, u32[]{:S(2)}, u32[]{:S(2)}) collective-permute-start(bf16[768,128]{1,0:T(8,128)(2,1)S(1)} %collective-permute-done.4.refs_10_.refs_22_), channel_id=1, source_target_pairs={{1,0},{0,1},{3,2},{2,3},{5,4},{4,5},{7,6},{6,7},{9,8},{8,9},{11,10... | collective-permute-start | bytes 589832 | tf_op jit(solution)/shard_map/ppermute | solution.py:65
  42.6 5.4 %collective-permute-start.15 = (bf16[768,128]{1,0:T(8,128)(2,1)S(1)}, bf16[768,128]{1,0:T(8,128)(2,1)S(1)}, u32[]{:S(2)}, u32[]{:S(2)}) collective-permute-start(bf16[768,128]{1,0:T(8,128)(2,1)S(1)} %collective-permute-done.3.refs_1_.refs_13_), channel_id=1, source_target_pairs={{16,0},{0,16},{17,1},{1,17},{18,2},{2,18},{19,3},{3,19},{20,4},{4,... | collective-permute-start | bytes 589832 | tf_op jit(solution)/shard_map/ppermute | solution.py:65
  44.9 3.5 %collective-permute-start.10 = (bf16[528,128]{1,0:T(8,128)(2,1)S(1)}, bf16[528,128]{1,0:T(8,128)(2,1)S(1)}, u32[]{:S(2)}, u32[]{:S(2)}) collective-permute-start(bf16[528,128]{1,0:T(8,128)(2,1)S(1)} %collective-permute-done.6.refs_2_.refs_6_), channel_id=1, source_target_pairs={{16,0},{0,16},{17,1},{1,17},{18,2},{2,18},{19,3},{3,19},{20,4},{4,... | collective-permute-start | bytes 405512 | tf_op jit(solution)/shard_map/ppermute | solution.py:65
  44.9 3.6 %collective-permute-start.11 = (bf16[528,128]{1,0:T(8,128)(2,1)S(1)}, bf16[528,128]{1,0:T(8,128)(2,1)S(1)}, u32[]{:S(2)}, u32[]{:S(2)}) collective-permute-start(bf16[528,128]{1,0:T(8,128)(2,1)S(1)} %collective-permute-done.7.refs_3_.refs_7_), channel_id=1, source_target_pairs={{16,0},{0,16},{17,1},{1,17},{18,2},{2,18},{19,3},{3,19},{20,4},{4,... | collective-permute-start | bytes 405512 | tf_op jit(solution)/shard_map/ppermute | solution.py:65
  45.4 3.5 %collective-permute-start.9 = (bf16[528,128]{1,0:T(8,128)(2,1)S(1)}, bf16[528,128]{1,0:T(8,128)(2,1)S(1)}, u32[]{:S(2)}, u32[]{:S(2)}) collective-permute-start(bf16[528,128]{1,0:T(8,128)(2,1)S(1)} %collective-permute-done.5.refs_1_.refs_5_), channel_id=1, source_target_pairs={{16,0},{0,16},{17,1},{1,17},{18,2},{2,18},{19,3},{3,19},{20,4},{4,... | collective-permute-start | bytes 405512 | tf_op jit(solution)/shard_map/ppermute | solution.py:65
  47.9 2.4 %collective-permute-start.22 = (bf16[768,128]{1,0:T(8,128)(2,1)S(1)}, bf16[768,128]{1,0:T(8,128)(2,1)S(1)}, u32[]{:S(2)}, u32[]{:S(2)}) collective-permute-start(bf16[768,128]{1,0:T(8,128)(2,1)S(1)} %collective-permute-done.4.refs_10_.refs_22_), channel_id=1, source_target_pairs={{16,0},{0,16},{17,1},{1,17},{18,2},{2,18},{19,3},{3,19},{20,4},{4,... | collective-permute-start | bytes 589832 | tf_op jit(solution)/shard_map/ppermute | solution.py:65
  47.9 2.4 %collective-permute-start.16 = (bf16[768,128]{1,0:T(8,128)(2,1)S(1)}, bf16[768,128]{1,0:T(8,128)(2,1)S(1)}, u32[]{:S(2)}, u32[]{:S(2)}) collective-permute-start(bf16[768,128]{1,0:T(8,128)(2,1)S(1)} %collective-permute-done.12.refs_2_.refs_14_), channel_id=1, source_target_pairs={{16,0},{0,16},{17,1},{1,17},{18,2},{2,18},{19,3},{3,19},{20,4},{4,... | collective-permute-start | bytes 589832 | tf_op jit(solution)/shard_map/ppermute | solution.py:65
  48.4 1.9 %collective-permute-start.21 = (bf16[768,128]{1,0:T(8,128)(2,1)S(1)}, bf16[768,128]{1,0:T(8,128)(2,1)S(1)}, u32[]{:S(2)}, u32[]{:S(2)}) collective-permute-start(bf16[768,128]{1,0:T(8,128)(2,1)S(1)} %collective-permute-done.18.refs_9_.refs_21_), channel_id=1, source_target_pairs={{16,0},{0,16},{17,1},{1,17},{18,2},{2,18},{19,3},{3,19},{20,4},{4,... | collective-permute-start | bytes 589832 | tf_op jit(solution)/shard_map/ppermute | solution.py:65
  48.5 1.9 %collective-permute-start.17 = (bf16[768,128]{1,0:T(8,128)(2,1)S(1)}, bf16[768,128]{1,0:T(8,128)(2,1)S(1)}, u32[]{:S(2)}, u32[]{:S(2)}) collective-permute-start(bf16[768,128]{1,0:T(8,128)(2,1)S(1)} %collective-permute-done.13.refs_3_.refs_15_), channel_id=1, source_target_pairs={{16,0},{0,16},{17,1},{1,17},{18,2},{2,18},{19,3},{3,19},{20,4},{4,... | collective-permute-start | bytes 589832 | tf_op jit(solution)/shard_map/ppermute | solution.py:65
  48.9 1.5 %collective-permute-start.23 = (bf16[768,128]{1,0:T(8,128)(2,1)S(1)}, bf16[768,128]{1,0:T(8,128)(2,1)S(1)}, u32[]{:S(2)}, u32[]{:S(2)}) collective-permute-start(bf16[768,128]{1,0:T(8,128)(2,1)S(1)} %collective-permute-done.19.refs_11_.refs_23_), channel_id=1, source_target_pairs={{16,0},{0,16},{17,1},{1,17},{18,2},{2,18},{19,3},{3,19},{20,4},{4,... | collective-permute-start | bytes 589832 | tf_op jit(solution)/shard_map/ppermute | solution.py:65
  51.9 8.4 %collective-permute-start.24 = (bf16[128,384]{1,0:T(8,128)(2,1)S(1)}, bf16[128,384]{1,0:T(8,128)(2,1)S(1)}, u32[]{:S(2)}, u32[]{:S(2)}) collective-permute-start(bf16[128,384]{1,0:T(8,128)(2,1)S(1)} %get-tuple-element.51), channel_id=1, source_target_pairs={{0,4},{4,0},{8,12},{12,8},{1,5},{5,1},{9,13},{13,9},{2,6},{6,2},{1... | collective-permute-start | bytes 294920 | tf_op jit(solution)/shard_map/ppermute | solution.py:76
  52.6 9.1 %collective-permute-start.25 = (bf16[128,384]{1,0:T(8,128)(2,1)S(1)}, bf16[128,384]{1,0:T(8,128)(2,1)S(1)}, u32[]{:S(2)}, u32[]{:S(2)}) collective-permute-start(bf16[128,384]{1,0:T(8,128)(2,1)S(1)} %get-tuple-element.52), channel_id=1, source_target_pairs={{0,8},{4,12},{8,0},{12,4},{1,9},{5,13},{9,1},{13,5},{2,10},{6,14},... | collective-permute-start | bytes 294920 | tf_op jit(solution)/shard_map/ppermute | solution.py:76
  55.9 9.3 %collective-permute-start.26 = (bf16[128,384]{1,0:T(8,128)(2,1)S(1)}, bf16[128,384]{1,0:T(8,128)(2,1)S(1)}, u32[]{:S(2)}, u32[]{:S(2)}) collective-permute-start(bf16[128,384]{1,0:T(8,128)(2,1)S(1)} %get-tuple-element.53), channel_id=1, source_target_pairs={{0,12},{4,8},{8,4},{12,0},{1,13},{5,9},{9,5},{13,1},{2,14},{6,10},... | collective-permute-start | bytes 294920 | tf_op jit(solution)/shard_map/ppermute | solution.py:76
  57.3 8.0 %collective-permute-start.28 = (bf16[144,128]{1,0:T(8,128)(2,1)S(1)}, bf16[144,128]{1,0:T(8,128)(2,1)S(1)}, u32[]{:S(2)}, u32[]{:S(2)}) collective-permute-start(bf16[144,128]{1,0:T(8,128)(2,1)S(1)} %get-tuple-element.54), channel_id=1, source_target_pairs={{0,4},{4,0},{8,12},{12,8},{1,5},{5,1},{9,13},{13,9},{2,6},{6,2},{1... | collective-permute-start | bytes 110600 | tf_op jit(solution)/shard_map/ppermute | solution.py:76
  57.8 10.9 %collective-permute-start.29 = (bf16[144,128]{1,0:T(8,128)(2,1)S(1)}, bf16[144,128]{1,0:T(8,128)(2,1)S(1)}, u32[]{:S(2)}, u32[]{:S(2)}) collective-permute-start(bf16[144,128]{1,0:T(8,128)(2,1)S(1)} %get-tuple-element.55), channel_id=1, source_target_pairs={{0,8},{4,12},{8,0},{12,4},{1,9},{5,13},{9,1},{13,5},{2,10},{6,14},... | collective-permute-start | bytes 110600 | tf_op jit(solution)/shard_map/ppermute | solution.py:76
  60.3 8.5 %collective-permute-start.30 = (bf16[144,128]{1,0:T(8,128)(2,1)S(1)}, bf16[144,128]{1,0:T(8,128)(2,1)S(1)}, u32[]{:S(2)}, u32[]{:S(2)}) collective-permute-start(bf16[144,128]{1,0:T(8,128)(2,1)S(1)} %get-tuple-element.56), channel_id=1, source_target_pairs={{0,12},{4,8},{8,4},{12,0},{1,13},{5,9},{9,5},{13,1},{2,14},{6,10},... | collective-permute-start | bytes 110600 | tf_op jit(solution)/shard_map/ppermute | solution.py:76
  65.1 5.0 %copy-start.3 = (f32[1,128,512]{2,1,0:T(8,128)S(1)}, f32[1,128,512]{2,1,0:T(8,128)}, u32[]{:S(2)}) copy-start(f32[1,128,512]{2,1,0:T(8,128)} %param.11) | copy-start | bytes 786436
  65.1 5.0 %copy-start.4 = (f32[1,512,128]{2,1,0:T(8,128)S(1)}, f32[1,512,128]{2,1,0:T(8,128)}, u32[]{:S(2)}) copy-start(f32[1,512,128]{2,1,0:T(8,128)} %param.12) | copy-start | bytes 786436
  65.2 4.9 %collective-permute-start.27 = (f32[128,384]{1,0:T(8,128)S(1)}, f32[128,384]{1,0:T(8,128)S(1)}, u32[]{:S(2)}, u32[]{:S(2)}) collective-permute-start(f32[128,384]{1,0:T(8,128)S(1)} %convert_add_fusion.refs_0_), channel_id=1, source_target_pairs={{16,0},{0,16},{17,1},{1,17},{18,2},{2,18},{19,3},{3,19},{20,4},{4,... | collective-permute-start | bytes 589832 | tf_op jit(solution)/shard_map/ppermute | solution.py:65
  68.8 1.3 %collective-permute-start.31 = (f32[144,128]{1,0:T(8,128)S(1)}, f32[144,128]{1,0:T(8,128)S(1)}, u32[]{:S(2)}, u32[]{:S(2)}) collective-permute-start(f32[144,128]{1,0:T(8,128)S(1)} %convert_add_fusion.1.refs_2_), channel_id=1, source_target_pairs={{16,0},{0,16},{17,1},{1,17},{18,2},{2,18},{19,3},{3,19},{20,4},{4,... | collective-permute-start | bytes 221192 | tf_op jit(solution)/shard_map/ppermute | solution.py:65
  81.0 8.8 %collective-permute-start.32 = (bf16[144,512]{1,0:T(8,128)(2,1)S(1)}, bf16[144,512]{1,0:T(8,128)(2,1)S(1)}, u32[]{:S(2)}, u32[]{:S(2)}) collective-permute-start(bf16[144,512]{1,0:T(8,128)(2,1)S(1)} %get-tuple-element.57.refs_0_), channel_id=1, source_target_pairs={{4,0},{0,4},{12,8},{8,12},{5,1},{1,5},{13,9},{9,13},{6,2},{2,6},{1... | collective-permute-start | bytes 442376 | tf_op jit(solution)/shard_map/ppermute | solution.py:65
  82.0 13.9 %collective-permute-start.33 = (bf16[144,512]{1,0:T(8,128)(2,1)S(1)}, bf16[144,512]{1,0:T(8,128)(2,1)S(1)}, u32[]{:S(2)}, u32[]{:S(2)}) collective-permute-start(bf16[144,512]{1,0:T(8,128)(2,1)S(1)} %get-tuple-element.57.refs_0_), channel_id=1, source_target_pairs={{8,0},{12,4},{0,8},{4,12},{9,1},{13,5},{1,9},{5,13},{10,2},{14,6},... | collective-permute-start | bytes 442376 | tf_op jit(solution)/shard_map/ppermute | solution.py:65
  84.4 11.5 %collective-permute-start.34 = (bf16[144,512]{1,0:T(8,128)(2,1)S(1)}, bf16[144,512]{1,0:T(8,128)(2,1)S(1)}, u32[]{:S(2)}, u32[]{:S(2)}) collective-permute-start(bf16[144,512]{1,0:T(8,128)(2,1)S(1)} %get-tuple-element.57.refs_0_), channel_id=1, source_target_pairs={{12,0},{8,4},{4,8},{0,12},{13,1},{9,5},{5,9},{1,13},{14,2},{10,6},... | collective-permute-start | bytes 442376 | tf_op jit(solution)/shard_map/ppermute | solution.py:65
  89.8 9.3 %collective-permute-start.35 = (f32[64,256]{1,0:T(8,128)S(1)}, f32[64,256]{1,0:T(8,128)S(1)}, u32[]{:S(2)}, u32[]{:S(2)}) collective-permute-start(f32[64,256]{1,0:T(8,128)S(1)} %get-tuple-element.65), channel_id=1, source_target_pairs={{0,1},{1,0},{2,3},{3,2},{4,5},{5,4},{6,7},{7,6},{8,9},{9,8},{10,11... | collective-permute-start | bytes 196616 | tf_op jit(solution)/shard_map/ppermute | solution.py:76
  90.4 8.6 %collective-permute-start.36 = (f32[64,256]{1,0:T(8,128)S(1)}, f32[64,256]{1,0:T(8,128)S(1)}, u32[]{:S(2)}, u32[]{:S(2)}) collective-permute-start(f32[64,256]{1,0:T(8,128)S(1)} %get-tuple-element.66), channel_id=1, source_target_pairs={{0,2},{1,3},{2,0},{3,1},{4,6},{5,7},{6,4},{7,5},{8,10},{9,11},{10,... | collective-permute-start | bytes 196616 | tf_op jit(solution)/shard_map/ppermute | solution.py:76
  91.0 8.1 %collective-permute-start.37 = (f32[64,256]{1,0:T(8,128)S(1)}, f32[64,256]{1,0:T(8,128)S(1)}, u32[]{:S(2)}, u32[]{:S(2)}) collective-permute-start(f32[64,256]{1,0:T(8,128)S(1)} %get-tuple-element.67), channel_id=1, source_target_pairs={{0,3},{1,2},{2,1},{3,0},{4,7},{5,6},{6,5},{7,4},{8,11},{9,10},{10,... | collective-permute-start | bytes 196616 | tf_op jit(solution)/shard_map/ppermute | solution.py:76

commit v6 on v4

--- a/solution.py
+++ b/solution.py
@@ -413,10 +413,9 @@
             jnp.concatenate([w_out, line], axis=0),
         )
     )
-    first_w, second_w, outer_w = swapped(first), swapped(second), swapped(outer)
-    outer_w, first_w, second_w = lax.optimization_barrier((outer_w, first_w, second_w))
+    outer_w, first_w, second_w = swapped(outer), swapped(first), swapped(second)
+    outer_near = peers_of(outer_w, "dp")
     first_near = [first_w, hop(first_w, "dp", 1), hop(first_w, "dp", 2)]
-    outer_near = peers_of(outer_w, "dp")
     second_near = [second_w, hop(second_w, "dp", 1), hop(second_w, "dp", 2)]
     outer_ws = over_seq(outer_near)
     def summed(arrays):
@@ -431,9 +430,6 @@
     )
     outer_all = peers_of(summed(sent_to(outer_part, "head")), "seq")
     if dps == 4:
-        first_near[1], second_near[2], unused = lax.optimization_barrier(
-            (first_near[1], second_near[2], outer_part[0])
-        )
         first_near.append(hop(first_near[1], "dp", 2))
         second_near.append(hop(second_near[2], "dp", 1))
     else:

time: 102 us -> 98.6 us (0.967)
  starting transfers between devices: 52.2 us -> 46.6 us
  waiting for transfers between devices: 29.8 us -> 32.3 us
    ppermute x26, starting transfers between devices: 38.8 us -> 32.6 us  [hop(): lax.ppermute(array, axis, [(mate(i, step, count), i) for i in range(count)])]
    ppermute x26, waiting for transfers between devices: 23 us -> 25.8 us  [hop(): lax.ppermute(array, axis, [(mate(i, step, count), i) for i in range(count)])]
  transfers between devices with their start and end apart: 38 -> 38, of which waited for: 16 -> 14; matrix products, arithmetic and copies ran while one was open for 0% -> 0% of each run, Pallas kernels for 4% -> 4%
where the time goes in v6:
time: 98.6 us; the launch traced here: 98.5 us
  starting transfers between devices  46.6 us (47%)
  waiting for transfers between devices  32.3 us (33%)
  Pallas kernels  16.7 us (17%)
  local copies, waits for them, and re-layouts  1.77 us (2%)
    ppermute x26, starting transfers between devices, hop(): lax.ppermute(array, axis, [(mate(i, step, count), i) for i in range(count)])  32.6 us
    ppermute x26, waiting for transfers between devices, hop(): lax.ppermute(array, axis, [(mate(i, step, count), i) for i in range(count)])  25.8 us
    pallas_call x4, Pallas kernels, call(): pl.pallas_call(kernel, out_shape=outs, in_specs=[SMEM] + [VMEM] * (len(op...  16.7 us
    ppermute x9, starting transfers between devices, sent_to(): lax.ppermute(arrays[j], axis, [(i, mate(i, j, count)) for i in range(coun...  12 us
    ppermute x9, waiting for transfers between devices, sent_to(): lax.ppermute(arrays[j], axis, [(i, mate(i, j, count)) for i in range(coun...  6.5 us
    ppermute x3, starting transfers between devices, swapped(): return lax.ppermute(array, ('seq', 'head', 'dp'), pairs)  2 us
  transfers between devices with their start and end apart: 38, of which 14 were waited for; matrix products, arithmetic and copies ran while one was open for 0% of the time, Pallas kernels for 4%

profile of v6, /device:TPU:0, one launch (start us, length us, event | category | flops | bytes accessed | tf_op | source)
XLA Modules:
  0.0 98.5 jit_solution(12875330594457077520)
XLA Ops:
  0.6 0.0 copy-start
  0.7 0.1 pad_add_fusion.place_ref
  0.7 1.1 %fusion.2 = (bf16[3,256,128]{2,1,0:T(8,128)(2,1)S(1)}, bf16[3,256,128]{2,1,0:T(8,128)(2,1)S(1)}) fusion(bf16[3,512,128]{2,1,0:T(8,128)(2,1)} %bitcast.26), kind=kLoop, calls=%fused_computation.10 | loop fusion | bytes 786432 | tf_op jit(solution)/shard_map/slice | solution.py:412
  1.8 0.0 copy-start.1
  1.9 0.1 reduce
  2.0 0.7 collective-permute-start
  2.6 0.7 collective-permute-start.12
  3.3 0.0 collective-permute-done.refs_0_.refs_4_
  3.3 3.0 %collective-permute-start.1 = (bf16[528,128]{1,0:T(8,128)(2,1)S(1)}, bf16[528,128]{1,0:T(8,128)(2,1)S(1)}, u32[]{:S(2)}, u32[]{:S(2)}) collective-permute-start(bf16[528,128]{1,0:T(8,128)(2,1)S(1)} %collective-permute-done.refs_0_.refs_4_), channel_id=1, source_target_pairs={{1,0},{0,1},{3,2},{2,3},{5,4},{4,5},{7,6},{6,7},{9,8},{8,9},{11,10... | collective-permute-start | bytes 405512 | tf_op jit(solution)/shard_map/ppermute | solution.py:65
  6.3 10.4 %collective-permute-start.2 = (bf16[528,128]{1,0:T(8,128)(2,1)S(1)}, bf16[528,128]{1,0:T(8,128)(2,1)S(1)}, u32[]{:S(2)}, u32[]{:S(2)}) collective-permute-start(bf16[528,128]{1,0:T(8,128)(2,1)S(1)} %collective-permute-done.refs_0_.refs_4_), channel_id=1, source_target_pairs={{2,0},{3,1},{0,2},{1,3},{6,4},{7,5},{4,6},{5,7},{10,8},{11,9},{8,1... | collective-permute-start | bytes 405512 | tf_op jit(solution)/shard_map/ppermute | solution.py:65
  16.7 0.7 collective-permute-start.20
  17.4 1.3 %collective-permute-start.3 = (bf16[528,128]{1,0:T(8,128)(2,1)S(1)}, bf16[528,128]{1,0:T(8,128)(2,1)S(1)}, u32[]{:S(2)}, u32[]{:S(2)}) collective-permute-start(bf16[528,128]{1,0:T(8,128)(2,1)S(1)} %collective-permute-done.refs_0_.refs_4_), channel_id=1, source_target_pairs={{3,0},{2,1},{1,2},{0,3},{7,4},{6,5},{5,6},{4,7},{11,8},{10,9},{9,1... | collective-permute-start | bytes 405512 | tf_op jit(solution)/shard_map/ppermute | solution.py:65
  18.7 0.0 collective-permute-done.12.refs_0_.refs_12_
  18.7 4.0 %collective-permute-start.4 = (bf16[528,128]{1,0:T(8,128)(2,1)S(1)}, bf16[528,128]{1,0:T(8,128)(2,1)S(1)}, u32[]{:S(2)}, u32[]{:S(2)}) collective-permute-start(bf16[528,128]{1,0:T(8,128)(2,1)S(1)} %collective-permute-done.refs_0_.refs_4_), channel_id=1, source_target_pairs={{16,0},{0,16},{17,1},{1,17},{18,2},{2,18},{19,3},{3,19},{20,4},{4,... | collective-permute-start | bytes 405512 | tf_op jit(solution)/shard_map/ppermute | solution.py:65
  22.7 0.1 collective-permute-start.5
  22.8 6.3 %collective-permute-done.2.refs_2_.refs_6_ = bf16[528,128]{1,0:T(8,128)(2,1)S(1)} collective-permute-done((bf16[528,128]{1,0:T(8,128)(2,1)S(1)}, bf16[528,128]{1,0:T(8,128)(2,1)S(1)}, u32[]{:S(2)}, u32[]{:S(2)}) %collective-permute-start.2) | collective-permute-done | bytes 135200 | tf_op jit(solution)/shard_map/ppermute | solution.py:65
  29.1 1.5 %collective-permute-start.13 = (bf16[768,128]{1,0:T(8,128)(2,1)S(1)}, bf16[768,128]{1,0:T(8,128)(2,1)S(1)}, u32[]{:S(2)}, u32[]{:S(2)}) collective-permute-start(bf16[768,128]{1,0:T(8,128)(2,1)S(1)} %collective-permute-done.12.refs_0_.refs_12_), channel_id=1, source_target_pairs={{1,0},{0,1},{3,2},{2,3},{5,4},{4,5},{7,6},{6,7},{9,8},{8,9},{11,10... | collective-permute-start | bytes 589832 | tf_op jit(solution)/shard_map/ppermute | solution.py:65
  30.6 2.5 %collective-permute-start.22 = (bf16[768,128]{1,0:T(8,128)(2,1)S(1)}, bf16[768,128]{1,0:T(8,128)(2,1)S(1)}, u32[]{:S(2)}, u32[]{:S(2)}) collective-permute-start(bf16[768,128]{1,0:T(8,128)(2,1)S(1)} %collective-permute-done.20.refs_8_.refs_20_), channel_id=1, source_target_pairs={{2,0},{3,1},{0,2},{1,3},{6,4},{7,5},{4,6},{5,7},{10,8},{11,9},{8,1... | collective-permute-start | bytes 589832 | tf_op jit(solution)/shard_map/ppermute | solution.py:65
  33.1 0.0 collective-permute-done.4.refs_4_.refs_8_
  33.1 0.1 collective-permute-start.14
  33.2 0.5 collective-permute-start.21
  33.7 0.0 collective-permute-done.6.refs_6_.refs_10_
  33.7 1.4 %collective-permute-done.7.refs_7_.refs_11_ = bf16[528,128]{1,0:T(8,128)(2,1)S(1)} collective-permute-done((bf16[528,128]{1,0:T(8,128)(2,1)S(1)}, bf16[528,128]{1,0:T(8,128)(2,1)S(1)}, u32[]{:S(2)}, u32[]{:S(2)}) %collective-permute-start.7) | collective-permute-done | bytes 135200 | tf_op jit(solution)/shard_map/ppermute | solution.py:65
  35.1 1.3 %shard_map.102 = (bf16[144,128]{1,0:T(8,128)(2,1)S(1)}, bf16[144,128]{1,0:T(8,128)(2,1)S(1)}, bf16[144,128]{1,0:T(8,128)(2,1)S(1)}, bf16[144,128]{1,0:T(8,128)(2,1)S(1)}) custom-call(s32[3]{0:T(128)S(1)} %pad_add_fusion.place_ref, bf16[128,1024]{1,0:T(8,128)(2,1)S(1)} %bitcast.21, bf16[128,1024]{1,0:T(8,128)(2,1)S(1)} %bitcast.23, ...), custom_call_target="tpu_custom_call" | custom-call | tf_op jit(solution)/shard_map/pallas_call | solution.py:369
  36.4 2.0 %collective-permute-start.10 = (bf16[144,128]{1,0:T(8,128)(2,1)S(1)}, bf16[144,128]{1,0:T(8,128)(2,1)S(1)}, u32[]{:S(2)}, u32[]{:S(2)}) collective-permute-start(bf16[144,128]{1,0:T(8,128)(2,1)S(1)} %get-tuple-element.37), channel_id=1, source_target_pairs={{0,12},{4,8},{8,4},{12,0},{1,13},{5,9},{9,5},{13,1},{2,14},{6,10},... | collective-permute-start | bytes 110600 | tf_op jit(solution)/shard_map/ppermute | solution.py:76
  38.3 0.0 collective-permute-done.13.refs_1_.refs_13_
  38.3 0.0 collective-permute-start.8
  38.3 0.4 collective-permute-done.22.refs_10_.refs_22_
  38.8 2.1 %collective-permute-start.9 = (bf16[144,128]{1,0:T(8,128)(2,1)S(1)}, bf16[144,128]{1,0:T(8,128)(2,1)S(1)}, u32[]{:S(2)}, u32[]{:S(2)}) collective-permute-start(bf16[144,128]{1,0:T(8,128)(2,1)S(1)} %get-tuple-element.36), channel_id=1, source_target_pairs={{0,8},{4,12},{8,0},{12,4},{1,9},{5,13},{9,1},{13,5},{2,10},{6,14},... | collective-permute-start | bytes 110600 | tf_op jit(solution)/shard_map/ppermute | solution.py:76
  40.8 1.7 %collective-permute-done.14.refs_2_.refs_14_ = bf16[768,128]{1,0:T(8,128)(2,1)S(1)} collective-permute-done((bf16[768,128]{1,0:T(8,128)(2,1)S(1)}, bf16[768,128]{1,0:T(8,128)(2,1)S(1)}, u32[]{:S(2)}, u32[]{:S(2)}) %collective-permute-start.14) | collective-permute-done | bytes 196640 | tf_op jit(solution)/shard_map/ppermute | solution.py:65
  42.6 0.0 collective-permute-start.16
  42.6 0.5 collective-permute-start.24
  43.1 1.7 %collective-permute-start.15 = (bf16[768,128]{1,0:T(8,128)(2,1)S(1)}, bf16[768,128]{1,0:T(8,128)(2,1)S(1)}, u32[]{:S(2)}, u32[]{:S(2)}) collective-permute-start(bf16[768,128]{1,0:T(8,128)(2,1)S(1)} %collective-permute-done.13.refs_1_.refs_13_), channel_id=1, source_target_pairs={{2,0},{3,1},{0,2},{1,3},{6,4},{7,5},{4,6},{5,7},{10,8},{11,9},{8,1... | collective-permute-start | bytes 589832 | tf_op jit(solution)/shard_map/ppermute | solution.py:65
  44.8 0.0 collective-permute-done.8
  44.9 1.2 %collective-permute-start.23 = (bf16[768,128]{1,0:T(8,128)(2,1)S(1)}, bf16[768,128]{1,0:T(8,128)(2,1)S(1)}, u32[]{:S(2)}, u32[]{:S(2)}) collective-permute-start(bf16[768,128]{1,0:T(8,128)(2,1)S(1)} %collective-permute-done.22.refs_10_.refs_22_), channel_id=1, source_target_pairs={{1,0},{0,1},{3,2},{2,3},{5,4},{4,5},{7,6},{6,7},{9,8},{8,9},{11,10... | collective-permute-start | bytes 589832 | tf_op jit(solution)/shard_map/ppermute | solution.py:65
  46.1 0.2 collective-permute-start.11
  46.3 0.3 collective-permute-start.26
  46.7 0.8 collective-permute-done.11.refs_3_
  47.5 0.2 collective-permute-start.18
  47.6 2.4 %collective-permute-done.15.refs_3_.refs_15_ = bf16[768,128]{1,0:T(8,128)(2,1)S(1)} collective-permute-done((bf16[768,128]{1,0:T(8,128)(2,1)S(1)}, bf16[768,128]{1,0:T(8,128)(2,1)S(1)}, u32[]{:S(2)}, u32[]{:S(2)}) %collective-permute-start.15) | collective-permute-done | bytes 196640 | tf_op jit(solution)/shard_map/ppermute | solution.py:65
  50.0 2.2 %collective-permute-done.23.refs_11_.refs_23_ = bf16[768,128]{1,0:T(8,128)(2,1)S(1)} collective-permute-done((bf16[768,128]{1,0:T(8,128)(2,1)S(1)}, bf16[768,128]{1,0:T(8,128)(2,1)S(1)}, u32[]{:S(2)}, u32[]{:S(2)}) %collective-permute-start.23) | collective-permute-done | bytes 196640 | tf_op jit(solution)/shard_map/ppermute | solution.py:65
  52.2 0.0 collective-permute-start.19
  52.2 0.5 collective-permute-start.27
  52.7 0.9 collective-permute-done.19.refs_7_.refs_19_
  53.6 0.3 collective-permute-done.27.refs_15_.refs_27_
  53.9 1.4 %shard_map.103 = (bf16[128,384]{1,0:T(8,128)(2,1)S(1)}, bf16[128,384]{1,0:T(8,128)(2,1)S(1)}, bf16[128,384]{1,0:T(8,128)(2,1)S(1)}, bf16[128,384]{1,0:T(8,128)(2,1)S(1)}) custom-call(s32[3]{0:T(128)S(1)} %pad_add_fusion.place_ref, bf16[128,1024]{1,0:T(8,128)(2,1)S(1)} %bitcast.22, bf16[768,128]{1,0:T(8,128)(2,1)S(1)} %collective-permute-done.12.refs_0_.refs_12_, ...), custom_call_target="tpu_custom_call" | custom-call | tf_op jit(solution)/shard_map/pallas_call | solution.py:369
  55.3 0.1 collective-permute-start.28
  55.4 0.6 collective-permute-start.29
  56.0 3.8 %collective-permute-start.30 = (bf16[128,384]{1,0:T(8,128)(2,1)S(1)}, bf16[128,384]{1,0:T(8,128)(2,1)S(1)}, u32[]{:S(2)}, u32[]{:S(2)}) collective-permute-start(bf16[128,384]{1,0:T(8,128)(2,1)S(1)} %get-tuple-element.44), channel_id=1, source_target_pairs={{0,12},{4,8},{8,4},{12,0},{1,13},{5,9},{9,5},{13,1},{2,14},{6,10},... | collective-permute-start | bytes 294920 | tf_op jit(solution)/shard_map/ppermute | solution.py:76
  59.8 1.7 %collective-permute-done.28 = bf16[128,384]{1,0:T(8,128)(2,1)S(1)} collective-permute-done((bf16[128,384]{1,0:T(8,128)(2,1)S(1)}, bf16[128,384]{1,0:T(8,128)(2,1)S(1)}, u32[]{:S(2)}, u32[]{:S(2)}) %collective-permute-start.28) | collective-permute-done | bytes 98336 | tf_op jit(solution)/shard_map/ppermute | solution.py:76
  61.5 4.8 %collective-permute-done.29 = bf16[128,384]{1,0:T(8,128)(2,1)S(1)} collective-permute-done((bf16[128,384]{1,0:T(8,128)(2,1)S(1)}, bf16[128,384]{1,0:T(8,128)(2,1)S(1)}, u32[]{:S(2)}, u32[]{:S(2)}) %collective-permute-start.29) | collective-permute-done | bytes 98336 | tf_op jit(solution)/shard_map/ppermute | solution.py:76
  66.3 0.1 convert_add_fusion.refs_0_
  66.3 0.1 collective-permute-start.31
  66.4 1.4 %collective-permute-done.31.refs_1_ = f32[128,384]{1,0:T(8,128)S(1)} collective-permute-done((f32[128,384]{1,0:T(8,128)S(1)}, f32[128,384]{1,0:T(8,128)S(1)}, u32[]{:S(2)}, u32[]{:S(2)}) %collective-permute-start.31) | collective-permute-done | bytes 196640 | tf_op jit(solution)/shard_map/ppermute | solution.py:65
  67.8 10.8 %shard_map.104 = (bf16[144,512]{1,0:T(8,128)(2,1)S(1)}, f32[64,256]{1,0:T(8,128)S(1)}, f32[64,256]{1,0:T(8,128)S(1)}, f32[64,256]{1,0:T(8,128)S(1)}, f32[64,256]{1,0:T(8,128)S(1)}) custom-call(s32[3]{0:T(128)S(1)} %pad_add_fusion.place_ref, f32[128,384]{1,0:T(8,128)S(1)} %convert_add_fusion.refs_0_, f32[128,384]{1,0:T(8,128)S(1)} %collective-permute-done.31.refs_1_, ...), custom_call_target="tpu_custom_call" | custom-call | tf_op jit(solution)/shard_map/pallas_call | solution.py:369
  78.7 2.0 %collective-permute-start.32 = (bf16[144,512]{1,0:T(8,128)(2,1)S(1)}, bf16[144,512]{1,0:T(8,128)(2,1)S(1)}, u32[]{:S(2)}, u32[]{:S(2)}) collective-permute-start(bf16[144,512]{1,0:T(8,128)(2,1)S(1)} %get-tuple-element.45.refs_0_), channel_id=1, source_target_pairs={{4,0},{0,4},{12,8},{8,12},{5,1},{1,5},{13,9},{9,13},{6,2},{2,6},{1... | collective-permute-start | bytes 442376 | tf_op jit(solution)/shard_map/ppermute | solution.py:65
  80.7 2.4 %collective-permute-start.34 = (bf16[144,512]{1,0:T(8,128)(2,1)S(1)}, bf16[144,512]{1,0:T(8,128)(2,1)S(1)}, u32[]{:S(2)}, u32[]{:S(2)}) collective-permute-start(bf16[144,512]{1,0:T(8,128)(2,1)S(1)} %get-tuple-element.45.refs_0_), channel_id=1, source_target_pairs={{12,0},{8,4},{4,8},{0,12},{13,1},{9,5},{5,9},{1,13},{14,2},{10,6},... | collective-permute-start | bytes 442376 | tf_op jit(solution)/shard_map/ppermute | solution.py:65
  83.2 3.5 %collective-permute-done.32.refs_1_ = bf16[144,512]{1,0:T(8,128)(2,1)S(1)} collective-permute-done((bf16[144,512]{1,0:T(8,128)(2,1)S(1)}, bf16[144,512]{1,0:T(8,128)(2,1)S(1)}, u32[]{:S(2)}, u32[]{:S(2)}) %collective-permute-start.32) | collective-permute-done | bytes 147488 | tf_op jit(solution)/shard_map/ppermute | solution.py:65
  86.6 1.2 %collective-permute-start.35 = (f32[64,256]{1,0:T(8,128)S(1)}, f32[64,256]{1,0:T(8,128)S(1)}, u32[]{:S(2)}, u32[]{:S(2)}) collective-permute-start(f32[64,256]{1,0:T(8,128)S(1)} %get-tuple-element.53), channel_id=1, source_target_pairs={{0,1},{1,0},{2,3},{3,2},{4,5},{5,4},{6,7},{7,6},{8,9},{9,8},{10,11... | collective-permute-start | bytes 196616 | tf_op jit(solution)/shard_map/ppermute | solution.py:76
  87.8 0.6 collective-permute-start.36
  88.4 1.7 %collective-permute-start.37 = (f32[64,256]{1,0:T(8,128)S(1)}, f32[64,256]{1,0:T(8,128)S(1)}, u32[]{:S(2)}, u32[]{:S(2)}) collective-permute-start(f32[64,256]{1,0:T(8,128)S(1)} %get-tuple-element.55), channel_id=1, source_target_pairs={{0,3},{1,2},{2,1},{3,0},{4,7},{5,6},{6,5},{7,4},{8,11},{9,10},{10,... | collective-permute-start | bytes 196616 | tf_op jit(solution)/shard_map/ppermute | solution.py:76
  90.1 4.5 %collective-permute-done.33.refs_2_ = bf16[144,512]{1,0:T(8,128)(2,1)S(1)} collective-permute-done((bf16[144,512]{1,0:T(8,128)(2,1)S(1)}, bf16[144,512]{1,0:T(8,128)(2,1)S(1)}, u32[]{:S(2)}, u32[]{:S(2)}) %collective-permute-start.33) | collective-permute-done | bytes 147488 | tf_op jit(solution)/shard_map/ppermute | solution.py:65
  94.6 3.1 %shard_map.105 = (bf16[128,1024]{1,0:T(8,128)(2,1)}, bf16[128,1024]{1,0:T(8,128)(2,1)}) custom-call(s32[3]{0:T(128)S(1)} %pad_add_fusion.place_ref, bf16[144,512]{1,0:T(8,128)(2,1)S(1)} %get-tuple-element.45.refs_0_, bf16[144,512]{1,0:T(8,128)(2,1)S(1)} %collective-permute-done.32.refs_1_, bf16[144,512]{1,0:T(8,128)(2,1)S(1)} %collective-permute-done.33.refs_2_, ...), custom_call_target="tpu_custom_call" | custom-call | tf_op jit(solution)/shard_map/pallas_call | solution.py:369
  97.8 0.6 slice_bitcast_fusion
  (37 shorter events, 0.1 us)
Async XLA Ops:
  0.6 1.2 %copy-start = (bf16[4096,1]{0,1:T(2,128)(2,1)S(1)}, bf16[4096,1]{0,1:T(2,128)(2,1)}, u32[]{:S(2)}) copy-start(bf16[4096,1]{0,1:T(2,128)(2,1)} %param.9) | copy-start | bytes 24580
  0.7 1.2 %copy-start.5 = (bf16[512,128]{1,0:T(8,128)(2,1)S(1)}, bf16[512,128]{1,0:T(8,128)(2,1)}, u32[]{:S(2)}) copy-start(bf16[512,128]{1,0:T(8,128)(2,1)} %param.10) | copy-start | bytes 393220
  0.7 34.3 %copy-start.2 = (bf16[1,128,1024]{2,1,0:T(8,128)(2,1)S(1)}, bf16[1,128,1024]{2,1,0:T(8,128)(2,1)}, u32[]{:S(2)}) copy-start(bf16[1,128,1024]{2,1,0:T(8,128)(2,1)} %param.13) | copy-start | bytes 786436
  1.8 33.2 %copy-start.1 = (bf16[1,128,1024]{2,1,0:T(8,128)(2,1)S(1)}, bf16[1,128,1024]{2,1,0:T(8,128)(2,1)}, u32[]{:S(2)}) copy-start(bf16[1,128,1024]{2,1,0:T(8,128)(2,1)} %param.7) | copy-start | bytes 786436
  2.0 1.4 %collective-permute-start = (bf16[528,128]{1,0:T(8,128)(2,1)S(1)}, bf16[528,128]{1,0:T(8,128)(2,1)S(1)}, u32[]{:S(2)}, u32[]{:S(2)}) collective-permute-start(bf16[528,128]{1,0:T(8,128)(2,1)S(1)} %fusion.1), channel_id=1, source_target_pairs={{0,0},{1,1},{2,4},{3,5},{4,2},{5,3},{6,6},{7,7},{8,16},{9,17},{10,... | collective-permute-start | bytes 405512 | tf_op jit(solution)/shard_map/ppermute | solution.py:400
  2.6 16.1 %collective-permute-start.12 = (bf16[768,128]{1,0:T(8,128)(2,1)S(1)}, bf16[768,128]{1,0:T(8,128)(2,1)S(1)}, u32[]{:S(2)}, u32[]{:S(2)}) collective-permute-start(bf16[768,128]{1,0:T(8,128)(2,1)S(1)} %bitcast.28), channel_id=1, source_target_pairs={{0,0},{1,1},{2,4},{3,5},{4,2},{5,3},{6,6},{7,7},{8,16},{9,17},{10,... | collective-permute-start | bytes 589832 | tf_op jit(solution)/shard_map/ppermute | solution.py:400
  3.3 19.4 %collective-permute-start.1 = (bf16[528,128]{1,0:T(8,128)(2,1)S(1)}, bf16[528,128]{1,0:T(8,128)(2,1)S(1)}, u32[]{:S(2)}, u32[]{:S(2)}) collective-permute-start(bf16[528,128]{1,0:T(8,128)(2,1)S(1)} %collective-permute-done.refs_0_.refs_4_), channel_id=1, source_target_pairs={{1,0},{0,1},{3,2},{2,3},{5,4},{4,5},{7,6},{6,7},{9,8},{8,9},{11,10... | collective-permute-start | bytes 405512 | tf_op jit(solution)/shard_map/ppermute | solution.py:65
  6.3 22.8 %collective-permute-start.2 = (bf16[528,128]{1,0:T(8,128)(2,1)S(1)}, bf16[528,128]{1,0:T(8,128)(2,1)S(1)}, u32[]{:S(2)}, u32[]{:S(2)}) collective-permute-start(bf16[528,128]{1,0:T(8,128)(2,1)S(1)} %collective-permute-done.refs_0_.refs_4_), channel_id=1, source_target_pairs={{2,0},{3,1},{0,2},{1,3},{6,4},{7,5},{4,6},{5,7},{10,8},{11,9},{8,1... | collective-permute-start | bytes 405512 | tf_op jit(solution)/shard_map/ppermute | solution.py:65
  16.7 12.4 %collective-permute-start.20 = (bf16[768,128]{1,0:T(8,128)(2,1)S(1)}, bf16[768,128]{1,0:T(8,128)(2,1)S(1)}, u32[]{:S(2)}, u32[]{:S(2)}) collective-permute-start(bf16[768,128]{1,0:T(8,128)(2,1)S(1)} %bitcast.27), channel_id=1, source_target_pairs={{0,0},{1,1},{2,4},{3,5},{4,2},{5,3},{6,6},{7,7},{8,16},{9,17},{10,... | collective-permute-start | bytes 589832 | tf_op jit(solution)/shard_map/ppermute | solution.py:400
  17.4 13.2 %collective-permute-start.3 = (bf16[528,128]{1,0:T(8,128)(2,1)S(1)}, bf16[528,128]{1,0:T(8,128)(2,1)S(1)}, u32[]{:S(2)}, u32[]{:S(2)}) collective-permute-start(bf16[528,128]{1,0:T(8,128)(2,1)S(1)} %collective-permute-done.refs_0_.refs_4_), channel_id=1, source_target_pairs={{3,0},{2,1},{1,2},{0,3},{7,4},{6,5},{5,6},{4,7},{11,8},{10,9},{9,1... | collective-permute-start | bytes 405512 | tf_op jit(solution)/shard_map/ppermute | solution.py:65
  18.7 14.4 %collective-permute-start.4 = (bf16[528,128]{1,0:T(8,128)(2,1)S(1)}, bf16[528,128]{1,0:T(8,128)(2,1)S(1)}, u32[]{:S(2)}, u32[]{:S(2)}) collective-permute-start(bf16[528,128]{1,0:T(8,128)(2,1)S(1)} %collective-permute-done.refs_0_.refs_4_), channel_id=1, source_target_pairs={{16,0},{0,16},{17,1},{1,17},{18,2},{2,18},{19,3},{3,19},{20,4},{4,... | collective-permute-start | bytes 405512 | tf_op jit(solution)/shard_map/ppermute | solution.py:65
  22.7 10.5 %collective-permute-start.5 = (bf16[528,128]{1,0:T(8,128)(2,1)S(1)}, bf16[528,128]{1,0:T(8,128)(2,1)S(1)}, u32[]{:S(2)}, u32[]{:S(2)}) collective-permute-start(bf16[528,128]{1,0:T(8,128)(2,1)S(1)} %collective-permute-done.1.refs_1_.refs_5_), channel_id=1, source_target_pairs={{16,0},{0,16},{17,1},{1,17},{18,2},{2,18},{19,3},{3,19},{20,4},{4,... | collective-permute-start | bytes 405512 | tf_op jit(solution)/shard_map/ppermute | solution.py:65
  29.1 4.6 %collective-permute-start.6 = (bf16[528,128]{1,0:T(8,128)(2,1)S(1)}, bf16[528,128]{1,0:T(8,128)(2,1)S(1)}, u32[]{:S(2)}, u32[]{:S(2)}) collective-permute-start(bf16[528,128]{1,0:T(8,128)(2,1)S(1)} %collective-permute-done.2.refs_2_.refs_6_), channel_id=1, source_target_pairs={{16,0},{0,16},{17,1},{1,17},{18,2},{2,18},{19,3},{3,19},{20,4},{4,... | collective-permute-start | bytes 405512 | tf_op jit(solution)/shard_map/ppermute | solution.py:65
  29.1 9.2 %collective-permute-start.13 = (bf16[768,128]{1,0:T(8,128)(2,1)S(1)}, bf16[768,128]{1,0:T(8,128)(2,1)S(1)}, u32[]{:S(2)}, u32[]{:S(2)}) collective-permute-start(bf16[768,128]{1,0:T(8,128)(2,1)S(1)} %collective-permute-done.12.refs_0_.refs_12_), channel_id=1, source_target_pairs={{1,0},{0,1},{3,2},{2,3},{5,4},{4,5},{7,6},{6,7},{9,8},{8,9},{11,10... | collective-permute-start | bytes 589832 | tf_op jit(solution)/shard_map/ppermute | solution.py:65
  30.6 8.2 %collective-permute-start.22 = (bf16[768,128]{1,0:T(8,128)(2,1)S(1)}, bf16[768,128]{1,0:T(8,128)(2,1)S(1)}, u32[]{:S(2)}, u32[]{:S(2)}) collective-permute-start(bf16[768,128]{1,0:T(8,128)(2,1)S(1)} %collective-permute-done.20.refs_8_.refs_20_), channel_id=1, source_target_pairs={{2,0},{3,1},{0,2},{1,3},{6,4},{7,5},{4,6},{5,7},{10,8},{11,9},{8,1... | collective-permute-start | bytes 589832 | tf_op jit(solution)/shard_map/ppermute | solution.py:65
  33.1 9.5 %collective-permute-start.14 = (bf16[768,128]{1,0:T(8,128)(2,1)S(1)}, bf16[768,128]{1,0:T(8,128)(2,1)S(1)}, u32[]{:S(2)}, u32[]{:S(2)}) collective-permute-start(bf16[768,128]{1,0:T(8,128)(2,1)S(1)} %collective-permute-done.12.refs_0_.refs_12_), channel_id=1, source_target_pairs={{2,0},{3,1},{0,2},{1,3},{6,4},{7,5},{4,6},{5,7},{10,8},{11,9},{8,1... | collective-permute-start | bytes 589832 | tf_op jit(solution)/shard_map/ppermute | solution.py:65
  33.2 9.4 %collective-permute-start.21 = (bf16[768,128]{1,0:T(8,128)(2,1)S(1)}, bf16[768,128]{1,0:T(8,128)(2,1)S(1)}, u32[]{:S(2)}, u32[]{:S(2)}) collective-permute-start(bf16[768,128]{1,0:T(8,128)(2,1)S(1)} %collective-permute-done.20.refs_8_.refs_20_), channel_id=1, source_target_pairs={{1,0},{0,1},{3,2},{2,3},{5,4},{4,5},{7,6},{6,7},{9,8},{8,9},{11,10... | collective-permute-start | bytes 589832 | tf_op jit(solution)/shard_map/ppermute | solution.py:65
  33.7 1.4 %collective-permute-start.7 = (bf16[528,128]{1,0:T(8,128)(2,1)S(1)}, bf16[528,128]{1,0:T(8,128)(2,1)S(1)}, u32[]{:S(2)}, u32[]{:S(2)}) collective-permute-start(bf16[528,128]{1,0:T(8,128)(2,1)S(1)} %collective-permute-done.3.refs_3_.refs_7_), channel_id=1, source_target_pairs={{16,0},{0,16},{17,1},{1,17},{18,2},{2,18},{19,3},{3,19},{20,4},{4,... | collective-permute-start | bytes 405512 | tf_op jit(solution)/shard_map/ppermute | solution.py:65
  36.4 6.7 %collective-permute-start.10 = (bf16[144,128]{1,0:T(8,128)(2,1)S(1)}, bf16[144,128]{1,0:T(8,128)(2,1)S(1)}, u32[]{:S(2)}, u32[]{:S(2)}) collective-permute-start(bf16[144,128]{1,0:T(8,128)(2,1)S(1)} %get-tuple-element.37), channel_id=1, source_target_pairs={{0,12},{4,8},{8,4},{12,0},{1,13},{5,9},{9,5},{13,1},{2,14},{6,10},... | collective-permute-start | bytes 110600 | tf_op jit(solution)/shard_map/ppermute | solution.py:76
  38.3 6.5 %collective-permute-start.8 = (bf16[144,128]{1,0:T(8,128)(2,1)S(1)}, bf16[144,128]{1,0:T(8,128)(2,1)S(1)}, u32[]{:S(2)}, u32[]{:S(2)}) collective-permute-start(bf16[144,128]{1,0:T(8,128)(2,1)S(1)} %get-tuple-element.35), channel_id=1, source_target_pairs={{0,4},{4,0},{8,12},{12,8},{1,5},{5,1},{9,13},{13,9},{2,6},{6,2},{1... | collective-permute-start | bytes 110600 | tf_op jit(solution)/shard_map/ppermute | solution.py:76
  38.8 6.1 %collective-permute-start.9 = (bf16[144,128]{1,0:T(8,128)(2,1)S(1)}, bf16[144,128]{1,0:T(8,128)(2,1)S(1)}, u32[]{:S(2)}, u32[]{:S(2)}) collective-permute-start(bf16[144,128]{1,0:T(8,128)(2,1)S(1)} %get-tuple-element.36), channel_id=1, source_target_pairs={{0,8},{4,12},{8,0},{12,4},{1,9},{5,13},{9,1},{13,5},{2,10},{6,14},... | collective-permute-start | bytes 110600 | tf_op jit(solution)/shard_map/ppermute | solution.py:76
  42.6 3.5 %collective-permute-start.16 = (bf16[768,128]{1,0:T(8,128)(2,1)S(1)}, bf16[768,128]{1,0:T(8,128)(2,1)S(1)}, u32[]{:S(2)}, u32[]{:S(2)}) collective-permute-start(bf16[768,128]{1,0:T(8,128)(2,1)S(1)} %collective-permute-done.12.refs_0_.refs_12_), channel_id=1, source_target_pairs={{16,0},{0,16},{17,1},{1,17},{18,2},{2,18},{19,3},{3,19},{20,4},{4,... | collective-permute-start | bytes 589832 | tf_op jit(solution)/shard_map/ppermute | solution.py:65
  42.6 3.8 %collective-permute-start.24 = (bf16[768,128]{1,0:T(8,128)(2,1)S(1)}, bf16[768,128]{1,0:T(8,128)(2,1)S(1)}, u32[]{:S(2)}, u32[]{:S(2)}) collective-permute-start(bf16[768,128]{1,0:T(8,128)(2,1)S(1)} %collective-permute-done.20.refs_8_.refs_20_), channel_id=1, source_target_pairs={{16,0},{0,16},{17,1},{1,17},{18,2},{2,18},{19,3},{3,19},{20,4},{4,... | collective-permute-start | bytes 589832 | tf_op jit(solution)/shard_map/ppermute | solution.py:65
  43.1 6.9 %collective-permute-start.15 = (bf16[768,128]{1,0:T(8,128)(2,1)S(1)}, bf16[768,128]{1,0:T(8,128)(2,1)S(1)}, u32[]{:S(2)}, u32[]{:S(2)}) collective-permute-start(bf16[768,128]{1,0:T(8,128)(2,1)S(1)} %collective-permute-done.13.refs_1_.refs_13_), channel_id=1, source_target_pairs={{2,0},{3,1},{0,2},{1,3},{6,4},{7,5},{4,6},{5,7},{10,8},{11,9},{8,1... | collective-permute-start | bytes 589832 | tf_op jit(solution)/shard_map/ppermute | solution.py:65
  44.8 7.3 %collective-permute-start.17 = (bf16[768,128]{1,0:T(8,128)(2,1)S(1)}, bf16[768,128]{1,0:T(8,128)(2,1)S(1)}, u32[]{:S(2)}, u32[]{:S(2)}) collective-permute-start(bf16[768,128]{1,0:T(8,128)(2,1)S(1)} %collective-permute-done.13.refs_1_.refs_13_), channel_id=1, source_target_pairs={{16,0},{0,16},{17,1},{1,17},{18,2},{2,18},{19,3},{3,19},{20,4},{4,... | collective-permute-start | bytes 589832 | tf_op jit(solution)/shard_map/ppermute | solution.py:65
  44.9 7.3 %collective-permute-start.23 = (bf16[768,128]{1,0:T(8,128)(2,1)S(1)}, bf16[768,128]{1,0:T(8,128)(2,1)S(1)}, u32[]{:S(2)}, u32[]{:S(2)}) collective-permute-start(bf16[768,128]{1,0:T(8,128)(2,1)S(1)} %collective-permute-done.22.refs_10_.refs_22_), channel_id=1, source_target_pairs={{1,0},{0,1},{3,2},{2,3},{5,4},{4,5},{7,6},{6,7},{9,8},{8,9},{11,10... | collective-permute-start | bytes 589832 | tf_op jit(solution)/shard_map/ppermute | solution.py:65
  46.1 1.3 %collective-permute-start.11 = (f32[144,128]{1,0:T(8,128)S(1)}, f32[144,128]{1,0:T(8,128)S(1)}, u32[]{:S(2)}, u32[]{:S(2)}) collective-permute-start(f32[144,128]{1,0:T(8,128)S(1)} %convert_add_fusion.1.refs_2_), channel_id=1, source_target_pairs={{16,0},{0,16},{17,1},{1,17},{18,2},{2,18},{19,3},{3,19},{20,4},{4,... | collective-permute-start | bytes 221192 | tf_op jit(solution)/shard_map/ppermute | solution.py:65
  46.3 6.3 %collective-permute-start.26 = (bf16[768,128]{1,0:T(8,128)(2,1)S(1)}, bf16[768,128]{1,0:T(8,128)(2,1)S(1)}, u32[]{:S(2)}, u32[]{:S(2)}) collective-permute-start(bf16[768,128]{1,0:T(8,128)(2,1)S(1)} %collective-permute-done.22.refs_10_.refs_22_), channel_id=1, source_target_pairs={{16,0},{0,16},{17,1},{1,17},{18,2},{2,18},{19,3},{3,19},{20,4},{4,... | collective-permute-start | bytes 589832 | tf_op jit(solution)/shard_map/ppermute | solution.py:65
  47.5 5.2 %collective-permute-start.18 = (bf16[768,128]{1,0:T(8,128)(2,1)S(1)}, bf16[768,128]{1,0:T(8,128)(2,1)S(1)}, u32[]{:S(2)}, u32[]{:S(2)}) collective-permute-start(bf16[768,128]{1,0:T(8,128)(2,1)S(1)} %collective-permute-done.14.refs_2_.refs_14_), channel_id=1, source_target_pairs={{16,0},{0,16},{17,1},{1,17},{18,2},{2,18},{19,3},{3,19},{20,4},{4,... | collective-permute-start | bytes 589832 | tf_op jit(solution)/shard_map/ppermute | solution.py:65
  50.0 2.7 %collective-permute-start.25 = (bf16[768,128]{1,0:T(8,128)(2,1)S(1)}, bf16[768,128]{1,0:T(8,128)(2,1)S(1)}, u32[]{:S(2)}, u32[]{:S(2)}) collective-permute-start(bf16[768,128]{1,0:T(8,128)(2,1)S(1)} %collective-permute-done.21.refs_9_.refs_21_), channel_id=1, source_target_pairs={{16,0},{0,16},{17,1},{1,17},{18,2},{2,18},{19,3},{3,19},{20,4},{4,... | collective-permute-start | bytes 589832 | tf_op jit(solution)/shard_map/ppermute | solution.py:65
  52.2 1.4 %collective-permute-start.19 = (bf16[768,128]{1,0:T(8,128)(2,1)S(1)}, bf16[768,128]{1,0:T(8,128)(2,1)S(1)}, u32[]{:S(2)}, u32[]{:S(2)}) collective-permute-start(bf16[768,128]{1,0:T(8,128)(2,1)S(1)} %collective-permute-done.15.refs_3_.refs_15_), channel_id=1, source_target_pairs={{16,0},{0,16},{17,1},{1,17},{18,2},{2,18},{19,3},{3,19},{20,4},{4,... | collective-permute-start | bytes 589832 | tf_op jit(solution)/shard_map/ppermute | solution.py:65
  52.2 1.7 %collective-permute-start.27 = (bf16[768,128]{1,0:T(8,128)(2,1)S(1)}, bf16[768,128]{1,0:T(8,128)(2,1)S(1)}, u32[]{:S(2)}, u32[]{:S(2)}) collective-permute-start(bf16[768,128]{1,0:T(8,128)(2,1)S(1)} %collective-permute-done.23.refs_11_.refs_23_), channel_id=1, source_target_pairs={{16,0},{0,16},{17,1},{1,17},{18,2},{2,18},{19,3},{3,19},{20,4},{4,... | collective-permute-start | bytes 589832 | tf_op jit(solution)/shard_map/ppermute | solution.py:65
  55.3 6.2 %collective-permute-start.28 = (bf16[128,384]{1,0:T(8,128)(2,1)S(1)}, bf16[128,384]{1,0:T(8,128)(2,1)S(1)}, u32[]{:S(2)}, u32[]{:S(2)}) collective-permute-start(bf16[128,384]{1,0:T(8,128)(2,1)S(1)} %get-tuple-element.42), channel_id=1, source_target_pairs={{0,4},{4,0},{8,12},{12,8},{1,5},{5,1},{9,13},{13,9},{2,6},{6,2},{1... | collective-permute-start | bytes 294920 | tf_op jit(solution)/shard_map/ppermute | solution.py:76
  55.4 10.9 %collective-permute-start.29 = (bf16[128,384]{1,0:T(8,128)(2,1)S(1)}, bf16[128,384]{1,0:T(8,128)(2,1)S(1)}, u32[]{:S(2)}, u32[]{:S(2)}) collective-permute-start(bf16[128,384]{1,0:T(8,128)(2,1)S(1)} %get-tuple-element.43), channel_id=1, source_target_pairs={{0,8},{4,12},{8,0},{12,4},{1,9},{5,13},{9,1},{13,5},{2,10},{6,14},... | collective-permute-start | bytes 294920 | tf_op jit(solution)/shard_map/ppermute | solution.py:76
  56.0 10.3 %collective-permute-start.30 = (bf16[128,384]{1,0:T(8,128)(2,1)S(1)}, bf16[128,384]{1,0:T(8,128)(2,1)S(1)}, u32[]{:S(2)}, u32[]{:S(2)}) collective-permute-start(bf16[128,384]{1,0:T(8,128)(2,1)S(1)} %get-tuple-element.44), channel_id=1, source_target_pairs={{0,12},{4,8},{8,4},{12,0},{1,13},{5,9},{9,5},{13,1},{2,14},{6,10},... | collective-permute-start | bytes 294920 | tf_op jit(solution)/shard_map/ppermute | solution.py:76
  66.3 1.6 %copy-start.3 = (f32[1,128,512]{2,1,0:T(8,128)S(1)}, f32[1,128,512]{2,1,0:T(8,128)}, u32[]{:S(2)}) copy-start(f32[1,128,512]{2,1,0:T(8,128)} %param.11) | copy-start | bytes 786436
  66.3 1.6 %copy-start.4 = (f32[1,512,128]{2,1,0:T(8,128)S(1)}, f32[1,512,128]{2,1,0:T(8,128)}, u32[]{:S(2)}) copy-start(f32[1,512,128]{2,1,0:T(8,128)} %param.12) | copy-start | bytes 786436
  66.3 1.5 %collective-permute-start.31 = (f32[128,384]{1,0:T(8,128)S(1)}, f32[128,384]{1,0:T(8,128)S(1)}, u32[]{:S(2)}, u32[]{:S(2)}) collective-permute-start(f32[128,384]{1,0:T(8,128)S(1)} %convert_add_fusion.refs_0_), channel_id=1, source_target_pairs={{16,0},{0,16},{17,1},{1,17},{18,2},{2,18},{19,3},{3,19},{20,4},{4,... | collective-permute-start | bytes 589832 | tf_op jit(solution)/shard_map/ppermute | solution.py:65
  78.7 7.9 %collective-permute-start.32 = (bf16[144,512]{1,0:T(8,128)(2,1)S(1)}, bf16[144,512]{1,0:T(8,128)(2,1)S(1)}, u32[]{:S(2)}, u32[]{:S(2)}) collective-permute-start(bf16[144,512]{1,0:T(8,128)(2,1)S(1)} %get-tuple-element.45.refs_0_), channel_id=1, source_target_pairs={{4,0},{0,4},{12,8},{8,12},{5,1},{1,5},{13,9},{9,13},{6,2},{2,6},{1... | collective-permute-start | bytes 442376 | tf_op jit(solution)/shard_map/ppermute | solution.py:65
  80.7 13.9 %collective-permute-start.33 = (bf16[144,512]{1,0:T(8,128)(2,1)S(1)}, bf16[144,512]{1,0:T(8,128)(2,1)S(1)}, u32[]{:S(2)}, u32[]{:S(2)}) collective-permute-start(bf16[144,512]{1,0:T(8,128)(2,1)S(1)} %get-tuple-element.45.refs_0_), channel_id=1, source_target_pairs={{8,0},{12,4},{0,8},{4,12},{9,1},{13,5},{1,9},{5,13},{10,2},{14,6},... | collective-permute-start | bytes 442376 | tf_op jit(solution)/shard_map/ppermute | solution.py:65
  80.7 13.9 %collective-permute-start.34 = (bf16[144,512]{1,0:T(8,128)(2,1)S(1)}, bf16[144,512]{1,0:T(8,128)(2,1)S(1)}, u32[]{:S(2)}, u32[]{:S(2)}) collective-permute-start(bf16[144,512]{1,0:T(8,128)(2,1)S(1)} %get-tuple-element.45.refs_0_), channel_id=1, source_target_pairs={{12,0},{8,4},{4,8},{0,12},{13,1},{9,5},{5,9},{1,13},{14,2},{10,6},... | collective-permute-start | bytes 442376 | tf_op jit(solution)/shard_map/ppermute | solution.py:65
  86.6 11.2 %collective-permute-start.35 = (f32[64,256]{1,0:T(8,128)S(1)}, f32[64,256]{1,0:T(8,128)S(1)}, u32[]{:S(2)}, u32[]{:S(2)}) collective-permute-start(f32[64,256]{1,0:T(8,128)S(1)} %get-tuple-element.53), channel_id=1, source_target_pairs={{0,1},{1,0},{2,3},{3,2},{4,5},{5,4},{6,7},{7,6},{8,9},{9,8},{10,11... | collective-permute-start | bytes 196616 | tf_op jit(solution)/shard_map/ppermute | solution.py:76
  87.8 10.0 %collective-permute-start.36 = (f32[64,256]{1,0:T(8,128)S(1)}, f32[64,256]{1,0:T(8,128)S(1)}, u32[]{:S(2)}, u32[]{:S(2)}) collective-permute-start(f32[64,256]{1,0:T(8,128)S(1)} %get-tuple-element.54), channel_id=1, source_target_pairs={{0,2},{1,3},{2,0},{3,1},{4,6},{5,7},{6,4},{7,5},{8,10},{9,11},{10,... | collective-permute-start | bytes 196616 | tf_op jit(solution)/shard_map/ppermute | solution.py:76
  88.4 9.4 %collective-permute-start.37 = (f32[64,256]{1,0:T(8,128)S(1)}, f32[64,256]{1,0:T(8,128)S(1)}, u32[]{:S(2)}, u32[]{:S(2)}) collective-permute-start(f32[64,256]{1,0:T(8,128)S(1)} %get-tuple-element.55), channel_id=1, source_target_pairs={{0,3},{1,2},{2,1},{3,0},{4,7},{5,6},{6,5},{7,4},{8,11},{9,10},{10,... | collective-permute-start | bytes 196616 | tf_op jit(solution)/shard_map/ppermute | solution.py:76

commit v7 on v6

--- a/solution.py
+++ b/solution.py
@@ -414,6 +414,7 @@
         )
     )
     outer_w, first_w, second_w = swapped(outer), swapped(first), swapped(second)
+    outer_w, first_w = lax.optimization_barrier((outer_w, first_w))
     outer_near = peers_of(outer_w, "dp")
     first_near = [first_w, hop(first_w, "dp", 1), hop(first_w, "dp", 2)]
     second_near = [second_w, hop(second_w, "dp", 1), hop(second_w, "dp", 2)]

time: 98.6 us -> 101 us (1.024)
  starting transfers between devices: 46.6 us -> 54.1 us
  waiting for transfers between devices: 32.3 us -> 27 us
    ppermute x26, starting transfers between devices: 32.6 us -> 40.6 us  [hop(): lax.ppermute(array, axis, [(mate(i, step, count), i) for i in range(count)])]
    ppermute x26, waiting for transfers between devices: 25.8 us -> 18.9 us  [hop(): lax.ppermute(array, axis, [(mate(i, step, count), i) for i in range(count)])]
    ppermute x9, waiting for transfers between devices: 6.5 us -> 8.12 us  [sent_to(): lax.ppermute(arrays[j], axis, [(i, mate(i, j, count)) for i in range(coun...]
  transfers between devices with their start and end apart: 38 -> 38, of which waited for: 14 -> 13; matrix products, arithmetic and copies ran while one was open for 0% -> 0% of each run, Pallas kernels for 4% -> 4%
where the time goes in v7:
time: 101 us
  starting transfers between devices  54.1 us (54%)
  waiting for transfers between devices  27 us (27%)
  Pallas kernels  16.7 us (17%)
  local copies, waits for them, and re-layouts  1.77 us (2%)
    ppermute x26, starting transfers between devices, hop(): lax.ppermute(array, axis, [(mate(i, step, count), i) for i in range(count)])  40.6 us
    ppermute x26, waiting for transfers between devices, hop(): lax.ppermute(array, axis, [(mate(i, step, count), i) for i in range(count)])  18.9 us
    pallas_call x4, Pallas kernels, call(): pl.pallas_call(kernel, out_shape=outs, in_specs=[SMEM] + [VMEM] * (len(op...  16.7 us
    ppermute x9, starting transfers between devices, sent_to(): lax.ppermute(arrays[j], axis, [(i, mate(i, j, count)) for i in range(coun...  11.5 us
    ppermute x9, waiting for transfers between devices, sent_to(): lax.ppermute(arrays[j], axis, [(i, mate(i, j, count)) for i in range(coun...  8.12 us
  transfers between devices with their start and end apart: 38, of which 13 were waited for; matrix products, arithmetic and copies ran while one was open for 0% of the time, Pallas kernels for 4%

profile of v7, /device:TPU:0, one launch (start us, length us, event | category | flops | bytes accessed | tf_op | source)
XLA Modules:
  0.0 100.7 jit_solution(5203306086134692399)
XLA Ops:
  0.6 0.0 copy-start
  0.7 0.1 pad_add_fusion.place_ref
  0.7 1.1 %fusion.2 = (bf16[3,256,128]{2,1,0:T(8,128)(2,1)S(1)}, bf16[3,256,128]{2,1,0:T(8,128)(2,1)S(1)}) fusion(bf16[3,512,128]{2,1,0:T(8,128)(2,1)} %bitcast.26), kind=kLoop, calls=%fused_computation.10 | loop fusion | bytes 786432 | tf_op jit(solution)/shard_map/slice | solution.py:412
  1.8 0.0 copy-start.1
  1.9 0.1 reduce
  2.0 0.7 collective-permute-start.1
  2.6 0.7 collective-permute-start
  3.3 0.0 collective-permute-done.refs_0_.refs_4_
  3.3 0.0 collective-permute-done.1.refs_0_.refs_12_
  3.3 3.0 %collective-permute-start.2 = (bf16[528,128]{1,0:T(8,128)(2,1)S(1)}, bf16[528,128]{1,0:T(8,128)(2,1)S(1)}, u32[]{:S(2)}, u32[]{:S(2)}) collective-permute-start(bf16[528,128]{1,0:T(8,128)(2,1)S(1)} %collective-permute-done.refs_0_.refs_4_), channel_id=1, source_target_pairs={{1,0},{0,1},{3,2},{2,3},{5,4},{4,5},{7,6},{6,7},{9,8},{8,9},{11,10... | collective-permute-start | bytes 405512 | tf_op jit(solution)/shard_map/ppermute | solution.py:65
  6.3 16.7 %collective-permute-start.3 = (bf16[528,128]{1,0:T(8,128)(2,1)S(1)}, bf16[528,128]{1,0:T(8,128)(2,1)S(1)}, u32[]{:S(2)}, u32[]{:S(2)}) collective-permute-start(bf16[528,128]{1,0:T(8,128)(2,1)S(1)} %collective-permute-done.refs_0_.refs_4_), channel_id=1, source_target_pairs={{2,0},{3,1},{0,2},{1,3},{6,4},{7,5},{4,6},{5,7},{10,8},{11,9},{8,1... | collective-permute-start | bytes 405512 | tf_op jit(solution)/shard_map/ppermute | solution.py:65
  23.1 0.7 collective-permute-start.20
  23.7 1.3 %collective-permute-start.4 = (bf16[528,128]{1,0:T(8,128)(2,1)S(1)}, bf16[528,128]{1,0:T(8,128)(2,1)S(1)}, u32[]{:S(2)}, u32[]{:S(2)}) collective-permute-start(bf16[528,128]{1,0:T(8,128)(2,1)S(1)} %collective-permute-done.refs_0_.refs_4_), channel_id=1, source_target_pairs={{3,0},{2,1},{1,2},{0,3},{7,4},{6,5},{5,6},{4,7},{11,8},{10,9},{9,1... | collective-permute-start | bytes 405512 | tf_op jit(solution)/shard_map/ppermute | solution.py:65
  25.0 1.2 %collective-permute-start.5 = (bf16[528,128]{1,0:T(8,128)(2,1)S(1)}, bf16[528,128]{1,0:T(8,128)(2,1)S(1)}, u32[]{:S(2)}, u32[]{:S(2)}) collective-permute-start(bf16[528,128]{1,0:T(8,128)(2,1)S(1)} %collective-permute-done.refs_0_.refs_4_), channel_id=1, source_target_pairs={{16,0},{0,16},{17,1},{1,17},{18,2},{2,18},{19,3},{3,19},{20,4},{4,... | collective-permute-start | bytes 405512 | tf_op jit(solution)/shard_map/ppermute | solution.py:65
  26.3 0.0 collective-permute-start.6
  26.3 0.0 collective-permute-done.3.refs_2_.refs_6_
  26.3 0.5 collective-permute-start.7
  26.8 1.5 %collective-permute-start.13 = (bf16[768,128]{1,0:T(8,128)(2,1)S(1)}, bf16[768,128]{1,0:T(8,128)(2,1)S(1)}, u32[]{:S(2)}, u32[]{:S(2)}) collective-permute-start(bf16[768,128]{1,0:T(8,128)(2,1)S(1)} %collective-permute-done.1.refs_0_.refs_12_), channel_id=1, source_target_pairs={{1,0},{0,1},{3,2},{2,3},{5,4},{4,5},{7,6},{6,7},{9,8},{8,9},{11,10... | collective-permute-start | bytes 589832 | tf_op jit(solution)/shard_map/ppermute | solution.py:65
  28.3 2.4 %collective-permute-done.4.refs_3_.refs_7_ = bf16[528,128]{1,0:T(8,128)(2,1)S(1)} collective-permute-done((bf16[528,128]{1,0:T(8,128)(2,1)S(1)}, bf16[528,128]{1,0:T(8,128)(2,1)S(1)}, u32[]{:S(2)}, u32[]{:S(2)}) %collective-permute-start.4) | collective-permute-done | bytes 135200 | tf_op jit(solution)/shard_map/ppermute | solution.py:65
  30.7 5.9 %collective-permute-start.14 = (bf16[768,128]{1,0:T(8,128)(2,1)S(1)}, bf16[768,128]{1,0:T(8,128)(2,1)S(1)}, u32[]{:S(2)}, u32[]{:S(2)}) collective-permute-start(bf16[768,128]{1,0:T(8,128)(2,1)S(1)} %collective-permute-done.1.refs_0_.refs_12_), channel_id=1, source_target_pairs={{2,0},{3,1},{0,2},{1,3},{6,4},{7,5},{4,6},{5,7},{10,8},{11,9},{8,1... | collective-permute-start | bytes 589832 | tf_op jit(solution)/shard_map/ppermute | solution.py:65
  36.7 0.0 collective-permute-start.16
  36.7 0.0 collective-permute-done.6.refs_5_.refs_9_
  36.7 0.2 collective-permute-start.22
  36.8 0.0 collective-permute-done.7.refs_6_.refs_10_
  36.8 0.4 collective-permute-start.8
  37.3 1.0 %collective-permute-done.8.refs_7_.refs_11_ = bf16[528,128]{1,0:T(8,128)(2,1)S(1)} collective-permute-done((bf16[528,128]{1,0:T(8,128)(2,1)S(1)}, bf16[528,128]{1,0:T(8,128)(2,1)S(1)}, u32[]{:S(2)}, u32[]{:S(2)}) %collective-permute-start.8) | collective-permute-done | bytes 135200 | tf_op jit(solution)/shard_map/ppermute | solution.py:65
  38.3 1.3 %shard_map.102 = (bf16[144,128]{1,0:T(8,128)(2,1)S(1)}, bf16[144,128]{1,0:T(8,128)(2,1)S(1)}, bf16[144,128]{1,0:T(8,128)(2,1)S(1)}, bf16[144,128]{1,0:T(8,128)(2,1)S(1)}) custom-call(s32[3]{0:T(128)S(1)} %pad_add_fusion.place_ref, bf16[128,1024]{1,0:T(8,128)(2,1)S(1)} %bitcast.21, bf16[128,1024]{1,0:T(8,128)(2,1)S(1)} %bitcast.23, ...), custom_call_target="tpu_custom_call" | custom-call | tf_op jit(solution)/shard_map/pallas_call | solution.py:369
  39.6 0.1 collective-permute-start.10
  39.7 0.0 collective-permute-done.13.refs_1_.refs_13_
  39.7 2.2 %collective-permute-start.11 = (bf16[144,128]{1,0:T(8,128)(2,1)S(1)}, bf16[144,128]{1,0:T(8,128)(2,1)S(1)}, u32[]{:S(2)}, u32[]{:S(2)}) collective-permute-start(bf16[144,128]{1,0:T(8,128)(2,1)S(1)} %get-tuple-element.41), channel_id=1, source_target_pairs={{0,12},{4,8},{8,4},{12,0},{1,13},{5,9},{9,5},{13,1},{2,14},{6,10},... | collective-permute-start | bytes 110600 | tf_op jit(solution)/shard_map/ppermute | solution.py:76
  41.9 1.3 %collective-permute-start.9 = (bf16[144,128]{1,0:T(8,128)(2,1)S(1)}, bf16[144,128]{1,0:T(8,128)(2,1)S(1)}, u32[]{:S(2)}, u32[]{:S(2)}) collective-permute-start(bf16[144,128]{1,0:T(8,128)(2,1)S(1)} %get-tuple-element.39), channel_id=1, source_target_pairs={{0,4},{4,0},{8,12},{12,8},{1,5},{5,1},{9,13},{13,9},{2,6},{6,2},{1... | collective-permute-start | bytes 110600 | tf_op jit(solution)/shard_map/ppermute | solution.py:76
  43.2 1.5 %collective-permute-start.21 = (bf16[768,128]{1,0:T(8,128)(2,1)S(1)}, bf16[768,128]{1,0:T(8,128)(2,1)S(1)}, u32[]{:S(2)}, u32[]{:S(2)}) collective-permute-start(bf16[768,128]{1,0:T(8,128)(2,1)S(1)} %collective-permute-done.20.refs_8_.refs_20_), channel_id=1, source_target_pairs={{1,0},{0,1},{3,2},{2,3},{5,4},{4,5},{7,6},{6,7},{9,8},{8,9},{11,10... | collective-permute-start | bytes 589832 | tf_op jit(solution)/shard_map/ppermute | solution.py:65
  44.7 1.0 %collective-permute-done.10 = bf16[144,128]{1,0:T(8,128)(2,1)S(1)} collective-permute-done((bf16[144,128]{1,0:T(8,128)(2,1)S(1)}, bf16[144,128]{1,0:T(8,128)(2,1)S(1)}, u32[]{:S(2)}, u32[]{:S(2)}) %collective-permute-start.10) | collective-permute-done | bytes 36896 | tf_op jit(solution)/shard_map/ppermute | solution.py:76
  45.7 1.0 %collective-permute-start.15 = (bf16[768,128]{1,0:T(8,128)(2,1)S(1)}, bf16[768,128]{1,0:T(8,128)(2,1)S(1)}, u32[]{:S(2)}, u32[]{:S(2)}) collective-permute-start(bf16[768,128]{1,0:T(8,128)(2,1)S(1)} %collective-permute-done.13.refs_1_.refs_13_), channel_id=1, source_target_pairs={{2,0},{3,1},{0,2},{1,3},{6,4},{7,5},{4,6},{5,7},{10,8},{11,9},{8,1... | collective-permute-start | bytes 589832 | tf_op jit(solution)/shard_map/ppermute | solution.py:65
  46.8 0.0 collective-permute-done.11
  46.8 0.0 collective-permute-start.17
  46.8 1.6 %collective-permute-start.23 = (bf16[768,128]{1,0:T(8,128)(2,1)S(1)}, bf16[768,128]{1,0:T(8,128)(2,1)S(1)}, u32[]{:S(2)}, u32[]{:S(2)}) collective-permute-start(bf16[768,128]{1,0:T(8,128)(2,1)S(1)} %collective-permute-done.22.refs_10_.refs_22_), channel_id=1, source_target_pairs={{1,0},{0,1},{3,2},{2,3},{5,4},{4,5},{7,6},{6,7},{9,8},{8,9},{11,10... | collective-permute-start | bytes 589832 | tf_op jit(solution)/shard_map/ppermute | solution.py:65
  48.3 1.1 %collective-permute-done.21.refs_9_.refs_21_ = bf16[768,128]{1,0:T(8,128)(2,1)S(1)} collective-permute-done((bf16[768,128]{1,0:T(8,128)(2,1)S(1)}, bf16[768,128]{1,0:T(8,128)(2,1)S(1)}, u32[]{:S(2)}, u32[]{:S(2)}) %collective-permute-start.21) | collective-permute-done | bytes 196640 | tf_op jit(solution)/shard_map/ppermute | solution.py:65
  49.5 0.5 collective-permute-start.26
  50.0 0.8 collective-permute-done.12.refs_3_
  50.7 0.2 collective-permute-start.18
  50.9 1.2 %collective-permute-done.15.refs_3_.refs_15_ = bf16[768,128]{1,0:T(8,128)(2,1)S(1)} collective-permute-done((bf16[768,128]{1,0:T(8,128)(2,1)S(1)}, bf16[768,128]{1,0:T(8,128)(2,1)S(1)}, u32[]{:S(2)}, u32[]{:S(2)}) %collective-permute-start.15) | collective-permute-done | bytes 196640 | tf_op jit(solution)/shard_map/ppermute | solution.py:65
  52.1 0.5 collective-permute-start.19
  52.6 1.5 %collective-permute-done.23.refs_11_.refs_23_ = bf16[768,128]{1,0:T(8,128)(2,1)S(1)} collective-permute-done((bf16[768,128]{1,0:T(8,128)(2,1)S(1)}, bf16[768,128]{1,0:T(8,128)(2,1)S(1)}, u32[]{:S(2)}, u32[]{:S(2)}) %collective-permute-start.23) | collective-permute-done | bytes 196640 | tf_op jit(solution)/shard_map/ppermute | solution.py:65
  54.1 1.4 %collective-permute-done.27.refs_15_.refs_27_ = bf16[768,128]{1,0:T(8,128)(2,1)S(1)} collective-permute-done((bf16[768,128]{1,0:T(8,128)(2,1)S(1)}, bf16[768,128]{1,0:T(8,128)(2,1)S(1)}, u32[]{:S(2)}, u32[]{:S(2)}) %collective-permute-start.27) | collective-permute-done | bytes 196640 | tf_op jit(solution)/shard_map/ppermute | solution.py:65
  55.5 1.4 %shard_map.103 = (bf16[128,384]{1,0:T(8,128)(2,1)S(1)}, bf16[128,384]{1,0:T(8,128)(2,1)S(1)}, bf16[128,384]{1,0:T(8,128)(2,1)S(1)}, bf16[128,384]{1,0:T(8,128)(2,1)S(1)}) custom-call(s32[3]{0:T(128)S(1)} %pad_add_fusion.place_ref, bf16[128,1024]{1,0:T(8,128)(2,1)S(1)} %bitcast.22, bf16[768,128]{1,0:T(8,128)(2,1)S(1)} %collective-permute-done.1.refs_0_.refs_12_, ...), custom_call_target="tpu_custom_call" | custom-call | tf_op jit(solution)/shard_map/pallas_call | solution.py:369
  57.0 1.2 %collective-permute-start.28 = (bf16[128,384]{1,0:T(8,128)(2,1)S(1)}, bf16[128,384]{1,0:T(8,128)(2,1)S(1)}, u32[]{:S(2)}, u32[]{:S(2)}) collective-permute-start(bf16[128,384]{1,0:T(8,128)(2,1)S(1)} %get-tuple-element.46), channel_id=1, source_target_pairs={{0,4},{4,0},{8,12},{12,8},{1,5},{5,1},{9,13},{13,9},{2,6},{6,2},{1... | collective-permute-start | bytes 294920 | tf_op jit(solution)/shard_map/ppermute | solution.py:76
  58.1 0.7 collective-permute-start.29
  58.9 2.5 %collective-permute-start.30 = (bf16[128,384]{1,0:T(8,128)(2,1)S(1)}, bf16[128,384]{1,0:T(8,128)(2,1)S(1)}, u32[]{:S(2)}, u32[]{:S(2)}) collective-permute-start(bf16[128,384]{1,0:T(8,128)(2,1)S(1)} %get-tuple-element.48), channel_id=1, source_target_pairs={{0,12},{4,8},{8,4},{12,0},{1,13},{5,9},{9,5},{13,1},{2,14},{6,10},... | collective-permute-start | bytes 294920 | tf_op jit(solution)/shard_map/ppermute | solution.py:76
  61.4 1.1 %collective-permute-done.28 = bf16[128,384]{1,0:T(8,128)(2,1)S(1)} collective-permute-done((bf16[128,384]{1,0:T(8,128)(2,1)S(1)}, bf16[128,384]{1,0:T(8,128)(2,1)S(1)}, u32[]{:S(2)}, u32[]{:S(2)}) %collective-permute-start.28) | collective-permute-done | bytes 98336 | tf_op jit(solution)/shard_map/ppermute | solution.py:76
  62.5 6.0 %collective-permute-done.29 = bf16[128,384]{1,0:T(8,128)(2,1)S(1)} collective-permute-done((bf16[128,384]{1,0:T(8,128)(2,1)S(1)}, bf16[128,384]{1,0:T(8,128)(2,1)S(1)}, u32[]{:S(2)}, u32[]{:S(2)}) %collective-permute-start.29) | collective-permute-done | bytes 98336 | tf_op jit(solution)/shard_map/ppermute | solution.py:76
  68.5 0.1 convert_add_fusion.refs_0_
  68.5 0.1 collective-permute-start.31
  68.6 1.4 %collective-permute-done.31.refs_1_ = f32[128,384]{1,0:T(8,128)S(1)} collective-permute-done((f32[128,384]{1,0:T(8,128)S(1)}, f32[128,384]{1,0:T(8,128)S(1)}, u32[]{:S(2)}, u32[]{:S(2)}) %collective-permute-start.31) | collective-permute-done | bytes 196640 | tf_op jit(solution)/shard_map/ppermute | solution.py:65
  70.1 10.8 %shard_map.104 = (bf16[144,512]{1,0:T(8,128)(2,1)S(1)}, f32[64,256]{1,0:T(8,128)S(1)}, f32[64,256]{1,0:T(8,128)S(1)}, f32[64,256]{1,0:T(8,128)S(1)}, f32[64,256]{1,0:T(8,128)S(1)}) custom-call(s32[3]{0:T(128)S(1)} %pad_add_fusion.place_ref, f32[128,384]{1,0:T(8,128)S(1)} %convert_add_fusion.refs_0_, f32[128,384]{1,0:T(8,128)S(1)} %collective-permute-done.31.refs_1_, ...), custom_call_target="tpu_custom_call" | custom-call | tf_op jit(solution)/shard_map/pallas_call | solution.py:369
  80.9 2.1 %collective-permute-start.32 = (bf16[144,512]{1,0:T(8,128)(2,1)S(1)}, bf16[144,512]{1,0:T(8,128)(2,1)S(1)}, u32[]{:S(2)}, u32[]{:S(2)}) collective-permute-start(bf16[144,512]{1,0:T(8,128)(2,1)S(1)} %get-tuple-element.49.refs_0_), channel_id=1, source_target_pairs={{4,0},{0,4},{12,8},{8,12},{5,1},{1,5},{13,9},{9,13},{6,2},{2,6},{1... | collective-permute-start | bytes 442376 | tf_op jit(solution)/shard_map/ppermute | solution.py:65
  83.0 2.4 %collective-permute-start.34 = (bf16[144,512]{1,0:T(8,128)(2,1)S(1)}, bf16[144,512]{1,0:T(8,128)(2,1)S(1)}, u32[]{:S(2)}, u32[]{:S(2)}) collective-permute-start(bf16[144,512]{1,0:T(8,128)(2,1)S(1)} %get-tuple-element.49.refs_0_), channel_id=1, source_target_pairs={{12,0},{8,4},{4,8},{0,12},{13,1},{9,5},{5,9},{1,13},{14,2},{10,6},... | collective-permute-start | bytes 442376 | tf_op jit(solution)/shard_map/ppermute | solution.py:65
  85.4 3.4 %collective-permute-done.32.refs_1_ = bf16[144,512]{1,0:T(8,128)(2,1)S(1)} collective-permute-done((bf16[144,512]{1,0:T(8,128)(2,1)S(1)}, bf16[144,512]{1,0:T(8,128)(2,1)S(1)}, u32[]{:S(2)}, u32[]{:S(2)}) %collective-permute-start.32) | collective-permute-done | bytes 147488 | tf_op jit(solution)/shard_map/ppermute | solution.py:65
  88.8 1.2 %collective-permute-start.35 = (f32[64,256]{1,0:T(8,128)S(1)}, f32[64,256]{1,0:T(8,128)S(1)}, u32[]{:S(2)}, u32[]{:S(2)}) collective-permute-start(f32[64,256]{1,0:T(8,128)S(1)} %get-tuple-element.57), channel_id=1, source_target_pairs={{0,1},{1,0},{2,3},{3,2},{4,5},{5,4},{6,7},{7,6},{8,9},{9,8},{10,11... | collective-permute-start | bytes 196616 | tf_op jit(solution)/shard_map/ppermute | solution.py:76
  90.1 1.7 %collective-permute-start.36 = (f32[64,256]{1,0:T(8,128)S(1)}, f32[64,256]{1,0:T(8,128)S(1)}, u32[]{:S(2)}, u32[]{:S(2)}) collective-permute-start(f32[64,256]{1,0:T(8,128)S(1)} %get-tuple-element.58), channel_id=1, source_target_pairs={{0,2},{1,3},{2,0},{3,1},{4,6},{5,7},{6,4},{7,5},{8,10},{9,11},{10,... | collective-permute-start | bytes 196616 | tf_op jit(solution)/shard_map/ppermute | solution.py:76
  91.8 0.5 collective-permute-start.37
  92.3 4.6 %collective-permute-done.33.refs_2_ = bf16[144,512]{1,0:T(8,128)(2,1)S(1)} collective-permute-done((bf16[144,512]{1,0:T(8,128)(2,1)S(1)}, bf16[144,512]{1,0:T(8,128)(2,1)S(1)}, u32[]{:S(2)}, u32[]{:S(2)}) %collective-permute-start.33) | collective-permute-done | bytes 147488 | tf_op jit(solution)/shard_map/ppermute | solution.py:65
  96.9 3.1 %shard_map.105 = (bf16[128,1024]{1,0:T(8,128)(2,1)}, bf16[128,1024]{1,0:T(8,128)(2,1)}) custom-call(s32[3]{0:T(128)S(1)} %pad_add_fusion.place_ref, bf16[144,512]{1,0:T(8,128)(2,1)S(1)} %get-tuple-element.49.refs_0_, bf16[144,512]{1,0:T(8,128)(2,1)S(1)} %collective-permute-done.32.refs_1_, bf16[144,512]{1,0:T(8,128)(2,1)S(1)} %collective-permute-done.33.refs_2_, ...), custom_call_target="tpu_custom_call" | custom-call | tf_op jit(solution)/shard_map/pallas_call | solution.py:369
  100.1 0.6 slice_bitcast_fusion
  (37 shorter events, 0.1 us)
Async XLA Ops:
  0.6 1.2 %copy-start = (bf16[4096,1]{0,1:T(2,128)(2,1)S(1)}, bf16[4096,1]{0,1:T(2,128)(2,1)}, u32[]{:S(2)}) copy-start(bf16[4096,1]{0,1:T(2,128)(2,1)} %param.9) | copy-start | bytes 24580
  0.7 1.2 %copy-start.5 = (bf16[512,128]{1,0:T(8,128)(2,1)S(1)}, bf16[512,128]{1,0:T(8,128)(2,1)}, u32[]{:S(2)}) copy-start(bf16[512,128]{1,0:T(8,128)(2,1)} %param.10) | copy-start | bytes 393220
  0.7 37.6 %copy-start.2 = (bf16[1,128,1024]{2,1,0:T(8,128)(2,1)S(1)}, bf16[1,128,1024]{2,1,0:T(8,128)(2,1)}, u32[]{:S(2)}) copy-start(bf16[1,128,1024]{2,1,0:T(8,128)(2,1)} %param.13) | copy-start | bytes 786436
  1.8 36.5 %copy-start.1 = (bf16[1,128,1024]{2,1,0:T(8,128)(2,1)S(1)}, bf16[1,128,1024]{2,1,0:T(8,128)(2,1)}, u32[]{:S(2)}) copy-start(bf16[1,128,1024]{2,1,0:T(8,128)(2,1)} %param.7) | copy-start | bytes 786436
  2.0 1.4 %collective-permute-start.1 = (bf16[768,128]{1,0:T(8,128)(2,1)S(1)}, bf16[768,128]{1,0:T(8,128)(2,1)S(1)}, u32[]{:S(2)}, u32[]{:S(2)}) collective-permute-start(bf16[768,128]{1,0:T(8,128)(2,1)S(1)} %bitcast.28), channel_id=1, source_target_pairs={{0,0},{1,1},{2,4},{3,5},{4,2},{5,3},{6,6},{7,7},{8,16},{9,17},{10,... | collective-permute-start | bytes 589832 | tf_op jit(solution)/shard_map/ppermute | solution.py:400
  2.6 0.7 collective-permute-start
  3.3 22.9 %collective-permute-start.2 = (bf16[528,128]{1,0:T(8,128)(2,1)S(1)}, bf16[528,128]{1,0:T(8,128)(2,1)S(1)}, u32[]{:S(2)}, u32[]{:S(2)}) collective-permute-start(bf16[528,128]{1,0:T(8,128)(2,1)S(1)} %collective-permute-done.refs_0_.refs_4_), channel_id=1, source_target_pairs={{1,0},{0,1},{3,2},{2,3},{5,4},{4,5},{7,6},{6,7},{9,8},{8,9},{11,10... | collective-permute-start | bytes 405512 | tf_op jit(solution)/shard_map/ppermute | solution.py:65
  6.3 19.9 %collective-permute-start.3 = (bf16[528,128]{1,0:T(8,128)(2,1)S(1)}, bf16[528,128]{1,0:T(8,128)(2,1)S(1)}, u32[]{:S(2)}, u32[]{:S(2)}) collective-permute-start(bf16[528,128]{1,0:T(8,128)(2,1)S(1)} %collective-permute-done.refs_0_.refs_4_), channel_id=1, source_target_pairs={{2,0},{3,1},{0,2},{1,3},{6,4},{7,5},{4,6},{5,7},{10,8},{11,9},{8,1... | collective-permute-start | bytes 405512 | tf_op jit(solution)/shard_map/ppermute | solution.py:65
  23.1 3.7 %collective-permute-start.20 = (bf16[768,128]{1,0:T(8,128)(2,1)S(1)}, bf16[768,128]{1,0:T(8,128)(2,1)S(1)}, u32[]{:S(2)}, u32[]{:S(2)}) collective-permute-start(bf16[768,128]{1,0:T(8,128)(2,1)S(1)} %bitcast.27), channel_id=1, source_target_pairs={{0,0},{1,1},{2,4},{3,5},{4,2},{5,3},{6,6},{7,7},{8,16},{9,17},{10,... | collective-permute-start | bytes 589832 | tf_op jit(solution)/shard_map/ppermute | solution.py:400
  23.7 7.0 %collective-permute-start.4 = (bf16[528,128]{1,0:T(8,128)(2,1)S(1)}, bf16[528,128]{1,0:T(8,128)(2,1)S(1)}, u32[]{:S(2)}, u32[]{:S(2)}) collective-permute-start(bf16[528,128]{1,0:T(8,128)(2,1)S(1)} %collective-permute-done.refs_0_.refs_4_), channel_id=1, source_target_pairs={{3,0},{2,1},{1,2},{0,3},{7,4},{6,5},{5,6},{4,7},{11,8},{10,9},{9,1... | collective-permute-start | bytes 405512 | tf_op jit(solution)/shard_map/ppermute | solution.py:65
  25.0 11.6 %collective-permute-start.5 = (bf16[528,128]{1,0:T(8,128)(2,1)S(1)}, bf16[528,128]{1,0:T(8,128)(2,1)S(1)}, u32[]{:S(2)}, u32[]{:S(2)}) collective-permute-start(bf16[528,128]{1,0:T(8,128)(2,1)S(1)} %collective-permute-done.refs_0_.refs_4_), channel_id=1, source_target_pairs={{16,0},{0,16},{17,1},{1,17},{18,2},{2,18},{19,3},{3,19},{20,4},{4,... | collective-permute-start | bytes 405512 | tf_op jit(solution)/shard_map/ppermute | solution.py:65
  26.3 10.4 %collective-permute-start.6 = (bf16[528,128]{1,0:T(8,128)(2,1)S(1)}, bf16[528,128]{1,0:T(8,128)(2,1)S(1)}, u32[]{:S(2)}, u32[]{:S(2)}) collective-permute-start(bf16[528,128]{1,0:T(8,128)(2,1)S(1)} %collective-permute-done.2.refs_1_.refs_5_), channel_id=1, source_target_pairs={{16,0},{0,16},{17,1},{1,17},{18,2},{2,18},{19,3},{3,19},{20,4},{4,... | collective-permute-start | bytes 405512 | tf_op jit(solution)/shard_map/ppermute | solution.py:65
  26.3 10.6 %collective-permute-start.7 = (bf16[528,128]{1,0:T(8,128)(2,1)S(1)}, bf16[528,128]{1,0:T(8,128)(2,1)S(1)}, u32[]{:S(2)}, u32[]{:S(2)}) collective-permute-start(bf16[528,128]{1,0:T(8,128)(2,1)S(1)} %collective-permute-done.3.refs_2_.refs_6_), channel_id=1, source_target_pairs={{16,0},{0,16},{17,1},{1,17},{18,2},{2,18},{19,3},{3,19},{20,4},{4,... | collective-permute-start | bytes 405512 | tf_op jit(solution)/shard_map/ppermute | solution.py:65
  26.8 12.9 %collective-permute-start.13 = (bf16[768,128]{1,0:T(8,128)(2,1)S(1)}, bf16[768,128]{1,0:T(8,128)(2,1)S(1)}, u32[]{:S(2)}, u32[]{:S(2)}) collective-permute-start(bf16[768,128]{1,0:T(8,128)(2,1)S(1)} %collective-permute-done.1.refs_0_.refs_12_), channel_id=1, source_target_pairs={{1,0},{0,1},{3,2},{2,3},{5,4},{4,5},{7,6},{6,7},{9,8},{8,9},{11,10... | collective-permute-start | bytes 589832 | tf_op jit(solution)/shard_map/ppermute | solution.py:65
  30.7 11.2 %collective-permute-start.14 = (bf16[768,128]{1,0:T(8,128)(2,1)S(1)}, bf16[768,128]{1,0:T(8,128)(2,1)S(1)}, u32[]{:S(2)}, u32[]{:S(2)}) collective-permute-start(bf16[768,128]{1,0:T(8,128)(2,1)S(1)} %collective-permute-done.1.refs_0_.refs_12_), channel_id=1, source_target_pairs={{2,0},{3,1},{0,2},{1,3},{6,4},{7,5},{4,6},{5,7},{10,8},{11,9},{8,1... | collective-permute-start | bytes 589832 | tf_op jit(solution)/shard_map/ppermute | solution.py:65
  36.7 6.5 %collective-permute-start.16 = (bf16[768,128]{1,0:T(8,128)(2,1)S(1)}, bf16[768,128]{1,0:T(8,128)(2,1)S(1)}, u32[]{:S(2)}, u32[]{:S(2)}) collective-permute-start(bf16[768,128]{1,0:T(8,128)(2,1)S(1)} %collective-permute-done.1.refs_0_.refs_12_), channel_id=1, source_target_pairs={{16,0},{0,16},{17,1},{1,17},{18,2},{2,18},{19,3},{3,19},{20,4},{4,... | collective-permute-start | bytes 589832 | tf_op jit(solution)/shard_map/ppermute | solution.py:65
  36.7 8.0 %collective-permute-start.22 = (bf16[768,128]{1,0:T(8,128)(2,1)S(1)}, bf16[768,128]{1,0:T(8,128)(2,1)S(1)}, u32[]{:S(2)}, u32[]{:S(2)}) collective-permute-start(bf16[768,128]{1,0:T(8,128)(2,1)S(1)} %collective-permute-done.20.refs_8_.refs_20_), channel_id=1, source_target_pairs={{2,0},{3,1},{0,2},{1,3},{6,4},{7,5},{4,6},{5,7},{10,8},{11,9},{8,1... | collective-permute-start | bytes 589832 | tf_op jit(solution)/shard_map/ppermute | solution.py:65
  36.8 1.5 %collective-permute-start.8 = (bf16[528,128]{1,0:T(8,128)(2,1)S(1)}, bf16[528,128]{1,0:T(8,128)(2,1)S(1)}, u32[]{:S(2)}, u32[]{:S(2)}) collective-permute-start(bf16[528,128]{1,0:T(8,128)(2,1)S(1)} %collective-permute-done.4.refs_3_.refs_7_), channel_id=1, source_target_pairs={{16,0},{0,16},{17,1},{1,17},{18,2},{2,18},{19,3},{3,19},{20,4},{4,... | collective-permute-start | bytes 405512 | tf_op jit(solution)/shard_map/ppermute | solution.py:65
  39.6 6.1 %collective-permute-start.10 = (bf16[144,128]{1,0:T(8,128)(2,1)S(1)}, bf16[144,128]{1,0:T(8,128)(2,1)S(1)}, u32[]{:S(2)}, u32[]{:S(2)}) collective-permute-start(bf16[144,128]{1,0:T(8,128)(2,1)S(1)} %get-tuple-element.40), channel_id=1, source_target_pairs={{0,8},{4,12},{8,0},{12,4},{1,9},{5,13},{9,1},{13,5},{2,10},{6,14},... | collective-permute-start | bytes 110600 | tf_op jit(solution)/shard_map/ppermute | solution.py:76
  39.7 7.1 %collective-permute-start.11 = (bf16[144,128]{1,0:T(8,128)(2,1)S(1)}, bf16[144,128]{1,0:T(8,128)(2,1)S(1)}, u32[]{:S(2)}, u32[]{:S(2)}) collective-permute-start(bf16[144,128]{1,0:T(8,128)(2,1)S(1)} %get-tuple-element.41), channel_id=1, source_target_pairs={{0,12},{4,8},{8,4},{12,0},{1,13},{5,9},{9,5},{13,1},{2,14},{6,10},... | collective-permute-start | bytes 110600 | tf_op jit(solution)/shard_map/ppermute | solution.py:76
  41.9 4.9 %collective-permute-start.9 = (bf16[144,128]{1,0:T(8,128)(2,1)S(1)}, bf16[144,128]{1,0:T(8,128)(2,1)S(1)}, u32[]{:S(2)}, u32[]{:S(2)}) collective-permute-start(bf16[144,128]{1,0:T(8,128)(2,1)S(1)} %get-tuple-element.39), channel_id=1, source_target_pairs={{0,4},{4,0},{8,12},{12,8},{1,5},{5,1},{9,13},{13,9},{2,6},{6,2},{1... | collective-permute-start | bytes 110600 | tf_op jit(solution)/shard_map/ppermute | solution.py:76
  43.2 6.3 %collective-permute-start.21 = (bf16[768,128]{1,0:T(8,128)(2,1)S(1)}, bf16[768,128]{1,0:T(8,128)(2,1)S(1)}, u32[]{:S(2)}, u32[]{:S(2)}) collective-permute-start(bf16[768,128]{1,0:T(8,128)(2,1)S(1)} %collective-permute-done.20.refs_8_.refs_20_), channel_id=1, source_target_pairs={{1,0},{0,1},{3,2},{2,3},{5,4},{4,5},{7,6},{6,7},{9,8},{8,9},{11,10... | collective-permute-start | bytes 589832 | tf_op jit(solution)/shard_map/ppermute | solution.py:65
  44.7 4.8 %collective-permute-start.24 = (bf16[768,128]{1,0:T(8,128)(2,1)S(1)}, bf16[768,128]{1,0:T(8,128)(2,1)S(1)}, u32[]{:S(2)}, u32[]{:S(2)}) collective-permute-start(bf16[768,128]{1,0:T(8,128)(2,1)S(1)} %collective-permute-done.20.refs_8_.refs_20_), channel_id=1, source_target_pairs={{16,0},{0,16},{17,1},{1,17},{18,2},{2,18},{19,3},{3,19},{20,4},{4,... | collective-permute-start | bytes 589832 | tf_op jit(solution)/shard_map/ppermute | solution.py:65
  45.7 6.4 %collective-permute-start.15 = (bf16[768,128]{1,0:T(8,128)(2,1)S(1)}, bf16[768,128]{1,0:T(8,128)(2,1)S(1)}, u32[]{:S(2)}, u32[]{:S(2)}) collective-permute-start(bf16[768,128]{1,0:T(8,128)(2,1)S(1)} %collective-permute-done.13.refs_1_.refs_13_), channel_id=1, source_target_pairs={{2,0},{3,1},{0,2},{1,3},{6,4},{7,5},{4,6},{5,7},{10,8},{11,9},{8,1... | collective-permute-start | bytes 589832 | tf_op jit(solution)/shard_map/ppermute | solution.py:65
  46.8 5.3 %collective-permute-start.17 = (bf16[768,128]{1,0:T(8,128)(2,1)S(1)}, bf16[768,128]{1,0:T(8,128)(2,1)S(1)}, u32[]{:S(2)}, u32[]{:S(2)}) collective-permute-start(bf16[768,128]{1,0:T(8,128)(2,1)S(1)} %collective-permute-done.13.refs_1_.refs_13_), channel_id=1, source_target_pairs={{16,0},{0,16},{17,1},{1,17},{18,2},{2,18},{19,3},{3,19},{20,4},{4,... | collective-permute-start | bytes 589832 | tf_op jit(solution)/shard_map/ppermute | solution.py:65
  46.8 7.3 %collective-permute-start.23 = (bf16[768,128]{1,0:T(8,128)(2,1)S(1)}, bf16[768,128]{1,0:T(8,128)(2,1)S(1)}, u32[]{:S(2)}, u32[]{:S(2)}) collective-permute-start(bf16[768,128]{1,0:T(8,128)(2,1)S(1)} %collective-permute-done.22.refs_10_.refs_22_), channel_id=1, source_target_pairs={{1,0},{0,1},{3,2},{2,3},{5,4},{4,5},{7,6},{6,7},{9,8},{8,9},{11,10... | collective-permute-start | bytes 589832 | tf_op jit(solution)/shard_map/ppermute | solution.py:65
  49.5 1.3 %collective-permute-start.12 = (f32[144,128]{1,0:T(8,128)S(1)}, f32[144,128]{1,0:T(8,128)S(1)}, u32[]{:S(2)}, u32[]{:S(2)}) collective-permute-start(f32[144,128]{1,0:T(8,128)S(1)} %convert_add_fusion.1.refs_2_), channel_id=1, source_target_pairs={{16,0},{0,16},{17,1},{1,17},{18,2},{2,18},{19,3},{3,19},{20,4},{4,... | collective-permute-start | bytes 221192 | tf_op jit(solution)/shard_map/ppermute | solution.py:65
  49.5 4.6 %collective-permute-start.26 = (bf16[768,128]{1,0:T(8,128)(2,1)S(1)}, bf16[768,128]{1,0:T(8,128)(2,1)S(1)}, u32[]{:S(2)}, u32[]{:S(2)}) collective-permute-start(bf16[768,128]{1,0:T(8,128)(2,1)S(1)} %collective-permute-done.22.refs_10_.refs_22_), channel_id=1, source_target_pairs={{16,0},{0,16},{17,1},{1,17},{18,2},{2,18},{19,3},{3,19},{20,4},{4,... | collective-permute-start | bytes 589832 | tf_op jit(solution)/shard_map/ppermute | solution.py:65
  50.7 3.4 %collective-permute-start.18 = (bf16[768,128]{1,0:T(8,128)(2,1)S(1)}, bf16[768,128]{1,0:T(8,128)(2,1)S(1)}, u32[]{:S(2)}, u32[]{:S(2)}) collective-permute-start(bf16[768,128]{1,0:T(8,128)(2,1)S(1)} %collective-permute-done.14.refs_2_.refs_14_), channel_id=1, source_target_pairs={{16,0},{0,16},{17,1},{1,17},{18,2},{2,18},{19,3},{3,19},{20,4},{4,... | collective-permute-start | bytes 589832 | tf_op jit(solution)/shard_map/ppermute | solution.py:65
  52.1 2.0 %collective-permute-start.25 = (bf16[768,128]{1,0:T(8,128)(2,1)S(1)}, bf16[768,128]{1,0:T(8,128)(2,1)S(1)}, u32[]{:S(2)}, u32[]{:S(2)}) collective-permute-start(bf16[768,128]{1,0:T(8,128)(2,1)S(1)} %collective-permute-done.21.refs_9_.refs_21_), channel_id=1, source_target_pairs={{16,0},{0,16},{17,1},{1,17},{18,2},{2,18},{19,3},{3,19},{20,4},{4,... | collective-permute-start | bytes 589832 | tf_op jit(solution)/shard_map/ppermute | solution.py:65
  52.1 2.0 %collective-permute-start.19 = (bf16[768,128]{1,0:T(8,128)(2,1)S(1)}, bf16[768,128]{1,0:T(8,128)(2,1)S(1)}, u32[]{:S(2)}, u32[]{:S(2)}) collective-permute-start(bf16[768,128]{1,0:T(8,128)(2,1)S(1)} %collective-permute-done.15.refs_3_.refs_15_), channel_id=1, source_target_pairs={{16,0},{0,16},{17,1},{1,17},{18,2},{2,18},{19,3},{3,19},{20,4},{4,... | collective-permute-start | bytes 589832 | tf_op jit(solution)/shard_map/ppermute | solution.py:65
  54.1 1.4 %collective-permute-start.27 = (bf16[768,128]{1,0:T(8,128)(2,1)S(1)}, bf16[768,128]{1,0:T(8,128)(2,1)S(1)}, u32[]{:S(2)}, u32[]{:S(2)}) collective-permute-start(bf16[768,128]{1,0:T(8,128)(2,1)S(1)} %collective-permute-done.23.refs_11_.refs_23_), channel_id=1, source_target_pairs={{16,0},{0,16},{17,1},{1,17},{18,2},{2,18},{19,3},{3,19},{20,4},{4,... | collective-permute-start | bytes 589832 | tf_op jit(solution)/shard_map/ppermute | solution.py:65
  57.0 5.6 %collective-permute-start.28 = (bf16[128,384]{1,0:T(8,128)(2,1)S(1)}, bf16[128,384]{1,0:T(8,128)(2,1)S(1)}, u32[]{:S(2)}, u32[]{:S(2)}) collective-permute-start(bf16[128,384]{1,0:T(8,128)(2,1)S(1)} %get-tuple-element.46), channel_id=1, source_target_pairs={{0,4},{4,0},{8,12},{12,8},{1,5},{5,1},{9,13},{13,9},{2,6},{6,2},{1... | collective-permute-start | bytes 294920 | tf_op jit(solution)/shard_map/ppermute | solution.py:76
  58.1 10.3 %collective-permute-start.29 = (bf16[128,384]{1,0:T(8,128)(2,1)S(1)}, bf16[128,384]{1,0:T(8,128)(2,1)S(1)}, u32[]{:S(2)}, u32[]{:S(2)}) collective-permute-start(bf16[128,384]{1,0:T(8,128)(2,1)S(1)} %get-tuple-element.47), channel_id=1, source_target_pairs={{0,8},{4,12},{8,0},{12,4},{1,9},{5,13},{9,1},{13,5},{2,10},{6,14},... | collective-permute-start | bytes 294920 | tf_op jit(solution)/shard_map/ppermute | solution.py:76
  58.9 9.6 %collective-permute-start.30 = (bf16[128,384]{1,0:T(8,128)(2,1)S(1)}, bf16[128,384]{1,0:T(8,128)(2,1)S(1)}, u32[]{:S(2)}, u32[]{:S(2)}) collective-permute-start(bf16[128,384]{1,0:T(8,128)(2,1)S(1)} %get-tuple-element.48), channel_id=1, source_target_pairs={{0,12},{4,8},{8,4},{12,0},{1,13},{5,9},{9,5},{13,1},{2,14},{6,10},... | collective-permute-start | bytes 294920 | tf_op jit(solution)/shard_map/ppermute | solution.py:76
  68.5 1.6 %copy-start.3 = (f32[1,128,512]{2,1,0:T(8,128)S(1)}, f32[1,128,512]{2,1,0:T(8,128)}, u32[]{:S(2)}) copy-start(f32[1,128,512]{2,1,0:T(8,128)} %param.11) | copy-start | bytes 786436
  68.5 1.6 %copy-start.4 = (f32[1,512,128]{2,1,0:T(8,128)S(1)}, f32[1,512,128]{2,1,0:T(8,128)}, u32[]{:S(2)}) copy-start(f32[1,512,128]{2,1,0:T(8,128)} %param.12) | copy-start | bytes 786436
  68.5 1.5 %collective-permute-start.31 = (f32[128,384]{1,0:T(8,128)S(1)}, f32[128,384]{1,0:T(8,128)S(1)}, u32[]{:S(2)}, u32[]{:S(2)}) collective-permute-start(f32[128,384]{1,0:T(8,128)S(1)} %convert_add_fusion.refs_0_), channel_id=1, source_target_pairs={{16,0},{0,16},{17,1},{1,17},{18,2},{2,18},{19,3},{3,19},{20,4},{4,... | collective-permute-start | bytes 589832 | tf_op jit(solution)/shard_map/ppermute | solution.py:65
  80.9 7.9 %collective-permute-start.32 = (bf16[144,512]{1,0:T(8,128)(2,1)S(1)}, bf16[144,512]{1,0:T(8,128)(2,1)S(1)}, u32[]{:S(2)}, u32[]{:S(2)}) collective-permute-start(bf16[144,512]{1,0:T(8,128)(2,1)S(1)} %get-tuple-element.49.refs_0_), channel_id=1, source_target_pairs={{4,0},{0,4},{12,8},{8,12},{5,1},{1,5},{13,9},{9,13},{6,2},{2,6},{1... | collective-permute-start | bytes 442376 | tf_op jit(solution)/shard_map/ppermute | solution.py:65
  83.0 13.9 %collective-permute-start.33 = (bf16[144,512]{1,0:T(8,128)(2,1)S(1)}, bf16[144,512]{1,0:T(8,128)(2,1)S(1)}, u32[]{:S(2)}, u32[]{:S(2)}) collective-permute-start(bf16[144,512]{1,0:T(8,128)(2,1)S(1)} %get-tuple-element.49.refs_0_), channel_id=1, source_target_pairs={{8,0},{12,4},{0,8},{4,12},{9,1},{13,5},{1,9},{5,13},{10,2},{14,6},... | collective-permute-start | bytes 442376 | tf_op jit(solution)/shard_map/ppermute | solution.py:65
  83.0 13.9 %collective-permute-start.34 = (bf16[144,512]{1,0:T(8,128)(2,1)S(1)}, bf16[144,512]{1,0:T(8,128)(2,1)S(1)}, u32[]{:S(2)}, u32[]{:S(2)}) collective-permute-start(bf16[144,512]{1,0:T(8,128)(2,1)S(1)} %get-tuple-element.49.refs_0_), channel_id=1, source_target_pairs={{12,0},{8,4},{4,8},{0,12},{13,1},{9,5},{5,9},{1,13},{14,2},{10,6},... | collective-permute-start | bytes 442376 | tf_op jit(solution)/shard_map/ppermute | solution.py:65
  88.8 11.2 %collective-permute-start.35 = (f32[64,256]{1,0:T(8,128)S(1)}, f32[64,256]{1,0:T(8,128)S(1)}, u32[]{:S(2)}, u32[]{:S(2)}) collective-permute-start(f32[64,256]{1,0:T(8,128)S(1)} %get-tuple-element.57), channel_id=1, source_target_pairs={{0,1},{1,0},{2,3},{3,2},{4,5},{5,4},{6,7},{7,6},{8,9},{9,8},{10,11... | collective-permute-start | bytes 196616 | tf_op jit(solution)/shard_map/ppermute | solution.py:76
  90.1 10.0 %collective-permute-start.36 = (f32[64,256]{1,0:T(8,128)S(1)}, f32[64,256]{1,0:T(8,128)S(1)}, u32[]{:S(2)}, u32[]{:S(2)}) collective-permute-start(f32[64,256]{1,0:T(8,128)S(1)} %get-tuple-element.58), channel_id=1, source_target_pairs={{0,2},{1,3},{2,0},{3,1},{4,6},{5,7},{6,4},{7,5},{8,10},{9,11},{10,... | collective-permute-start | bytes 196616 | tf_op jit(solution)/shard_map/ppermute | solution.py:76
  91.8 8.3 %collective-permute-start.37 = (f32[64,256]{1,0:T(8,128)S(1)}, f32[64,256]{1,0:T(8,128)S(1)}, u32[]{:S(2)}, u32[]{:S(2)}) collective-permute-start(f32[64,256]{1,0:T(8,128)S(1)} %get-tuple-element.59), channel_id=1, source_target_pairs={{0,3},{1,2},{2,1},{3,0},{4,7},{5,6},{6,5},{7,4},{8,11},{9,10},{10,... | collective-permute-start | bytes 196616 | tf_op jit(solution)/shard_map/ppermute | solution.py:76

commit v8 on v6

--- a/solution.py
+++ b/solution.py
@@ -190,6 +190,9 @@
         if isinstance(i, int):
             return slice(i * MB, (i + 1) * MB)
         return pl.ds(pl.multiple_of(i * MB, MB), MB)
+
+    def is_last(i):
+        return isinstance(i, int) and i == blocks - 1
 
     def forward(i):
         at = at_block(i)
@@ -218,8 +221,9 @@
         g2b = g2.astype(BF16)
         p = mm(g2b, w2, NN)
         g1f = p * g1
-        w1c[...] = w1c[...] - mm(k, e * g1f, TN)
-        w2c[...] = w2c[...] - mm(e * g2, x2b, TN)
+        if not is_last(i):
+            w1c[...] = w1c[...] - mm(k, e * g1f, TN)
+            w2c[...] = w2c[...] - mm(e * g2, x2b, TN)
         g1b = g1f.astype(BF16)
         b1 = mm(qb, kb, NT)
         a1 = (b1 * mask).astype(BF16)
@@ -269,8 +273,9 @@
         d1, d2 = w1c[...].astype(BF16), w2c[...].astype(BF16)
         x2b, g1, g1f, g2 = x2s[i], g1s[i], gfs[i], g2s[i]
         n, s, cc = ns[i], ss[i], cs[i]
-        dh1 = -mm(k, d1, NN)
-        dh2 = -mm(x2b, d2, NT)
+        last = is_last(i)
+        dh1 = jnp.zeros_like(g1f) if last else -mm(k, d1, NN)
+        dh2 = jnp.zeros_like(g2) if last else -mm(x2b, d2, NT)
         dg1 = dg1s[i] + e * dh1
         dp = (dg1 * g1).astype(BF16)
         dg2 = dg2s[i] + e * dh2 + mm(dp, w2, NT)
@@ -280,11 +285,17 @@
         dn = dr - cc * dt - rs[i] * mt
         du = s * (dn - mean(dn) - n * (mean(dn * n) + mean(dg2 * g2)))
         dub = du.astype(BF16)
-        mixed = jnp.concatenate([(-e * g2).astype(BF16), dub], axis=1)
-        dx2 = dx2s[i] + mm(mixed, jnp.concatenate([d2, w2], axis=0), NN)
+        if last:
+            dx2 = dx2s[i] + mm(dub, w2, NN)
+        else:
+            mixed = jnp.concatenate([(-e * g2).astype(BF16), dub], axis=1)
+            dx2 = dx2s[i] + mm(mixed, jnp.concatenate([d2, w2], axis=0), NN)
         dz1 = (dg1 * pgs[i] + dx2 * g1).astype(BF16)
-        mixed = jnp.concatenate([(-e * g1f).astype(BF16), dz1], axis=1)
-        dk = dks[i] + dr + mm(mixed, jnp.concatenate([d1, w1], axis=1), NT)
+        if last:
+            dk = dks[i] + dr + mm(dz1, w1, NT)
+        else:
+            mixed = jnp.concatenate([(-e * g1f).astype(BF16), dz1], axis=1)
+            dk = dks[i] + dr + mm(mixed, jnp.concatenate([d1, w1], axis=1), NT)
         w1c[...] = w1c[...] + mm(
             jnp.concatenate([q, k], axis=0), jnp.concatenate([zqs[i], dz1], axis=0), TN
         )

time: 98.6 us -> 98.3 us (level)
  transfers between devices with their start and end apart: 38 -> 38, of which waited for: 14 -> 14; matrix products, arithmetic and copies ran while one was open for 0% -> 0% of each run, Pallas kernels for 4% -> 5%
where the time goes in v8:
time: 98.3 us; the launch traced here: 98.2 us
  starting transfers between devices  46.6 us (47%)
  waiting for transfers between devices  32.3 us (33%)
  Pallas kernels  16.4 us (17%)
  local copies, waits for them, and re-layouts  1.77 us (2%)
    ppermute x26, starting transfers between devices, hop(): lax.ppermute(array, axis, [(mate(i, step, count), i) for i in range(count)])  32.6 us
    ppermute x26, waiting for transfers between devices, hop(): lax.ppermute(array, axis, [(mate(i, step, count), i) for i in range(count)])  25.8 us
    pallas_call x4, Pallas kernels, call(): pl.pallas_call(kernel, out_shape=outs, in_specs=[SMEM] + [VMEM] * (len(op...  16.4 us
    ppermute x9, starting transfers between devices, sent_to(): lax.ppermute(arrays[j], axis, [(i, mate(i, j, count)) for i in range(coun...  12 us
    ppermute x9, waiting for transfers between devices, sent_to(): lax.ppermute(arrays[j], axis, [(i, mate(i, j, count)) for i in range(coun...  6.5 us
    ppermute x3, starting transfers between devices, swapped(): return lax.ppermute(array, ('seq', 'head', 'dp'), pairs)  2 us
  transfers between devices with their start and end apart: 38, of which 14 were waited for; matrix products, arithmetic and copies ran while one was open for 0% of the time, Pallas kernels for 5%

profile of v8, /device:TPU:0, one launch (start us, length us, event | category | flops | bytes accessed | tf_op | source)
XLA Modules:
  0.0 98.2 jit_solution(8582611202513963626)
XLA Ops:
  0.6 0.0 copy-start
  0.7 0.1 pad_add_fusion.place_ref
  0.7 1.1 %fusion.2 = (bf16[3,256,128]{2,1,0:T(8,128)(2,1)S(1)}, bf16[3,256,128]{2,1,0:T(8,128)(2,1)S(1)}) fusion(bf16[3,512,128]{2,1,0:T(8,128)(2,1)} %bitcast.26), kind=kLoop, calls=%fused_computation.10 | loop fusion | bytes 786432 | tf_op jit(solution)/shard_map/slice | solution.py:423
  1.8 0.0 copy-start.1
  1.9 0.1 reduce
  2.0 0.7 collective-permute-start
  2.6 0.7 collective-permute-start.12
  3.3 0.0 collective-permute-done.refs_0_.refs_4_
  3.3 3.0 %collective-permute-start.1 = (bf16[528,128]{1,0:T(8,128)(2,1)S(1)}, bf16[528,128]{1,0:T(8,128)(2,1)S(1)}, u32[]{:S(2)}, u32[]{:S(2)}) collective-permute-start(bf16[528,128]{1,0:T(8,128)(2,1)S(1)} %collective-permute-done.refs_0_.refs_4_), channel_id=1, source_target_pairs={{1,0},{0,1},{3,2},{2,3},{5,4},{4,5},{7,6},{6,7},{9,8},{8,9},{11,10... | collective-permute-start | bytes 405512 | tf_op jit(solution)/shard_map/ppermute | solution.py:65
  6.3 10.4 %collective-permute-start.2 = (bf16[528,128]{1,0:T(8,128)(2,1)S(1)}, bf16[528,128]{1,0:T(8,128)(2,1)S(1)}, u32[]{:S(2)}, u32[]{:S(2)}) collective-permute-start(bf16[528,128]{1,0:T(8,128)(2,1)S(1)} %collective-permute-done.refs_0_.refs_4_), channel_id=1, source_target_pairs={{2,0},{3,1},{0,2},{1,3},{6,4},{7,5},{4,6},{5,7},{10,8},{11,9},{8,1... | collective-permute-start | bytes 405512 | tf_op jit(solution)/shard_map/ppermute | solution.py:65
  16.7 0.7 collective-permute-start.20
  17.4 1.3 %collective-permute-start.3 = (bf16[528,128]{1,0:T(8,128)(2,1)S(1)}, bf16[528,128]{1,0:T(8,128)(2,1)S(1)}, u32[]{:S(2)}, u32[]{:S(2)}) collective-permute-start(bf16[528,128]{1,0:T(8,128)(2,1)S(1)} %collective-permute-done.refs_0_.refs_4_), channel_id=1, source_target_pairs={{3,0},{2,1},{1,2},{0,3},{7,4},{6,5},{5,6},{4,7},{11,8},{10,9},{9,1... | collective-permute-start | bytes 405512 | tf_op jit(solution)/shard_map/ppermute | solution.py:65
  18.7 0.0 collective-permute-done.12.refs_0_.refs_12_
  18.7 4.0 %collective-permute-start.4 = (bf16[528,128]{1,0:T(8,128)(2,1)S(1)}, bf16[528,128]{1,0:T(8,128)(2,1)S(1)}, u32[]{:S(2)}, u32[]{:S(2)}) collective-permute-start(bf16[528,128]{1,0:T(8,128)(2,1)S(1)} %collective-permute-done.refs_0_.refs_4_), channel_id=1, source_target_pairs={{16,0},{0,16},{17,1},{1,17},{18,2},{2,18},{19,3},{3,19},{20,4},{4,... | collective-permute-start | bytes 405512 | tf_op jit(solution)/shard_map/ppermute | solution.py:65
  22.7 0.1 collective-permute-start.5
  22.8 6.3 %collective-permute-done.2.refs_2_.refs_6_ = bf16[528,128]{1,0:T(8,128)(2,1)S(1)} collective-permute-done((bf16[528,128]{1,0:T(8,128)(2,1)S(1)}, bf16[528,128]{1,0:T(8,128)(2,1)S(1)}, u32[]{:S(2)}, u32[]{:S(2)}) %collective-permute-start.2) | collective-permute-done | bytes 135200 | tf_op jit(solution)/shard_map/ppermute | solution.py:65
  29.1 1.5 %collective-permute-start.13 = (bf16[768,128]{1,0:T(8,128)(2,1)S(1)}, bf16[768,128]{1,0:T(8,128)(2,1)S(1)}, u32[]{:S(2)}, u32[]{:S(2)}) collective-permute-start(bf16[768,128]{1,0:T(8,128)(2,1)S(1)} %collective-permute-done.12.refs_0_.refs_12_), channel_id=1, source_target_pairs={{1,0},{0,1},{3,2},{2,3},{5,4},{4,5},{7,6},{6,7},{9,8},{8,9},{11,10... | collective-permute-start | bytes 589832 | tf_op jit(solution)/shard_map/ppermute | solution.py:65
  30.6 2.5 %collective-permute-start.22 = (bf16[768,128]{1,0:T(8,128)(2,1)S(1)}, bf16[768,128]{1,0:T(8,128)(2,1)S(1)}, u32[]{:S(2)}, u32[]{:S(2)}) collective-permute-start(bf16[768,128]{1,0:T(8,128)(2,1)S(1)} %collective-permute-done.20.refs_8_.refs_20_), channel_id=1, source_target_pairs={{2,0},{3,1},{0,2},{1,3},{6,4},{7,5},{4,6},{5,7},{10,8},{11,9},{8,1... | collective-permute-start | bytes 589832 | tf_op jit(solution)/shard_map/ppermute | solution.py:65
  33.1 0.0 collective-permute-done.4.refs_4_.refs_8_
  33.1 0.1 collective-permute-start.14
  33.2 0.0 collective-permute-done.5.refs_5_.refs_9_
  33.2 0.5 collective-permute-start.21
  33.7 1.4 %collective-permute-done.7.refs_7_.refs_11_ = bf16[528,128]{1,0:T(8,128)(2,1)S(1)} collective-permute-done((bf16[528,128]{1,0:T(8,128)(2,1)S(1)}, bf16[528,128]{1,0:T(8,128)(2,1)S(1)}, u32[]{:S(2)}, u32[]{:S(2)}) %collective-permute-start.7) | collective-permute-done | bytes 135200 | tf_op jit(solution)/shard_map/ppermute | solution.py:65
  35.1 1.3 %shard_map.102 = (bf16[144,128]{1,0:T(8,128)(2,1)S(1)}, bf16[144,128]{1,0:T(8,128)(2,1)S(1)}, bf16[144,128]{1,0:T(8,128)(2,1)S(1)}, bf16[144,128]{1,0:T(8,128)(2,1)S(1)}) custom-call(s32[3]{0:T(128)S(1)} %pad_add_fusion.place_ref, bf16[128,1024]{1,0:T(8,128)(2,1)S(1)} %bitcast.21, bf16[128,1024]{1,0:T(8,128)(2,1)S(1)} %bitcast.23, ...), custom_call_target="tpu_custom_call" | custom-call | tf_op jit(solution)/shard_map/pallas_call | solution.py:380
  36.4 2.0 %collective-permute-start.10 = (bf16[144,128]{1,0:T(8,128)(2,1)S(1)}, bf16[144,128]{1,0:T(8,128)(2,1)S(1)}, u32[]{:S(2)}, u32[]{:S(2)}) collective-permute-start(bf16[144,128]{1,0:T(8,128)(2,1)S(1)} %get-tuple-element.37), channel_id=1, source_target_pairs={{0,12},{4,8},{8,4},{12,0},{1,13},{5,9},{9,5},{13,1},{2,14},{6,10},... | collective-permute-start | bytes 110600 | tf_op jit(solution)/shard_map/ppermute | solution.py:76
  38.3 0.0 collective-permute-done.13.refs_1_.refs_13_
  38.3 0.0 collective-permute-start.8
  38.3 0.4 collective-permute-done.22.refs_10_.refs_22_
  38.8 2.1 %collective-permute-start.9 = (bf16[144,128]{1,0:T(8,128)(2,1)S(1)}, bf16[144,128]{1,0:T(8,128)(2,1)S(1)}, u32[]{:S(2)}, u32[]{:S(2)}) collective-permute-start(bf16[144,128]{1,0:T(8,128)(2,1)S(1)} %get-tuple-element.36), channel_id=1, source_target_pairs={{0,8},{4,12},{8,0},{12,4},{1,9},{5,13},{9,1},{13,5},{2,10},{6,14},... | collective-permute-start | bytes 110600 | tf_op jit(solution)/shard_map/ppermute | solution.py:76
  40.8 1.7 %collective-permute-done.14.refs_2_.refs_14_ = bf16[768,128]{1,0:T(8,128)(2,1)S(1)} collective-permute-done((bf16[768,128]{1,0:T(8,128)(2,1)S(1)}, bf16[768,128]{1,0:T(8,128)(2,1)S(1)}, u32[]{:S(2)}, u32[]{:S(2)}) %collective-permute-start.14) | collective-permute-done | bytes 196640 | tf_op jit(solution)/shard_map/ppermute | solution.py:65
  42.6 0.5 collective-permute-start.24
  43.1 1.7 %collective-permute-start.15 = (bf16[768,128]{1,0:T(8,128)(2,1)S(1)}, bf16[768,128]{1,0:T(8,128)(2,1)S(1)}, u32[]{:S(2)}, u32[]{:S(2)}) collective-permute-start(bf16[768,128]{1,0:T(8,128)(2,1)S(1)} %collective-permute-done.13.refs_1_.refs_13_), channel_id=1, source_target_pairs={{2,0},{3,1},{0,2},{1,3},{6,4},{7,5},{4,6},{5,7},{10,8},{11,9},{8,1... | collective-permute-start | bytes 589832 | tf_op jit(solution)/shard_map/ppermute | solution.py:65
  44.9 1.2 %collective-permute-start.23 = (bf16[768,128]{1,0:T(8,128)(2,1)S(1)}, bf16[768,128]{1,0:T(8,128)(2,1)S(1)}, u32[]{:S(2)}, u32[]{:S(2)}) collective-permute-start(bf16[768,128]{1,0:T(8,128)(2,1)S(1)} %collective-permute-done.22.refs_10_.refs_22_), channel_id=1, source_target_pairs={{1,0},{0,1},{3,2},{2,3},{5,4},{4,5},{7,6},{6,7},{9,8},{8,9},{11,10... | collective-permute-start | bytes 589832 | tf_op jit(solution)/shard_map/ppermute | solution.py:65
  46.1 0.2 collective-permute-start.11
  46.3 0.3 collective-permute-start.26
  46.7 0.8 collective-permute-done.11.refs_3_
  47.5 0.2 collective-permute-start.18
  47.6 2.4 %collective-permute-done.15.refs_3_.refs_15_ = bf16[768,128]{1,0:T(8,128)(2,1)S(1)} collective-permute-done((bf16[768,128]{1,0:T(8,128)(2,1)S(1)}, bf16[768,128]{1,0:T(8,128)(2,1)S(1)}, u32[]{:S(2)}, u32[]{:S(2)}) %collective-permute-start.15) | collective-permute-done | bytes 196640 | tf_op jit(solution)/shard_map/ppermute | solution.py:65
  50.0 2.2 %collective-permute-done.23.refs_11_.refs_23_ = bf16[768,128]{1,0:T(8,128)(2,1)S(1)} collective-permute-done((bf16[768,128]{1,0:T(8,128)(2,1)S(1)}, bf16[768,128]{1,0:T(8,128)(2,1)S(1)}, u32[]{:S(2)}, u32[]{:S(2)}) %collective-permute-start.23) | collective-permute-done | bytes 196640 | tf_op jit(solution)/shard_map/ppermute | solution.py:65
  52.2 0.5 collective-permute-start.27
  52.7 0.9 collective-permute-done.19.refs_7_.refs_19_
  53.6 0.3 collective-permute-done.27.refs_15_.refs_27_
  53.9 1.4 %shard_map.103 = (bf16[128,384]{1,0:T(8,128)(2,1)S(1)}, bf16[128,384]{1,0:T(8,128)(2,1)S(1)}, bf16[128,384]{1,0:T(8,128)(2,1)S(1)}, bf16[128,384]{1,0:T(8,128)(2,1)S(1)}) custom-call(s32[3]{0:T(128)S(1)} %pad_add_fusion.place_ref, bf16[128,1024]{1,0:T(8,128)(2,1)S(1)} %bitcast.22, bf16[768,128]{1,0:T(8,128)(2,1)S(1)} %collective-permute-done.12.refs_0_.refs_12_, ...), custom_call_target="tpu_custom_call" | custom-call | tf_op jit(solution)/shard_map/pallas_call | solution.py:380
  55.3 0.1 collective-permute-start.28
  55.4 0.6 collective-permute-start.29
  56.0 3.8 %collective-permute-start.30 = (bf16[128,384]{1,0:T(8,128)(2,1)S(1)}, bf16[128,384]{1,0:T(8,128)(2,1)S(1)}, u32[]{:S(2)}, u32[]{:S(2)}) collective-permute-start(bf16[128,384]{1,0:T(8,128)(2,1)S(1)} %get-tuple-element.44), channel_id=1, source_target_pairs={{0,12},{4,8},{8,4},{12,0},{1,13},{5,9},{9,5},{13,1},{2,14},{6,10},... | collective-permute-start | bytes 294920 | tf_op jit(solution)/shard_map/ppermute | solution.py:76
  59.8 1.7 %collective-permute-done.28 = bf16[128,384]{1,0:T(8,128)(2,1)S(1)} collective-permute-done((bf16[128,384]{1,0:T(8,128)(2,1)S(1)}, bf16[128,384]{1,0:T(8,128)(2,1)S(1)}, u32[]{:S(2)}, u32[]{:S(2)}) %collective-permute-start.28) | collective-permute-done | bytes 98336 | tf_op jit(solution)/shard_map/ppermute | solution.py:76
  61.5 4.8 %collective-permute-done.29 = bf16[128,384]{1,0:T(8,128)(2,1)S(1)} collective-permute-done((bf16[128,384]{1,0:T(8,128)(2,1)S(1)}, bf16[128,384]{1,0:T(8,128)(2,1)S(1)}, u32[]{:S(2)}, u32[]{:S(2)}) %collective-permute-start.29) | collective-permute-done | bytes 98336 | tf_op jit(solution)/shard_map/ppermute | solution.py:76
  66.3 0.0 collective-permute-done.30
  66.3 0.1 convert_add_fusion.refs_0_
  66.3 0.1 collective-permute-start.31
  66.4 1.4 %collective-permute-done.31.refs_1_ = f32[128,384]{1,0:T(8,128)S(1)} collective-permute-done((f32[128,384]{1,0:T(8,128)S(1)}, f32[128,384]{1,0:T(8,128)S(1)}, u32[]{:S(2)}, u32[]{:S(2)}) %collective-permute-start.31) | collective-permute-done | bytes 196640 | tf_op jit(solution)/shard_map/ppermute | solution.py:65
  67.8 10.5 %shard_map.104 = (bf16[144,512]{1,0:T(8,128)(2,1)S(1)}, f32[64,256]{1,0:T(8,128)S(1)}, f32[64,256]{1,0:T(8,128)S(1)}, f32[64,256]{1,0:T(8,128)S(1)}, f32[64,256]{1,0:T(8,128)S(1)}) custom-call(s32[3]{0:T(128)S(1)} %pad_add_fusion.place_ref, f32[128,384]{1,0:T(8,128)S(1)} %convert_add_fusion.refs_0_, f32[128,384]{1,0:T(8,128)S(1)} %collective-permute-done.31.refs_1_, ...), custom_call_target="tpu_custom_call" | custom-call | tf_op jit(solution)/shard_map/pallas_call | solution.py:380
  78.4 2.0 %collective-permute-start.32 = (bf16[144,512]{1,0:T(8,128)(2,1)S(1)}, bf16[144,512]{1,0:T(8,128)(2,1)S(1)}, u32[]{:S(2)}, u32[]{:S(2)}) collective-permute-start(bf16[144,512]{1,0:T(8,128)(2,1)S(1)} %get-tuple-element.45.refs_0_), channel_id=1, source_target_pairs={{4,0},{0,4},{12,8},{8,12},{5,1},{1,5},{13,9},{9,13},{6,2},{2,6},{1... | collective-permute-start | bytes 442376 | tf_op jit(solution)/shard_map/ppermute | solution.py:65
  80.4 0.0 collective-permute-start.33
  80.4 2.4 %collective-permute-start.34 = (bf16[144,512]{1,0:T(8,128)(2,1)S(1)}, bf16[144,512]{1,0:T(8,128)(2,1)S(1)}, u32[]{:S(2)}, u32[]{:S(2)}) collective-permute-start(bf16[144,512]{1,0:T(8,128)(2,1)S(1)} %get-tuple-element.45.refs_0_), channel_id=1, source_target_pairs={{12,0},{8,4},{4,8},{0,12},{13,1},{9,5},{5,9},{1,13},{14,2},{10,6},... | collective-permute-start | bytes 442376 | tf_op jit(solution)/shard_map/ppermute | solution.py:65
  82.9 3.5 %collective-permute-done.32.refs_1_ = bf16[144,512]{1,0:T(8,128)(2,1)S(1)} collective-permute-done((bf16[144,512]{1,0:T(8,128)(2,1)S(1)}, bf16[144,512]{1,0:T(8,128)(2,1)S(1)}, u32[]{:S(2)}, u32[]{:S(2)}) %collective-permute-start.32) | collective-permute-done | bytes 147488 | tf_op jit(solution)/shard_map/ppermute | solution.py:65
  86.3 1.2 %collective-permute-start.35 = (f32[64,256]{1,0:T(8,128)S(1)}, f32[64,256]{1,0:T(8,128)S(1)}, u32[]{:S(2)}, u32[]{:S(2)}) collective-permute-start(f32[64,256]{1,0:T(8,128)S(1)} %get-tuple-element.53), channel_id=1, source_target_pairs={{0,1},{1,0},{2,3},{3,2},{4,5},{5,4},{6,7},{7,6},{8,9},{9,8},{10,11... | collective-permute-start | bytes 196616 | tf_op jit(solution)/shard_map/ppermute | solution.py:76
  87.5 0.6 collective-permute-start.36
  88.1 1.7 %collective-permute-start.37 = (f32[64,256]{1,0:T(8,128)S(1)}, f32[64,256]{1,0:T(8,128)S(1)}, u32[]{:S(2)}, u32[]{:S(2)}) collective-permute-start(f32[64,256]{1,0:T(8,128)S(1)} %get-tuple-element.55), channel_id=1, source_target_pairs={{0,3},{1,2},{2,1},{3,0},{4,7},{5,6},{6,5},{7,4},{8,11},{9,10},{10,... | collective-permute-start | bytes 196616 | tf_op jit(solution)/shard_map/ppermute | solution.py:76
  89.8 4.5 %collective-permute-done.33.refs_2_ = bf16[144,512]{1,0:T(8,128)(2,1)S(1)} collective-permute-done((bf16[144,512]{1,0:T(8,128)(2,1)S(1)}, bf16[144,512]{1,0:T(8,128)(2,1)S(1)}, u32[]{:S(2)}, u32[]{:S(2)}) %collective-permute-start.33) | collective-permute-done | bytes 147488 | tf_op jit(solution)/shard_map/ppermute | solution.py:65
  94.4 0.0 collective-permute-done.34.refs_3_
  94.4 3.1 %shard_map.105 = (bf16[128,1024]{1,0:T(8,128)(2,1)}, bf16[128,1024]{1,0:T(8,128)(2,1)}) custom-call(s32[3]{0:T(128)S(1)} %pad_add_fusion.place_ref, bf16[144,512]{1,0:T(8,128)(2,1)S(1)} %get-tuple-element.45.refs_0_, bf16[144,512]{1,0:T(8,128)(2,1)S(1)} %collective-permute-done.32.refs_1_, bf16[144,512]{1,0:T(8,128)(2,1)S(1)} %collective-permute-done.33.refs_2_, ...), custom_call_target="tpu_custom_call" | custom-call | tf_op jit(solution)/shard_map/pallas_call | solution.py:380
  97.5 0.6 slice_bitcast_fusion
  (37 shorter events, 0.1 us)
Async XLA Ops:
  0.6 1.2 %copy-start = (bf16[4096,1]{0,1:T(2,128)(2,1)S(1)}, bf16[4096,1]{0,1:T(2,128)(2,1)}, u32[]{:S(2)}) copy-start(bf16[4096,1]{0,1:T(2,128)(2,1)} %param.9) | copy-start | bytes 24580
  0.7 1.2 %copy-start.5 = (bf16[512,128]{1,0:T(8,128)(2,1)S(1)}, bf16[512,128]{1,0:T(8,128)(2,1)}, u32[]{:S(2)}) copy-start(bf16[512,128]{1,0:T(8,128)(2,1)} %param.10) | copy-start | bytes 393220
  0.7 34.3 %copy-start.2 = (bf16[1,128,1024]{2,1,0:T(8,128)(2,1)S(1)}, bf16[1,128,1024]{2,1,0:T(8,128)(2,1)}, u32[]{:S(2)}) copy-start(bf16[1,128,1024]{2,1,0:T(8,128)(2,1)} %param.13) | copy-start | bytes 786436
  1.8 33.2 %copy-start.1 = (bf16[1,128,1024]{2,1,0:T(8,128)(2,1)S(1)}, bf16[1,128,1024]{2,1,0:T(8,128)(2,1)}, u32[]{:S(2)}) copy-start(bf16[1,128,1024]{2,1,0:T(8,128)(2,1)} %param.7) | copy-start | bytes 786436
  2.0 1.4 %collective-permute-start = (bf16[528,128]{1,0:T(8,128)(2,1)S(1)}, bf16[528,128]{1,0:T(8,128)(2,1)S(1)}, u32[]{:S(2)}, u32[]{:S(2)}) collective-permute-start(bf16[528,128]{1,0:T(8,128)(2,1)S(1)} %fusion.1), channel_id=1, source_target_pairs={{0,0},{1,1},{2,4},{3,5},{4,2},{5,3},{6,6},{7,7},{8,16},{9,17},{10,... | collective-permute-start | bytes 405512 | tf_op jit(solution)/shard_map/ppermute | solution.py:411
  2.6 16.1 %collective-permute-start.12 = (bf16[768,128]{1,0:T(8,128)(2,1)S(1)}, bf16[768,128]{1,0:T(8,128)(2,1)S(1)}, u32[]{:S(2)}, u32[]{:S(2)}) collective-permute-start(bf16[768,128]{1,0:T(8,128)(2,1)S(1)} %bitcast.28), channel_id=1, source_target_pairs={{0,0},{1,1},{2,4},{3,5},{4,2},{5,3},{6,6},{7,7},{8,16},{9,17},{10,... | collective-permute-start | bytes 589832 | tf_op jit(solution)/shard_map/ppermute | solution.py:411
  3.3 19.4 %collective-permute-start.1 = (bf16[528,128]{1,0:T(8,128)(2,1)S(1)}, bf16[528,128]{1,0:T(8,128)(2,1)S(1)}, u32[]{:S(2)}, u32[]{:S(2)}) collective-permute-start(bf16[528,128]{1,0:T(8,128)(2,1)S(1)} %collective-permute-done.refs_0_.refs_4_), channel_id=1, source_target_pairs={{1,0},{0,1},{3,2},{2,3},{5,4},{4,5},{7,6},{6,7},{9,8},{8,9},{11,10... | collective-permute-start | bytes 405512 | tf_op jit(solution)/shard_map/ppermute | solution.py:65
  6.3 22.8 %collective-permute-start.2 = (bf16[528,128]{1,0:T(8,128)(2,1)S(1)}, bf16[528,128]{1,0:T(8,128)(2,1)S(1)}, u32[]{:S(2)}, u32[]{:S(2)}) collective-permute-start(bf16[528,128]{1,0:T(8,128)(2,1)S(1)} %collective-permute-done.refs_0_.refs_4_), channel_id=1, source_target_pairs={{2,0},{3,1},{0,2},{1,3},{6,4},{7,5},{4,6},{5,7},{10,8},{11,9},{8,1... | collective-permute-start | bytes 405512 | tf_op jit(solution)/shard_map/ppermute | solution.py:65
  16.7 12.4 %collective-permute-start.20 = (bf16[768,128]{1,0:T(8,128)(2,1)S(1)}, bf16[768,128]{1,0:T(8,128)(2,1)S(1)}, u32[]{:S(2)}, u32[]{:S(2)}) collective-permute-start(bf16[768,128]{1,0:T(8,128)(2,1)S(1)} %bitcast.27), channel_id=1, source_target_pairs={{0,0},{1,1},{2,4},{3,5},{4,2},{5,3},{6,6},{7,7},{8,16},{9,17},{10,... | collective-permute-start | bytes 589832 | tf_op jit(solution)/shard_map/ppermute | solution.py:411
  17.4 13.2 %collective-permute-start.3 = (bf16[528,128]{1,0:T(8,128)(2,1)S(1)}, bf16[528,128]{1,0:T(8,128)(2,1)S(1)}, u32[]{:S(2)}, u32[]{:S(2)}) collective-permute-start(bf16[528,128]{1,0:T(8,128)(2,1)S(1)} %collective-permute-done.refs_0_.refs_4_), channel_id=1, source_target_pairs={{3,0},{2,1},{1,2},{0,3},{7,4},{6,5},{5,6},{4,7},{11,8},{10,9},{9,1... | collective-permute-start | bytes 405512 | tf_op jit(solution)/shard_map/ppermute | solution.py:65
  18.7 14.4 %collective-permute-start.4 = (bf16[528,128]{1,0:T(8,128)(2,1)S(1)}, bf16[528,128]{1,0:T(8,128)(2,1)S(1)}, u32[]{:S(2)}, u32[]{:S(2)}) collective-permute-start(bf16[528,128]{1,0:T(8,128)(2,1)S(1)} %collective-permute-done.refs_0_.refs_4_), channel_id=1, source_target_pairs={{16,0},{0,16},{17,1},{1,17},{18,2},{2,18},{19,3},{3,19},{20,4},{4,... | collective-permute-start | bytes 405512 | tf_op jit(solution)/shard_map/ppermute | solution.py:65
  22.7 10.5 %collective-permute-start.5 = (bf16[528,128]{1,0:T(8,128)(2,1)S(1)}, bf16[528,128]{1,0:T(8,128)(2,1)S(1)}, u32[]{:S(2)}, u32[]{:S(2)}) collective-permute-start(bf16[528,128]{1,0:T(8,128)(2,1)S(1)} %collective-permute-done.1.refs_1_.refs_5_), channel_id=1, source_target_pairs={{16,0},{0,16},{17,1},{1,17},{18,2},{2,18},{19,3},{3,19},{20,4},{4,... | collective-permute-start | bytes 405512 | tf_op jit(solution)/shard_map/ppermute | solution.py:65
  29.1 4.6 %collective-permute-start.6 = (bf16[528,128]{1,0:T(8,128)(2,1)S(1)}, bf16[528,128]{1,0:T(8,128)(2,1)S(1)}, u32[]{:S(2)}, u32[]{:S(2)}) collective-permute-start(bf16[528,128]{1,0:T(8,128)(2,1)S(1)} %collective-permute-done.2.refs_2_.refs_6_), channel_id=1, source_target_pairs={{16,0},{0,16},{17,1},{1,17},{18,2},{2,18},{19,3},{3,19},{20,4},{4,... | collective-permute-start | bytes 405512 | tf_op jit(solution)/shard_map/ppermute | solution.py:65
  29.1 9.2 %collective-permute-start.13 = (bf16[768,128]{1,0:T(8,128)(2,1)S(1)}, bf16[768,128]{1,0:T(8,128)(2,1)S(1)}, u32[]{:S(2)}, u32[]{:S(2)}) collective-permute-start(bf16[768,128]{1,0:T(8,128)(2,1)S(1)} %collective-permute-done.12.refs_0_.refs_12_), channel_id=1, source_target_pairs={{1,0},{0,1},{3,2},{2,3},{5,4},{4,5},{7,6},{6,7},{9,8},{8,9},{11,10... | collective-permute-start | bytes 589832 | tf_op jit(solution)/shard_map/ppermute | solution.py:65
  30.6 8.2 %collective-permute-start.22 = (bf16[768,128]{1,0:T(8,128)(2,1)S(1)}, bf16[768,128]{1,0:T(8,128)(2,1)S(1)}, u32[]{:S(2)}, u32[]{:S(2)}) collective-permute-start(bf16[768,128]{1,0:T(8,128)(2,1)S(1)} %collective-permute-done.20.refs_8_.refs_20_), channel_id=1, source_target_pairs={{2,0},{3,1},{0,2},{1,3},{6,4},{7,5},{4,6},{5,7},{10,8},{11,9},{8,1... | collective-permute-start | bytes 589832 | tf_op jit(solution)/shard_map/ppermute | solution.py:65
  33.1 9.5 %collective-permute-start.14 = (bf16[768,128]{1,0:T(8,128)(2,1)S(1)}, bf16[768,128]{1,0:T(8,128)(2,1)S(1)}, u32[]{:S(2)}, u32[]{:S(2)}) collective-permute-start(bf16[768,128]{1,0:T(8,128)(2,1)S(1)} %collective-permute-done.12.refs_0_.refs_12_), channel_id=1, source_target_pairs={{2,0},{3,1},{0,2},{1,3},{6,4},{7,5},{4,6},{5,7},{10,8},{11,9},{8,1... | collective-permute-start | bytes 589832 | tf_op jit(solution)/shard_map/ppermute | solution.py:65
  33.2 9.4 %collective-permute-start.21 = (bf16[768,128]{1,0:T(8,128)(2,1)S(1)}, bf16[768,128]{1,0:T(8,128)(2,1)S(1)}, u32[]{:S(2)}, u32[]{:S(2)}) collective-permute-start(bf16[768,128]{1,0:T(8,128)(2,1)S(1)} %collective-permute-done.20.refs_8_.refs_20_), channel_id=1, source_target_pairs={{1,0},{0,1},{3,2},{2,3},{5,4},{4,5},{7,6},{6,7},{9,8},{8,9},{11,10... | collective-permute-start | bytes 589832 | tf_op jit(solution)/shard_map/ppermute | solution.py:65
  33.7 1.4 %collective-permute-start.7 = (bf16[528,128]{1,0:T(8,128)(2,1)S(1)}, bf16[528,128]{1,0:T(8,128)(2,1)S(1)}, u32[]{:S(2)}, u32[]{:S(2)}) collective-permute-start(bf16[528,128]{1,0:T(8,128)(2,1)S(1)} %collective-permute-done.3.refs_3_.refs_7_), channel_id=1, source_target_pairs={{16,0},{0,16},{17,1},{1,17},{18,2},{2,18},{19,3},{3,19},{20,4},{4,... | collective-permute-start | bytes 405512 | tf_op jit(solution)/shard_map/ppermute | solution.py:65
  36.4 6.7 %collective-permute-start.10 = (bf16[144,128]{1,0:T(8,128)(2,1)S(1)}, bf16[144,128]{1,0:T(8,128)(2,1)S(1)}, u32[]{:S(2)}, u32[]{:S(2)}) collective-permute-start(bf16[144,128]{1,0:T(8,128)(2,1)S(1)} %get-tuple-element.37), channel_id=1, source_target_pairs={{0,12},{4,8},{8,4},{12,0},{1,13},{5,9},{9,5},{13,1},{2,14},{6,10},... | collective-permute-start | bytes 110600 | tf_op jit(solution)/shard_map/ppermute | solution.py:76
  38.3 6.5 %collective-permute-start.8 = (bf16[144,128]{1,0:T(8,128)(2,1)S(1)}, bf16[144,128]{1,0:T(8,128)(2,1)S(1)}, u32[]{:S(2)}, u32[]{:S(2)}) collective-permute-start(bf16[144,128]{1,0:T(8,128)(2,1)S(1)} %get-tuple-element.35), channel_id=1, source_target_pairs={{0,4},{4,0},{8,12},{12,8},{1,5},{5,1},{9,13},{13,9},{2,6},{6,2},{1... | collective-permute-start | bytes 110600 | tf_op jit(solution)/shard_map/ppermute | solution.py:76
  38.8 6.1 %collective-permute-start.9 = (bf16[144,128]{1,0:T(8,128)(2,1)S(1)}, bf16[144,128]{1,0:T(8,128)(2,1)S(1)}, u32[]{:S(2)}, u32[]{:S(2)}) collective-permute-start(bf16[144,128]{1,0:T(8,128)(2,1)S(1)} %get-tuple-element.36), channel_id=1, source_target_pairs={{0,8},{4,12},{8,0},{12,4},{1,9},{5,13},{9,1},{13,5},{2,10},{6,14},... | collective-permute-start | bytes 110600 | tf_op jit(solution)/shard_map/ppermute | solution.py:76
  42.6 3.5 %collective-permute-start.16 = (bf16[768,128]{1,0:T(8,128)(2,1)S(1)}, bf16[768,128]{1,0:T(8,128)(2,1)S(1)}, u32[]{:S(2)}, u32[]{:S(2)}) collective-permute-start(bf16[768,128]{1,0:T(8,128)(2,1)S(1)} %collective-permute-done.12.refs_0_.refs_12_), channel_id=1, source_target_pairs={{16,0},{0,16},{17,1},{1,17},{18,2},{2,18},{19,3},{3,19},{20,4},{4,... | collective-permute-start | bytes 589832 | tf_op jit(solution)/shard_map/ppermute | solution.py:65
  42.6 3.8 %collective-permute-start.24 = (bf16[768,128]{1,0:T(8,128)(2,1)S(1)}, bf16[768,128]{1,0:T(8,128)(2,1)S(1)}, u32[]{:S(2)}, u32[]{:S(2)}) collective-permute-start(bf16[768,128]{1,0:T(8,128)(2,1)S(1)} %collective-permute-done.20.refs_8_.refs_20_), channel_id=1, source_target_pairs={{16,0},{0,16},{17,1},{1,17},{18,2},{2,18},{19,3},{3,19},{20,4},{4,... | collective-permute-start | bytes 589832 | tf_op jit(solution)/shard_map/ppermute | solution.py:65
  43.1 6.9 %collective-permute-start.15 = (bf16[768,128]{1,0:T(8,128)(2,1)S(1)}, bf16[768,128]{1,0:T(8,128)(2,1)S(1)}, u32[]{:S(2)}, u32[]{:S(2)}) collective-permute-start(bf16[768,128]{1,0:T(8,128)(2,1)S(1)} %collective-permute-done.13.refs_1_.refs_13_), channel_id=1, source_target_pairs={{2,0},{3,1},{0,2},{1,3},{6,4},{7,5},{4,6},{5,7},{10,8},{11,9},{8,1... | collective-permute-start | bytes 589832 | tf_op jit(solution)/shard_map/ppermute | solution.py:65
  44.8 7.3 %collective-permute-start.17 = (bf16[768,128]{1,0:T(8,128)(2,1)S(1)}, bf16[768,128]{1,0:T(8,128)(2,1)S(1)}, u32[]{:S(2)}, u32[]{:S(2)}) collective-permute-start(bf16[768,128]{1,0:T(8,128)(2,1)S(1)} %collective-permute-done.13.refs_1_.refs_13_), channel_id=1, source_target_pairs={{16,0},{0,16},{17,1},{1,17},{18,2},{2,18},{19,3},{3,19},{20,4},{4,... | collective-permute-start | bytes 589832 | tf_op jit(solution)/shard_map/ppermute | solution.py:65
  44.9 7.3 %collective-permute-start.23 = (bf16[768,128]{1,0:T(8,128)(2,1)S(1)}, bf16[768,128]{1,0:T(8,128)(2,1)S(1)}, u32[]{:S(2)}, u32[]{:S(2)}) collective-permute-start(bf16[768,128]{1,0:T(8,128)(2,1)S(1)} %collective-permute-done.22.refs_10_.refs_22_), channel_id=1, source_target_pairs={{1,0},{0,1},{3,2},{2,3},{5,4},{4,5},{7,6},{6,7},{9,8},{8,9},{11,10... | collective-permute-start | bytes 589832 | tf_op jit(solution)/shard_map/ppermute | solution.py:65
  46.1 1.3 %collective-permute-start.11 = (f32[144,128]{1,0:T(8,128)S(1)}, f32[144,128]{1,0:T(8,128)S(1)}, u32[]{:S(2)}, u32[]{:S(2)}) collective-permute-start(f32[144,128]{1,0:T(8,128)S(1)} %convert_add_fusion.1.refs_2_), channel_id=1, source_target_pairs={{16,0},{0,16},{17,1},{1,17},{18,2},{2,18},{19,3},{3,19},{20,4},{4,... | collective-permute-start | bytes 221192 | tf_op jit(solution)/shard_map/ppermute | solution.py:65
  46.3 6.3 %collective-permute-start.26 = (bf16[768,128]{1,0:T(8,128)(2,1)S(1)}, bf16[768,128]{1,0:T(8,128)(2,1)S(1)}, u32[]{:S(2)}, u32[]{:S(2)}) collective-permute-start(bf16[768,128]{1,0:T(8,128)(2,1)S(1)} %collective-permute-done.22.refs_10_.refs_22_), channel_id=1, source_target_pairs={{16,0},{0,16},{17,1},{1,17},{18,2},{2,18},{19,3},{3,19},{20,4},{4,... | collective-permute-start | bytes 589832 | tf_op jit(solution)/shard_map/ppermute | solution.py:65
  47.5 5.2 %collective-permute-start.18 = (bf16[768,128]{1,0:T(8,128)(2,1)S(1)}, bf16[768,128]{1,0:T(8,128)(2,1)S(1)}, u32[]{:S(2)}, u32[]{:S(2)}) collective-permute-start(bf16[768,128]{1,0:T(8,128)(2,1)S(1)} %collective-permute-done.14.refs_2_.refs_14_), channel_id=1, source_target_pairs={{16,0},{0,16},{17,1},{1,17},{18,2},{2,18},{19,3},{3,19},{20,4},{4,... | collective-permute-start | bytes 589832 | tf_op jit(solution)/shard_map/ppermute | solution.py:65
  50.0 2.7 %collective-permute-start.25 = (bf16[768,128]{1,0:T(8,128)(2,1)S(1)}, bf16[768,128]{1,0:T(8,128)(2,1)S(1)}, u32[]{:S(2)}, u32[]{:S(2)}) collective-permute-start(bf16[768,128]{1,0:T(8,128)(2,1)S(1)} %collective-permute-done.21.refs_9_.refs_21_), channel_id=1, source_target_pairs={{16,0},{0,16},{17,1},{1,17},{18,2},{2,18},{19,3},{3,19},{20,4},{4,... | collective-permute-start | bytes 589832 | tf_op jit(solution)/shard_map/ppermute | solution.py:65
  52.2 1.4 %collective-permute-start.19 = (bf16[768,128]{1,0:T(8,128)(2,1)S(1)}, bf16[768,128]{1,0:T(8,128)(2,1)S(1)}, u32[]{:S(2)}, u32[]{:S(2)}) collective-permute-start(bf16[768,128]{1,0:T(8,128)(2,1)S(1)} %collective-permute-done.15.refs_3_.refs_15_), channel_id=1, source_target_pairs={{16,0},{0,16},{17,1},{1,17},{18,2},{2,18},{19,3},{3,19},{20,4},{4,... | collective-permute-start | bytes 589832 | tf_op jit(solution)/shard_map/ppermute | solution.py:65
  52.2 1.7 %collective-permute-start.27 = (bf16[768,128]{1,0:T(8,128)(2,1)S(1)}, bf16[768,128]{1,0:T(8,128)(2,1)S(1)}, u32[]{:S(2)}, u32[]{:S(2)}) collective-permute-start(bf16[768,128]{1,0:T(8,128)(2,1)S(1)} %collective-permute-done.23.refs_11_.refs_23_), channel_id=1, source_target_pairs={{16,0},{0,16},{17,1},{1,17},{18,2},{2,18},{19,3},{3,19},{20,4},{4,... | collective-permute-start | bytes 589832 | tf_op jit(solution)/shard_map/ppermute | solution.py:65
  55.3 6.2 %collective-permute-start.28 = (bf16[128,384]{1,0:T(8,128)(2,1)S(1)}, bf16[128,384]{1,0:T(8,128)(2,1)S(1)}, u32[]{:S(2)}, u32[]{:S(2)}) collective-permute-start(bf16[128,384]{1,0:T(8,128)(2,1)S(1)} %get-tuple-element.42), channel_id=1, source_target_pairs={{0,4},{4,0},{8,12},{12,8},{1,5},{5,1},{9,13},{13,9},{2,6},{6,2},{1... | collective-permute-start | bytes 294920 | tf_op jit(solution)/shard_map/ppermute | solution.py:76
  55.4 10.9 %collective-permute-start.29 = (bf16[128,384]{1,0:T(8,128)(2,1)S(1)}, bf16[128,384]{1,0:T(8,128)(2,1)S(1)}, u32[]{:S(2)}, u32[]{:S(2)}) collective-permute-start(bf16[128,384]{1,0:T(8,128)(2,1)S(1)} %get-tuple-element.43), channel_id=1, source_target_pairs={{0,8},{4,12},{8,0},{12,4},{1,9},{5,13},{9,1},{13,5},{2,10},{6,14},... | collective-permute-start | bytes 294920 | tf_op jit(solution)/shard_map/ppermute | solution.py:76
  56.0 10.3 %collective-permute-start.30 = (bf16[128,384]{1,0:T(8,128)(2,1)S(1)}, bf16[128,384]{1,0:T(8,128)(2,1)S(1)}, u32[]{:S(2)}, u32[]{:S(2)}) collective-permute-start(bf16[128,384]{1,0:T(8,128)(2,1)S(1)} %get-tuple-element.44), channel_id=1, source_target_pairs={{0,12},{4,8},{8,4},{12,0},{1,13},{5,9},{9,5},{13,1},{2,14},{6,10},... | collective-permute-start | bytes 294920 | tf_op jit(solution)/shard_map/ppermute | solution.py:76
  66.3 1.6 %copy-start.3 = (f32[1,128,512]{2,1,0:T(8,128)S(1)}, f32[1,128,512]{2,1,0:T(8,128)}, u32[]{:S(2)}) copy-start(f32[1,128,512]{2,1,0:T(8,128)} %param.11) | copy-start | bytes 786436
  66.3 1.6 %copy-start.4 = (f32[1,512,128]{2,1,0:T(8,128)S(1)}, f32[1,512,128]{2,1,0:T(8,128)}, u32[]{:S(2)}) copy-start(f32[1,512,128]{2,1,0:T(8,128)} %param.12) | copy-start | bytes 786436
  66.3 1.5 %collective-permute-start.31 = (f32[128,384]{1,0:T(8,128)S(1)}, f32[128,384]{1,0:T(8,128)S(1)}, u32[]{:S(2)}, u32[]{:S(2)}) collective-permute-start(f32[128,384]{1,0:T(8,128)S(1)} %convert_add_fusion.refs_0_), channel_id=1, source_target_pairs={{16,0},{0,16},{17,1},{1,17},{18,2},{2,18},{19,3},{3,19},{20,4},{4,... | collective-permute-start | bytes 589832 | tf_op jit(solution)/shard_map/ppermute | solution.py:65
  78.4 7.9 %collective-permute-start.32 = (bf16[144,512]{1,0:T(8,128)(2,1)S(1)}, bf16[144,512]{1,0:T(8,128)(2,1)S(1)}, u32[]{:S(2)}, u32[]{:S(2)}) collective-permute-start(bf16[144,512]{1,0:T(8,128)(2,1)S(1)} %get-tuple-element.45.refs_0_), channel_id=1, source_target_pairs={{4,0},{0,4},{12,8},{8,12},{5,1},{1,5},{13,9},{9,13},{6,2},{2,6},{1... | collective-permute-start | bytes 442376 | tf_op jit(solution)/shard_map/ppermute | solution.py:65
  80.4 13.9 %collective-permute-start.33 = (bf16[144,512]{1,0:T(8,128)(2,1)S(1)}, bf16[144,512]{1,0:T(8,128)(2,1)S(1)}, u32[]{:S(2)}, u32[]{:S(2)}) collective-permute-start(bf16[144,512]{1,0:T(8,128)(2,1)S(1)} %get-tuple-element.45.refs_0_), channel_id=1, source_target_pairs={{8,0},{12,4},{0,8},{4,12},{9,1},{13,5},{1,9},{5,13},{10,2},{14,6},... | collective-permute-start | bytes 442376 | tf_op jit(solution)/shard_map/ppermute | solution.py:65
  80.4 13.9 %collective-permute-start.34 = (bf16[144,512]{1,0:T(8,128)(2,1)S(1)}, bf16[144,512]{1,0:T(8,128)(2,1)S(1)}, u32[]{:S(2)}, u32[]{:S(2)}) collective-permute-start(bf16[144,512]{1,0:T(8,128)(2,1)S(1)} %get-tuple-element.45.refs_0_), channel_id=1, source_target_pairs={{12,0},{8,4},{4,8},{0,12},{13,1},{9,5},{5,9},{1,13},{14,2},{10,6},... | collective-permute-start | bytes 442376 | tf_op jit(solution)/shard_map/ppermute | solution.py:65
  86.3 11.2 %collective-permute-start.35 = (f32[64,256]{1,0:T(8,128)S(1)}, f32[64,256]{1,0:T(8,128)S(1)}, u32[]{:S(2)}, u32[]{:S(2)}) collective-permute-start(f32[64,256]{1,0:T(8,128)S(1)} %get-tuple-element.53), channel_id=1, source_target_pairs={{0,1},{1,0},{2,3},{3,2},{4,5},{5,4},{6,7},{7,6},{8,9},{9,8},{10,11... | collective-permute-start | bytes 196616 | tf_op jit(solution)/shard_map/ppermute | solution.py:76
  87.5 10.0 %collective-permute-start.36 = (f32[64,256]{1,0:T(8,128)S(1)}, f32[64,256]{1,0:T(8,128)S(1)}, u32[]{:S(2)}, u32[]{:S(2)}) collective-permute-start(f32[64,256]{1,0:T(8,128)S(1)} %get-tuple-element.54), channel_id=1, source_target_pairs={{0,2},{1,3},{2,0},{3,1},{4,6},{5,7},{6,4},{7,5},{8,10},{9,11},{10,... | collective-permute-start | bytes 196616 | tf_op jit(solution)/shard_map/ppermute | solution.py:76
  88.1 9.4 %collective-permute-start.37 = (f32[64,256]{1,0:T(8,128)S(1)}, f32[64,256]{1,0:T(8,128)S(1)}, u32[]{:S(2)}, u32[]{:S(2)}) collective-permute-start(f32[64,256]{1,0:T(8,128)S(1)} %get-tuple-element.55), channel_id=1, source_target_pairs={{0,3},{1,2},{2,1},{3,0},{4,7},{5,6},{6,5},{7,4},{8,11},{9,10},{10,... | collective-permute-start | bytes 196616 | tf_op jit(solution)/shard_map/ppermute | solution.py:76
